TPU v7x, 32 devices: a whole 2x2x4 slice. The times are simulated.
32 devices in a mesh: wide: 8 (over z, y), narrow: 4 (over x, core).
Axes of the slice: x: 2, y: 2, z: 4, core: 2. Of those that a mesh axis runs over, the one named last changes fastest.
Arguments:
- tables_in: bfloat16 [8192, 768], P(('wide', 'narrow')), may hold values from -6 to 6
- cotangent: bfloat16 [8192, 768], P(('wide', 'narrow')), may hold values from -6 to 6
- cell_ids: int32 [32, 256], P(('wide', 'narrow')), may hold values from 0 to 241, as said below
- lengths: int32 [32], P(('wide', 'narrow')), may hold values from 64 to 256
- qkv_weight: bfloat16 [2, 768, 2304], P(None, 'narrow'), may hold values from -0.21875 to 0.21875
- q_bias: bfloat16 [2, 768], P(None, 'narrow'), may hold values from -3 to 3
- v_bias: bfloat16 [2, 768], P(None, 'narrow'), may hold values from -3 to 3
- o_weight: bfloat16 [2, 768, 768], P(None, 'narrow'), may hold values from -0.875 to 0.875
- o_bias: bfloat16 [2, 768], P(None, 'narrow'), may hold values from -2 to 2
- norm1_gain: bfloat16 [2, 768], P(None, 'narrow'), may hold values from 0.5 to 1.5
- norm1_bias: bfloat16 [2, 768], P(None, 'narrow'), may hold values from -2 to 2
- in_weight: bfloat16 [2, 768, 3072], P(None, 'narrow'), may hold values from -0.21875 to 0.21875
- in_bias: bfloat16 [2, 3072], P(None, 'narrow'), may hold values from -3 to 3
- out_weight: bfloat16 [2, 3072, 768], P(None, 'narrow'), may hold values from -0.109375 to 0.109375
- out_bias: bfloat16 [2, 768], P(None, 'narrow'), may hold values from -2 to 2
- norm2_gain: bfloat16 [2, 768], P(None, 'narrow'), may hold values from 0.5 to 1.5
- norm2_bias: bfloat16 [2, 768], P(None, 'narrow'), may hold values from -2 to 2
Outputs:
- mixed_out: bfloat16 [8192, 768], P(('wide', 'narrow'))
- input_grad: bfloat16 [8192, 768], P(('wide', 'narrow'))
- qkv_grad: float32 [2, 768, 2304], P(None, 'narrow')
- q_bias_grad: float32 [2, 768], P(None, 'narrow')
- v_bias_grad: float32 [2, 768], P(None, 'narrow')
- o_weight_grad: float32 [2, 768, 768], P(None, 'narrow')
- o_bias_grad: float32 [2, 768], P(None, 'narrow')
- norm1_gain_grad: float32 [2, 768], P(None, 'narrow')
- norm1_bias_grad: float32 [2, 768], P(None, 'narrow')
- in_weight_grad: float32 [2, 768, 3072], P(None, 'narrow')
- in_bias_grad: float32 [2, 3072], P(None, 'narrow')
- out_weight_grad: float32 [2, 3072, 768], P(None, 'narrow')
- out_bias_grad: float32 [2, 768], P(None, 'narrow')
- norm2_gain_grad: float32 [2, 768], P(None, 'narrow')
- norm2_bias_grad: float32 [2, 768], P(None, 'narrow')
Inputs may be any that keep to these rules, and one draw needn't show every extreme that they name: `cell_ids`: along a table the ids never fall; id 0 marks the question tokens at the table's head, never fewer than 16 of them; every other id marks one cell of that table.
All inputs are finite; a program needn't handle non-finite values.
Results may differ from a plain program's by a relative error of at most 0.023.
Values may be sent and summed in bfloat16 or wider, within the bound.
No kernel may reach another device: no remote copies, remote signals or barrier semaphores. Data moves between devices by JAX's collectives and lax.ppermute only.
A program may use at most 320 MiB of HBM per device.

v0:
```python
import math

import jax
import jax.numpy as jnp
from jax import lax
from jax.sharding import PartitionSpec as P

HEADS = 12


norm_eps = 1e-12
masked_score = -1000000000.0


def from_behind(block, axis, distance):
    devices = range(lax.axis_size(axis))
    route = [((i - distance) % len(devices), i) for i in devices]
    return lax.ppermute(block, axis, route)


def shifted_2(value, axis, steps):
    count = lax.axis_size(axis)
    initial, last = (max(0, -steps), min(count, count - steps))
    return lax.ppermute(value, axis, [(source, source + steps) for source in range(initial, last)])


def plain_dot(lhs_mat, rhs_mat):
    return jnp.dot(lhs_mat, rhs_mat, preferred_element_type=jnp.float32)


def rows_dot(lhs_mat, rhs_mat):
    return lax.dot_general(
        lhs_mat, rhs_mat, (((0,), (0,)), ((), ())), preferred_element_type=jnp.float32
    )


def cols_dot(lhs_mat, rhs_mat):
    return lax.dot_general(
        lhs_mat, rhs_mat, (((1,), (1,)), ((), ())), preferred_element_type=jnp.float32
    )


def normalize(residual, gain_vec, shift_bias):
    center = residual - jnp.mean(residual, axis=-1, keepdims=True)
    spread = jnp.mean(center * center, axis=-1, keepdims=True)
    inverse = lax.rsqrt(spread + norm_eps)
    unit_rows = center * inverse
    return (
        unit_rows * gain_vec.astype(jnp.float32) + shift_bias.astype(jnp.float32),
        unit_rows,
        inverse,
    )


def normalize_back(grad_unit, unit_rows, inverse):
    centered = grad_unit - jnp.mean(grad_unit, axis=-1, keepdims=True)
    return inverse * (
        centered - unit_rows * jnp.mean(grad_unit * unit_rows, axis=-1, keepdims=True)
    )


def table_scores(query_rows, key_rows, cell_row, length, head_count):
    seq_len, model_width = query_rows.shape
    head_size = model_width // head_count
    query_h = query_rows.reshape(seq_len, head_count, head_size)
    key_h = key_rows.reshape(seq_len, head_count, head_size)
    raw_scores = jnp.einsum("qhd,khd->hqk", query_h, key_h, preferred_element_type=jnp.float32) * (
        1.0 / math.sqrt(head_size)
    )
    position = jnp.arange(seq_len, dtype=jnp.int32)
    same_cell = (
        (cell_row[:, None] == cell_row[None, :])
        | (cell_row[None, :] == 0)
        | (cell_row[:, None] == 0)
    )
    allowed = same_cell & (position[None, :] < length)
    return jnp.where(allowed[None], raw_scores, masked_score)


def table_forward(query_rows, key_rows, value_rows, cell_row, length, head_count):
    seq_len, model_width = value_rows.shape
    scores = table_scores(query_rows, key_rows, cell_row, length, head_count)
    row_top = jnp.max(scores, axis=-1, keepdims=True)
    shifted = jnp.exp(scores - row_top)
    row_total = jnp.sum(shifted, axis=-1, keepdims=True)
    attn_probs = (shifted / row_total).astype(jnp.bfloat16)
    value_h = value_rows.reshape(seq_len, head_count, model_width // head_count)
    context = jnp.einsum("hqk,khd->qhd", attn_probs, value_h, preferred_element_type=jnp.float32)
    return (
        context.reshape(seq_len, model_width).astype(jnp.bfloat16),
        (row_top + jnp.log(row_total))[..., 0],
    )


def table_backward(
    query_rows, key_rows, value_rows, d_context, log_total, cell_row, length, head_count
):
    seq_len, model_width = query_rows.shape
    head_size = model_width // head_count
    score_scale = 1.0 / math.sqrt(head_size)
    scores = table_scores(query_rows, key_rows, cell_row, length, head_count)
    attn_probs = jnp.exp(scores - log_total[:, :, None])
    query_h = query_rows.reshape(seq_len, head_count, head_size)
    key_h = key_rows.reshape(seq_len, head_count, head_size)
    value_h = value_rows.reshape(seq_len, head_count, head_size)
    grad_h = d_context.reshape(seq_len, head_count, head_size)
    d_probs = jnp.einsum("qhd,khd->hqk", grad_h, value_h, preferred_element_type=jnp.float32)
    row_inner = jnp.sum(attn_probs * d_probs, axis=-1, keepdims=True)
    d_scores = (attn_probs * (d_probs - row_inner)).astype(jnp.bfloat16)
    d_query = (
        jnp.einsum("hqk,khd->qhd", d_scores, key_h, preferred_element_type=jnp.float32)
        * score_scale
    )
    d_key = (
        jnp.einsum("hqk,qhd->khd", d_scores, query_h, preferred_element_type=jnp.float32)
        * score_scale
    )
    d_value = jnp.einsum(
        "hqk,qhd->khd", attn_probs.astype(jnp.bfloat16), grad_h, preferred_element_type=jnp.float32
    )
    return (
        d_query.reshape(seq_len, model_width),
        d_key.reshape(seq_len, model_width),
        d_value.reshape(seq_len, model_width),
    )


def layer_forward(inputs, cell_rows, length_rows, full_layer, head_count):
    (
        w_qkv,
        b_query,
        b_value,
        w_attn,
        b_attn,
        gain_one,
        bias_one,
        w_in,
        b_in,
        w_out,
        b_out,
        gain_two,
        bias_two,
    ) = full_layer
    model_width = inputs.shape[1]
    tables, seq_len = cell_rows.shape
    projected = plain_dot(inputs, w_qkv)
    query_rows = (projected[:, :model_width] + b_query.astype(jnp.float32)).astype(jnp.bfloat16)
    key_rows = projected[:, model_width : 2 * model_width].astype(jnp.bfloat16)
    value_rows = (projected[:, 2 * model_width :] + b_value.astype(jnp.float32)).astype(
        jnp.bfloat16
    )

    def per_table(pieces):
        return table_forward(pieces[0], pieces[1], pieces[2], pieces[3], pieces[4], head_count)

    context, log_total = lax.map(
        per_table,
        (
            query_rows.reshape(tables, seq_len, model_width),
            key_rows.reshape(tables, seq_len, model_width),
            value_rows.reshape(tables, seq_len, model_width),
            cell_rows,
            length_rows,
        ),
    )
    context = context.reshape(tables * seq_len, model_width)
    attention = plain_dot(context, w_attn) + b_attn.astype(jnp.float32)
    normed, unit_attn, scale_attn = normalize(
        inputs.astype(jnp.float32) + attention, gain_one, bias_one
    )
    normed_low = normed.astype(jnp.bfloat16)
    pre_act = plain_dot(normed_low, w_in) + b_in.astype(jnp.float32)
    hidden = jax.nn.gelu(pre_act, approximate=False).astype(jnp.bfloat16)
    ffn_out = plain_dot(hidden, w_out) + b_out.astype(jnp.float32)
    result, unit_ffn, scale_ffn = normalize(normed + ffn_out, gain_two, bias_two)
    stored = (
        inputs,
        query_rows,
        key_rows,
        value_rows,
        context,
        log_total,
        unit_attn,
        scale_attn,
        normed_low,
        pre_act,
        hidden,
        unit_ffn,
        scale_ffn,
    )
    return (result.astype(jnp.bfloat16), stored)


def layer_backward(stored, grad_rows, cell_rows, length_rows, full_layer, head_count):
    (
        inputs,
        query_rows,
        key_rows,
        value_rows,
        context,
        log_total,
        unit_attn,
        scale_attn,
        normed_low,
        pre_act,
        hidden,
        unit_ffn,
        scale_ffn,
    ) = stored
    (
        w_qkv,
        b_query,
        b_value,
        w_attn,
        b_attn,
        gain_one,
        bias_one,
        w_in,
        b_in,
        w_out,
        b_out,
        gain_two,
        bias_two,
    ) = full_layer
    model_width = inputs.shape[1]
    tables, seq_len = cell_rows.shape
    grad_out = grad_rows.astype(jnp.float32)
    d_gain_two = jnp.sum(grad_out * unit_ffn, axis=0)
    d_bias_two = jnp.sum(grad_out, axis=0)
    d_resid_two = normalize_back(grad_out * gain_two.astype(jnp.float32), unit_ffn, scale_ffn)
    d_ffn = d_resid_two.astype(jnp.bfloat16)
    d_b_out = jnp.sum(d_ffn, axis=0, dtype=jnp.float32)
    d_w_out = rows_dot(hidden, d_ffn)
    d_hidden = cols_dot(d_ffn, w_out)
    gelu_pull = jax.vjp(lambda values_in: jax.nn.gelu(values_in, approximate=False), pre_act)[1]
    d_pre = gelu_pull(d_hidden)[0].astype(jnp.bfloat16)
    d_b_in = jnp.sum(d_pre, axis=0, dtype=jnp.float32)
    d_w_in = rows_dot(normed_low, d_pre)
    d_normed = d_resid_two + cols_dot(d_pre, w_in)
    d_gain_one = jnp.sum(d_normed * unit_attn, axis=0)
    d_bias_one = jnp.sum(d_normed, axis=0)
    d_resid_one = normalize_back(d_normed * gain_one.astype(jnp.float32), unit_attn, scale_attn)
    d_attention = d_resid_one.astype(jnp.bfloat16)
    d_b_attn = jnp.sum(d_attention, axis=0, dtype=jnp.float32)
    d_w_attn = rows_dot(context, d_attention)
    d_context = cols_dot(d_attention, w_attn).astype(jnp.bfloat16)

    def per_table(pieces):
        return table_backward(
            pieces[0], pieces[1], pieces[2], pieces[3], pieces[4], pieces[5], pieces[6], head_count
        )

    d_query, d_key, d_value = lax.map(
        per_table,
        (
            query_rows.reshape(tables, seq_len, model_width),
            key_rows.reshape(tables, seq_len, model_width),
            value_rows.reshape(tables, seq_len, model_width),
            d_context.reshape(tables, seq_len, model_width),
            log_total,
            cell_rows,
            length_rows,
        ),
    )
    d_query = d_query.reshape(tables * seq_len, model_width).astype(jnp.bfloat16)
    d_key = d_key.reshape(tables * seq_len, model_width).astype(jnp.bfloat16)
    d_value = d_value.reshape(tables * seq_len, model_width).astype(jnp.bfloat16)
    d_projected = jnp.concatenate([d_query, d_key, d_value], axis=1)
    d_b_query = jnp.sum(d_query, axis=0, dtype=jnp.float32)
    d_b_value = jnp.sum(d_value, axis=0, dtype=jnp.float32)
    d_w_qkv = rows_dot(inputs, d_projected)
    d_inputs = d_resid_one + cols_dot(d_projected, w_qkv)
    gradients = (
        d_w_qkv,
        d_b_query,
        d_b_value,
        d_w_attn,
        d_b_attn,
        d_gain_one,
        d_bias_one,
        d_w_in,
        d_b_in,
        d_w_out,
        d_b_out,
        d_gain_two,
        d_bias_two,
    )
    return (d_inputs.astype(jnp.bfloat16), gradients)


def body(
    tables_in,
    cotangent,
    cell_ids,
    lengths,
    qkv_weight,
    q_bias,
    v_bias,
    o_weight,
    o_bias,
    norm1_gain,
    norm1_bias,
    in_weight,
    in_bias,
    out_weight,
    out_bias,
    norm2_gain,
    norm2_bias,
):
    section_width = lax.axis_size("wide") // 2
    section_index = lax.axis_index("wide") // section_width
    is_first = section_index == 0
    head_count = HEADS
    token_rows, model_width = tables_in.shape
    tables, seq_len = cell_ids.shape
    swapped = from_behind(jnp.where(is_first, cotangent, tables_in), "wide", section_width)
    other_cells, other_lengths = from_behind((cell_ids, lengths), "wide", section_width)
    micro_inputs = (tables_in, swapped)
    micro_grads = (swapped, cotangent)
    micro_cells = (
        jnp.where(is_first, cell_ids, other_cells),
        jnp.where(is_first, other_cells, cell_ids),
    )
    micro_lengths = (
        jnp.where(is_first, lengths, other_lengths),
        jnp.where(is_first, other_lengths, lengths),
    )
    own_layer = [
        lax.dynamic_index_in_dim(weight, section_index, 0, keepdims=False)
        for weight in (
            qkv_weight,
            q_bias,
            v_bias,
            o_weight,
            o_bias,
            norm1_gain,
            norm1_bias,
            in_weight,
            in_bias,
            out_weight,
            out_bias,
            norm2_gain,
            norm2_bias,
        )
    ]
    full_layer = (
        lax.all_gather(own_layer[0], "narrow", axis=0, tiled=True),
        lax.all_gather(own_layer[1], "narrow", axis=0, tiled=True),
        lax.all_gather(own_layer[2], "narrow", axis=0, tiled=True),
        lax.all_gather(own_layer[3], "narrow", axis=0, tiled=True),
        lax.all_gather(own_layer[4], "narrow", axis=0, tiled=True),
        lax.all_gather(own_layer[5], "narrow", axis=0, tiled=True),
        lax.all_gather(own_layer[6], "narrow", axis=0, tiled=True),
        lax.all_gather(own_layer[7], "narrow", axis=0, tiled=True),
        lax.all_gather(own_layer[8], "narrow", axis=0, tiled=True),
        lax.all_gather(own_layer[9], "narrow", axis=0, tiled=True),
        lax.all_gather(own_layer[10], "narrow", axis=0, tiled=True),
        lax.all_gather(own_layer[11], "narrow", axis=0, tiled=True),
        lax.all_gather(own_layer[12], "narrow", axis=0, tiled=True),
    )
    hidden_width = full_layer[7].shape[1]

    def run_forward(inputs, cell_rows, length_rows):
        return layer_forward(inputs, cell_rows, length_rows, full_layer, head_count)

    def spare_forward(inputs, cell_rows, length_rows):
        zero_float = jnp.zeros((token_rows, model_width), jnp.float32)
        zero_low = jnp.zeros((token_rows, model_width), jnp.bfloat16)
        column = jnp.zeros((token_rows, 1), jnp.float32)
        stored = (
            zero_low,
            zero_low,
            zero_low,
            zero_low,
            zero_low,
            jnp.zeros((tables, head_count, seq_len), jnp.float32),
            zero_float,
            column,
            zero_low,
            jnp.zeros((token_rows, hidden_width), jnp.float32),
            jnp.zeros((token_rows, hidden_width), jnp.bfloat16),
            zero_float,
            column,
        )
        return (zero_low, stored)

    def run_backward(stored, grad_rows, cell_rows, length_rows):
        return layer_backward(stored, grad_rows, cell_rows, length_rows, full_layer, head_count)

    def spare_backward(*operands):
        return (
            jnp.zeros((token_rows, model_width), jnp.bfloat16),
            tuple((jnp.zeros(weight.shape, jnp.float32) for weight in full_layer)),
        )

    micro_count = 2
    arrived = jnp.zeros_like(tables_in)
    returned = jnp.zeros_like(tables_in)
    forward_inputs = []
    forward_cells = []
    forward_lengths = []
    forward_kept = []
    forward_outputs = []
    backward_rows = []
    totals = tuple((jnp.zeros(weight.shape, jnp.float32) for weight in full_layer))
    for tick_index in range(micro_count + 2):
        if tick_index <= micro_count:
            first_micro = min(tick_index, micro_count - 1)
            second_micro = max(tick_index - 1, 0)
            active = jnp.where(is_first, tick_index < micro_count, tick_index >= 1)
            inputs_now = jnp.where(is_first, micro_inputs[first_micro], arrived)
            cells_now = jnp.where(is_first, micro_cells[first_micro], micro_cells[second_micro])
            lengths_now = jnp.where(
                is_first, micro_lengths[first_micro], micro_lengths[second_micro]
            )
            result_now, kept_now = lax.cond(
                active, run_forward, spare_forward, inputs_now, cells_now, lengths_now
            )
            forward_inputs.append(inputs_now)
            forward_cells.append(cells_now)
            forward_lengths.append(lengths_now)
            forward_kept.append(kept_now)
            forward_outputs.append(result_now)
            if tick_index < micro_count:
                arrived = shifted_2(result_now, "wide", section_width)
        if tick_index >= 1:
            early_tick = min(max(tick_index - 2, 0), micro_count)
            late_tick = min(tick_index, micro_count)
            active = jnp.where(is_first, tick_index >= 2, tick_index <= micro_count)
            grad_now = jnp.where(
                is_first, returned, micro_grads[min(tick_index - 1, micro_count - 1)]
            )
            cells_back = jnp.where(is_first, forward_cells[early_tick], forward_cells[late_tick])
            lengths_back = jnp.where(
                is_first, forward_lengths[early_tick], forward_lengths[late_tick]
            )
            kept_back = jax.tree.map(
                lambda near_value, far_value: jnp.where(is_first, near_value, far_value),
                forward_kept[early_tick],
                forward_kept[late_tick],
            )
            d_rows, gradients = lax.cond(
                active, run_backward, spare_backward, kept_back, grad_now, cells_back, lengths_back
            )
            totals = tuple((running + gradient for running, gradient in zip(totals, gradients)))
            backward_rows.append(d_rows)
            if tick_index <= micro_count:
                returned = shifted_2(d_rows, "wide", -section_width)
    handed = from_behind(
        jnp.where(is_first, backward_rows[2], forward_outputs[1]), "wide", section_width
    )
    mixed_out = jnp.where(is_first, handed, forward_outputs[2])
    input_grad = jnp.where(is_first, backward_rows[1], handed)
    shards = (
        lax.psum_scatter(
            totals[0].astype(jnp.bfloat16), "narrow", scatter_dimension=0, tiled=True
        ).astype(jnp.float32),
        lax.psum_scatter(
            totals[1].astype(jnp.bfloat16), "narrow", scatter_dimension=0, tiled=True
        ).astype(jnp.float32),
        lax.psum_scatter(
            totals[2].astype(jnp.bfloat16), "narrow", scatter_dimension=0, tiled=True
        ).astype(jnp.float32),
        lax.psum_scatter(
            totals[3].astype(jnp.bfloat16), "narrow", scatter_dimension=0, tiled=True
        ).astype(jnp.float32),
        lax.psum_scatter(
            totals[4].astype(jnp.bfloat16), "narrow", scatter_dimension=0, tiled=True
        ).astype(jnp.float32),
        lax.psum_scatter(
            totals[5].astype(jnp.bfloat16), "narrow", scatter_dimension=0, tiled=True
        ).astype(jnp.float32),
        lax.psum_scatter(
            totals[6].astype(jnp.bfloat16), "narrow", scatter_dimension=0, tiled=True
        ).astype(jnp.float32),
        lax.psum_scatter(
            totals[7].astype(jnp.bfloat16), "narrow", scatter_dimension=0, tiled=True
        ).astype(jnp.float32),
        lax.psum_scatter(
            totals[8].astype(jnp.bfloat16), "narrow", scatter_dimension=0, tiled=True
        ).astype(jnp.float32),
        lax.psum_scatter(
            totals[9].astype(jnp.bfloat16), "narrow", scatter_dimension=0, tiled=True
        ).astype(jnp.float32),
        lax.psum_scatter(
            totals[10].astype(jnp.bfloat16), "narrow", scatter_dimension=0, tiled=True
        ).astype(jnp.float32),
        lax.psum_scatter(
            totals[11].astype(jnp.bfloat16), "narrow", scatter_dimension=0, tiled=True
        ).astype(jnp.float32),
        lax.psum_scatter(
            totals[12].astype(jnp.bfloat16), "narrow", scatter_dimension=0, tiled=True
        ).astype(jnp.float32),
    )

    def by_section(one_shard):
        blank_rows = jnp.zeros_like(one_shard)
        return jnp.stack(
            [jnp.where(is_first, one_shard, blank_rows), jnp.where(is_first, blank_rows, one_shard)]
        )

    results = lax.psum(
        (
            by_section(shards[0]),
            by_section(shards[1]),
            by_section(shards[2]),
            by_section(shards[3]),
            by_section(shards[4]),
            by_section(shards[5]),
            by_section(shards[6]),
            by_section(shards[7]),
            by_section(shards[8]),
            by_section(shards[9]),
            by_section(shards[10]),
            by_section(shards[11]),
            by_section(shards[12]),
        ),
        "wide",
    )
    return (
        mixed_out,
        input_grad,
        results[0],
        results[1],
        results[2],
        results[3],
        results[4],
        results[5],
        results[6],
        results[7],
        results[8],
        results[9],
        results[10],
        results[11],
        results[12],
    )


def solution(mesh):
    placed = (
        P(("wide", "narrow"), None),
        P(("wide", "narrow"), None),
        P(("wide", "narrow"), None),
        P(("wide", "narrow")),
        P(None, "narrow", None),
        P(None, "narrow"),
        P(None, "narrow"),
        P(None, "narrow", None),
        P(None, "narrow"),
        P(None, "narrow"),
        P(None, "narrow"),
        P(None, "narrow", None),
        P(None, "narrow"),
        P(None, "narrow", None),
        P(None, "narrow"),
        P(None, "narrow"),
        P(None, "narrow"),
    )
    return jax.shard_map(
        body,
        mesh=mesh,
        in_specs=placed,
        out_specs=(
            P(("wide", "narrow"), None),
            P(("wide", "narrow"), None),
            P(None, "narrow", None),
            P(None, "narrow"),
            P(None, "narrow"),
            P(None, "narrow", None),
            P(None, "narrow"),
            P(None, "narrow"),
            P(None, "narrow"),
            P(None, "narrow", None),
            P(None, "narrow"),
            P(None, "narrow", None),
            P(None, "narrow"),
            P(None, "narrow"),
            P(None, "narrow"),
        ),
        check_vma=False,
    )
```

profile of v0, /device:TPU:0, one launch (start us, length us, event | category | flops | bytes accessed | tf_op | source)
XLA Modules:
  0.0 1088.6 jit_solution(4235055731354511011)
XLA Ops:
  7.3 1.8 constant_dynamic-slice_fusion.9
  9.2 2.1 constant_dynamic-slice_fusion.12
  12.7 2.4 constant_dynamic-slice_fusion.3
  15.1 4.1 collective-permute-start.2
  20.1 2.8 collective-permute-start
  26.9 10.5 all-reduce.20
  40.5 5.2 all-gather.8
  52.0 11.3 %all-gather.18.cloned.1.call-done = bf16[1,768,2304]{2,1,0:T(8,128)(2,1)} async-done(((bf16[1,192,2304]{2,1,0:T(8,128)(2,1)}), bf16[1,768,2304]{2,1,0:T(8,128)(2,1)}) %all-gather.18.cloned.1.call-update) | async-done | bytes 3538960 | tf_op jit(solution)/shard_map/all_gather | solution.py:347
  63.4 39.6 %all-gather.22.cloned.1.call-done = bf16[1,768,3072]{2,1,0:T(8,128)(2,1)} async-done(((bf16[1,192,3072]{2,1,0:T(8,128)(2,1)}), bf16[1,768,3072]{2,1,0:T(8,128)(2,1)}) %all-gather.22.cloned.1.call-update) | async-done | bytes 4718608 | tf_op jit(solution)/shard_map/all_gather | solution.py:354
  103.0 39.5 %all-gather.24.cloned.1.call-done = bf16[1,3072,768]{2,1,0:T(8,128)(2,1)} async-done(((bf16[1,768,768]{2,1,0:T(8,128)(2,1)}), bf16[1,3072,768]{2,1,0:T(8,128)(2,1)}) %all-gather.24.cloned.1.call-update) | async-done | bytes 4718608 | tf_op jit(solution)/shard_map/all_gather | solution.py:356
  143.2 30.4 %conditional.4 = (bf16[256,768]{1,0:T(8,128)(2,1)S(1)}, bf16[256,768]{1,0:T(8,128)(2,1)S(1)}, bf16[256,768]{1,0:T(8,128)(2,1)}, bf16[256,768]{1,0:T(8,128)(2,1)}...) conditional(s32[]{:T(128)} %convert_element_type.591, () %tuple.79, ...), branch_computations={%region_0.1_spmd, %region_1.8_spmd} | conditional | flops 3892911360 | bytes 125271344 | solution.py:416
  143.8 3.2 fusion.246
  153.9 3.7 fusion.15
  159.9 9.2 fusion.2
  177.6 7.0 collective-permute-done.3
  185.7 3.1 fusion.226
  192.7 3.1 fusion.183
  197.0 9.1 broadcast_add_fusion
  206.1 4.0 fusion.245
  211.5 5.1 collective-permute-start.4
  217.7 18.4 %conditional.6 = (bf16[256,768]{1,0:T(8,128)(2,1)}, f32[768,2304]{1,0:T(8,128)}, f32[768]{0:T(1024)S(1)}, f32[768]{0:T(1024)S(1)}, f32[768,768]{1,0:T(8,128)}, /...) conditional(s32[]{:T(128)} %convert_element_type.602, () %tuple.83, ...), branch_computations={%region_22.23_spmd, %region_23.38_spmd} | conditional | flops 7836657664 | bytes 178437808 | solution.py:442
  218.8 4.2 broadcast.1366
  223.0 3.3 broadcast.1361
  237.8 2.0 copy-done.4
  239.8 11.6 %conditional.5 = (bf16[256,768]{1,0:T(8,128)(2,1)}, bf16[256,768]{1,0:T(8,128)(2,1)S(1)}, bf16[256,768]{1,0:T(8,128)(2,1)}, bf16[256,768]{1,0:T(8,128)(2,1)}, bf...) conditional(s32[]{:T(128)} %convert_element_type.602, () %tuple.81, ...), branch_computations={%region_14.15_spmd, %region_15.22_spmd} | conditional | flops 3892911360 | bytes 107838416 | solution.py:416
  239.8 2.0 broadcast.1323
  251.5 35.6 %collective-permute-done.5 = bf16[256,768]{1,0:T(8,128)(2,1)} collective-permute-done((bf16[256,768]{1,0:T(8,128)(2,1)}, bf16[256,768]{1,0:T(8,128)(2,1)}, u32[]{:S(2)}, u32[]{:S(2)}) %collective-permute-start.5) | collective-permute-done | bytes 393248 | tf_op jit(solution)/shard_map/ppermute | solution.py:24
  287.0 2.3 fusion.190
  290.8 10.7 convert_reduce_fusion.12
  305.7 1.9 copy.163
  309.4 1.9 copy.164
  313.1 1.9 copy.161
  315.8 2.0 copy.162
  323.2 3.3 fusion.177
  328.2 2.0 fusion.199
  330.2 43.9 %collective-permute-done.6 = bf16[256,768]{1,0:T(8,128)(2,1)S(1)} collective-permute-done((bf16[256,768]{1,0:T(8,128)(2,1)S(1)}, bf16[256,768]{1,0:T(8,128)(2,1)S(1)}, u32[]{:S(2)}, u32[]{:S(2)}) %collective-permute-start.6) | collective-permute-done | bytes 393248 | tf_op jit(solution)/shard_map/ppermute | solution.py:24
  374.3 53.7 %conditional.7 = (bf16[256,768]{1,0:T(8,128)(2,1)}, f32[768,2304]{1,0:T(8,128)}, f32[768]{0:T(1024)S(1)}, f32[768]{0:T(1024)S(1)}, f32[768,768]{1,0:T(8,128)}, /...) conditional(s32[]{:T(128)} %convert_element_type.591, () %tuple.78, ...), branch_computations={%region_43.44_spmd, %region_44.59_spmd} | conditional | flops 7836657664 | bytes 165854832 | solution.py:442
  376.1 10.4 convert_reduce_fusion.6
  394.0 2.3 fusion.249
  396.9 3.1 multiply_reduce_fusion.8
  402.9 4.0 fusion.118
  406.8 3.9 fusion.105
  412.3 1.9 fusion.121
  414.2 6.5 fusion.119
  420.8 7.1 fusion.101
  428.0 4.5 add_convert_fusion.5
  432.7 4.1 fusion.196
  436.7 9.9 add_convert_fusion.4
  449.8 9.7 add_convert_fusion.2
  462.4 9.5 add_convert_fusion.3
  474.2 34.7 %reduce-scatter.5.cloned.1.call-done = bf16[192,2304]{1,0:T(8,128)(2,1)} async-done(((bf16[768,2304]{1,0:T(8,128)(2,1)}), bf16[192,2304]{1,0:T(8,128)(2,1)}) %reduce-scatter.5.cloned.1.call-update) | async-done | bytes 884752 | tf_op jit(solution)/shard_map/reduce_scatter | solution.py:455
  510.3 2.0 pad_maximum_fusion.8
  512.4 47.5 %reduce-scatter.11.cloned.1.call-done = bf16[768,768]{1,0:T(8,128)(2,1)} async-done(((bf16[3072,768]{1,0:T(8,128)(2,1)}), bf16[768,768]{1,0:T(8,128)(2,1)}) %reduce-scatter.11.cloned.1.call-update) | async-done | bytes 1179664 | tf_op jit(solution)/shard_map/reduce_scatter | solution.py:482
  561.5 2.5 pad_maximum_fusion.7
  564.0 47.1 %reduce-scatter.9.cloned.1.call-done = bf16[192,3072]{1,0:T(8,128)(2,1)} async-done(((bf16[768,3072]{1,0:T(8,128)(2,1)}), bf16[192,3072]{1,0:T(8,128)(2,1)}) %reduce-scatter.9.cloned.1.call-update) | async-done | bytes 1179664 | tf_op jit(solution)/shard_map/reduce_scatter | solution.py:476
  611.1 1.8 fusion.164
  612.9 2.7 pad_maximum_fusion.6
  618.3 2.5 collective-permute-start.7
  621.0 10.9 %all-reduce.19 = (bf16[768]{0:T(1024)(128)(2,1)S(1)}, bf16[768]{0:T(1024)(128)(2,1)S(1)}, bf16[768]{0:T(1024)(128)(2,1)S(1)}, bf16[768]{0:T(1024)(128)(2,1)S(1)}...) all-reduce(bf16[768]{0:T(1024)(128)(2,1)S(1)} %add_convert_fusion.1, ...), channel_id=16, replica_groups=mesh['wide'=8,'narrow'=4] {'narrow'}, use_global_device_ids=true, to_apply=%region_62.63.clone | all-reduce | flops 9216 | bytes 36864
  632.8 54.6 %all-reduce.17 = (f32[2,192]{1,0:T(2,128)}, f32[2,192]{1,0:T(2,128)}, f32[2,192]{1,0:T(2,128)}, f32[2,192]{1,0:T(2,128)}, f32[2,192]{1,0:T(2,128)}, /*index=5*/f...) all-reduce(f32[2,192]{1,0:T(2,128)S(1)} %pad_maximum_fusion.14, ...), channel_id=1, replica_groups=mesh['wide'=8,'narrow'=4] {'wide'}, use_global_device_ids=true, to_apply=%region_63.64 | all-reduce | flops 4608 | bytes 36864 | tf_op jit(solution)/shard_map/psum | solution.py:502
  688.4 382.6 %all-reduce.23.cloned.1.call-done = (f32[2,192,2304]{2,1,0:T(8,128)}, f32[2,192,768]{2,1,0:T(8,128)}, f32[2,192,3072]{2,1,0:T(8,128)}, f32[2,768,768]{2,1,0:T(8,128)}) async-done(((f32[2,192,2304]{2,1,0:T(8,128)}, f32[2,192,768]{2,1,0:T(8,128)}, f32[2,192,3072]{2,1,0:T(8,128)}, f32[2,768,768]{2,1,0:T(8,128)}), (f32[2,192,2304]{2,1,0:T(8,128)}, f32[2,192,768]{2,1,0:T(8,128)}, f32[2,192,3072]{2,1,0:T(8,128)}, ...) | async-done | bytes 14155792 | tf_op jit(solution)/shard_map/psum | solution.py:502
  1071.0 4.2 copy.321
  1076.2 2.4 copy.323
  1079.7 2.2 copy.324
  (596 shorter events, 100.5 us)
Async XLA Ops:
  7.2 44.8 %all-gather.20.cloned.1.call-start = ((), (), s32[]{:S(2)}) async-start(), calls=%async_computation.9 | async-start | bytes 1474560 | tf_op jit(solution)/shard_map/all_gather | solution.py:350
  9.1 54.2 %all-gather.18.cloned.1.call-start = ((), (), s32[]{:S(2)}) async-start(), calls=%async_computation.8 | async-start | bytes 4423680 | tf_op jit(solution)/shard_map/all_gather | solution.py:347
  11.4 91.6 %all-gather.22.cloned.1.call-start = ((), (), s32[]{:S(2)}) async-start(), calls=%async_computation.10 | async-start | bytes 5898240 | tf_op jit(solution)/shard_map/all_gather | solution.py:354
  12.6 12.4 %copy-start.171 = (bf16[2,192]{1,0:T(2,128)(2,1)S(1)}, bf16[2,192]{1,0:T(2,128)(2,1)}, u32[]{:S(2)}) copy-start(bf16[2,192]{1,0:T(2,128)(2,1)} %param.30) | copy-start | bytes 2308
  12.6 12.7 %copy-start.172 = (bf16[2,192]{1,0:T(2,128)(2,1)S(1)}, bf16[2,192]{1,0:T(2,128)(2,1)}, u32[]{:S(2)}) copy-start(bf16[2,192]{1,0:T(2,128)(2,1)} %param.33) | copy-start | bytes 2308
  12.6 12.7 %copy-start.173 = (bf16[2,192]{1,0:T(2,128)(2,1)S(1)}, bf16[2,192]{1,0:T(2,128)(2,1)}, u32[]{:S(2)}) copy-start(bf16[2,192]{1,0:T(2,128)(2,1)} %param.34) | copy-start | bytes 2308
  12.6 13.2 %copy-start.174 = (bf16[2,192]{1,0:T(2,128)(2,1)S(1)}, bf16[2,192]{1,0:T(2,128)(2,1)}, u32[]{:S(2)}) copy-start(bf16[2,192]{1,0:T(2,128)(2,1)} %param.35) | copy-start | bytes 2308
  12.6 13.1 %copy-start.175 = (bf16[2,192]{1,0:T(2,128)(2,1)S(1)}, bf16[2,192]{1,0:T(2,128)(2,1)}, u32[]{:S(2)}) copy-start(bf16[2,192]{1,0:T(2,128)(2,1)} %param.39) | copy-start | bytes 2308
  12.6 13.6 %copy-start.176 = (bf16[2,192]{1,0:T(2,128)(2,1)S(1)}, bf16[2,192]{1,0:T(2,128)(2,1)}, u32[]{:S(2)}) copy-start(bf16[2,192]{1,0:T(2,128)(2,1)} %param.40) | copy-start | bytes 2308
  12.6 13.6 %copy-start.177 = (bf16[2,192]{1,0:T(2,128)(2,1)S(1)}, bf16[2,192]{1,0:T(2,128)(2,1)}, u32[]{:S(2)}) copy-start(bf16[2,192]{1,0:T(2,128)(2,1)} %param.41) | copy-start | bytes 2308
  12.6 27.8 %copy-start.167 = (bf16[2,768]{1,0:T(2,128)(2,1)S(1)}, bf16[2,768]{1,0:T(2,128)(2,1)}, u32[]{:S(2)}) copy-start(bf16[2,768]{1,0:T(2,128)(2,1)} %param.37) | copy-start | bytes 9220
  12.7 129.8 %all-gather.24.cloned.1.call-start = ((), (), s32[]{:S(2)}) async-start(), calls=%async_computation.11 | async-start | bytes 5898240 | tf_op jit(solution)/shard_map/all_gather | solution.py:356
  15.1 457.0 %reduce-scatter.7.cloned.1.call-start = ((), (), s32[]{:S(2)}) async-start(), calls=%async_computation.5 | async-start | bytes 1474560 | tf_op jit(solution)/shard_map/reduce_scatter | solution.py:464
  15.1 32.9 %collective-permute-start.2 = (s32[1]{0:T(128)}, s32[1]{0:T(128)}, u32[]{:S(2)}, u32[]{:S(2)}) collective-permute-start(s32[1]{0:T(128)} %param.28), channel_id=1, source_target_pairs={{16,0},{20,4},{24,8},{28,12},{0,16},{4,20},{8,24},{12,28},{17,1},{... | collective-permute-start | bytes 20 | tf_op jit(solution)/shard_map/ppermute | solution.py:18
  19.3 30.6 %collective-permute-start.1 = (s32[1,256]{1,0:T(1,128)S(1)}, s32[1,256]{1,0:T(1,128)S(1)}, u32[]{:S(2)}, u32[]{:S(2)}) collective-permute-start(s32[1,256]{1,0:T(1,128)S(1)} %copy-done.178), channel_id=1, source_target_pairs={{16,0},{20,4},{24,8},{28,12},{0,16},{4,20},{8,24},{12,28},{17,1},{... | collective-permute-start | bytes 3080 | tf_op jit(solution)/shard_map/ppermute | solution.py:18
  20.1 157.5 %collective-permute-start = (bf16[256,768]{1,0:T(8,128)(2,1)}, bf16[256,768]{1,0:T(8,128)(2,1)}, u32[]{:S(2)}, u32[]{:S(2)}) collective-permute-start(bf16[256,768]{1,0:T(8,128)(2,1)} %broadcast_select_fusion.24), channel_id=1, source_target_pairs={{16,0},{20,4},{24,8},{28,12},{0,16},{4,20},{8,24},{12,28},{17,1},{... | collective-permute-start | bytes 1179656 | tf_op jit(solution)/shard_map/ppermute | solution.py:18
  37.4 105.1 %copy-start.107 = (bf16[768]{0:T(1024)(128)(2,1)}, bf16[768]{0:T(1024)(128)(2,1)S(1)}, u32[]{:S(2)}) copy-start(bf16[768]{0:T(1024)(128)(2,1)S(1)} %get-tuple-element.1387) | copy-start | bytes 4612
  37.4 105.1 %copy-start.109 = (bf16[768]{0:T(1024)(128)(2,1)}, bf16[768]{0:T(1024)(128)(2,1)S(1)}, u32[]{:S(2)}) copy-start(bf16[768]{0:T(1024)(128)(2,1)S(1)} %get-tuple-element.1390) | copy-start | bytes 4612
  37.4 105.1 %copy-start.120 = (bf16[768]{0:T(1024)(128)(2,1)}, bf16[768]{0:T(1024)(128)(2,1)S(1)}, u32[]{:S(2)}) copy-start(bf16[768]{0:T(1024)(128)(2,1)S(1)} %get-tuple-element.1384) | copy-start | bytes 4612
  37.4 105.1 %copy-start.122 = (bf16[768]{0:T(1024)(128)(2,1)}, bf16[768]{0:T(1024)(128)(2,1)S(1)}, u32[]{:S(2)}) copy-start(bf16[768]{0:T(1024)(128)(2,1)S(1)} %get-tuple-element.1385) | copy-start | bytes 4612
  37.4 105.1 %copy-start.124 = (bf16[768]{0:T(1024)(128)(2,1)}, bf16[768]{0:T(1024)(128)(2,1)S(1)}, u32[]{:S(2)}) copy-start(bf16[768]{0:T(1024)(128)(2,1)S(1)} %get-tuple-element.1386) | copy-start | bytes 4612
  37.5 105.1 %copy-start.126 = (bf16[768]{0:T(1024)(128)(2,1)}, bf16[768]{0:T(1024)(128)(2,1)S(1)}, u32[]{:S(2)}) copy-start(bf16[768]{0:T(1024)(128)(2,1)S(1)} %get-tuple-element.1388) | copy-start | bytes 4612
  37.5 105.1 %copy-start.128 = (bf16[768]{0:T(1024)(128)(2,1)}, bf16[768]{0:T(1024)(128)(2,1)S(1)}, u32[]{:S(2)}) copy-start(bf16[768]{0:T(1024)(128)(2,1)S(1)} %get-tuple-element.1389) | copy-start | bytes 4612
  37.5 105.1 %copy-start.132 = (bf16[768]{0:T(1024)(128)(2,1)}, bf16[768]{0:T(1024)(128)(2,1)S(1)}, u32[]{:S(2)}) copy-start(bf16[768]{0:T(1024)(128)(2,1)S(1)} %get-tuple-element.1391) | copy-start | bytes 4612
  45.7 96.9 %copy-start.102 = (bf16[3072]{0:T(1024)(128)(2,1)}, bf16[3072]{0:T(1024)(128)(2,1)S(1)}, u32[]{:S(2)}) copy-start(bf16[3072]{0:T(1024)(128)(2,1)S(1)} %reduce.27) | copy-start | bytes 18436
  50.9 91.6 %copy-start.115 = (s32[1,256]{1,0:T(1,128)}, s32[1,256]{1,0:T(1,128)S(1)}, u32[]{:S(2)}) copy-start(s32[1,256]{1,0:T(1,128)S(1)} %get-tuple-element.1424) | copy-start | bytes 3076
  50.9 91.6 %copy-start.118 = (s32[1,256]{1,0:T(1,128)}, s32[1,256]{1,0:T(1,128)S(1)}, u32[]{:S(2)}) copy-start(s32[1,256]{1,0:T(1,128)S(1)} %get-tuple-element.1425) | copy-start | bytes 3076
  143.8 13.9 %copy-start.13 = (bf16[256,768]{1,0:T(8,128)(2,1)}, bf16[256,768]{1,0:T(8,128)(2,1)S(1)}, u32[]{:S(2)}) copy-start(bf16[256,768]{1,0:T(8,128)(2,1)S(1)} %broadcast_select_fusion) | copy-start | bytes 1179652 | tf_op jit(solution)/shard_map/cond
  174.3 14.5 %copy-start.42 = (f32[256,768]{1,0:T(8,128)}, f32[256,768]{1,0:T(8,128)S(1)}, u32[]{:S(2)}) copy-start(f32[256,768]{1,0:T(8,128)S(1)} %get-tuple-element.937) | copy-start | bytes 2359300
  174.3 10.4 collective-permute-start.3
  188.9 28.1 %copy-start.46 = (bf16[256,768]{1,0:T(8,128)(2,1)}, bf16[256,768]{1,0:T(8,128)(2,1)S(1)}, u32[]{:S(2)}) copy-start(bf16[256,768]{1,0:T(8,128)(2,1)S(1)} %slice.68) | copy-start | bytes 1179652
  196.9 20.1 %copy-start.29 = (f32[256,768]{1,0:T(8,128)}, f32[256,768]{1,0:T(8,128)S(1)}, u32[]{:S(2)}) copy-start(f32[256,768]{1,0:T(8,128)S(1)} %get-tuple-element.1432) | copy-start | bytes 2359300
  196.9 20.1 %copy-start.68 = (bf16[256,768]{1,0:T(8,128)(2,1)}, bf16[256,768]{1,0:T(8,128)(2,1)S(1)}, u32[]{:S(2)}) copy-start(bf16[256,768]{1,0:T(8,128)(2,1)S(1)} %get-tuple-element.1431) | copy-start | bytes 1179652
  211.5 26.2 %collective-permute-start.4 = (bf16[256,768]{1,0:T(8,128)(2,1)}, bf16[256,768]{1,0:T(8,128)(2,1)}, u32[]{:S(2)}, u32[]{:S(2)}) collective-permute-start(bf16[256,768]{1,0:T(8,128)(2,1)} %get-tuple-element.1429), channel_id=1, source_target_pairs={{0,16},{4,20},{8,24},{12,28},{1,17},{5,21},{9,25},{13,29},{2,18},{... | collective-permute-start | bytes 1179656 | tf_op jit(solution)/shard_map/ppermute | solution.py:24
  216.9 20.6 %copy-start.158 = (s32[1,256]{1,0:T(1,128)S(1)}, s32[1,256]{1,0:T(1,128)}, u32[]{:S(2)}) copy-start(s32[1,256]{1,0:T(1,128)} %get-tuple-element.1423) | copy-start | bytes 3076
  216.9 20.6 %copy-start.168 = (pred[256]{0:T(512)(128)(4,1)S(1)}, pred[256]{0:T(512)(128)(4,1)}, u32[]{:S(2)}) copy-start(pred[256]{0:T(512)(128)(4,1)} %get-tuple-element.1422) | copy-start | bytes 772
  216.9 20.7 %copy-start.103 = (bf16[3072]{0:T(1024)(128)(2,1)S(1)}, bf16[3072]{0:T(1024)(128)(2,1)}, u32[]{:S(2)}) copy-start(bf16[3072]{0:T(1024)(128)(2,1)} %copy-done.102) | copy-start | bytes 18436
  216.9 20.7 %copy-start.116 = (s32[1,256]{1,0:T(1,128)S(1)}, s32[1,256]{1,0:T(1,128)}, u32[]{:S(2)}) copy-start(s32[1,256]{1,0:T(1,128)} %copy-done.115) | copy-start | bytes 3076
  217.0 20.7 %copy-start.121 = (bf16[768]{0:T(1024)(128)(2,1)S(1)}, bf16[768]{0:T(1024)(128)(2,1)}, u32[]{:S(2)}) copy-start(bf16[768]{0:T(1024)(128)(2,1)} %copy-done.120) | copy-start | bytes 4612
  217.0 20.7 %copy-start.123 = (bf16[768]{0:T(1024)(128)(2,1)S(1)}, bf16[768]{0:T(1024)(128)(2,1)}, u32[]{:S(2)}) copy-start(bf16[768]{0:T(1024)(128)(2,1)} %copy-done.122) | copy-start | bytes 4612
  217.0 20.7 %copy-start.125 = (bf16[768]{0:T(1024)(128)(2,1)S(1)}, bf16[768]{0:T(1024)(128)(2,1)}, u32[]{:S(2)}) copy-start(bf16[768]{0:T(1024)(128)(2,1)} %copy-done.124) | copy-start | bytes 4612
  217.0 20.7 %copy-start.127 = (bf16[768]{0:T(1024)(128)(2,1)S(1)}, bf16[768]{0:T(1024)(128)(2,1)}, u32[]{:S(2)}) copy-start(bf16[768]{0:T(1024)(128)(2,1)} %copy-done.126) | copy-start | bytes 4612
  217.0 20.7 %copy-start.129 = (bf16[768]{0:T(1024)(128)(2,1)S(1)}, bf16[768]{0:T(1024)(128)(2,1)}, u32[]{:S(2)}) copy-start(bf16[768]{0:T(1024)(128)(2,1)} %copy-done.128) | copy-start | bytes 4612
  217.0 20.7 %copy-start.133 = (bf16[768]{0:T(1024)(128)(2,1)S(1)}, bf16[768]{0:T(1024)(128)(2,1)}, u32[]{:S(2)}) copy-start(bf16[768]{0:T(1024)(128)(2,1)} %copy-done.132) | copy-start | bytes 4612
  236.1 50.9 %collective-permute-start.5 = (bf16[256,768]{1,0:T(8,128)(2,1)}, bf16[256,768]{1,0:T(8,128)(2,1)}, u32[]{:S(2)}, u32[]{:S(2)}) collective-permute-start(bf16[256,768]{1,0:T(8,128)(2,1)} %get-tuple-element.948), channel_id=1, source_target_pairs={{16,0},{20,4},{24,8},{28,12},{17,1},{21,5},{25,9},{29,13},{18,2},{... | collective-permute-start | bytes 1179656 | tf_op jit(solution)/shard_map/ppermute | solution.py:24
  251.4 39.4 %copy-start.179 = (bf16[1,3072,768]{2,1,0:T(8,128)(2,1)S(1)}, bf16[1,3072,768]{2,1,0:T(8,128)(2,1)}, u32[]{:S(2)}) copy-start(bf16[1,3072,768]{2,1,0:T(8,128)(2,1)} %all-gather.24.cloned.1.call-done) | copy-start | bytes 14155780
  319.6 54.6 %slice-start.16 = ((s8[4718592]{0:T(1024)(128)(4,1)}), s8[4194304]{0:T(1024)(128)(4,1)S(1)}, s32[]{:S(2)}) async-start(s8[4718592]{0:T(1024)(128)(4,1)} %bitcast.348), calls=%async_computation.29 | async-start | bytes 8388608
  321.9 52.3 %slice-start.17 = ((s8[4718592]{0:T(1024)(128)(4,1)}), s8[524288]{0:T(1024)(128)(4,1)S(1)}, s32[]{:S(2)}) async-start(s8[4718592]{0:T(1024)(128)(4,1)} %bitcast.348), calls=%async_computation.30 | async-start | bytes 1048576
  323.2 51.0 %slice-start.4 = ((s8[4718592]{0:T(1024)(128)(4,1)}), s8[4194304]{0:T(1024)(128)(4,1)S(1)}, s32[]{:S(2)}) async-start(s8[4718592]{0:T(1024)(128)(4,1)} %bitcast.237), calls=%async_computation.17 | async-start | bytes 8388608
  323.2 51.0 %slice-start.5 = ((s8[4718592]{0:T(1024)(128)(4,1)}), s8[524288]{0:T(1024)(128)(4,1)S(1)}, s32[]{:S(2)}) async-start(s8[4718592]{0:T(1024)(128)(4,1)} %bitcast.237), calls=%async_computation.18 | async-start | bytes 1048576
  323.2 51.0 %copy-start.181 = (f32[256,3072]{1,0:T(8,128)S(1)}, f32[256,3072]{1,0:T(8,128)}, u32[]{:S(2)}) copy-start(f32[256,3072]{1,0:T(8,128)} %copy-done.180) | copy-start | bytes 9437188
  326.6 47.7 %copy-start.97 = (bf16[256,768]{1,0:T(8,128)(2,1)}, bf16[256,768]{1,0:T(8,128)(2,1)S(1)}, u32[]{:S(2)}) copy-start(bf16[256,768]{1,0:T(8,128)(2,1)S(1)} %fusion.177) | copy-start | bytes 1179652
  326.6 47.6 %copy-start.20 = (pred[256,3072]{1,0:T(32,128)(4,1)S(1)}, pred[256,3072]{1,0:T(32,128)(4,1)}, u32[]{:S(2)}) copy-start(pred[256,3072]{1,0:T(32,128)(4,1)} %copy-done.19) | copy-start | bytes 2359300
  326.6 47.6 %copy-start.30 = (f32[256,768]{1,0:T(8,128)S(1)}, f32[256,768]{1,0:T(8,128)}, u32[]{:S(2)}) copy-start(f32[256,768]{1,0:T(8,128)} %copy-done.29) | copy-start | bytes 2359300
  326.6 47.6 %copy-start.41 = (f32[256,768]{1,0:T(8,128)S(1)}, f32[256,768]{1,0:T(8,128)}, u32[]{:S(2)}) copy-start(f32[256,768]{1,0:T(8,128)} %copy-done.40) | copy-start | bytes 2359300
  326.6 47.6 %copy-start.47 = (bf16[256,768]{1,0:T(8,128)(2,1)S(1)}, bf16[256,768]{1,0:T(8,128)(2,1)}, u32[]{:S(2)}) copy-start(bf16[256,768]{1,0:T(8,128)(2,1)} %copy-done.46) | copy-start | bytes 1179652
  326.6 47.6 %copy-start.82 = (bf16[256,768]{1,0:T(8,128)(2,1)S(1)}, bf16[256,768]{1,0:T(8,128)(2,1)}, u32[]{:S(2)}) copy-start(bf16[256,768]{1,0:T(8,128)(2,1)} %param.26) | copy-start | bytes 1179652
  326.7 47.5 %collective-permute-start.6 = (bf16[256,768]{1,0:T(8,128)(2,1)S(1)}, bf16[256,768]{1,0:T(8,128)(2,1)S(1)}, u32[]{:S(2)}, u32[]{:S(2)}) collective-permute-start(bf16[256,768]{1,0:T(8,128)(2,1)S(1)} %fusion.177), channel_id=1, source_target_pairs={{16,0},{20,4},{24,8},{28,12},{17,1},{21,5},{25,9},{29,13},{18,2},{... | collective-permute-start | bytes 1179656 | tf_op jit(solution)/shard_map/ppermute | solution.py:24
  432.6 76.4 %reduce-scatter.5.cloned.1.call-start = ((), (), s32[]{:S(2)}) async-start(), calls=%async_computation.4 | async-start | bytes 4423680 | tf_op jit(solution)/shard_map/reduce_scatter | solution.py:455
  446.6 113.3 %reduce-scatter.11.cloned.1.call-start = ((), (), s32[]{:S(2)}) async-start(), calls=%async_computation.7 | async-start | bytes 5898240 | tf_op jit(solution)/shard_map/reduce_scatter | solution.py:482
  459.6 151.5 %reduce-scatter.9.cloned.1.call-start = ((), (), s32[]{:S(2)}) async-start(), calls=%async_computation.6 | async-start | bytes 5898240 | tf_op jit(solution)/shard_map/reduce_scatter | solution.py:476
  472.0 599.0 %all-reduce.23.cloned.1.call-start = ((), (), s32[]{:S(2)}) async-start(), calls=%async_computation.12 | async-start | bytes 28311552 | tf_op jit(solution)/shard_map/psum | solution.py:502
  615.7 71.7 %copy-start.98 = (bf16[256,768]{1,0:T(8,128)(2,1)S(1)}, bf16[256,768]{1,0:T(8,128)(2,1)}, u32[]{:S(2)}) copy-start(bf16[256,768]{1,0:T(8,128)(2,1)} %copy-done.97) | copy-start | bytes 1179652
  618.3 69.1 %collective-permute-start.7 = (bf16[256,768]{1,0:T(8,128)(2,1)S(1)}, bf16[256,768]{1,0:T(8,128)(2,1)S(1)}, u32[]{:S(2)}, u32[]{:S(2)}) collective-permute-start(bf16[256,768]{1,0:T(8,128)(2,1)S(1)} %broadcast_select_fusion.16), channel_id=1, source_target_pairs={{16,0},{20,4},{24,8},{28,12},{0,16},{4,20},{8,24},{12,28},{17,1},{... | collective-permute-start | bytes 1179656 | tf_op jit(solution)/shard_map/ppermute | solution.py:18
  (127 other events, 629.1 us)
Sparse Core Ops, SparseCore 0:
  10.2 20.1 all-gather.19
  32.5 30.8 all-gather.17
  65.5 37.4 all-gather.21
  104.9 37.4 all-gather.23
  432.7 32.5 reduce-scatter.6
  468.5 40.4 reduce-scatter.4
  512.0 47.8 reduce-scatter.10
  563.2 47.8 reduce-scatter.8
  616.9 454.0 all-reduce.22
where the time goes:
time: 1090 us
  waiting for transfers between devices  689 us (63%)
  matrix products  115 us (11%)
  blocking collectives  81.3 us (7%)
  other arithmetic  80.3 us (7%)
  local copies, waits for them, and re-layouts  73.9 us (7%)
  between operations  20.1 us (2%)
  starting transfers between devices  19.6 us (2%)
    psum x1, waiting for transfers between devices, body(): lax.psum((by_section(shards[0]), by_section(shards[1]), by_section(shards...  383 us
    ppermute x4, waiting for transfers between devices, shifted_2(): lax.ppermute(value, axis, [(source, source + steps) for source in range(i...  86.5 us
    psum x1, blocking collectives, body(): lax.psum((by_section(shards[0]), by_section(shards[1]), by_section(shards...  54.6 us
    reduce_scatter x1, waiting for transfers between devices, body(): lax.psum_scatter(totals[9].astype(jnp.bfloat16), 'narrow', scatter_dimens...  47.5 us
    reduce_scatter x1, waiting for transfers between devices, body(): lax.psum_scatter(totals[7].astype(jnp.bfloat16), 'narrow', scatter_dimens...  47.1 us
    all_gather x1, waiting for transfers between devices, body(): lax.all_gather(own_layer[7], 'narrow', axis=0, tiled=True)  39.6 us
    all_gather x1, waiting for transfers between devices, body(): lax.all_gather(own_layer[9], 'narrow', axis=0, tiled=True)  39.5 us
    reduce_scatter x1, waiting for transfers between devices, body(): lax.psum_scatter(totals[0].astype(jnp.bfloat16), 'narrow', scatter_dimens...  34.7 us
  transfers between devices with their start and end apart: 17, of which 10 were waited for; matrix products, arithmetic and copies ran while one was open for 11% of the time, Pallas kernels for 0%

commit v1 on v0

v1 whole, which is shorter than its diff:
```python
import functools
import math

import jax
import jax.numpy as jnp
from jax import lax
from jax.experimental import pallas as pl
from jax.experimental.pallas import tpu as pltpu
from jax.sharding import PartitionSpec as P

HEADS = 12
norm_eps = 1e-12
masked_score = -1000000000.0
low = jnp.bfloat16
f32 = jnp.float32
VMEM_BYTES = 56 * 1024 * 1024
HALVINGS = 3


def swap(value, axis, bit):
    count = lax.axis_size(axis)
    return lax.ppermute(value, axis, [(i, i ^ bit) for i in range(count)])


def dot(a, b):
    return jnp.dot(a, b, preferred_element_type=f32)


def dot_nt(a, b):
    return lax.dot_general(a, b, (((1,), (1,)), ((), ())), preferred_element_type=f32)


def dot_tn(a, b):
    return lax.dot_general(a, b, (((0,), (0,)), ((), ())), preferred_element_type=f32)


def normalize(residual):
    center = residual - jnp.mean(residual, axis=-1, keepdims=True)
    inverse = lax.rsqrt(jnp.mean(center * center, axis=-1, keepdims=True) + norm_eps)
    return center * inverse, inverse


def normalize_back(grad_unit, unit, inverse):
    centered = grad_unit - jnp.mean(grad_unit, axis=-1, keepdims=True)
    return inverse * (centered - unit * jnp.mean(grad_unit * unit, axis=-1, keepdims=True))


def weight_copies(ids, layer, pieces, target, columns, sems, base):
    own, core, near_x, far_x, near_d, far_d = pieces
    rows = own.shape[1]
    half = rows // 2
    n, y = ids[0], ids[4]
    copies = []

    def add(source, start, count):
        where = target.at[pl.ds(pl.multiple_of(start, half), count), :]
        copies.append(pltpu.make_async_copy(source, where, sems.at[base + len(copies)]))

    def part(ref):
        return ref.at[:, pl.ds(columns, target.shape[1])]

    add(own.at[layer], n * rows, rows)
    add(core.at[layer], ids[1] * rows, rows)
    add(part(near_x), ids[2] * rows + y * half, half)
    add(part(far_x), ids[2] * rows + (1 - y) * half, half)
    add(part(near_d), ids[3] * rows + y * half, half)
    add(part(far_d), ids[3] * rows + (1 - y) * half, half)
    return copies


def begin(copies):
    for copy in copies:
        copy.start()


def finish(copies):
    for copy in copies:
        copy.wait()


def attn_copies(layer, ids, refs, w_qkv, w_o, sems):
    qkv_own, qkv_core, o_own, o_core, near_x, far_x, near_d, far_d = refs
    halves = (near_x, far_x, near_d, far_d)
    qkv = weight_copies(ids, layer, (qkv_own, qkv_core) + halves, w_qkv, 0, sems, 0)
    o = weight_copies(ids, layer, (o_own, o_core) + halves, w_o, w_qkv.shape[1], sems, 6)
    return qkv, o


def ffn_copies(layer, ids, refs, w_in, w_out, sems):
    in_copies = weight_copies(ids, layer, refs[:6], w_in, 0, sems, 0)
    out_copies = weight_copies(ids, layer, refs[6:], w_out, 0, sems, 6)
    return in_copies, out_copies


def attn_fwd_kernel(layer, ids, length, x, cell_row, cell_col, qkv_bias, small, *rest):
    weights, rest = rest[:8], rest[8:]
    qkv_rows, probs, context, unit_out, inverse_out, w_qkv, w_o, mask, sems = rest
    tokens, width = x.shape
    qkv_copies, o_copies = attn_copies(layer, ids, weights, w_qkv, w_o, sems)
    begin(qkv_copies)
    begin(o_copies)
    position = lax.broadcasted_iota(jnp.int32, (1, tokens), 1)
    key_cell, query_cell = cell_row[...], cell_col[...]
    allowed = (query_cell == key_cell) | (key_cell == 0) | (query_cell == 0)
    allowed = allowed & (position < length[0])
    mask[...] = jnp.where(allowed, 0.0, masked_score)
    scale = 1.0 / math.sqrt(width // HEADS)
    finish(qkv_copies)
    tile = width // 2

    @pl.loop(0, 6)
    def _(t):
        columns = pl.ds(pl.multiple_of(t * tile, tile), tile)
        rows = dot(x[...], w_qkv[:, columns]) + qkv_bias[:, columns]
        qkv_rows[:, columns] = (rows * jnp.where(t < 2, scale, 1.0)).astype(low)

    pair_width = 2 * width // HEADS
    first = lax.broadcasted_iota(jnp.int32, (1, pair_width), 1) < pair_width // 2

    @pl.loop(0, HEADS // 2)
    def _(pair):
        start = pl.multiple_of(pair * pair_width, pair_width)
        query = qkv_rows[:, pl.ds(start, pair_width)]
        key = qkv_rows[:, pl.ds(width + start, pair_width)]
        value = qkv_rows[:, pl.ds(2 * width + start, pair_width)]
        sides = []
        for side in range(2):
            mine = first if side == 0 else jnp.logical_not(first)
            scores = dot_nt(jnp.where(mine, query, jnp.zeros_like(query)), key) + mask[...]
            shifted = jnp.exp(scores - jnp.max(scores, axis=-1, keepdims=True))
            total = jnp.sum(shifted, axis=-1, keepdims=True)
            prob = (shifted / total).astype(low)
            probs[2 * pair + side] = prob
            sides.append(dot(prob, value))
        context[:, pl.ds(start, pair_width)] = jnp.where(first, sides[0], sides[1]).astype(low)

    finish(o_copies)
    residual = x[...].astype(f32) + (dot(context[...], w_o[...]) + small[2:3, :])
    unit, inverse = normalize(residual)
    unit_out[...] = unit
    inverse_out[...] = inverse


def ffn_fwd_kernel(layer, ids, unit_one, in_bias, small, *rest):
    weights, rest = rest[:12], rest[12:]
    hidden, slope, unit_out, inverse_out, result, w_in, w_out, normed_low, sems = rest
    in_copies, out_copies = ffn_copies(layer, ids, weights, w_in, w_out, sems)
    begin(in_copies)
    begin(out_copies)
    normed = unit_one[...] * small[3:4, :] + small[4:5, :]
    normed_low[...] = normed.astype(low)
    finish(in_copies)
    tile = w_in.shape[1] // 8

    @pl.loop(0, 8)
    def _(t):
        columns = pl.ds(pl.multiple_of(t * tile, tile), tile)
        pre = dot(normed_low[...], w_in[:, columns]) + in_bias[:, columns]
        cdf = 0.5 * (1.0 + lax.erf(pre * (1.0 / math.sqrt(2.0))))
        density = jnp.exp(-0.5 * pre * pre) * (1.0 / math.sqrt(2.0 * math.pi))
        hidden[:, columns] = (pre * cdf).astype(low)
        slope[:, columns] = cdf + pre * density

    finish(out_copies)
    residual = unit_one[...] * small[3:4, :] + small[4:5, :] + (dot(hidden[...], w_out[...]) + small[5:6, :])
    unit, inverse = normalize(residual)
    unit_out[...] = unit
    inverse_out[...] = inverse
    result[...] = (unit * small[6:7, :] + small[7:8, :]).astype(low)


def store_rows(stage, ids, product, piece, *more):
    share = product.shape[0] // 4
    for owner in range(4):
        away = ids[0] ^ owner
        block = product[owner * share : (owner + 1) * share].astype(low)
        stage[(away & 1, away >> 1, piece ^ ids[5]) + more] = block


def send_out(stage, kept, sent, sems):
    copies = [
        pltpu.make_async_copy(stage.at[1], sent, sems.at[0]),
        pltpu.make_async_copy(stage.at[0], kept, sems.at[1]),
    ]
    begin(copies)
    finish(copies)


def ffn_bwd_kernel(
    layer, ids, grad, unit_two, inverse_two, unit_one, inverse_one, hidden, slope, small, *rest
):
    weights, rest = rest[:12], rest[12:]
    d_resid, small_grads, in_bias_grad, kept, sent = rest[:5]
    w_in, w_out, d_ffn, d_resid_two, d_pre, normed_t, stage, sems, out_sems = rest[5:]
    in_copies, out_copies = ffn_copies(layer, ids, weights, w_in, w_out, sems)
    begin(out_copies)
    begin(in_copies)
    g = grad[...].astype(f32)
    unit = unit_two[...]
    small_grads[0:1, :] = jnp.sum(g * unit, axis=0, keepdims=True)
    small_grads[1:2, :] = jnp.sum(g, axis=0, keepdims=True)
    d_two = normalize_back(g * small[6:7, :], unit, inverse_two[...])
    d_resid_two[...] = d_two
    d_low = d_two.astype(low)
    d_ffn[...] = d_low
    small_grads[2:3, :] = jnp.sum(d_low.astype(f32), axis=0, keepdims=True)
    normed = unit_one[...] * small[3:4, :] + small[4:5, :]
    normed_t[...] = normed.astype(low).T
    finish(out_copies)
    tile = w_in.shape[1] // 8
    share = d_ffn.shape[1] // 4

    @pl.loop(0, 8)
    def _(t):
        columns = pl.ds(pl.multiple_of(t * tile, tile), tile)
        d_hidden = dot_nt(d_ffn[...], w_out[columns, :])
        d_tile = (d_hidden * slope[:, columns]).astype(low)
        d_pre[:, columns] = d_tile
        in_bias_grad[:, columns] = jnp.sum(d_tile.astype(f32), axis=0, keepdims=True)
        store_rows(stage, ids, dot(normed_t[...], d_tile), t, 0)
        out_grad = dot_tn(hidden[:, columns], d_ffn[...])
        away = ids[0] ^ (t // 2)
        for row_group in range(2):
            for column_group in range(2):
                piece = ((t % 2) * 2 + row_group) * 2 + column_group
                block = out_grad[
                    row_group * share : (row_group + 1) * share,
                    column_group * tile : (column_group + 1) * tile,
                ]
                stage[away & 1, away >> 1, piece ^ ids[5], 1] = block.astype(low)

    finish(in_copies)
    d_normed = d_resid_two[...] + dot_nt(d_pre[...], w_in[...])
    unit = unit_one[...]
    small_grads[3:4, :] = jnp.sum(d_normed * unit, axis=0, keepdims=True)
    small_grads[4:5, :] = jnp.sum(d_normed, axis=0, keepdims=True)
    small_grads[5:8, :] = jnp.zeros((3, unit.shape[1]), f32)
    d_resid[...] = normalize_back(d_normed * small[3:4, :], unit, inverse_one[...])
    send_out(stage, kept, sent, out_sems)


def attn_bwd_kernel(layer, ids, d_resid, x, qkv_rows, probs, context, *rest):
    weights, rest = rest[:8], rest[8:]
    d_input, small_grads, kept, sent = rest[:4]
    w_qkv, w_o, d_attn, d_context, d_qkv, x_t, stage, sems, out_sems = rest[4:]
    tokens, width = x.shape
    qkv_copies, o_copies = attn_copies(layer, ids, weights, w_qkv, w_o, sems)
    begin(o_copies)
    begin(qkv_copies)
    d_low = d_resid[...].astype(low)
    d_attn[...] = d_low
    small_grads[2:3, :] = jnp.sum(d_low.astype(f32), axis=0, keepdims=True)
    x_t[...] = x[...].T
    tile = width // 2
    for half in range(2):
        product = dot_tn(context[...], d_attn[:, half * tile : (half + 1) * tile])
        store_rows(stage, ids, product, 6 + half, 0)
    finish(o_copies)
    d_context[...] = dot_nt(d_attn[...], w_o[...]).astype(low)
    pair_width = 2 * width // HEADS
    first = lax.broadcasted_iota(jnp.int32, (1, pair_width), 1) < pair_width // 2
    scale = 1.0 / math.sqrt(width // HEADS)

    @pl.loop(0, HEADS // 2)
    def _(pair):
        start = pl.multiple_of(pair * pair_width, pair_width)
        at_query = pl.ds(start, pair_width)
        at_key = pl.ds(width + start, pair_width)
        at_value = pl.ds(2 * width + start, pair_width)
        query, key, value = qkv_rows[:, at_query], qkv_rows[:, at_key], qkv_rows[:, at_value]
        d_ctx = d_context[:, at_query]
        sides = []
        for side in range(2):
            mine = first if side == 0 else jnp.logical_not(first)
            prob_low = probs[2 * pair + side]
            prob = prob_low.astype(f32)
            d_prob = dot_nt(jnp.where(mine, d_ctx, jnp.zeros_like(d_ctx)), value)
            inner = jnp.sum(prob * d_prob, axis=-1, keepdims=True)
            d_scores = (prob * (d_prob - inner)).astype(low)
            sides.append((dot(d_scores, key), dot_tn(d_scores, query), dot_tn(prob_low, d_ctx)))
        d_qkv[:, at_query] = (jnp.where(first, sides[0][0], sides[1][0]) * scale).astype(low)
        d_qkv[:, at_key] = jnp.where(first, sides[0][1], sides[1][1]).astype(low)
        d_qkv[:, at_value] = jnp.where(first, sides[0][2], sides[1][2]).astype(low)

    @pl.loop(0, 6)
    def _(t):
        columns = pl.ds(pl.multiple_of(t * tile, tile), tile)
        store_rows(stage, ids, dot(x_t[...], d_qkv[:, columns]), t, 0)

    small_grads[0:1, :] = jnp.sum(d_qkv[:, :width].astype(f32), axis=0, keepdims=True)
    small_grads[1:2, :] = jnp.sum(d_qkv[:, 2 * width :].astype(f32), axis=0, keepdims=True)
    small_grads[3:8, :] = jnp.zeros((5, width), f32)
    finish(qkv_copies)
    d_input[...] = (d_resid[...] + dot_nt(d_qkv[...], w_qkv[...])).astype(low)
    send_out(stage, kept, sent, out_sems)


def unpack_kernel(ids, *rest):
    chunks, outs = rest[:8], rest[8:12]
    buffer, wide_buffer, in_sems, out_sems = rest[12:]
    qkv, o, w_in, w_out = outs
    share, tile = buffer.shape[2:]
    for layer in range(2):
        a_near, a_far, f_near, f_far = chunks[4 * layer : 4 * layer + 4]
        for piece in range(8):
            place = piece ^ ids[5]
            for slab in range(3):
                near, far = (a_near, a_far) if slab == 0 else (f_near, f_far)
                which = 0 if slab == 0 else slab - 1
                slot = (layer * 3 + slab) * 8 + piece

                @pl.when(place < 4)
                def _():
                    source = near.at[place, which]
                    pltpu.make_async_copy(source, buffer.at[slab * 8 + piece, layer], in_sems.at[slot]).start()

                @pl.when(place >= 4)
                def _():
                    source = far.at[place - 4, which]
                    pltpu.make_async_copy(source, buffer.at[slab * 8 + piece, layer], in_sems.at[slot]).start()

    copies = []
    for layer in range(2):
        a_near = chunks[4 * layer]
        for slab in range(3):
            for piece in range(8):
                slot = (layer * 3 + slab) * 8 + piece
                landed = buffer.at[slab * 8 + piece, layer]
                pltpu.make_async_copy(a_near.at[0, 0], landed, in_sems.at[slot]).wait()
                wide_buffer[slab * 8 + piece, layer] = landed[...].astype(f32)
                if slab == 0 and piece < 6:
                    target = qkv.at[layer, :, pl.ds(piece * tile, tile)]
                elif slab == 0:
                    target = o.at[layer, :, pl.ds((piece - 6) * tile, tile)]
                elif slab == 1:
                    target = w_in.at[layer, :, pl.ds(piece * tile, tile)]
                else:
                    rows = pl.ds((piece // 2) * share, share)
                    target = w_out.at[layer, rows, pl.ds((piece % 2) * tile, tile)]
                copy = pltpu.make_async_copy(wide_buffer.at[slab * 8 + piece, layer], target, out_sems.at[slot])
                copy.start()
                copies.append(copy)
    finish(copies)


SMEM = pl.BlockSpec(memory_space=pltpu.SMEM)
VMEM = pl.BlockSpec(memory_space=pltpu.VMEM)
ANY = pl.BlockSpec(memory_space=pl.ANY)


def call(kernel, name, in_specs, out_specs, out_shape, scratch, flops, moved, args):
    return pl.pallas_call(
        kernel,
        name=name,
        in_specs=in_specs,
        out_specs=out_specs,
        out_shape=out_shape,
        scratch_shapes=scratch,
        compiler_params=pltpu.CompilerParams(vmem_limit_bytes=VMEM_BYTES),
        cost_estimate=pl.CostEstimate(flops=flops, bytes_accessed=moved, transcendentals=0),
    )(*args)


def shape(dims, kind):
    return jax.ShapeDtypeStruct(dims, kind)


def reverse_bits(value, bits):
    result = jnp.zeros_like(value)
    for bit in range(bits):
        result = result | (((value >> bit) & 1) << (bits - 1 - bit))
    return result


def added(a, b):
    return (a.astype(f32) + b.astype(f32)).astype(low)


def reduce_chunk(kept, sent, wide_bits):
    split = (2,) * HALVINGS
    kept = kept.reshape((2,) + split + kept.shape[2:])
    sent = sent.reshape((2,) + split + sent.shape[2:])
    received = swap(sent, "narrow", 1)
    for axis, bit in [("narrow", 2)] + [("wide", 1 << b) for b in range(HALVINGS)]:
        send = added(kept[1], received[1])
        kept = added(kept[0], received[0])
        received = swap(send, axis, bit)
    piece = added(kept, received)
    for b in range(HALVINGS, wide_bits):
        piece = added(piece, swap(piece, "wide", 1 << b))
    block = piece[None]
    for b in range(HALVINGS - 1, 0, -1):
        block = jnp.concatenate([block, swap(block, "wide", 1 << b)], axis=0)
    return block, swap(block, "wide", 1)


def body(
    tables_in,
    cotangent,
    cell_ids,
    lengths,
    qkv_weight,
    q_bias,
    v_bias,
    o_weight,
    o_bias,
    norm1_gain,
    norm1_bias,
    in_weight,
    in_bias,
    out_weight,
    out_bias,
    norm2_gain,
    norm2_bias,
):
    tokens, width = tables_in.shape
    layers, share, ffn = in_weight.shape
    ffn_share = out_weight.shape[1]
    wide_count = lax.axis_size("wide")
    wide_bits = wide_count.bit_length() - 1
    assert wide_count == 1 << wide_bits and wide_bits >= HALVINGS and lax.axis_size("narrow") == 4
    tile = ffn // 8
    me = lax.axis_index("narrow").astype(jnp.int32)
    wide_me = lax.axis_index("wide").astype(jnp.int32)
    y = wide_me & 1
    order = reverse_bits(wide_me & (2**HALVINGS - 1), HALVINGS)
    ids = jnp.stack([me, me ^ 1, me ^ 2, me ^ 3, y, order])

    short = [q_bias, v_bias, o_bias, norm1_gain, norm1_bias, out_bias, norm2_gain, norm2_bias]
    packed = jnp.concatenate([jnp.stack(short, axis=1), in_bias.reshape(layers, 4, share)], axis=1)
    packed = lax.all_gather(packed, "narrow", axis=0).astype(f32)
    small = packed[:, :, :8].transpose(1, 2, 0, 3).reshape(layers, 8, width)
    full_in_bias = packed[:, :, 8:].transpose(1, 0, 2, 3).reshape(layers, 1, ffn)
    qkv_bias = jnp.concatenate([small[:, 0], jnp.zeros((layers, width), f32), small[:, 1]], axis=1)
    qkv_bias = qkv_bias.reshape(layers, 1, 3 * width)

    core = [swap(weight, "narrow", 1) for weight in (qkv_weight, o_weight, in_weight, out_weight)]

    def half_of(weight, layer):
        rows = weight.shape[1] // 2
        return lax.dynamic_slice(weight, (layer, y * rows, 0), (1, rows, weight.shape[2]))[0]

    def spread(half):
        near_x = swap(half, "narrow", 2)
        far_x = swap(near_x, "wide", 1)
        return near_x, far_x, swap(near_x, "narrow", 1), swap(far_x, "narrow", 1)

    attn_weights, ffn_weights = [], []
    for layer in range(layers):
        joint = jnp.concatenate([half_of(qkv_weight, layer), half_of(o_weight, layer)], axis=1)
        attn_weights.append((qkv_weight, core[0], o_weight, core[1]) + spread(joint))
        ffn_weights.append(
            (in_weight, core[2])
            + spread(half_of(in_weight, layer))
            + (out_weight, core[3])
            + spread(half_of(out_weight, layer))
        )

    cell_col = cell_ids.reshape(tokens, 1)
    w_qkv = pltpu.VMEM((width, 3 * width), low)
    w_o = pltpu.VMEM((width, width), low)
    w_in = pltpu.VMEM((width, ffn), low)
    w_out = pltpu.VMEM((ffn, width), low)
    copy_sems = pltpu.SemaphoreType.DMA((12,))
    pair_sems = pltpu.SemaphoreType.DMA((2,))
    rows_f32 = shape((tokens, width), f32)
    column_f32 = shape((tokens, 1), f32)
    rows_low = shape((tokens, width), low)
    attn_flops = 2 * tokens * width * (4 * width + 2 * tokens)
    ffn_flops = 4 * tokens * width * ffn
    attn_bytes = 8 * width * width
    ffn_bytes = 4 * width * ffn

    def attn_forward(layer, x):
        return call(
            functools.partial(attn_fwd_kernel, layer),
            "attn_fwd",
            [SMEM, SMEM] + [VMEM] * 5 + [ANY] * 8,
            [VMEM] * 5,
            [
                shape((tokens, 3 * width), low),
                shape((HEADS, tokens, tokens), low),
                rows_low,
                rows_f32,
                column_f32,
            ],
            [w_qkv, w_o, pltpu.VMEM((tokens, tokens), f32), copy_sems],
            attn_flops,
            2 * attn_bytes,
            (ids, lengths, x, cell_ids, cell_col, qkv_bias[layer], small[layer]) + attn_weights[layer],
        )

    def ffn_forward(layer, unit_one):
        return call(
            functools.partial(ffn_fwd_kernel, layer),
            "ffn_fwd",
            [SMEM] + [VMEM] * 3 + [ANY] * 12,
            [VMEM] * 5,
            [
                shape((tokens, ffn), low),
                shape((tokens, ffn), f32),
                rows_f32,
                column_f32,
                rows_low,
            ],
            [w_in, w_out, pltpu.VMEM((tokens, width), low), copy_sems],
            ffn_flops,
            2 * ffn_bytes,
            (ids, unit_one, full_in_bias[layer], small[layer]) + ffn_weights[layer],
        )

    def ffn_backward(layer, grad, unit_two, inverse_two, unit_one, inverse_one, hidden, slope):
        pieces = shape((2, 8, 2, share, tile), low)
        return call(
            functools.partial(ffn_bwd_kernel, layer),
            "ffn_bwd",
            [SMEM] + [VMEM] * 8 + [ANY] * 12,
            [VMEM] * 3 + [ANY] * 2,
            [rows_f32, shape((8, width), f32), shape((1, ffn), f32), pieces, pieces],
            [
                w_in,
                w_out,
                pltpu.VMEM((tokens, width), low),
                pltpu.VMEM((tokens, width), f32),
                pltpu.VMEM((tokens, ffn), low),
                pltpu.VMEM((width, tokens), low),
                pltpu.VMEM((2, 2, 8, 2, share, tile), low),
                copy_sems,
                pair_sems,
            ],
            2 * ffn_flops,
            3 * ffn_bytes,
            (ids, grad, unit_two, inverse_two, unit_one, inverse_one, hidden, slope, small[layer])
            + ffn_weights[layer],
        )

    def attn_backward(layer, d_resid, x, qkv_rows, probs, context):
        pieces = shape((2, 8, 1, share, tile), low)
        return call(
            functools.partial(attn_bwd_kernel, layer),
            "attn_bwd",
            [SMEM] + [VMEM] * 5 + [ANY] * 8,
            [VMEM] * 2 + [ANY] * 2,
            [rows_low, shape((8, width), f32), pieces, pieces],
            [
                w_qkv,
                w_o,
                pltpu.VMEM((tokens, width), low),
                pltpu.VMEM((tokens, width), low),
                pltpu.VMEM((tokens, 3 * width), low),
                pltpu.VMEM((width, tokens), low),
                pltpu.VMEM((2, 2, 8, 1, share, tile), low),
                copy_sems,
                pair_sems,
            ],
            2 * attn_flops,
            3 * attn_bytes,
            (ids, d_resid, x, qkv_rows, probs, context) + attn_weights[layer],
        )

    stored = []
    x = tables_in
    for layer in range(layers):
        qkv_rows, probs, context, unit_one, inverse_one = attn_forward(layer, x)
        hidden, slope, unit_two, inverse_two, result = ffn_forward(layer, unit_one)
        stored.append((x, qkv_rows, probs, context, unit_one, inverse_one, hidden, slope, unit_two, inverse_two))
        x = result
    mixed_out = x

    grad = cotangent
    chunks = [None] * (2 * layers)
    attn_small, ffn_small, in_bias_grads = [None] * layers, [None] * layers, [None] * layers
    for layer in reversed(range(layers)):
        x, qkv_rows, probs, context, unit_one, inverse_one, hidden, slope, unit_two, inverse_two = stored[layer]
        d_resid, ffn_small[layer], in_bias_grads[layer], kept, sent = ffn_backward(
            layer, grad, unit_two, inverse_two, unit_one, inverse_one, hidden, slope
        )
        chunks[2 * layer + 1] = reduce_chunk(kept, sent, wide_bits)
        grad, attn_small[layer], kept, sent = attn_backward(layer, d_resid, x, qkv_rows, probs, context)
        chunks[2 * layer] = reduce_chunk(kept, sent, wide_bits)

    flat = [part for pair in chunks for part in pair]
    qkv_grad, o_grad, in_grad, out_grad = call(
        unpack_kernel,
        "unpack",
        [SMEM] + [ANY] * 8,
        [ANY] * 4,
        [
            shape((layers, share, 3 * width), f32),
            shape((layers, share, width), f32),
            shape((layers, share, ffn), f32),
            shape((layers, ffn_share, width), f32),
        ],
        [
            pltpu.VMEM((24, layers, share, tile), low),
            pltpu.VMEM((24, layers, share, tile), f32),
            pltpu.SemaphoreType.DMA((48,)),
            pltpu.SemaphoreType.DMA((48,)),
        ],
        0,
        6 * layers * 3 * share * ffn,
        (ids, *flat),
    )

    rows = jnp.stack(
        [jnp.concatenate([attn_small[i][:3], ffn_small[i][:5]], axis=0) for i in range(layers)]
    )
    rows, in_rows = lax.psum((rows, jnp.stack(in_bias_grads)), ("wide", "narrow"))
    rows = lax.dynamic_slice(rows, (0, 0, me * share), (layers, 8, share))
    in_rows = lax.dynamic_slice(in_rows, (0, 0, me * ffn_share), (layers, 1, ffn_share))[:, 0]
    return (
        mixed_out,
        grad,
        qkv_grad,
        rows[:, 0],
        rows[:, 1],
        o_grad,
        rows[:, 2],
        rows[:, 6],
        rows[:, 7],
        in_grad,
        in_rows,
        out_grad,
        rows[:, 5],
        rows[:, 3],
        rows[:, 4],
    )


def solution(mesh):
    by_table = P(("wide", "narrow"), None)
    matrix = P(None, "narrow", None)
    vector = P(None, "narrow")
    return jax.shard_map(
        body,
        mesh=mesh,
        in_specs=(
            by_table,
            by_table,
            by_table,
            P(("wide", "narrow")),
            matrix,
            vector,
            vector,
            matrix,
            vector,
            vector,
            vector,
            matrix,
            vector,
            matrix,
            vector,
            vector,
            vector,
        ),
        out_specs=(
            by_table,
            by_table,
            matrix,
            vector,
            vector,
            matrix,
            vector,
            vector,
            vector,
            matrix,
            vector,
            matrix,
            vector,
            vector,
            vector,
        ),
        check_vma=False,
    )
```

time: 1090 us -> 738 us (0.68); the launches traced: 1090 us -> 726 us
  waiting for transfers between devices: 689 us -> 463 us
  Pallas kernels: 0 us -> 122 us
  matrix products: 115 us -> 0 us
  blocking collectives: 81.3 us -> 5.23 us
  other arithmetic: 80.3 us -> 16.6 us
  starting transfers between devices: 19.6 us -> 58.3 us
  local copies, waits for them, and re-layouts: 73.9 us -> 44.4 us
    psum x1, waiting for transfers between devices: 383 us -> 118 us  [body(): lax.psum((rows, jnp.stack(in_bias_grads)), ('wide', 'narrow'))]
    ppermute x8 -> x60, waiting for transfers between devices: 86.5 us -> 345 us  [swap(): return lax.ppermute(value, axis, [(i, i ^ bit) for i in range(count)])]
    reduce_scatter x4 -> x0, waiting for transfers between devices: 129 us -> none  [the longest x1 47.5 us: body(): lax.psum_scatter(totals[9].astype(jnp.bfloat16), 'narrow', scatter_dimens...]
    pallas_call x0 -> x9, Pallas kernels: none -> 122 us  [call(): pl.pallas_call(kernel, name=name, in_specs=in_specs, out_specs=out_specs,...]
    dot_general x38 -> x0, matrix products: 115 us -> none  [the longest x8 34.3 us: cols_dot(): lax.dot_general(lhs_mat, rhs_mat, (((1,), (1,)), ((), ())), preferred_ele...]
    all_gather x4 -> x0, waiting for transfers between devices: 90.4 us -> none  [the longest x1 39.6 us: body(): lax.all_gather(own_layer[7], 'narrow', axis=0, tiled=True)]
    psum x1 -> x0, blocking collectives: 54.6 us -> none  [body(): lax.psum((by_section(shards[0]), by_section(shards[1]), by_section(shards...]
    ppermute x8 -> x60, starting transfers between devices: 19.3 us -> 58.2 us  [swap(): return lax.ppermute(value, axis, [(i, i ^ bit) for i in range(count)])]
  transfers between devices with their start and end apart: 17 -> 61, of which waited for: 10 -> 25; matrix products, arithmetic and copies ran while one was open for 11% -> 8% of each run, Pallas kernels for 0% -> 7%
where the time goes in v1:
time: 738 us; the launch traced here: 726 us
  waiting for transfers between devices  463 us (63%)
  Pallas kernels  122 us (17%)
  starting transfers between devices  58.3 us (8%)
  local copies, waits for them, and re-layouts  44.4 us (6%)
  other arithmetic  16.6 us (2%)
  between operations  15.8 us (2%)
    ppermute x60, waiting for transfers between devices, swap(): return lax.ppermute(value, axis, [(i, i ^ bit) for i in range(count)])  345 us
    pallas_call x9, Pallas kernels, call(): pl.pallas_call(kernel, name=name, in_specs=in_specs, out_specs=out_specs,...  122 us
    psum x1, waiting for transfers between devices, body(): lax.psum((rows, jnp.stack(in_bias_grads)), ('wide', 'narrow'))  118 us
    ppermute x60, starting transfers between devices, swap(): return lax.ppermute(value, axis, [(i, i ^ bit) for i in range(count)])  58.2 us
  transfers between devices with their start and end apart: 61, of which 25 were waited for; matrix products, arithmetic and copies ran while one was open for 8% of the time, Pallas kernels for 7%

profile of v1, /device:TPU:0, one launch (start us, length us, event | category | flops | bytes accessed | tf_op | source)
XLA Modules:
  0.0 725.6 jit_solution(3519533482200807962)
XLA Ops:
  7.7 1.7 dynamic-slice_bitcast_fusion.6
  9.4 2.1 dynamic-slice_bitcast_fusion.4
  12.4 2.5 collective-permute-start.2
  17.5 2.1 collective-permute-start.12
  19.8 2.1 collective-permute-start.20
  21.8 7.5 %collective-permute-done.2.rest_4_ = bf16[96,3072]{1,0:T(8,128)(2,1)S(1)} collective-permute-done((bf16[96,3072]{1,0:T(8,128)(2,1)}, bf16[96,3072]{1,0:T(8,128)(2,1)S(1)}, u32[]{:S(2)}, u32[]{:S(2)}) %collective-permute-start.2) | collective-permute-done | bytes 589856 | tf_op jit(solution)/shard_map/ppermute | solution.py:22
  29.3 2.0 collective-permute-start.24
  31.2 10.8 %collective-permute-done.7.rest_2_ = bf16[96,3072]{1,0:T(8,128)(2,1)} collective-permute-done((bf16[96,3072]{1,0:T(8,128)(2,1)}, bf16[96,3072]{1,0:T(8,128)(2,1)}, u32[]{:S(2)}, u32[]{:S(2)}) %collective-permute-start.7) | collective-permute-done | bytes 589856 | tf_op jit(solution)/shard_map/ppermute | solution.py:22
  42.0 2.0 collective-permute-start.3
  44.0 10.7 %collective-permute-done.12.rest_8_ = bf16[384,768]{1,0:T(8,128)(2,1)} collective-permute-done((bf16[384,768]{1,0:T(8,128)(2,1)S(1)}, bf16[384,768]{1,0:T(8,128)(2,1)}, u32[]{:S(2)}, u32[]{:S(2)}) %collective-permute-start.12) | collective-permute-done | bytes 589856 | tf_op jit(solution)/shard_map/ppermute | solution.py:22
  54.7 12.5 %collective-permute-done.16.rest_4_ = bf16[96,3072]{1,0:T(8,128)(2,1)S(1)} collective-permute-done((bf16[96,3072]{1,0:T(8,128)(2,1)S(1)}, bf16[96,3072]{1,0:T(8,128)(2,1)S(1)}, u32[]{:S(2)}, u32[]{:S(2)}) %collective-permute-start.16) | collective-permute-done | bytes 589856 | tf_op jit(solution)/shard_map/ppermute | solution.py:22
  67.2 2.0 collective-permute-start.8
  69.2 10.7 %collective-permute-done.20.rest_2_ = bf16[96,3072]{1,0:T(8,128)(2,1)S(1)} collective-permute-done((bf16[96,3072]{1,0:T(8,128)(2,1)S(1)}, bf16[96,3072]{1,0:T(8,128)(2,1)S(1)}, u32[]{:S(2)}, u32[]{:S(2)}) %collective-permute-start.20) | collective-permute-done | bytes 589856 | tf_op jit(solution)/shard_map/ppermute | solution.py:22
  79.9 12.4 %collective-permute-done.24.rest_8_ = bf16[384,768]{1,0:T(8,128)(2,1)S(1)} collective-permute-done((bf16[384,768]{1,0:T(8,128)(2,1)S(1)}, bf16[384,768]{1,0:T(8,128)(2,1)S(1)}, u32[]{:S(2)}, u32[]{:S(2)}) %collective-permute-start.24) | collective-permute-done | bytes 589856 | tf_op jit(solution)/shard_map/ppermute | solution.py:22
  92.3 1.8 collective-permute-start.13
  102.6 5.2 all-gather
  110.0 1.6 reshape.833
  113.7 1.6 reshape.791
  116.0 8.2 %collective-permute-done.17.rest_5_ = bf16[96,3072]{1,0:T(8,128)(2,1)} collective-permute-done((bf16[96,3072]{1,0:T(8,128)(2,1)}, bf16[96,3072]{1,0:T(8,128)(2,1)}, u32[]{:S(2)}, u32[]{:S(2)}) %collective-permute-start.17) | collective-permute-done | bytes 589856 | tf_op jit(solution)/shard_map/ppermute | solution.py:22
  124.5 1.7 collective-permute-start.25
  126.3 14.5 %collective-permute-done.21.rest_3_ = bf16[96,3072]{1,0:T(8,128)(2,1)} collective-permute-done((bf16[96,3072]{1,0:T(8,128)(2,1)}, bf16[96,3072]{1,0:T(8,128)(2,1)}, u32[]{:S(2)}, u32[]{:S(2)}) %collective-permute-start.21) | collective-permute-done | bytes 589856 | tf_op jit(solution)/shard_map/ppermute | solution.py:22
  140.8 11.1 %collective-permute-done.25.rest_9_ = bf16[384,768]{1,0:T(8,128)(2,1)} collective-permute-done((bf16[384,768]{1,0:T(8,128)(2,1)}, bf16[384,768]{1,0:T(8,128)(2,1)}, u32[]{:S(2)}, u32[]{:S(2)}) %collective-permute-start.25) | collective-permute-done | bytes 589856 | tf_op jit(solution)/shard_map/ppermute | solution.py:22
  162.9 13.1 %attn_fwd.2 = (bf16[256,2304]{1,0:T(8,128)(2,1)}, bf16[12,256,256]{2,1,0:T(8,128)(2,1)}, bf16[256,768]{1,0:T(8,128)(2,1)}, f32[256,768]{1,0:T(8,128)}, f32[256,1]{1,0:T(8,128)}) custom-call(s32[6]{0:T(128)} %stack.69.ids, s32[1]{0:T(128)S(6)} %copy.150.length, bf16[256,768]{1,0:T(8,128)(2,1)} %x.3, s32[1,256]{1,0:T(1,128)} %cell_row.3, ...), custom_call_target="tpu_custom_call" | custom-call | flops 1409286144 | bytes 9437184 | tf_op jit(solution)/shard_map/attn_fwd/pallas_call | solution.py:352
  176.0 10.0 %ffn_fwd.2 = (bf16[256,3072]{1,0:T(8,128)(2,1)}, f32[256,3072]{1,0:T(8,128)}, f32[256,768]{1,0:T(8,128)}, f32[256,1]{1,0:T(8,128)}, bf16[256,768]{1,0:T(8,128)(2,1)}) custom-call(s32[6]{0:T(128)} %stack.69.ids, f32[256,768]{1,0:T(8,128)} %get-tuple-element.57.unit_one, f32[1,3072]{1,0:T(1,128)} %squeeze.51.in_bias, f32[8,768]{1,0:T(8,128)} %squeeze.48.small, ...), custom_call_target="tpu_custom_call" | custom-call | flops 2415919104 | bytes 18874368 | tf_op jit(solution)/shard_map/ffn_fwd/pallas_call | solution.py:352
  186.0 13.0 %attn_fwd.3 = (bf16[256,2304]{1,0:T(8,128)(2,1)}, bf16[12,256,256]{2,1,0:T(8,128)(2,1)}, bf16[256,768]{1,0:T(8,128)(2,1)}, f32[256,768]{1,0:T(8,128)}, f32[256,1]{1,0:T(8,128)}) custom-call(s32[6]{0:T(128)} %stack.69.ids, s32[1]{0:T(128)S(6)} %copy.150.length, bf16[256,768]{1,0:T(8,128)(2,1)} %get-tuple-element.58.x, s32[1,256]{1,0:T(1,128)} %cell_row.3, ...), custom_call_target="tpu_custom_call" | custom-call | flops 1409286144 | bytes 9437184 | tf_op jit(solution)/shard_map/attn_fwd/pallas_call | solution.py:352
  200.1 10.0 %ffn_fwd.3 = (bf16[256,3072]{1,0:T(8,128)(2,1)}, f32[256,3072]{1,0:T(8,128)}, f32[256,768]{1,0:T(8,128)}, f32[256,1]{1,0:T(8,128)}, bf16[256,768]{1,0:T(8,128)(2,1)}) custom-call(s32[6]{0:T(128)} %stack.69.ids, f32[256,768]{1,0:T(8,128)} %get-tuple-element.59.unit_one, f32[1,3072]{1,0:T(1,128)} %squeeze.57.in_bias, f32[8,768]{1,0:T(8,128)} %squeeze.54.small, ...), custom_call_target="tpu_custom_call" | custom-call | flops 2415919104 | bytes 18874368 | tf_op jit(solution)/shard_map/ffn_fwd/pallas_call | solution.py:352
  210.1 17.6 %ffn_bwd.2 = (f32[256,768]{1,0:T(8,128)}, f32[8,768]{1,0:T(8,128)}, f32[1,3072]{1,0:T(1,128)}, bf16[2,8,2,192,384]{4,3,2,1,0:T(8,128)(2,1)}, bf16[2,8,2,192,384]{4,3,2,1,0:T(8,128)(2,1)}) custom-call(s32[6]{0:T(128)} %stack.69.ids, bf16[256,768]{1,0:T(8,128)(2,1)} %grad.1, f32[256,768]{1,0:T(8,128)} %get-tuple-element.61.unit_two, ...), custom_call_target="tpu_custom_call" | custom-call | flops 4831838208 | bytes 28311552 | tf_op jit(solution)/shard_map/ffn_bwd/pallas_call | solution.py:352
  227.7 15.8 %attn_bwd.2 = (bf16[256,768]{1,0:T(8,128)(2,1)}, f32[8,768]{1,0:T(8,128)}, bf16[2,8,1,192,384]{4,3,2,1,0:T(8,128)(2,1)}, bf16[2,8,1,192,384]{4,3,2,1,0:T(8,128)(2,1)}) custom-call(s32[6]{0:T(128)} %stack.69.ids, f32[256,768]{1,0:T(8,128)} %get-tuple-element.66.d_resid, bf16[256,768]{1,0:T(8,128)(2,1)} %get-tuple-element.58.x, ...), custom_call_target="tpu_custom_call" | custom-call | flops 2818572288 | bytes 14155776 | tf_op jit(solution)/shard_map/attn_bwd/pallas_call | solution.py:352
  243.5 17.4 %ffn_bwd.3 = (f32[256,768]{1,0:T(8,128)}, f32[8,768]{1,0:T(8,128)}, f32[1,3072]{1,0:T(1,128)}, bf16[2,8,2,192,384]{4,3,2,1,0:T(8,128)(2,1)}, bf16[2,8,2,192,384]{4,3,2,1,0:T(8,128)(2,1)}) custom-call(s32[6]{0:T(128)} %stack.69.ids, bf16[256,768]{1,0:T(8,128)(2,1)} %get-tuple-element.70.grad, f32[256,768]{1,0:T(8,128)} %get-tuple-element.71.unit_two, ...), custom_call_target="tpu_custom_call" | custom-call | flops 4831838208 | bytes 28311552 | tf_op jit(solution)/shard_map/ffn_bwd/pallas_call | solution.py:352
  261.6 15.6 %attn_bwd.3 = (bf16[256,768]{1,0:T(8,128)(2,1)}, f32[8,768]{1,0:T(8,128)}, bf16[2,8,1,192,384]{4,3,2,1,0:T(8,128)(2,1)}, bf16[2,8,1,192,384]{4,3,2,1,0:T(8,128)(2,1)}) custom-call(s32[6]{0:T(128)} %stack.69.ids, f32[256,768]{1,0:T(8,128)} %get-tuple-element.76.d_resid, bf16[256,768]{1,0:T(8,128)(2,1)} %x.3, bf16[256,2304]{1,0:T(8,128)(2,1)} %get-tuple-element.77.qkv_rows, ...), custom_call_target="tpu_custom_call" | custom-call | flops 2818572288 | bytes 14155776 | tf_op jit(solution)/shard_map/attn_bwd/pallas_call | solution.py:352
  277.8 3.1 fusion.51
  282.0 5.3 fusion.3
  288.9 3.0 fusion.1
  292.4 2.0 fusion.53
  295.4 1.6 collective-permute-start.29
  297.8 43.8 %collective-permute-done.37 = bf16[2,2,2,2,192,384]{5,4,3,2,1,0:T(8,128)(2,1)S(1)} collective-permute-done((bf16[2,2,2,2,192,384]{5,4,3,2,1,0:T(8,128)(2,1)}, bf16[2,2,2,2,192,384]{5,4,3,2,1,0:T(8,128)(2,1)S(1)}, u32[]{:S(2)}, u32[]{:S(2)}) %collective-permute-start.37) | collective-permute-done | bytes 2359328 | tf_op jit(solution)/shard_map/ppermute | solution.py:22
  342.7 49.5 %collective-permute-done.53 = bf16[2,2,2,2,192,384]{5,4,3,2,1,0:T(8,128)(2,1)S(1)} collective-permute-done((bf16[2,2,2,2,192,384]{5,4,3,2,1,0:T(8,128)(2,1)}, bf16[2,2,2,2,192,384]{5,4,3,2,1,0:T(8,128)(2,1)S(1)}, u32[]{:S(2)}, u32[]{:S(2)}) %collective-permute-start.53) | collective-permute-done | bytes 2359328 | tf_op jit(solution)/shard_map/ppermute | solution.py:22
  393.9 23.6 %collective-permute-done.29 = bf16[2,2,2,1,192,384]{5,4,2,3,1,0:T(8,128)(2,1)S(1)} collective-permute-done((bf16[2,2,2,1,192,384]{5,4,2,3,1,0:T(8,128)(2,1)S(1)}, bf16[2,2,2,1,192,384]{5,4,2,3,1,0:T(8,128)(2,1)S(1)}, u32[]{:S(2)}, u32[]{:S(2)}) %collective-permute-start.29) | collective-permute-done | bytes 1179680 | tf_op jit(solution)/shard_map/ppermute | solution.py:22
  418.2 24.1 %collective-permute-done.45 = bf16[2,2,2,1,192,384]{5,4,2,3,1,0:T(8,128)(2,1)S(1)} collective-permute-done((bf16[2,2,2,1,192,384]{5,4,2,3,1,0:T(8,128)(2,1)S(1)}, bf16[2,2,2,1,192,384]{5,4,2,3,1,0:T(8,128)(2,1)S(1)}, u32[]{:S(2)}, u32[]{:S(2)}) %collective-permute-start.45) | collective-permute-done | bytes 1179680 | tf_op jit(solution)/shard_map/ppermute | solution.py:22
  443.3 1.6 collective-permute-start.39
  445.9 1.6 collective-permute-start.31
  447.6 10.0 %collective-permute-done.46 = bf16[2,2,1,192,384]{4,3,2,1,0:T(8,128)(2,1)S(1)} collective-permute-done((bf16[2,2,1,192,384]{4,3,2,1,0:T(8,128)(2,1)S(1)}, bf16[2,2,1,192,384]{4,3,2,1,0:T(8,128)(2,1)S(1)}, u32[]{:S(2)}, u32[]{:S(2)}) %collective-permute-start.46) | collective-permute-done | bytes 589856 | tf_op jit(solution)/shard_map/ppermute | solution.py:22
  457.7 1.6 collective-permute-start.47
  459.7 2.7 collective-permute-start.40
  462.4 16.2 %collective-permute-done.55 = bf16[2,2,192,384]{3,2,1,0:T(8,128)(2,1)S(1)} collective-permute-done((bf16[2,2,192,384]{3,2,1,0:T(8,128)(2,1)S(1)}, bf16[2,2,192,384]{3,2,1,0:T(8,128)(2,1)S(1)}, u32[]{:S(2)}, u32[]{:S(2)}) %collective-permute-start.55) | collective-permute-done | bytes 589856 | tf_op jit(solution)/shard_map/ppermute | solution.py:22
  478.7 1.7 collective-permute-start.56
  480.4 9.8 %collective-permute-done.31 = bf16[2,1,192,384]{3,2,1,0:T(8,128)(2,1)S(1)} collective-permute-done((bf16[2,1,192,384]{3,2,1,0:T(8,128)(2,1)S(1)}, bf16[2,1,192,384]{3,2,1,0:T(8,128)(2,1)S(1)}, u32[]{:S(2)}, u32[]{:S(2)}) %collective-permute-start.31) | collective-permute-done | bytes 294944 | tf_op jit(solution)/shard_map/ppermute | solution.py:22
  490.8 3.2 collective-permute-start.41
  494.0 20.1 %collective-permute-done.56 = bf16[2,192,384]{2,1,0:T(8,128)(2,1)S(1)} collective-permute-done((bf16[2,192,384]{2,1,0:T(8,128)(2,1)S(1)}, bf16[2,192,384]{2,1,0:T(8,128)(2,1)S(1)}, u32[]{:S(2)}, u32[]{:S(2)}) %collective-permute-start.56) | collective-permute-done | bytes 294944 | tf_op jit(solution)/shard_map/ppermute | solution.py:22
  514.4 3.2 collective-permute-start.48
  517.6 10.7 %collective-permute-done.41 = bf16[1,2,192,384]{3,2,1,0:T(8,128)(2,1)S(1)} collective-permute-done((bf16[1,2,192,384]{3,2,1,0:T(8,128)(2,1)S(1)}, bf16[1,2,192,384]{3,2,1,0:T(8,128)(2,1)S(1)}, u32[]{:S(2)}, u32[]{:S(2)}) %collective-permute-start.41) | collective-permute-done | bytes 294944 | tf_op jit(solution)/shard_map/ppermute | solution.py:22
  529.7 5.0 collective-permute-done.57
  535.5 3.5 collective-permute-start.33
  539.1 20.2 %collective-permute-done.33 = bf16[1,1,192,384]{3,2,1,0:T(8,128)(2,1)S(1)} collective-permute-done((bf16[1,1,192,384]{3,2,1,0:T(8,128)(2,1)S(1)}, bf16[1,1,192,384]{3,2,1,0:T(8,128)(2,1)S(1)}, u32[]{:S(2)}, u32[]{:S(2)}) %collective-permute-start.33) | collective-permute-done | bytes 147488 | tf_op jit(solution)/shard_map/ppermute | solution.py:22
  559.4 2.0 collective-permute-start.34
  561.5 1.8 collective-permute-start.43
  563.3 5.3 collective-permute-done.58
  568.8 1.8 collective-permute-start.59
  571.4 3.5 collective-permute-done.34
  575.0 1.8 collective-permute-start.35
  576.8 4.3 collective-permute-done.50
  581.3 1.8 collective-permute-start.51
  583.7 118.3 %all-reduce.3.cloned.1.call-done = (f32[2,8,768]{2,1,0:T(8,128)}, f32[2,1,3072]{2,0,1:T(2,128)}) async-done(((f32[2,8,768]{2,1,0:T(8,128)}, f32[2,1,3072]{2,0,1:T(2,128)}), (f32[2,8,768]{2,1,0:T(8,128)}, f32[2,1,3072]{2,0,1:T(2,128)})) %all-reduce.3.cloned.1.call-update) | async-done | bytes 73744 | tf_op jit(solution)/shard_map/psum | solution.py:608
  709.2 9.1 %unpack.1 = (f32[2,192,2304]{2,1,0:T(8,128)}, f32[2,192,768]{2,1,0:T(8,128)}, f32[2,192,3072]{2,1,0:T(8,128)}, f32[2,768,768]{2,1,0:T(8,128)}) custom-call(s32[6]{0:T(128)} %stack.69.ids, bf16[4,1,192,384]{3,2,1,0:T(8,128)(2,1)} %copy-done.13, bf16[4,1,192,384]{3,2,1,0:T(8,128)(2,1)} %collective-permute-done.35.rest_1_, bf16[4,2,192,384]{3,2,1,0:T(8,128)(2,1)} %copy-done.2, ...), custom_call_target="tpu_custom_call" | custom-call | bytes 21233664 | tf_op jit(solution)/shard_map/unpack/pallas_call | solution.py:352
  (225 shorter events, 53.3 us)
Async XLA Ops:
  7.2 694.9 %all-reduce.3.cloned.1.call-start = ((), (), s32[]{:S(2)}) async-start(), calls=%async_computation | async-start | bytes 147456 | tf_op jit(solution)/shard_map/psum | solution.py:608
  7.2 12.5 %collective-permute-start.1 = (bf16[2,192,768]{2,1,0:T(8,128)(2,1)}, bf16[2,192,768]{2,1,0:T(8,128)(2,1)S(1)}, u32[]{:S(2)}, u32[]{:S(2)}) collective-permute-start(bf16[2,192,768]{2,1,0:T(8,128)(2,1)} %rest_2_.7), channel_id=1, source_target_pairs={{0,1},{1,0},{2,3},{3,2},{4,5},{5,4},{6,7},{7,6},{8,9},{9,8},{10,11... | collective-permute-start | bytes 1769480 | tf_op jit(solution)/shard_map/ppermute | solution.py:22
  12.4 16.9 %collective-permute-start.2 = (bf16[96,3072]{1,0:T(8,128)(2,1)}, bf16[96,3072]{1,0:T(8,128)(2,1)S(1)}, u32[]{:S(2)}, u32[]{:S(2)}) collective-permute-start(bf16[96,3072]{1,0:T(8,128)(2,1)} %pad_maximum_fusion.2), channel_id=1, source_target_pairs={{0,2},{1,3},{2,0},{3,1},{4,6},{5,7},{6,4},{7,5},{8,10},{9,11},{10,... | collective-permute-start | bytes 1769480 | tf_op jit(solution)/shard_map/ppermute | solution.py:22
  16.0 26.0 %collective-permute-start.7 = (bf16[96,3072]{1,0:T(8,128)(2,1)}, bf16[96,3072]{1,0:T(8,128)(2,1)}, u32[]{:S(2)}, u32[]{:S(2)}) collective-permute-start(bf16[96,3072]{1,0:T(8,128)(2,1)} %get-tuple-element.130), channel_id=1, source_target_pairs={{0,2},{1,3},{2,0},{3,1},{4,6},{5,7},{6,4},{7,5},{8,10},{9,11},{10,... | collective-permute-start | bytes 1769480 | tf_op jit(solution)/shard_map/ppermute | solution.py:22
  17.5 37.1 %collective-permute-start.12 = (bf16[384,768]{1,0:T(8,128)(2,1)S(1)}, bf16[384,768]{1,0:T(8,128)(2,1)}, u32[]{:S(2)}, u32[]{:S(2)}) collective-permute-start(bf16[384,768]{1,0:T(8,128)(2,1)S(1)} %get-tuple-element.128), channel_id=1, source_target_pairs={{0,2},{1,3},{2,0},{3,1},{4,6},{5,7},{6,4},{7,5},{8,10},{9,11},{10,... | collective-permute-start | bytes 1769480 | tf_op jit(solution)/shard_map/ppermute | solution.py:22
  19.7 47.6 %collective-permute-start.16 = (bf16[96,3072]{1,0:T(8,128)(2,1)S(1)}, bf16[96,3072]{1,0:T(8,128)(2,1)S(1)}, u32[]{:S(2)}, u32[]{:S(2)}) collective-permute-start(bf16[96,3072]{1,0:T(8,128)(2,1)S(1)} %pad_maximum_fusion.3), channel_id=1, source_target_pairs={{0,2},{1,3},{2,0},{3,1},{4,6},{5,7},{6,4},{7,5},{8,10},{9,11},{10,... | collective-permute-start | bytes 1769480 | tf_op jit(solution)/shard_map/ppermute | solution.py:22
  19.8 143.1 %copy-start.1 = (bf16[2,192,768]{2,1,0:T(8,128)(2,1)}, bf16[2,192,768]{2,1,0:T(8,128)(2,1)S(1)}, u32[]{:S(2)}) copy-start(bf16[2,192,768]{2,1,0:T(8,128)(2,1)S(1)} %collective-permute-done.1.rest_3_) | copy-start | bytes 1769476
  19.8 60.1 %collective-permute-start.20 = (bf16[96,3072]{1,0:T(8,128)(2,1)S(1)}, bf16[96,3072]{1,0:T(8,128)(2,1)S(1)}, u32[]{:S(2)}, u32[]{:S(2)}) collective-permute-start(bf16[96,3072]{1,0:T(8,128)(2,1)S(1)} %copy-done.17), channel_id=1, source_target_pairs={{0,2},{1,3},{2,0},{3,1},{4,6},{5,7},{6,4},{7,5},{8,10},{9,11},{10,... | collective-permute-start | bytes 1769480 | tf_op jit(solution)/shard_map/ppermute | solution.py:22
  29.3 133.6 %copy-start.5 = (bf16[96,3072]{1,0:T(8,128)(2,1)}, bf16[96,3072]{1,0:T(8,128)(2,1)S(1)}, u32[]{:S(2)}) copy-start(bf16[96,3072]{1,0:T(8,128)(2,1)S(1)} %collective-permute-done.2.rest_4_) | copy-start | bytes 1769476
  29.3 63.0 %collective-permute-start.24 = (bf16[384,768]{1,0:T(8,128)(2,1)S(1)}, bf16[384,768]{1,0:T(8,128)(2,1)S(1)}, u32[]{:S(2)}, u32[]{:S(2)}) collective-permute-start(bf16[384,768]{1,0:T(8,128)(2,1)S(1)} %get-tuple-element.127), channel_id=1, source_target_pairs={{0,2},{1,3},{2,0},{3,1},{4,6},{5,7},{6,4},{7,5},{8,10},{9,11},{10,... | collective-permute-start | bytes 1769480 | tf_op jit(solution)/shard_map/ppermute | solution.py:22
  42.0 52.0 %collective-permute-start.3 = (bf16[96,3072]{1,0:T(8,128)(2,1)S(1)}, bf16[96,3072]{1,0:T(8,128)(2,1)S(1)}, u32[]{:S(2)}, u32[]{:S(2)}) collective-permute-start(bf16[96,3072]{1,0:T(8,128)(2,1)S(1)} %collective-permute-done.2.rest_4_), channel_id=1, source_target_pairs={{0,4},{4,0},{8,12},{12,8},{16,20},{20,16},{24,28},{28,24},{1,5},{5... | collective-permute-start | bytes 1769480 | tf_op jit(solution)/shard_map/ppermute | solution.py:22
  54.7 39.4 %collective-permute-start.4 = (bf16[96,3072]{1,0:T(8,128)(2,1)S(1)}, bf16[96,3072]{1,0:T(8,128)(2,1)S(1)}, u32[]{:S(2)}, u32[]{:S(2)}) collective-permute-start(bf16[96,3072]{1,0:T(8,128)(2,1)S(1)} %collective-permute-done.2.rest_4_), channel_id=1, source_target_pairs={{0,1},{1,0},{2,3},{3,2},{4,5},{5,4},{6,7},{7,6},{8,9},{9,8},{10,11... | collective-permute-start | bytes 1769480 | tf_op jit(solution)/shard_map/ppermute | solution.py:22
  67.2 40.6 %collective-permute-start.8 = (bf16[96,3072]{1,0:T(8,128)(2,1)}, bf16[96,3072]{1,0:T(8,128)(2,1)}, u32[]{:S(2)}, u32[]{:S(2)}) collective-permute-start(bf16[96,3072]{1,0:T(8,128)(2,1)} %collective-permute-done.7.rest_2_), channel_id=1, source_target_pairs={{0,4},{4,0},{8,12},{12,8},{16,20},{20,16},{24,28},{28,24},{1,5},{5... | collective-permute-start | bytes 1769480 | tf_op jit(solution)/shard_map/ppermute | solution.py:22
  79.9 28.3 %collective-permute-start.9 = (bf16[96,3072]{1,0:T(8,128)(2,1)}, bf16[96,3072]{1,0:T(8,128)(2,1)}, u32[]{:S(2)}, u32[]{:S(2)}) collective-permute-start(bf16[96,3072]{1,0:T(8,128)(2,1)} %collective-permute-done.7.rest_2_), channel_id=1, source_target_pairs={{0,1},{1,0},{2,3},{3,2},{4,5},{5,4},{6,7},{7,6},{8,9},{9,8},{10,11... | collective-permute-start | bytes 1769480 | tf_op jit(solution)/shard_map/ppermute | solution.py:22
  92.3 16.0 %collective-permute-start.13 = (bf16[384,768]{1,0:T(8,128)(2,1)}, bf16[384,768]{1,0:T(8,128)(2,1)}, u32[]{:S(2)}, u32[]{:S(2)}) collective-permute-start(bf16[384,768]{1,0:T(8,128)(2,1)} %collective-permute-done.12.rest_8_), channel_id=1, source_target_pairs={{0,4},{4,0},{8,12},{12,8},{16,20},{20,16},{24,28},{28,24},{1,5},{5... | collective-permute-start | bytes 1769480 | tf_op jit(solution)/shard_map/ppermute | solution.py:22
  94.1 15.2 %collective-permute-start.14 = (bf16[384,768]{1,0:T(8,128)(2,1)}, bf16[384,768]{1,0:T(8,128)(2,1)}, u32[]{:S(2)}, u32[]{:S(2)}) collective-permute-start(bf16[384,768]{1,0:T(8,128)(2,1)} %collective-permute-done.12.rest_8_), channel_id=1, source_target_pairs={{0,1},{1,0},{2,3},{3,2},{4,5},{5,4},{6,7},{7,6},{8,9},{9,8},{10,11... | collective-permute-start | bytes 1769480 | tf_op jit(solution)/shard_map/ppermute | solution.py:22
  94.9 57.1 %collective-permute-start = (bf16[2,192,2304]{2,1,0:T(8,128)(2,1)}, bf16[2,192,2304]{2,1,0:T(8,128)(2,1)}, u32[]{:S(2)}, u32[]{:S(2)}) collective-permute-start(bf16[2,192,2304]{2,1,0:T(8,128)(2,1)} %rest_0_.15), channel_id=1, source_target_pairs={{0,1},{1,0},{2,3},{3,2},{4,5},{5,4},{6,7},{7,6},{8,9},{9,8},{10,11... | collective-permute-start | bytes 5308424 | tf_op jit(solution)/shard_map/ppermute | solution.py:22
  107.8 49.4 %collective-permute-start.6 = (bf16[2,192,3072]{2,1,0:T(8,128)(2,1)S(1)}, bf16[2,192,3072]{2,1,0:T(8,128)(2,1)}, u32[]{:S(2)}, u32[]{:S(2)}) collective-permute-start(bf16[2,192,3072]{2,1,0:T(8,128)(2,1)S(1)} %copy-done), channel_id=1, source_target_pairs={{0,1},{1,0},{2,3},{3,2},{4,5},{5,4},{6,7},{7,6},{8,9},{9,8},{10,11... | collective-permute-start | bytes 7077896 | tf_op jit(solution)/shard_map/ppermute | solution.py:22
  108.1 49.5 %collective-permute-start.11 = (bf16[2,768,768]{2,1,0:T(8,128)(2,1)}, bf16[2,768,768]{2,1,0:T(8,128)(2,1)}, u32[]{:S(2)}, u32[]{:S(2)}) collective-permute-start(bf16[2,768,768]{2,1,0:T(8,128)(2,1)} %rest_6_.7), channel_id=1, source_target_pairs={{0,1},{1,0},{2,3},{3,2},{4,5},{5,4},{6,7},{7,6},{8,9},{9,8},{10,11... | collective-permute-start | bytes 7077896 | tf_op jit(solution)/shard_map/ppermute | solution.py:22
  108.3 15.9 %collective-permute-start.17 = (bf16[96,3072]{1,0:T(8,128)(2,1)}, bf16[96,3072]{1,0:T(8,128)(2,1)}, u32[]{:S(2)}, u32[]{:S(2)}) collective-permute-start(bf16[96,3072]{1,0:T(8,128)(2,1)} %copy-done.8), channel_id=1, source_target_pairs={{0,4},{4,0},{8,12},{12,8},{16,20},{20,16},{24,28},{28,24},{1,5},{5... | collective-permute-start | bytes 1769480 | tf_op jit(solution)/shard_map/ppermute | solution.py:22
  109.3 15.2 %collective-permute-start.18 = (bf16[96,3072]{1,0:T(8,128)(2,1)}, bf16[96,3072]{1,0:T(8,128)(2,1)}, u32[]{:S(2)}, u32[]{:S(2)}) collective-permute-start(bf16[96,3072]{1,0:T(8,128)(2,1)} %copy-done.8), channel_id=1, source_target_pairs={{0,1},{1,0},{2,3},{3,2},{4,5},{5,4},{6,7},{7,6},{8,9},{9,8},{10,11... | collective-permute-start | bytes 1769480 | tf_op jit(solution)/shard_map/ppermute | solution.py:22
  124.2 16.6 %collective-permute-start.21 = (bf16[96,3072]{1,0:T(8,128)(2,1)}, bf16[96,3072]{1,0:T(8,128)(2,1)}, u32[]{:S(2)}, u32[]{:S(2)}) collective-permute-start(bf16[96,3072]{1,0:T(8,128)(2,1)} %copy-done.9), channel_id=1, source_target_pairs={{0,4},{4,0},{8,12},{12,8},{16,20},{20,16},{24,28},{28,24},{1,5},{5... | collective-permute-start | bytes 1769480 | tf_op jit(solution)/shard_map/ppermute | solution.py:22
  124.5 27.4 %collective-permute-start.25 = (bf16[384,768]{1,0:T(8,128)(2,1)}, bf16[384,768]{1,0:T(8,128)(2,1)}, u32[]{:S(2)}, u32[]{:S(2)}) collective-permute-start(bf16[384,768]{1,0:T(8,128)(2,1)} %copy-done.10), channel_id=1, source_target_pairs={{0,4},{4,0},{8,12},{12,8},{16,20},{20,16},{24,28},{28,24},{1,5},{5... | collective-permute-start | bytes 1769480 | tf_op jit(solution)/shard_map/ppermute | solution.py:22
  140.8 13.0 %collective-permute-start.5 = (bf16[96,3072]{1,0:T(8,128)(2,1)}, bf16[96,3072]{1,0:T(8,128)(2,1)}, u32[]{:S(2)}, u32[]{:S(2)}) collective-permute-start(bf16[96,3072]{1,0:T(8,128)(2,1)} %copy-done.6), channel_id=1, source_target_pairs={{0,1},{1,0},{2,3},{3,2},{4,5},{5,4},{6,7},{7,6},{8,9},{9,8},{10,11... | collective-permute-start | bytes 1769480 | tf_op jit(solution)/shard_map/ppermute | solution.py:22
  151.9 4.7 collective-permute-start.10
  151.9 5.2 collective-permute-start.15
  153.8 32.2 %collective-permute-start.19 = (bf16[96,3072]{1,0:T(8,128)(2,1)}, bf16[96,3072]{1,0:T(8,128)(2,1)}, u32[]{:S(2)}, u32[]{:S(2)}) collective-permute-start(bf16[96,3072]{1,0:T(8,128)(2,1)} %collective-permute-done.17.rest_5_), channel_id=1, source_target_pairs={{0,1},{1,0},{2,3},{3,2},{4,5},{5,4},{6,7},{7,6},{8,9},{9,8},{10,11... | collective-permute-start | bytes 1769480 | tf_op jit(solution)/shard_map/ppermute | solution.py:22
  156.6 42.4 %collective-permute-start.22 = (bf16[96,3072]{1,0:T(8,128)(2,1)}, bf16[96,3072]{1,0:T(8,128)(2,1)}, u32[]{:S(2)}, u32[]{:S(2)}) collective-permute-start(bf16[96,3072]{1,0:T(8,128)(2,1)} %copy-done.9), channel_id=1, source_target_pairs={{0,1},{1,0},{2,3},{3,2},{4,5},{5,4},{6,7},{7,6},{8,9},{9,8},{10,11... | collective-permute-start | bytes 1769480 | tf_op jit(solution)/shard_map/ppermute | solution.py:22
  157.1 41.9 %collective-permute-start.26 = (bf16[384,768]{1,0:T(8,128)(2,1)}, bf16[384,768]{1,0:T(8,128)(2,1)}, u32[]{:S(2)}, u32[]{:S(2)}) collective-permute-start(bf16[384,768]{1,0:T(8,128)(2,1)} %copy-done.10), channel_id=1, source_target_pairs={{0,1},{1,0},{2,3},{3,2},{4,5},{5,4},{6,7},{7,6},{8,9},{9,8},{10,11... | collective-permute-start | bytes 1769480 | tf_op jit(solution)/shard_map/ppermute | solution.py:22
  157.2 41.8 %collective-permute-start.23 = (bf16[96,3072]{1,0:T(8,128)(2,1)}, bf16[96,3072]{1,0:T(8,128)(2,1)S(1)}, u32[]{:S(2)}, u32[]{:S(2)}) collective-permute-start(bf16[96,3072]{1,0:T(8,128)(2,1)} %collective-permute-done.21.rest_3_), channel_id=1, source_target_pairs={{0,1},{1,0},{2,3},{3,2},{4,5},{5,4},{6,7},{7,6},{8,9},{9,8},{10,11... | collective-permute-start | bytes 1769480 | tf_op jit(solution)/shard_map/ppermute | solution.py:22
  157.6 41.4 %collective-permute-start.27 = (bf16[384,768]{1,0:T(8,128)(2,1)}, bf16[384,768]{1,0:T(8,128)(2,1)S(1)}, u32[]{:S(2)}, u32[]{:S(2)}) collective-permute-start(bf16[384,768]{1,0:T(8,128)(2,1)} %collective-permute-done.25.rest_9_), channel_id=1, source_target_pairs={{0,1},{1,0},{2,3},{3,2},{4,5},{5,4},{6,7},{7,6},{8,9},{9,8},{10,11... | collective-permute-start | bytes 1769480 | tf_op jit(solution)/shard_map/ppermute | solution.py:22
  261.0 21.1 %collective-permute-start.36 = (bf16[2,2,2,2,2,192,384]{6,5,4,3,2,1,0:T(8,128)(2,1)}, bf16[2,2,2,2,2,192,384]{6,5,4,3,2,1,0:T(8,128)(2,1)}, u32[]{:S(2)}, u32[]{:S(2)}) collective-permute-start(bf16[2,2,2,2,2,192,384]{6,5,4,3,2,1,0:T(8,128)(2,1)} %bitcast.325), channel_id=1, source_target_pairs={{0,1},{1,0},{2,3},{3,2},{4,5},{5,4},{6,7},{7,6},{8,9},{9,8},{10,11... | collective-permute-start | bytes 14155784 | tf_op jit(solution)/shard_map/ppermute | solution.py:22
  261.5 27.4 %collective-permute-start.52 = (bf16[2,2,2,2,2,192,384]{6,5,4,3,2,1,0:T(8,128)(2,1)}, bf16[2,2,2,2,2,192,384]{6,5,4,3,2,1,0:T(8,128)(2,1)S(1)}, u32[]{:S(2)}, u32[]{:S(2)}) collective-permute-start(bf16[2,2,2,2,2,192,384]{6,5,4,3,2,1,0:T(8,128)(2,1)} %bitcast.324), channel_id=1, source_target_pairs={{0,1},{1,0},{2,3},{3,2},{4,5},{5,4},{6,7},{7,6},{8,9},{9,8},{10,11... | collective-permute-start | bytes 14155784 | tf_op jit(solution)/shard_map/ppermute | solution.py:22
  277.2 17.9 %collective-permute-start.28 = (bf16[2,2,2,2,1,192,384]{6,5,3,2,1,4,0:T(8,128)(2,1)}, bf16[2,2,2,2,1,192,384]{6,5,3,2,1,4,0:T(8,128)(2,1)S(1)}, u32[]{:S(2)}, u32[]{:S(2)}) collective-permute-start(bf16[2,2,2,2,1,192,384]{6,5,3,2,1,4,0:T(8,128)(2,1)} %bitcast.327), channel_id=1, source_target_pairs={{0,1},{1,0},{2,3},{3,2},{4,5},{5,4},{6,7},{7,6},{8,9},{9,8},{10,11... | collective-permute-start | bytes 7077896 | tf_op jit(solution)/shard_map/ppermute | solution.py:22
  277.7 19.2 %collective-permute-start.44 = (bf16[2,2,2,2,1,192,384]{6,5,3,2,1,4,0:T(8,128)(2,1)}, bf16[2,2,2,2,1,192,384]{6,5,3,2,1,4,0:T(8,128)(2,1)S(1)}, u32[]{:S(2)}, u32[]{:S(2)}) collective-permute-start(bf16[2,2,2,2,1,192,384]{6,5,3,2,1,4,0:T(8,128)(2,1)} %bitcast.326), channel_id=1, source_target_pairs={{0,1},{1,0},{2,3},{3,2},{4,5},{5,4},{6,7},{7,6},{8,9},{9,8},{10,11... | collective-permute-start | bytes 7077896 | tf_op jit(solution)/shard_map/ppermute | solution.py:22
  287.4 54.3 %collective-permute-start.37 = (bf16[2,2,2,2,192,384]{5,4,3,2,1,0:T(8,128)(2,1)}, bf16[2,2,2,2,192,384]{5,4,3,2,1,0:T(8,128)(2,1)S(1)}, u32[]{:S(2)}, u32[]{:S(2)}) collective-permute-start(bf16[2,2,2,2,192,384]{5,4,3,2,1,0:T(8,128)(2,1)} %get-tuple-element.112), channel_id=1, source_target_pairs={{0,2},{1,3},{2,0},{3,1},{4,6},{5,7},{6,4},{7,5},{8,10},{9,11},{10,... | collective-permute-start | bytes 7077896 | tf_op jit(solution)/shard_map/ppermute | solution.py:22
  291.8 100.4 %collective-permute-start.53 = (bf16[2,2,2,2,192,384]{5,4,3,2,1,0:T(8,128)(2,1)}, bf16[2,2,2,2,192,384]{5,4,3,2,1,0:T(8,128)(2,1)S(1)}, u32[]{:S(2)}, u32[]{:S(2)}) collective-permute-start(bf16[2,2,2,2,192,384]{5,4,3,2,1,0:T(8,128)(2,1)} %get-tuple-element.106), channel_id=1, source_target_pairs={{0,2},{1,3},{2,0},{3,1},{4,6},{5,7},{6,4},{7,5},{8,10},{9,11},{10,... | collective-permute-start | bytes 7077896 | tf_op jit(solution)/shard_map/ppermute | solution.py:22
  295.4 122.1 %collective-permute-start.29 = (bf16[2,2,2,1,192,384]{5,4,2,3,1,0:T(8,128)(2,1)S(1)}, bf16[2,2,2,1,192,384]{5,4,2,3,1,0:T(8,128)(2,1)S(1)}, u32[]{:S(2)}, u32[]{:S(2)}) collective-permute-start(bf16[2,2,2,1,192,384]{5,4,2,3,1,0:T(8,128)(2,1)S(1)} %fusion.10), channel_id=1, source_target_pairs={{0,2},{1,3},{2,0},{3,1},{4,6},{5,7},{6,4},{7,5},{8,10},{9,11},{10,... | collective-permute-start | bytes 3538952 | tf_op jit(solution)/shard_map/ppermute | solution.py:22
  297.2 145.1 %collective-permute-start.45 = (bf16[2,2,2,1,192,384]{5,4,2,3,1,0:T(8,128)(2,1)S(1)}, bf16[2,2,2,1,192,384]{5,4,2,3,1,0:T(8,128)(2,1)S(1)}, u32[]{:S(2)}, u32[]{:S(2)}) collective-permute-start(bf16[2,2,2,1,192,384]{5,4,2,3,1,0:T(8,128)(2,1)S(1)} %fusion.11), channel_id=1, source_target_pairs={{0,2},{1,3},{2,0},{3,1},{4,6},{5,7},{6,4},{7,5},{8,10},{9,11},{10,... | collective-permute-start | bytes 3538952 | tf_op jit(solution)/shard_map/ppermute | solution.py:22
  342.4 100.6 %collective-permute-start.38 = (bf16[2,2,2,192,384]{4,3,2,1,0:T(8,128)(2,1)S(1)}, bf16[2,2,2,192,384]{4,3,2,1,0:T(8,128)(2,1)S(1)}, u32[]{:S(2)}, u32[]{:S(2)}) collective-permute-start(bf16[2,2,2,192,384]{4,3,2,1,0:T(8,128)(2,1)S(1)} %get-tuple-element.110), channel_id=1, source_target_pairs={{0,4},{4,0},{8,12},{12,8},{16,20},{20,16},{24,28},{28,24},{1,5},{5... | collective-permute-start | bytes 3538952 | tf_op jit(solution)/shard_map/ppermute | solution.py:22
  392.9 52.0 %collective-permute-start.54 = (bf16[2,2,2,192,384]{4,3,2,1,0:T(8,128)(2,1)S(1)}, bf16[2,2,2,192,384]{4,3,2,1,0:T(8,128)(2,1)S(1)}, u32[]{:S(2)}, u32[]{:S(2)}) collective-permute-start(bf16[2,2,2,192,384]{4,3,2,1,0:T(8,128)(2,1)S(1)} %get-tuple-element.104), channel_id=1, source_target_pairs={{0,4},{4,0},{8,12},{12,8},{16,20},{20,16},{24,28},{28,24},{1,5},{5... | collective-permute-start | bytes 3538952 | tf_op jit(solution)/shard_map/ppermute | solution.py:22
  417.8 28.0 %collective-permute-start.30 = (bf16[2,2,1,192,384]{4,3,2,1,0:T(8,128)(2,1)S(1)}, bf16[2,2,1,192,384]{4,3,2,1,0:T(8,128)(2,1)S(1)}, u32[]{:S(2)}, u32[]{:S(2)}) collective-permute-start(bf16[2,2,1,192,384]{4,3,2,1,0:T(8,128)(2,1)S(1)} %get-tuple-element.124), channel_id=1, source_target_pairs={{0,4},{4,0},{8,12},{12,8},{16,20},{20,16},{24,28},{28,24},{1,5},{5... | collective-permute-start | bytes 1769480 | tf_op jit(solution)/shard_map/ppermute | solution.py:22
  442.6 14.9 %collective-permute-start.46 = (bf16[2,2,1,192,384]{4,3,2,1,0:T(8,128)(2,1)S(1)}, bf16[2,2,1,192,384]{4,3,2,1,0:T(8,128)(2,1)S(1)}, u32[]{:S(2)}, u32[]{:S(2)}) collective-permute-start(bf16[2,2,1,192,384]{4,3,2,1,0:T(8,128)(2,1)S(1)} %get-tuple-element.118), channel_id=1, source_target_pairs={{0,4},{4,0},{8,12},{12,8},{16,20},{20,16},{24,28},{28,24},{1,5},{5... | collective-permute-start | bytes 1769480 | tf_op jit(solution)/shard_map/ppermute | solution.py:22
  443.3 16.3 %collective-permute-start.39 = (bf16[2,2,192,384]{3,2,1,0:T(8,128)(2,1)S(1)}, bf16[2,2,192,384]{3,2,1,0:T(8,128)(2,1)S(1)}, u32[]{:S(2)}, u32[]{:S(2)}) collective-permute-start(bf16[2,2,192,384]{3,2,1,0:T(8,128)(2,1)S(1)} %get-tuple-element.122), channel_id=1, source_target_pairs={{0,8},{4,12},{8,0},{12,4},{16,24},{20,28},{24,16},{28,20},{1,9},{5... | collective-permute-start | bytes 1769480 | tf_op jit(solution)/shard_map/ppermute | solution.py:22
  445.3 33.3 %collective-permute-start.55 = (bf16[2,2,192,384]{3,2,1,0:T(8,128)(2,1)S(1)}, bf16[2,2,192,384]{3,2,1,0:T(8,128)(2,1)S(1)}, u32[]{:S(2)}, u32[]{:S(2)}) collective-permute-start(bf16[2,2,192,384]{3,2,1,0:T(8,128)(2,1)S(1)} %get-tuple-element.116), channel_id=1, source_target_pairs={{0,8},{4,12},{8,0},{12,4},{16,24},{20,28},{24,16},{28,20},{1,9},{5... | collective-permute-start | bytes 1769480 | tf_op jit(solution)/shard_map/ppermute | solution.py:22
  445.9 44.3 %collective-permute-start.31 = (bf16[2,1,192,384]{3,2,1,0:T(8,128)(2,1)S(1)}, bf16[2,1,192,384]{3,2,1,0:T(8,128)(2,1)S(1)}, u32[]{:S(2)}, u32[]{:S(2)}) collective-permute-start(bf16[2,1,192,384]{3,2,1,0:T(8,128)(2,1)S(1)} %get-tuple-element.136), channel_id=1, source_target_pairs={{0,8},{4,12},{8,0},{12,4},{16,24},{20,28},{24,16},{28,20},{1,9},{5... | collective-permute-start | bytes 884744 | tf_op jit(solution)/shard_map/ppermute | solution.py:22
  457.7 56.6 %collective-permute-start.47 = (bf16[2,1,192,384]{3,2,1,0:T(8,128)(2,1)S(1)}, bf16[2,1,192,384]{3,2,1,0:T(8,128)(2,1)S(1)}, u32[]{:S(2)}, u32[]{:S(2)}) collective-permute-start(bf16[2,1,192,384]{3,2,1,0:T(8,128)(2,1)S(1)} %get-tuple-element.134), channel_id=1, source_target_pairs={{0,8},{4,12},{8,0},{12,4},{16,24},{20,28},{24,16},{28,20},{1,9},{5... | collective-permute-start | bytes 884744 | tf_op jit(solution)/shard_map/ppermute | solution.py:22
  459.7 31.0 %collective-permute-start.40 = (bf16[2,192,384]{2,1,0:T(8,128)(2,1)S(1)}, bf16[2,192,384]{2,1,0:T(8,128)(2,1)S(1)}, u32[]{:S(2)}, u32[]{:S(2)}) collective-permute-start(bf16[2,192,384]{2,1,0:T(8,128)(2,1)S(1)} %fusion.33), channel_id=1, source_target_pairs={{0,16},{4,20},{8,24},{12,28},{16,0},{20,4},{24,8},{28,12},{1,17},{... | collective-permute-start | bytes 884744 | tf_op jit(solution)/shard_map/ppermute | solution.py:22
  478.7 35.5 %collective-permute-start.56 = (bf16[2,192,384]{2,1,0:T(8,128)(2,1)S(1)}, bf16[2,192,384]{2,1,0:T(8,128)(2,1)S(1)}, u32[]{:S(2)}, u32[]{:S(2)}) collective-permute-start(bf16[2,192,384]{2,1,0:T(8,128)(2,1)S(1)} %fusion.37), channel_id=1, source_target_pairs={{0,16},{4,20},{8,24},{12,28},{16,0},{20,4},{24,8},{28,12},{1,17},{... | collective-permute-start | bytes 884744 | tf_op jit(solution)/shard_map/ppermute | solution.py:22
  490.3 45.1 %collective-permute-start.32 = (bf16[1,192,384]{2,1,0:T(8,128)(2,1)S(1)}, bf16[1,192,384]{2,1,0:T(8,128)(2,1)S(1)}, u32[]{:S(2)}, u32[]{:S(2)}) collective-permute-start(bf16[1,192,384]{2,1,0:T(8,128)(2,1)S(1)} %fusion.46), channel_id=1, source_target_pairs={{0,16},{4,20},{8,24},{12,28},{16,0},{20,4},{24,8},{28,12},{1,17},{... | collective-permute-start | bytes 442376 | tf_op jit(solution)/shard_map/ppermute | solution.py:22
  490.8 37.5 %collective-permute-start.41 = (bf16[1,2,192,384]{3,2,1,0:T(8,128)(2,1)S(1)}, bf16[1,2,192,384]{3,2,1,0:T(8,128)(2,1)S(1)}, u32[]{:S(2)}, u32[]{:S(2)}) collective-permute-start(bf16[1,2,192,384]{3,2,1,0:T(8,128)(2,1)S(1)} %fusion.32), channel_id=1, source_target_pairs={{0,16},{4,20},{8,24},{12,28},{16,0},{20,4},{24,8},{28,12},{1,17},{... | collective-permute-start | bytes 884744 | tf_op jit(solution)/shard_map/ppermute | solution.py:22
  514.2 20.5 %collective-permute-start.57 = (bf16[1,2,192,384]{3,2,1,0:T(8,128)(2,1)S(1)}, bf16[1,2,192,384]{3,2,1,0:T(8,128)(2,1)S(1)}, u32[]{:S(2)}, u32[]{:S(2)}) collective-permute-start(bf16[1,2,192,384]{3,2,1,0:T(8,128)(2,1)S(1)} %fusion.36), channel_id=1, source_target_pairs={{0,16},{4,20},{8,24},{12,28},{16,0},{20,4},{24,8},{28,12},{1,17},{... | collective-permute-start | bytes 884744 | tf_op jit(solution)/shard_map/ppermute | solution.py:22
  514.4 24.6 %collective-permute-start.48 = (bf16[1,192,384]{2,1,0:T(8,128)(2,1)S(1)}, bf16[1,192,384]{2,1,0:T(8,128)(2,1)S(1)}, u32[]{:S(2)}, u32[]{:S(2)}) collective-permute-start(bf16[1,192,384]{2,1,0:T(8,128)(2,1)S(1)} %fusion.49), channel_id=1, source_target_pairs={{0,16},{4,20},{8,24},{12,28},{16,0},{20,4},{24,8},{28,12},{1,17},{... | collective-permute-start | bytes 442376 | tf_op jit(solution)/shard_map/ppermute | solution.py:22
  528.4 32.9 %collective-permute-start.42 = (bf16[2,2,192,384]{3,2,1,0:T(8,128)(2,1)S(1)}, bf16[2,2,192,384]{3,2,1,0:T(8,128)(2,1)S(1)}, u32[]{:S(2)}, u32[]{:S(2)}) collective-permute-start(bf16[2,2,192,384]{3,2,1,0:T(8,128)(2,1)S(1)} %pad_maximum_fusion.5), channel_id=1, source_target_pairs={{0,8},{4,12},{8,0},{12,4},{16,24},{20,28},{24,16},{28,20},{1,9},{5... | collective-permute-start | bytes 1769480 | tf_op jit(solution)/shard_map/ppermute | solution.py:22
  534.8 33.8 %collective-permute-start.58 = (bf16[2,2,192,384]{3,2,1,0:T(8,128)(2,1)S(1)}, bf16[2,2,192,384]{3,2,1,0:T(8,128)(2,1)S(1)}, u32[]{:S(2)}, u32[]{:S(2)}) collective-permute-start(bf16[2,2,192,384]{3,2,1,0:T(8,128)(2,1)S(1)} %pad_maximum_fusion.7), channel_id=1, source_target_pairs={{0,8},{4,12},{8,0},{12,4},{16,24},{20,28},{24,16},{28,20},{1,9},{5... | collective-permute-start | bytes 1769480 | tf_op jit(solution)/shard_map/ppermute | solution.py:22
  535.5 23.8 %collective-permute-start.33 = (bf16[1,1,192,384]{3,2,1,0:T(8,128)(2,1)S(1)}, bf16[1,1,192,384]{3,2,1,0:T(8,128)(2,1)S(1)}, u32[]{:S(2)}, u32[]{:S(2)}) collective-permute-start(bf16[1,1,192,384]{3,2,1,0:T(8,128)(2,1)S(1)} %fusion.45), channel_id=1, source_target_pairs={{0,16},{4,20},{8,24},{12,28},{16,0},{20,4},{24,8},{28,12},{1,17},{... | collective-permute-start | bytes 442376 | tf_op jit(solution)/shard_map/ppermute | solution.py:22
  539.0 31.6 %collective-permute-start.49 = (bf16[1,1,192,384]{3,2,1,0:T(8,128)(2,1)S(1)}, bf16[1,1,192,384]{3,2,1,0:T(8,128)(2,1)S(1)}, u32[]{:S(2)}, u32[]{:S(2)}) collective-permute-start(bf16[1,1,192,384]{3,2,1,0:T(8,128)(2,1)S(1)} %fusion.48), channel_id=1, source_target_pairs={{0,16},{4,20},{8,24},{12,28},{16,0},{20,4},{24,8},{28,12},{1,17},{... | collective-permute-start | bytes 442376 | tf_op jit(solution)/shard_map/ppermute | solution.py:22
  559.4 15.6 %collective-permute-start.34 = (bf16[2,1,192,384]{3,2,1,0:T(8,128)(2,1)S(1)}, bf16[2,1,192,384]{3,2,1,0:T(8,128)(2,1)S(1)}, u32[]{:S(2)}, u32[]{:S(2)}) collective-permute-start(bf16[2,1,192,384]{3,2,1,0:T(8,128)(2,1)S(1)} %pad_maximum_fusion.8), channel_id=1, source_target_pairs={{0,8},{4,12},{8,0},{12,4},{16,24},{20,28},{24,16},{28,20},{1,9},{5... | collective-permute-start | bytes 884744 | tf_op jit(solution)/shard_map/ppermute | solution.py:22
  561.5 147.6 %collective-permute-start.43 = (bf16[4,2,192,384]{3,2,1,0:T(8,128)(2,1)S(1)}, bf16[4,2,192,384]{3,2,1,0:T(8,128)(2,1)}, u32[]{:S(2)}, u32[]{:S(2)}) collective-permute-start(bf16[4,2,192,384]{3,2,1,0:T(8,128)(2,1)S(1)} %pad_maximum_fusion.rest_2_), channel_id=1, source_target_pairs={{0,4},{4,0},{8,12},{12,8},{16,20},{20,16},{24,28},{28,24},{1,5},{5... | collective-permute-start | bytes 3538952 | tf_op jit(solution)/shard_map/ppermute | solution.py:22
  568.8 140.3 %collective-permute-start.59 = (bf16[4,2,192,384]{3,2,1,0:T(8,128)(2,1)S(1)}, bf16[4,2,192,384]{3,2,1,0:T(8,128)(2,1)}, u32[]{:S(2)}, u32[]{:S(2)}) collective-permute-start(bf16[4,2,192,384]{3,2,1,0:T(8,128)(2,1)S(1)} %pad_maximum_fusion.1.rest_6_), channel_id=1, source_target_pairs={{0,4},{4,0},{8,12},{12,8},{16,20},{20,16},{24,28},{28,24},{1,5},{5... | collective-permute-start | bytes 3538952 | tf_op jit(solution)/shard_map/ppermute | solution.py:22
  570.6 10.5 %collective-permute-start.50 = (bf16[2,1,192,384]{3,2,1,0:T(8,128)(2,1)S(1)}, bf16[2,1,192,384]{3,2,1,0:T(8,128)(2,1)S(1)}, u32[]{:S(2)}, u32[]{:S(2)}) collective-permute-start(bf16[2,1,192,384]{3,2,1,0:T(8,128)(2,1)S(1)} %pad_maximum_fusion.9), channel_id=1, source_target_pairs={{0,8},{4,12},{8,0},{12,4},{16,24},{20,28},{24,16},{28,20},{1,9},{5... | collective-permute-start | bytes 884744 | tf_op jit(solution)/shard_map/ppermute | solution.py:22
  575.0 134.1 %copy-start.13 = (bf16[4,1,192,384]{3,2,1,0:T(8,128)(2,1)}, bf16[4,1,192,384]{3,2,1,0:T(8,128)(2,1)S(1)}, u32[]{:S(2)}) copy-start(bf16[4,1,192,384]{3,2,1,0:T(8,128)(2,1)S(1)} %pad_maximum_fusion.4.rest_0_) | copy-start | bytes 1769476
  575.0 134.1 %collective-permute-start.35 = (bf16[4,1,192,384]{3,2,1,0:T(8,128)(2,1)S(1)}, bf16[4,1,192,384]{3,2,1,0:T(8,128)(2,1)}, u32[]{:S(2)}, u32[]{:S(2)}) collective-permute-start(bf16[4,1,192,384]{3,2,1,0:T(8,128)(2,1)S(1)} %pad_maximum_fusion.4.rest_0_), channel_id=1, source_target_pairs={{0,4},{4,0},{8,12},{12,8},{16,20},{20,16},{24,28},{28,24},{1,5},{5... | collective-permute-start | bytes 1769480 | tf_op jit(solution)/shard_map/ppermute | solution.py:22
  581.3 127.9 %collective-permute-start.51 = (bf16[4,1,192,384]{3,2,1,0:T(8,128)(2,1)S(1)}, bf16[4,1,192,384]{3,2,1,0:T(8,128)(2,1)}, u32[]{:S(2)}, u32[]{:S(2)}) collective-permute-start(bf16[4,1,192,384]{3,2,1,0:T(8,128)(2,1)S(1)} %pad_maximum_fusion.6.rest_4_), channel_id=1, source_target_pairs={{0,4},{4,0},{8,12},{12,8},{16,20},{20,16},{24,28},{28,24},{1,5},{5... | collective-permute-start | bytes 1769480 | tf_op jit(solution)/shard_map/ppermute | solution.py:22
  (32 other events, 1014.0 us)
Sparse Core Ops, SparseCore 0:
  583.8 118.1 all-reduce.2

commit v2 on v1

v2 whole, which is shorter than its diff:
```python
import functools
import math

import jax
import jax.numpy as jnp
from jax import lax
from jax.experimental import pallas as pl
from jax.experimental.pallas import tpu as pltpu
from jax.sharding import PartitionSpec as P

HEADS = 12
norm_eps = 1e-12
masked_score = -1000000000.0
low = jnp.bfloat16
f32 = jnp.float32
VMEM_BYTES = 56 * 1024 * 1024
HALVINGS = 3


def swap(value, axis, bit):
    count = lax.axis_size(axis)
    return lax.ppermute(value, axis, [(i, i ^ bit) for i in range(count)])


def dot(a, b):
    return jnp.dot(a, b, preferred_element_type=f32)


def dot_nt(a, b):
    return lax.dot_general(a, b, (((1,), (1,)), ((), ())), preferred_element_type=f32)


def dot_tn(a, b):
    return lax.dot_general(a, b, (((0,), (0,)), ((), ())), preferred_element_type=f32)


def normalize(residual):
    center = residual - jnp.mean(residual, axis=-1, keepdims=True)
    inverse = lax.rsqrt(jnp.mean(center * center, axis=-1, keepdims=True) + norm_eps)
    return center * inverse, inverse


def normalize_back(grad_unit, unit, inverse):
    centered = grad_unit - jnp.mean(grad_unit, axis=-1, keepdims=True)
    return inverse * (centered - unit * jnp.mean(grad_unit * unit, axis=-1, keepdims=True))


def weight_copies(ids, layer, pieces, target, columns, sems, base):
    own, core, near_x, far_x, near_d, far_d = pieces
    rows = own.shape[1]
    half = rows // 2
    n, y = ids[0], ids[4]
    copies = []

    def add(source, start, count):
        where = target.at[pl.ds(pl.multiple_of(start, half), count), :]
        copies.append(pltpu.make_async_copy(source, where, sems.at[base + len(copies)]))

    def part(ref):
        return ref.at[:, pl.ds(columns, target.shape[1])]

    add(own.at[layer], n * rows, rows)
    add(core.at[layer], ids[1] * rows, rows)
    add(part(near_x), ids[2] * rows + y * half, half)
    add(part(far_x), ids[2] * rows + (1 - y) * half, half)
    add(part(near_d), ids[3] * rows + y * half, half)
    add(part(far_d), ids[3] * rows + (1 - y) * half, half)
    return copies


def begin(copies):
    for copy in copies:
        copy.start()


def finish(copies):
    for copy in copies:
        copy.wait()


def attn_copies(layer, ids, refs, w_qkv, w_o, sems):
    qkv_own, qkv_core, o_own, o_core, near_x, far_x, near_d, far_d = refs
    halves = (near_x, far_x, near_d, far_d)
    qkv = weight_copies(ids, layer, (qkv_own, qkv_core) + halves, w_qkv, 0, sems, 0)
    o = weight_copies(ids, layer, (o_own, o_core) + halves, w_o, w_qkv.shape[1], sems, 6)
    return qkv, o


def ffn_copies(layer, ids, refs, w_in, w_out, sems):
    in_copies = weight_copies(ids, layer, refs[:6], w_in, 0, sems, 0)
    out_copies = weight_copies(ids, layer, refs[6:], w_out, 0, sems, 6)
    return in_copies, out_copies


def attn_fwd_kernel(layer, ids, length, x, cell_row, cell_col, qkv_bias, small, *rest):
    weights, rest = rest[:8], rest[8:]
    qkv_rows, probs, context, unit_out, inverse_out, w_qkv, w_o, mask, sems = rest
    tokens, width = x.shape
    qkv_copies, o_copies = attn_copies(layer, ids, weights, w_qkv, w_o, sems)
    begin(qkv_copies)
    begin(o_copies)
    position = lax.broadcasted_iota(jnp.int32, (1, tokens), 1)
    key_cell, query_cell = cell_row[...], cell_col[...]
    allowed = (query_cell == key_cell) | (key_cell == 0) | (query_cell == 0)
    allowed = allowed & (position < length[0])
    mask[...] = jnp.where(allowed, 0.0, masked_score)
    scale = 1.0 / math.sqrt(width // HEADS)
    finish(qkv_copies)
    tile = width // 2

    @pl.loop(0, 6)
    def _(t):
        columns = pl.ds(pl.multiple_of(t * tile, tile), tile)
        rows = dot(x[...], w_qkv[:, columns]) + qkv_bias[layer, :, columns]
        qkv_rows[:, columns] = (rows * jnp.where(t < 2, scale, 1.0)).astype(low)

    pair_width = 2 * width // HEADS
    first = lax.broadcasted_iota(jnp.int32, (1, pair_width), 1) < pair_width // 2

    @pl.loop(0, HEADS // 2)
    def _(pair):
        start = pl.multiple_of(pair * pair_width, pair_width)
        query = qkv_rows[:, pl.ds(start, pair_width)]
        key = qkv_rows[:, pl.ds(width + start, pair_width)]
        value = qkv_rows[:, pl.ds(2 * width + start, pair_width)]
        sides = []
        for side in range(2):
            mine = first if side == 0 else jnp.logical_not(first)
            scores = dot_nt(jnp.where(mine, query, jnp.zeros_like(query)), key) + mask[...]
            shifted = jnp.exp(scores - jnp.max(scores, axis=-1, keepdims=True))
            total = jnp.sum(shifted, axis=-1, keepdims=True)
            prob = (shifted / total).astype(low)
            probs[2 * pair + side] = prob
            sides.append(dot(prob, value))
        context[:, pl.ds(start, pair_width)] = jnp.where(first, sides[0], sides[1]).astype(low)

    finish(o_copies)
    residual = x[...].astype(f32) + (dot(context[...], w_o[...]) + small[layer, 2:3, :])
    unit, inverse = normalize(residual)
    unit_out[...] = unit
    inverse_out[...] = inverse


def ffn_fwd_kernel(layer, ids, unit_one, in_bias, small, *rest):
    weights, rest = rest[:12], rest[12:]
    hidden, slope, unit_out, inverse_out, result, w_in, w_out, normed_low, sems = rest
    in_copies, out_copies = ffn_copies(layer, ids, weights, w_in, w_out, sems)
    begin(in_copies)
    begin(out_copies)
    normed = unit_one[...] * small[layer, 3:4, :] + small[layer, 4:5, :]
    normed_low[...] = normed.astype(low)
    finish(in_copies)
    tile = w_in.shape[1] // 8

    @pl.loop(0, 8)
    def _(t):
        columns = pl.ds(pl.multiple_of(t * tile, tile), tile)
        pre = dot(normed_low[...], w_in[:, columns]) + in_bias[layer, :, columns]
        cdf = 0.5 * (1.0 + lax.erf(pre * (1.0 / math.sqrt(2.0))))
        density = jnp.exp(-0.5 * pre * pre) * (1.0 / math.sqrt(2.0 * math.pi))
        hidden[:, columns] = (pre * cdf).astype(low)
        slope[:, columns] = cdf + pre * density

    finish(out_copies)
    residual = unit_one[...] * small[layer, 3:4, :] + small[layer, 4:5, :] + (dot(hidden[...], w_out[...]) + small[layer, 5:6, :])
    unit, inverse = normalize(residual)
    unit_out[...] = unit
    inverse_out[...] = inverse
    result[...] = (unit * small[layer, 6:7, :] + small[layer, 7:8, :]).astype(low)


def store_rows(stage, ids, product, piece):
    share = product.shape[0] // 4
    for owner in range(4):
        away = ids[0] ^ owner
        block = product[owner * share : (owner + 1) * share].astype(low)
        stage[away & 1, away >> 1, piece ^ ids[5]] = block


def send_out(stage, kept, sent, sems, base):
    return [
        pltpu.make_async_copy(stage.at[1], sent, sems.at[base]),
        pltpu.make_async_copy(stage.at[0], kept, sems.at[base + 1]),
    ]


def ffn_bwd_kernel(
    layer, ids, grad, unit_two, inverse_two, unit_one, inverse_one, hidden, slope, small, *rest
):
    weights, rest = rest[:12], rest[12:]
    d_resid, small_grads, in_bias_grad, in_kept, in_sent, out_kept, out_sent = rest[:7]
    w_in, w_out, d_ffn, d_resid_two, d_pre, normed_t, in_stage, out_stage, sems, out_sems = rest[7:]
    in_copies, out_copies = ffn_copies(layer, ids, weights, w_in, w_out, sems)
    begin(out_copies)
    begin(in_copies)
    g = grad[...].astype(f32)
    unit = unit_two[...]
    small_grads[0:1, :] = jnp.sum(g * unit, axis=0, keepdims=True)
    small_grads[1:2, :] = jnp.sum(g, axis=0, keepdims=True)
    d_two = normalize_back(g * small[layer, 6:7, :], unit, inverse_two[...])
    d_resid_two[...] = d_two
    d_low = d_two.astype(low)
    d_ffn[...] = d_low
    small_grads[2:3, :] = jnp.sum(d_low.astype(f32), axis=0, keepdims=True)
    normed = unit_one[...] * small[layer, 3:4, :] + small[layer, 4:5, :]
    normed_t[...] = normed.astype(low).T
    finish(out_copies)
    tile = w_in.shape[1] // 8
    share = d_ffn.shape[1] // 4

    @pl.loop(0, 8)
    def _(t):
        columns = pl.ds(pl.multiple_of(t * tile, tile), tile)
        d_hidden = dot_nt(d_ffn[...], w_out[columns, :])
        d_tile = (d_hidden * slope[:, columns]).astype(low)
        d_pre[:, columns] = d_tile
        in_bias_grad[:, columns] = jnp.sum(d_tile.astype(f32), axis=0, keepdims=True)
        store_rows(in_stage, ids, dot(normed_t[...], d_tile), t)
        out_grad = dot_tn(hidden[:, columns], d_ffn[...])
        away = ids[0] ^ (t // 2)
        for row_group in range(2):
            for column_group in range(2):
                piece = ((t % 2) * 2 + row_group) * 2 + column_group
                block = out_grad[
                    row_group * share : (row_group + 1) * share,
                    column_group * tile : (column_group + 1) * tile,
                ]
                out_stage[away & 1, away >> 1, piece ^ ids[5]] = block.astype(low)

    going = send_out(out_stage, out_kept, out_sent, out_sems, 0)
    going += send_out(in_stage, in_kept, in_sent, out_sems, 2)
    begin(going)
    finish(in_copies)
    d_normed = d_resid_two[...] + dot_nt(d_pre[...], w_in[...])
    unit = unit_one[...]
    small_grads[3:4, :] = jnp.sum(d_normed * unit, axis=0, keepdims=True)
    small_grads[4:5, :] = jnp.sum(d_normed, axis=0, keepdims=True)
    small_grads[5:8, :] = jnp.zeros((3, unit.shape[1]), f32)
    d_resid[...] = normalize_back(d_normed * small[layer, 3:4, :], unit, inverse_one[...])
    finish(going)


def attn_bwd_kernel(layer, ids, d_resid, x, qkv_rows, probs, context, *rest):
    weights, rest = rest[:8], rest[8:]
    d_input, small_grads, kept, sent = rest[:4]
    w_qkv, w_o, d_attn, d_context, d_qkv, x_t, stage, sems, out_sems = rest[4:]
    tokens, width = x.shape
    qkv_copies, o_copies = attn_copies(layer, ids, weights, w_qkv, w_o, sems)
    begin(o_copies)
    begin(qkv_copies)
    d_low = d_resid[...].astype(low)
    d_attn[...] = d_low
    small_grads[2:3, :] = jnp.sum(d_low.astype(f32), axis=0, keepdims=True)
    x_t[...] = x[...].T
    tile = width // 2
    for half in range(2):
        product = dot_tn(context[...], d_attn[:, half * tile : (half + 1) * tile])
        store_rows(stage, ids, product, 6 + half)
    finish(o_copies)
    d_context[...] = dot_nt(d_attn[...], w_o[...]).astype(low)
    pair_width = 2 * width // HEADS
    first = lax.broadcasted_iota(jnp.int32, (1, pair_width), 1) < pair_width // 2
    scale = 1.0 / math.sqrt(width // HEADS)

    @pl.loop(0, HEADS // 2)
    def _(pair):
        start = pl.multiple_of(pair * pair_width, pair_width)
        at_query = pl.ds(start, pair_width)
        at_key = pl.ds(width + start, pair_width)
        at_value = pl.ds(2 * width + start, pair_width)
        query, key, value = qkv_rows[:, at_query], qkv_rows[:, at_key], qkv_rows[:, at_value]
        d_ctx = d_context[:, at_query]
        sides = []
        for side in range(2):
            mine = first if side == 0 else jnp.logical_not(first)
            prob_low = probs[2 * pair + side]
            prob = prob_low.astype(f32)
            d_prob = dot_nt(jnp.where(mine, d_ctx, jnp.zeros_like(d_ctx)), value)
            inner = jnp.sum(prob * d_prob, axis=-1, keepdims=True)
            d_scores = (prob * (d_prob - inner)).astype(low)
            sides.append((dot(d_scores, key), dot_tn(d_scores, query), dot_tn(prob_low, d_ctx)))
        d_qkv[:, at_query] = (jnp.where(first, sides[0][0], sides[1][0]) * scale).astype(low)
        d_qkv[:, at_key] = jnp.where(first, sides[0][1], sides[1][1]).astype(low)
        d_qkv[:, at_value] = jnp.where(first, sides[0][2], sides[1][2]).astype(low)

    @pl.loop(0, 6)
    def _(t):
        columns = pl.ds(pl.multiple_of(t * tile, tile), tile)
        store_rows(stage, ids, dot(x_t[...], d_qkv[:, columns]), t)

    going = send_out(stage, kept, sent, out_sems, 0)
    begin(going)
    small_grads[0:1, :] = jnp.sum(d_qkv[:, :width].astype(f32), axis=0, keepdims=True)
    small_grads[1:2, :] = jnp.sum(d_qkv[:, 2 * width :].astype(f32), axis=0, keepdims=True)
    small_grads[3:8, :] = jnp.zeros((5, width), f32)
    finish(qkv_copies)
    d_input[...] = (d_resid[...] + dot_nt(d_qkv[...], w_qkv[...])).astype(low)
    finish(going)


def unpack_kernel(layer, slab, ids, near, far, *rest):
    outs, scratch = rest[:-4], rest[-4:]
    outs = outs[len(outs) // 2 :] if layer == 0 else outs
    buffer, wide_buffer, in_sems, out_sems = scratch
    share, tile = buffer.shape[1:]
    for piece in range(8):
        place = piece ^ ids[5]

        @pl.when(place < 4)
        def _():
            pltpu.make_async_copy(near.at[place], buffer.at[piece], in_sems.at[piece]).start()

        @pl.when(place >= 4)
        def _():
            pltpu.make_async_copy(far.at[place - 4], buffer.at[piece], in_sems.at[piece]).start()

    copies = []
    for piece in range(8):
        pltpu.make_async_copy(near.at[0], buffer.at[piece], in_sems.at[piece]).wait()
        wide_buffer[piece] = buffer[piece].astype(f32)
        columns = pl.ds(piece * tile, tile)
        if slab == "in":
            target = outs[0].at[layer, :, columns]
        elif slab == "out":
            rows = pl.ds((piece // 2) * share, share)
            target = outs[0].at[layer, rows, pl.ds((piece % 2) * tile, tile)]
        elif piece < 6:
            target = outs[0].at[layer, :, columns]
        else:
            target = outs[1].at[layer, :, pl.ds((piece - 6) * tile, tile)]
        copies.append(pltpu.make_async_copy(wide_buffer.at[piece], target, out_sems.at[piece]))
        copies[-1].start()
    finish(copies)


SMEM = pl.BlockSpec(memory_space=pltpu.SMEM)
VMEM = pl.BlockSpec(memory_space=pltpu.VMEM)
ANY = pl.BlockSpec(memory_space=pl.ANY)


def call(kernel, name, in_specs, out_specs, out_shape, scratch, args, aliases=()):
    return pl.pallas_call(
        kernel,
        name=name,
        in_specs=in_specs,
        out_specs=out_specs,
        out_shape=out_shape,
        scratch_shapes=scratch,
        input_output_aliases=dict(aliases),
        compiler_params=pltpu.CompilerParams(vmem_limit_bytes=VMEM_BYTES),
        cost_estimate=pl.CostEstimate(flops=1, bytes_accessed=1, transcendentals=0),
    )(*args)


def shape(dims, kind):
    return jax.ShapeDtypeStruct(dims, kind)


def reverse_bits(value, bits):
    result = jnp.zeros_like(value)
    for bit in range(bits):
        result = result | (((value >> bit) & 1) << (bits - 1 - bit))
    return result


def added(a, b):
    return (a.astype(f32) + b.astype(f32)).astype(low)


class Order:
    def __init__(self):
        self.last = None

    def after(self, values):
        if self.last is None:
            return values
        values, self.last = lax.optimization_barrier((values, self.last))
        return values

    def wait(self, values):
        values = self.after(values)
        self.last = values
        return values


STEPS = {"x": ("narrow", 2, 0), "y": ("wide", 1, 1), "z": ("wide", 2, 2), "w": ("wide", 4, 3)}
BACK = "wzy"


class Slab:
    def __init__(self, way, wide_bits, kept, sent):
        self.way, self.wide_bits = way, wide_bits
        self.dims = "xyzw"
        self.kept = kept.reshape((2, 2, 2, 2) + kept.shape[2:])
        self.flying = swap(sent.reshape(self.kept.shape), "narrow", 1)
        self.stage = 0

    def step(self, order):
        received = order.after(self.flying)
        if self.stage < len(self.way):
            name = self.way[self.stage]
            at = self.dims.index(name)
            self.dims = self.dims.replace(name, "")
            kept, got = jnp.moveaxis(self.kept, at, 0), jnp.moveaxis(received, at, 0)
            send = added(kept[1], got[1])
            self.kept = added(kept[0], got[0])
            axis, bit, _ = STEPS[name]
            self.flying = swap(send, axis, bit)
            order.last = send
        elif self.stage == len(self.way):
            piece = added(self.kept, received)
            for b in range(HALVINGS, self.wide_bits):
                piece = added(piece, swap(piece, "wide", 1 << b))
            self.block = piece[None]
            order.last = self.block
            self.flying = swap(self.block, "wide", STEPS[BACK[0]][1])
        elif self.stage < len(self.way) + len(BACK):
            self.block = jnp.concatenate([self.block, received], axis=0)
            order.last = self.block
            self.flying = swap(self.block, "wide", STEPS[BACK[self.stage - len(self.way)]][1])
        else:
            self.far = received
        self.stage += 1


def plan(ways, kernels, megabytes):
    rate, core_rate = 0.091, 0.3
    trips = []
    for way in ways:
        size, trip = megabytes / 2, [("c", megabytes / 2 / core_rate)]
        for name in way:
            size /= 2
            trip.append((name, (4 if name == "w" else 2) * size / rate))
        for name in BACK:
            trip.append((name, (4 if name == "w" else 2) * size / rate))
            size *= 2
        trips.append(trip)
    free = dict.fromkeys("cxyzw", 0.0)
    now, flying, result, waiting = 0.0, [], [], list(kernels)

    def launch(slab, stage):
        name, time = trips[slab][stage]
        start = max(free[name], now)
        if name == "w":
            start = max(start, free["z"])
            free["z"] = start + time / 2
        free[name] = start + time
        flying.append((start + time + 0.7, slab, stage))

    while waiting or flying:
        landed = [event for event in flying if event[0] <= now]
        if not landed and waiting:
            kernel, time, slabs = waiting.pop(0)
            now += time
            result.append(("kernel", kernel))
            for slab in slabs:
                now += 0.8
                launch(slab, 0)
            continue
        event = min(landed, key=lambda e: e[1]) if landed else min(flying)
        flying.remove(event)
        done, slab, stage = event
        now = max(now, done) + (1.5 if stage <= len(ways[slab]) else 0.6)
        result.append(("step", slab))
        if stage + 1 < len(trips[slab]):
            now += 0.8
            launch(slab, stage + 1)
    return result


def body(
    tables_in,
    cotangent,
    cell_ids,
    lengths,
    qkv_weight,
    q_bias,
    v_bias,
    o_weight,
    o_bias,
    norm1_gain,
    norm1_bias,
    in_weight,
    in_bias,
    out_weight,
    out_bias,
    norm2_gain,
    norm2_bias,
):
    tokens, width = tables_in.shape
    layers, share, ffn = in_weight.shape
    ffn_share = out_weight.shape[1]
    wide_count = lax.axis_size("wide")
    wide_bits = wide_count.bit_length() - 1
    assert wide_count == 1 << wide_bits and wide_bits >= HALVINGS and lax.axis_size("narrow") == 4
    tile = ffn // 8
    me = lax.axis_index("narrow").astype(jnp.int32)
    wide_me = lax.axis_index("wide").astype(jnp.int32)
    y = wide_me & 1
    place = reverse_bits(wide_me & (2**HALVINGS - 1), HALVINGS)
    ids = jnp.stack([me, me ^ 1, me ^ 2, me ^ 3, y, place])

    short = [q_bias, v_bias, o_bias, norm1_gain, norm1_bias, out_bias, norm2_gain, norm2_bias]
    packed = jnp.concatenate([jnp.stack(short, axis=1), in_bias.reshape(layers, 4, share)], axis=1)
    packed = lax.all_gather(packed, "narrow", axis=0).astype(f32)
    small = packed[:, :, :8].transpose(1, 2, 0, 3).reshape(layers, 8, width)
    full_in_bias = packed[:, :, 8:].transpose(1, 0, 2, 3).reshape(layers, 1, ffn)
    qkv_bias = jnp.concatenate([small[:, 0], jnp.zeros((layers, width), f32), small[:, 1]], axis=1)
    qkv_bias = qkv_bias.reshape(layers, 1, 3 * width)
    cell_col = cell_ids.reshape(tokens, 1)
    order = Order()

    core = [swap(weight, "narrow", 1) for weight in (qkv_weight, o_weight, in_weight, out_weight)]

    def half_of(weight, layer):
        rows = weight.shape[1] // 2
        return lax.dynamic_slice(weight, (layer, y * rows, 0), (1, rows, weight.shape[2]))[0]

    halves = []
    for layer in range(layers):
        joint = jnp.concatenate([half_of(qkv_weight, layer), half_of(o_weight, layer)], axis=1)
        halves += [joint, half_of(in_weight, layer), half_of(out_weight, layer)]
    near_x = [swap(half, "narrow", 2) for half in halves]
    far_x, near_d, far_d = [None] * len(halves), [None] * len(halves), [None] * len(halves)
    ids, small, full_in_bias, qkv_bias, cell_col = order.wait((ids, small, full_in_bias, qkv_bias, cell_col))

    def arrive(*events):
        for kind, i in events:
            if kind == "x":
                near_x[i] = order.wait(near_x[i])
                far_x[i] = swap(near_x[i], "wide", 1)
                near_d[i] = swap(near_x[i], "narrow", 1)
            elif kind == "y":
                far_x[i] = order.wait(far_x[i])
                far_d[i] = swap(far_x[i], "narrow", 1)
            else:
                near_d[i], far_d[i] = order.wait((near_d[i], far_d[i]))

    def group(i):
        return near_x[i], far_x[i], near_d[i], far_d[i]

    def attn_weights(layer):
        return (qkv_weight, core[0], o_weight, core[1]) + group(3 * layer)

    def ffn_weights(layer):
        return (in_weight, core[2]) + group(3 * layer + 1) + (out_weight, core[3]) + group(3 * layer + 2)

    w_qkv = pltpu.VMEM((width, 3 * width), low)
    w_o = pltpu.VMEM((width, width), low)
    w_in = pltpu.VMEM((width, ffn), low)
    w_out = pltpu.VMEM((ffn, width), low)
    copy_sems = pltpu.SemaphoreType.DMA((12,))
    rows_f32 = shape((tokens, width), f32)
    rows_low = shape((tokens, width), low)
    column_f32 = shape((tokens, 1), f32)
    pieces = shape((2, 8, share, tile), low)
    stage = pltpu.VMEM((2, 2, 8, share, tile), low)

    def attn_forward(layer, x):
        x = order.after(x)
        outs = call(
            functools.partial(attn_fwd_kernel, layer),
            "attn_fwd",
            [SMEM, SMEM] + [VMEM] * 5 + [ANY] * 8,
            [VMEM] * 5,
            [shape((tokens, 3 * width), low), shape((HEADS, tokens, tokens), low), rows_low, rows_f32, column_f32],
            [w_qkv, w_o, pltpu.VMEM((tokens, tokens), f32), copy_sems],
            (ids, lengths, x, cell_ids, cell_col, qkv_bias, small) + attn_weights(layer),
        )
        order.last = outs[-1]
        return outs

    def ffn_forward(layer, unit_one):
        unit_one = order.after(unit_one)
        outs = call(
            functools.partial(ffn_fwd_kernel, layer),
            "ffn_fwd",
            [SMEM] + [VMEM] * 3 + [ANY] * 12,
            [VMEM] * 5,
            [shape((tokens, ffn), low), shape((tokens, ffn), f32), rows_f32, column_f32, rows_low],
            [w_in, w_out, pltpu.VMEM((tokens, width), low), copy_sems],
            (ids, unit_one, full_in_bias, small) + ffn_weights(layer),
        )
        order.last = outs[-2]
        return outs

    def ffn_backward(layer, grad, unit_two, inverse_two, unit_one, inverse_one, hidden, slope):
        grad = order.after(grad)
        outs = call(
            functools.partial(ffn_bwd_kernel, layer),
            "ffn_bwd",
            [SMEM] + [VMEM] * 8 + [ANY] * 12,
            [VMEM] * 3 + [ANY] * 4,
            [rows_f32, shape((8, width), f32), shape((1, ffn), f32)] + [pieces] * 4,
            [
                w_in,
                w_out,
                pltpu.VMEM((tokens, width), low),
                pltpu.VMEM((tokens, width), f32),
                pltpu.VMEM((tokens, ffn), low),
                pltpu.VMEM((width, tokens), low),
                stage,
                stage,
                copy_sems,
                pltpu.SemaphoreType.DMA((4,)),
            ],
            (ids, grad, unit_two, inverse_two, unit_one, inverse_one, hidden, slope, small) + ffn_weights(layer),
        )
        order.last = outs[1]
        return outs

    def attn_backward(layer, d_resid, x, qkv_rows, probs, context):
        d_resid = order.after(d_resid)
        outs = call(
            functools.partial(attn_bwd_kernel, layer),
            "attn_bwd",
            [SMEM] + [VMEM] * 5 + [ANY] * 8,
            [VMEM] * 2 + [ANY] * 2,
            [rows_low, shape((8, width), f32), pieces, pieces],
            [
                w_qkv,
                w_o,
                pltpu.VMEM((tokens, width), low),
                pltpu.VMEM((tokens, width), low),
                pltpu.VMEM((tokens, 3 * width), low),
                pltpu.VMEM((width, tokens), low),
                stage,
                copy_sems,
                pltpu.SemaphoreType.DMA((2,)),
            ],
            (ids, d_resid, x, qkv_rows, probs, context) + attn_weights(layer),
        )
        order.last = outs[1]
        return outs

    def unpack(layer, slab, near, far, earlier):
        dims = {
            "attn": [(layers, share, 3 * width), (layers, share, width)],
            "in": [(layers, share, ffn)],
            "out": [(layers, ffn_share, width)],
        }[slab]
        near, far = order.after((near, far))
        outs = call(
            functools.partial(unpack_kernel, layer, slab),
            "unpack",
            [SMEM] + [ANY] * (2 + len(earlier)),
            [ANY] * len(dims),
            [shape(d, f32) for d in dims],
            [
                pltpu.VMEM((8, share, tile), low),
                pltpu.VMEM((8, share, tile), f32),
                pltpu.SemaphoreType.DMA((8,)),
                pltpu.SemaphoreType.DMA((8,)),
            ],
            (ids, near, far, *earlier),
            {3 + i: i for i in range(len(earlier))},
        )
        return outs

    arrive(("x", 0), ("y", 0), ("x", 1), ("d", 0), ("x", 2))
    first_attn = attn_forward(0, tables_in)
    arrive(("x", 3), ("y", 1), ("y", 2), ("d", 1), ("d", 2))
    first_ffn = ffn_forward(0, first_attn[3])
    arrive(("x", 4), ("y", 3), ("d", 3))
    second_attn = attn_forward(1, first_ffn[4])
    arrive(("x", 5), ("y", 4), ("y", 5), ("d", 4), ("d", 5))
    second_ffn = ffn_forward(1, second_attn[3])
    mixed_out = second_ffn[4]
    inputs = (tables_in, first_ffn[4])
    attn_kept, ffn_kept = (first_attn, second_attn), (first_ffn, second_ffn)

    ways = ("xyzw", "yxzw", "xyzw", "xyzw", "xyzw", "yxzw")
    kernels = (("ffn1", 17, (0, 1)), ("attn1", 16, (2,)), ("ffn0", 17, (3, 4)), ("attn0", 16, (5,)))
    slabs = [None] * 6
    grad = cotangent
    attn_small, ffn_small, in_bias_grads = [None] * layers, [None] * layers, [None] * layers
    unpacked = {"attn": (), "in": (), "out": ()}
    small_sums = None
    small_steps = [("narrow", 1), ("narrow", 2)] + [("wide", 1 << b) for b in range(wide_bits)]
    steps_left = 0
    for action, which in plan(ways, kernels, width * ffn * 2e-6):
        if action == "kernel":
            layer = int(which[-1])
            _, _, _, unit_one, inverse_one = attn_kept[layer]
            if which[:-1] == "ffn":
                hidden, slope, unit_two, inverse_two, _ = ffn_kept[layer]
                d_resid, ffn_small[layer], in_bias_grads[layer], in_kept, in_sent, out_kept, out_sent = ffn_backward(
                    layer, grad, unit_two, inverse_two, unit_one, inverse_one, hidden, slope
                )
                base = 3 * (layers - 1 - layer)
                slabs[base] = Slab(ways[base], wide_bits, out_kept, out_sent)
                slabs[base + 1] = Slab(ways[base + 1], wide_bits, in_kept, in_sent)
            else:
                qkv_rows, probs, context, _, _ = attn_kept[layer]
                grad, attn_small[layer], kept, sent = attn_backward(
                    layer, d_resid, inputs[layer], qkv_rows, probs, context
                )
                base = 3 * (layers - 1 - layer) + 2
                slabs[base] = Slab(ways[base], wide_bits, kept, sent)
            if which == "attn0":
                small_sums = jnp.stack(
                    [
                        jnp.concatenate([attn_small[i][:3], ffn_small[i][:5], in_bias_grads[i].reshape(4, width)])
                        for i in range(layers)
                    ]
                )
                small_sums = order.after(small_sums)
                steps_left = len(small_steps)
            continue
        slab = slabs[which]
        slab.step(order)
        if steps_left:
            axis, bit = small_steps[-steps_left]
            small_sums = order.wait(small_sums + swap(small_sums, axis, bit))
            steps_left -= 1
            if not steps_left:
                rows = lax.dynamic_slice(small_sums, (0, 0, me * share), (layers, 8, share))
                in_rows = lax.dynamic_slice(small_sums, (0, 8 + me, 0), (layers, 1, ffn_share))
                vectors = [rows[:, i] for i in range(8)] + [in_rows[:, 0]]
        if slab.stage == len(ways[which]) + len(BACK) + 1:
            name = ("out", "in", "attn")[which % 3]
            if which == len(slabs) - 1:
                vectors = order.wait(vectors)
            unpacked[name] = unpack(
                layers - 1 - which // 3, name, slab.block, slab.far, unpacked[name]
            )
    qkv_grad, o_grad = unpacked["attn"]
    (in_grad,), (out_grad,) = unpacked["in"], unpacked["out"]
    return (
        mixed_out,
        grad,
        qkv_grad,
        vectors[0],
        vectors[1],
        o_grad,
        vectors[2],
        vectors[6],
        vectors[7],
        in_grad,
        vectors[8],
        out_grad,
        vectors[5],
        vectors[3],
        vectors[4],
    )


def solution(mesh):
    by_table = P(("wide", "narrow"), None)
    matrix = P(None, "narrow", None)
    vector = P(None, "narrow")
    return jax.shard_map(
        body,
        mesh=mesh,
        in_specs=(
            by_table,
            by_table,
            by_table,
            P(("wide", "narrow")),
            matrix,
            vector,
            vector,
            matrix,
            vector,
            vector,
            vector,
            matrix,
            vector,
            matrix,
            vector,
            vector,
            vector,
        ),
        out_specs=(
            by_table,
            by_table,
            matrix,
            vector,
            vector,
            matrix,
            vector,
            vector,
            vector,
            matrix,
            vector,
            matrix,
            vector,
            vector,
            vector,
        ),
        check_vma=False,
    )
```

time: 738 us -> 501 us (0.68)
  waiting for transfers between devices: 463 us -> 192 us
  blocking collectives: 5.23 us -> 24.6 us
  Pallas kernels: 122 us -> 141 us
  starting transfers between devices: 58.3 us -> 73.7 us
  between operations: 15.8 us -> 2.81 us
  local copies, waits for them, and re-layouts: 44.4 us -> 34.9 us
  other arithmetic: 16.6 us -> 25.9 us
    ppermute x60 -> x81, waiting for transfers between devices: 345 us -> 192 us  [swap(): return lax.ppermute(value, axis, [(i, i ^ bit) for i in range(count)])]
    psum x1 -> x0, waiting for transfers between devices: 118 us -> none  [body(): lax.psum((rows, jnp.stack(in_bias_grads)), ('wide', 'narrow'))]
    pallas_call x9 -> x14, Pallas kernels: 122 us -> 141 us  [call(): pl.pallas_call(kernel, name=name, in_specs=in_specs, out_specs=out_specs,...]
    all_gather x1, blocking collectives: 5.23 us -> 24.6 us  [body(): packed = lax.all_gather(packed, 'narrow', axis=0).astype(f32)]
    ppermute x60 -> x81, starting transfers between devices: 58.2 us -> 73.7 us  [swap(): return lax.ppermute(value, axis, [(i, i ^ bit) for i in range(count)])]
    convert_element_type x18 -> x24, other arithmetic: 12.8 us -> 21.3 us  [added(): return (a.astype(f32) + b.astype(f32)).astype(low)]
    reshape x0 -> x8, local copies, waits for them, and re-layouts: none -> 8.11 us  [the longest x2 5.48 us: __init__(): self.flying = swap(sent.reshape(self.kept.shape), 'narrow', 1)]
  transfers between devices with their start and end apart: 61 -> 81, of which waited for: 25 -> 35; matrix products, arithmetic and copies ran while one was open for 8% -> 10% of each run, Pallas kernels for 7% -> 22%
where the time goes in v2:
time: 501 us; the launch traced here: 495 us
  waiting for transfers between devices  192 us (38%)
  Pallas kernels  141 us (28%)
  starting transfers between devices  73.7 us (15%)
  local copies, waits for them, and re-layouts  34.9 us (7%)
  other arithmetic  25.9 us (5%)
  blocking collectives  24.6 us (5%)
    ppermute x81, waiting for transfers between devices, swap(): return lax.ppermute(value, axis, [(i, i ^ bit) for i in range(count)])  192 us
    pallas_call x14, Pallas kernels, call(): pl.pallas_call(kernel, name=name, in_specs=in_specs, out_specs=out_specs,...  141 us
    ppermute x81, starting transfers between devices, swap(): return lax.ppermute(value, axis, [(i, i ^ bit) for i in range(count)])  73.7 us
    all_gather x1, blocking collectives, body(): packed = lax.all_gather(packed, 'narrow', axis=0).astype(f32)  24.6 us
    convert_element_type x24, other arithmetic, added(): return (a.astype(f32) + b.astype(f32)).astype(low)  21.3 us
    unnamed x127, local copies, waits for them, and re-layouts  13.9 us
  transfers between devices with their start and end apart: 81, of which 35 were waited for; matrix products, arithmetic and copies ran while one was open for 10% of the time, Pallas kernels for 22%

profile of v2, /device:TPU:0, one launch (start us, length us, event | category | flops | bytes accessed | tf_op | source)
XLA Modules:
  0.0 494.9 jit_solution(2438825898969227528)
XLA Ops:
  0.7 2.5 dynamic-slice_bitcast_fusion
  3.2 2.9 collective-permute-start
  8.9 24.6 %all-gather = bf16[8,12,192]{2,1,0:T(8,128)(2,1)S(1)} all-gather(bf16[2,12,192]{2,1,0:T(8,128)(2,1)S(1)} %concatenate.61), channel_id=2, replica_groups=mesh['wide'=8,'narrow'=4] {'narrow'}, dimensions={0}, use_global_device_ids=true | all-gather | bytes 46080 | tf_op jit(solution)/shard_map/all_gather | solution.py:505
  35.8 1.8 collective-permute-start.3
  40.6 11.1 %collective-permute-done.3.rest_5_ = bf16[96,3072]{1,0:T(8,128)(2,1)S(1)} collective-permute-done((bf16[96,3072]{1,0:T(8,128)(2,1)}, bf16[96,3072]{1,0:T(8,128)(2,1)S(1)}, u32[]{:S(2)}, u32[]{:S(2)}) %collective-permute-start.3) | collective-permute-done | bytes 589856 | tf_op jit(solution)/shard_map/ppermute | solution.py:22
  56.1 1.9 collective-permute-start.10
  58.0 11.9 %collective-permute-done.11.rest_4_ = bf16[96,3072]{1,0:T(8,128)(2,1)S(1)} collective-permute-done((bf16[96,3072]{1,0:T(8,128)(2,1)S(1)}, bf16[96,3072]{1,0:T(8,128)(2,1)S(1)}, u32[]{:S(2)}, u32[]{:S(2)}) %collective-permute-start.11) | collective-permute-done | bytes 589856 | tf_op jit(solution)/shard_map/ppermute | solution.py:22
  75.0 13.0 %attn_fwd.2 = (bf16[256,2304]{1,0:T(8,128)(2,1)}, bf16[12,256,256]{2,1,0:T(8,128)(2,1)}, bf16[256,768]{1,0:T(8,128)(2,1)}, f32[256,768]{1,0:T(8,128)}, f32[256,1]{1,0:T(8,128)}) custom-call(s32[6]{0:T(128)} %stack.60.ids, s32[1]{0:T(128)S(6)} %copy.152.length, bf16[256,768]{1,0:T(8,128)(2,1)} %x.2, s32[1,256]{1,0:T(1,128)} %cell_row.3, ...), custom_call_target="tpu_custom_call" | custom-call | flops 1 | bytes 1 | tf_op jit(solution)/shard_map/attn_fwd/pallas_call | solution.py:342
  94.0 10.0 %ffn_fwd.2 = (bf16[256,3072]{1,0:T(8,128)(2,1)}, f32[256,3072]{1,0:T(8,128)}, f32[256,768]{1,0:T(8,128)}, f32[256,1]{1,0:T(8,128)}, bf16[256,768]{1,0:T(8,128)(2,1)}) custom-call(s32[6]{0:T(128)} %stack.60.ids, f32[256,768]{1,0:T(8,128)} %get-tuple-element.178.unit_one, f32[2,1,3072]{2,1,0:T(1,128)} %reshape.385.in_bias, f32[2,8,768]{2,1,0:T(8,128)} %copy-done.7, ...), custom_call_target="tpu_custom_call" | custom-call | flops 1 | bytes 1 | tf_op jit(solution)/shard_map/ffn_fwd/pallas_call | solution.py:342
  104.0 2.1 collective-permute-done.19.rest_2_
  110.6 12.9 %attn_fwd.3 = (bf16[256,2304]{1,0:T(8,128)(2,1)}, bf16[12,256,256]{2,1,0:T(8,128)(2,1)}, bf16[256,768]{1,0:T(8,128)(2,1)}, f32[256,768]{1,0:T(8,128)}, f32[256,1]{1,0:T(8,128)}) custom-call(s32[6]{0:T(128)} %stack.60.ids, s32[1]{0:T(128)S(6)} %copy.152.length, bf16[256,768]{1,0:T(8,128)(2,1)} %get-tuple-element.185.x, s32[1,256]{1,0:T(1,128)} %cell_row.3, ...), custom_call_target="tpu_custom_call" | custom-call | flops 1 | bytes 1 | tf_op jit(solution)/shard_map/attn_fwd/pallas_call | solution.py:342
  125.1 13.6 %collective-permute-done.23.rest_9_ = bf16[384,768]{1,0:T(8,128)(2,1)S(1)} collective-permute-done((bf16[384,768]{1,0:T(8,128)(2,1)S(1)}, bf16[384,768]{1,0:T(8,128)(2,1)S(1)}, u32[]{:S(2)}, u32[]{:S(2)}) %collective-permute-start.23) | collective-permute-done | bytes 589856 | tf_op jit(solution)/shard_map/ppermute | solution.py:22
  138.8 1.9 collective-permute-done.25.rest_11_
  141.5 10.0 %ffn_fwd.3 = (bf16[256,3072]{1,0:T(8,128)(2,1)}, f32[256,3072]{1,0:T(8,128)}, f32[256,768]{1,0:T(8,128)}, f32[256,1]{1,0:T(8,128)}, bf16[256,768]{1,0:T(8,128)(2,1)}) custom-call(s32[6]{0:T(128)} %stack.60.ids, f32[256,768]{1,0:T(8,128)} %get-tuple-element.195.unit_one, f32[2,1,3072]{2,1,0:T(1,128)} %reshape.385.in_bias, f32[2,8,768]{2,1,0:T(8,128)} %copy-done.7, ...), custom_call_target="tpu_custom_call" | custom-call | flops 1 | bytes 1 | tf_op jit(solution)/shard_map/ffn_fwd/pallas_call | solution.py:342
  151.6 17.8 %ffn_bwd.2 = (f32[256,768]{1,0:T(8,128)}, f32[8,768]{1,0:T(8,128)}, f32[1,3072]{1,0:T(1,128)}, bf16[2,8,192,384]{3,2,1,0:T(8,128)(2,1)}, bf16[2,8,192,384]{3,2,1...) custom-call(s32[6]{0:T(128)} %stack.60.ids, bf16[256,768]{1,0:T(8,128)(2,1)} %grad, ...), custom_call_target="tpu_custom_call" | custom-call | flops 1 | bytes 1 | tf_op jit(solution)/shard_map/ffn_bwd/pallas_call | solution.py:342
  169.6 3.4 copy.109
  173.3 15.7 %attn_bwd.2 = (bf16[256,768]{1,0:T(8,128)(2,1)}, f32[8,768]{1,0:T(8,128)}, bf16[2,8,192,384]{3,2,1,0:T(8,128)(2,1)}, bf16[2,8,192,384]{3,2,1,0:T(8,128)(2,1)}) custom-call(s32[6]{0:T(128)} %stack.60.ids, f32[256,768]{1,0:T(8,128)} %get-tuple-element.204.d_resid, bf16[256,768]{1,0:T(8,128)(2,1)} %get-tuple-element.185.x, ...), custom_call_target="tpu_custom_call" | custom-call | flops 1 | bytes 1 | tf_op jit(solution)/shard_map/attn_bwd/pallas_call | solution.py:342
  190.7 2.0 fusion.77
  193.4 3.7 fusion.5
  197.1 3.3 add_convert_fusion.2
  200.4 17.5 %ffn_bwd.3 = (f32[256,768]{1,0:T(8,128)}, f32[8,768]{1,0:T(8,128)}, f32[1,3072]{1,0:T(1,128)}, bf16[2,8,192,384]{3,2,1,0:T(8,128)(2,1)}, bf16[2,8,192,384]{3,2,1...) custom-call(s32[6]{0:T(128)} %stack.60.ids, ...), custom_call_target="tpu_custom_call" | custom-call | flops 1 | bytes 1 | tf_op jit(solution)/shard_map/ffn_bwd/pallas_call | solution.py:342
  220.5 3.4 fusion.2
  223.8 25.6 %attn_bwd.3 = (bf16[256,768]{1,0:T(8,128)(2,1)}, f32[8,768]{1,0:T(8,128)}, bf16[2,8,192,384]{3,2,1,0:T(8,128)(2,1)}, bf16[2,8,192,384]{3,2,1,0:T(8,128)(2,1)}) custom-call(s32[6]{0:T(128)} %stack.60.ids, f32[256,768]{1,0:T(8,128)} %get-tuple-element.225.d_resid, bf16[256,768]{1,0:T(8,128)(2,1)} %x.2, bf16[256,2304]{1,0:T(8,128)(2,1)} %get-tuple-element.226.qkv_rows, ...), custom_call_target="tpu_custom_call" | custom-call | flops 1 | bytes 1 | tf_op jit(solution)/shard_map/attn_bwd/pallas_call | solution.py:342
  251.5 2.1 copy.111
  260.5 25.0 %collective-permute-done.34 = f32[2,12,768]{2,1,0:T(8,128)S(1)} collective-permute-done((f32[2,12,768]{2,1,0:T(8,128)S(1)}, f32[2,12,768]{2,1,0:T(8,128)S(1)}, u32[]{:S(2)}, u32[]{:S(2)}) %collective-permute-start.34) | collective-permute-done | bytes 73760 | tf_op jit(solution)/shard_map/ppermute | solution.py:22
  292.3 2.3 fusion.1
  296.3 2.3 fusion
  299.4 3.2 collective-permute-start.44
  303.2 3.1 collective-permute-done.44
  309.8 7.8 %collective-permute-done.45 = bf16[2,192,384]{2,1,0:T(8,128)(2,1)S(1)} collective-permute-done((bf16[2,192,384]{2,1,0:T(8,128)(2,1)S(1)}, bf16[2,192,384]{2,1,0:T(8,128)(2,1)S(1)}, u32[]{:S(2)}, u32[]{:S(2)}) %collective-permute-start.45) | collective-permute-done | bytes 294944 | tf_op jit(solution)/shard_map/ppermute | solution.py:22
  317.7 2.0 collective-permute-start.47
  319.8 2.5 collective-permute-start.46
  323.4 4.9 collective-permute-done.47
  330.1 6.6 %collective-permute-done.40 = bf16[2,2,2,192,384]{4,3,2,1,0:T(8,128)(2,1)S(1)} collective-permute-done((bf16[2,2,2,192,384]{4,3,2,1,0:T(8,128)(2,1)S(1)}, bf16[2,2,2,192,384]{4,3,2,1,0:T(8,128)(2,1)S(1)}, u32[]{:S(2)}, u32[]{:S(2)}) %collective-permute-start.40) | collective-permute-done | bytes 1179680 | tf_op jit(solution)/shard_map/ppermute | solution.py:22
  336.8 3.6 collective-permute-start.53
  341.2 5.0 %collective-permute-done.53 = bf16[192,384]{1,0:T(8,128)(2,1)S(1)} collective-permute-done((bf16[192,384]{1,0:T(8,128)(2,1)S(1)}, bf16[192,384]{1,0:T(8,128)(2,1)S(1)}, u32[]{:S(2)}, u32[]{:S(2)}) %collective-permute-start.53) | collective-permute-done | bytes 147488 | tf_op jit(solution)/shard_map/ppermute | solution.py:22
  347.6 3.7 collective-permute-done.51
  352.0 2.6 collective-permute-start.55
  355.6 7.0 %collective-permute-done.55 = bf16[1,192,384]{2,1,0:T(8,128)(2,1)S(1)} collective-permute-done((bf16[1,192,384]{2,1,0:T(8,128)(2,1)S(1)}, bf16[1,192,384]{2,1,0:T(8,128)(2,1)S(1)}, u32[]{:S(2)}, u32[]{:S(2)}) %collective-permute-start.55) | collective-permute-done | bytes 147488 | tf_op jit(solution)/shard_map/ppermute | solution.py:22
  362.6 3.8 collective-permute-start.58
  366.7 2.5 collective-permute-start.61
  369.2 9.3 %collective-permute-done.58 = bf16[2,192,384]{2,1,0:T(8,128)(2,1)S(1)} collective-permute-done((bf16[2,192,384]{2,1,0:T(8,128)(2,1)S(1)}, bf16[2,192,384]{2,1,0:T(8,128)(2,1)S(1)}, u32[]{:S(2)}, u32[]{:S(2)}) %collective-permute-start.58) | collective-permute-done | bytes 294944 | tf_op jit(solution)/shard_map/ppermute | solution.py:22
  380.5 4.6 collective-permute-done.61
  385.2 3.5 collective-permute-done.60
  389.0 2.1 collective-permute-start.62
  391.1 4.9 collective-permute-done.64
  396.1 10.4 %collective-permute-done.63 = bf16[2,192,384]{2,1,0:T(8,128)(2,1)S(1)} collective-permute-done((bf16[2,192,384]{2,1,0:T(8,128)(2,1)S(1)}, bf16[2,192,384]{2,1,0:T(8,128)(2,1)S(1)}, u32[]{:S(2)}, u32[]{:S(2)}) %collective-permute-start.63) | collective-permute-done | bytes 294944 | tf_op jit(solution)/shard_map/ppermute | solution.py:22
  406.6 3.9 collective-permute-done.62
  413.0 6.4 %collective-permute-done.65 = bf16[192,384]{1,0:T(8,128)(2,1)S(1)} collective-permute-done((bf16[192,384]{1,0:T(8,128)(2,1)S(1)}, bf16[192,384]{1,0:T(8,128)(2,1)S(1)}, u32[]{:S(2)}, u32[]{:S(2)}) %collective-permute-start.65) | collective-permute-done | bytes 147488 | tf_op jit(solution)/shard_map/ppermute | solution.py:22
  422.6 7.4 %collective-permute-done.69 = bf16[2,192,384]{2,1,0:T(8,128)(2,1)S(1)} collective-permute-done((bf16[2,192,384]{2,1,0:T(8,128)(2,1)S(1)}, bf16[2,192,384]{2,1,0:T(8,128)(2,1)S(1)}, u32[]{:S(2)}, u32[]{:S(2)}) %collective-permute-start.69) | collective-permute-done | bytes 294944 | tf_op jit(solution)/shard_map/ppermute | solution.py:22
  430.3 2.0 collective-permute-start.74
  433.1 5.4 %collective-permute-done.71 = bf16[2,192,384]{2,1,0:T(8,128)(2,1)S(1)} collective-permute-done((bf16[2,192,384]{2,1,0:T(8,128)(2,1)S(1)}, bf16[2,192,384]{2,1,0:T(8,128)(2,1)S(1)}, u32[]{:S(2)}, u32[]{:S(2)}) %collective-permute-start.71) | collective-permute-done | bytes 294944 | tf_op jit(solution)/shard_map/ppermute | solution.py:22
  441.7 3.7 collective-permute-done.75
  446.1 2.5 collective-permute-done.80.far
  457.5 3.1 unpack.10.rest_0_
  461.3 3.1 unpack.8.rest_0_
  464.4 7.5 %collective-permute-done.76.far = bf16[4,192,384]{2,1,0:T(8,128)(2,1)} collective-permute-done((bf16[4,192,384]{2,1,0:T(8,128)(2,1)S(1)}, bf16[4,192,384]{2,1,0:T(8,128)(2,1)}, u32[]{:S(2)}, u32[]{:S(2)}) %collective-permute-start.76) | collective-permute-done | bytes 589856 | tf_op jit(solution)/shard_map/ppermute | solution.py:22
  471.9 3.1 unpack.6
  475.0 3.2 collective-permute-done.79.far
  478.2 3.1 unpack.11
  481.4 3.2 collective-permute-done.72.far
  484.5 3.1 unpack.7
  487.7 3.1 collective-permute-done.77.far
  491.6 3.1 unpack.9
  (339 shorter events, 87.5 us)
Async XLA Ops:
  3.2 48.5 %collective-permute-start = (bf16[384,768]{1,0:T(8,128)(2,1)}, bf16[384,768]{1,0:T(8,128)(2,1)}, u32[]{:S(2)}, u32[]{:S(2)}) collective-permute-start(bf16[384,768]{1,0:T(8,128)(2,1)} %get-tuple-element.342), channel_id=1, source_target_pairs={{0,2},{1,3},{2,0},{3,1},{4,6},{5,7},{6,4},{7,5},{8,10},{9,11},{10,... | collective-permute-start | bytes 1769480 | tf_op jit(solution)/shard_map/ppermute | solution.py:22
  8.6 27.2 %collective-permute-start.1 = (bf16[96,3072]{1,0:T(8,128)(2,1)}, bf16[96,3072]{1,0:T(8,128)(2,1)}, u32[]{:S(2)}, u32[]{:S(2)}) collective-permute-start(bf16[96,3072]{1,0:T(8,128)(2,1)} %pad_maximum_fusion), channel_id=1, source_target_pairs={{0,2},{1,3},{2,0},{3,1},{4,6},{5,7},{6,4},{7,5},{8,10},{9,11},{10,... | collective-permute-start | bytes 1769480 | tf_op jit(solution)/shard_map/ppermute | solution.py:22
  35.8 15.9 %collective-permute-start.3 = (bf16[96,3072]{1,0:T(8,128)(2,1)}, bf16[96,3072]{1,0:T(8,128)(2,1)S(1)}, u32[]{:S(2)}, u32[]{:S(2)}) collective-permute-start(bf16[96,3072]{1,0:T(8,128)(2,1)} %collective-permute-done.1.rest_4_), channel_id=1, source_target_pairs={{0,4},{4,0},{8,12},{12,8},{16,20},{20,16},{24,28},{28,24},{1,5},{5... | collective-permute-start | bytes 1769480 | tf_op jit(solution)/shard_map/ppermute | solution.py:22
  38.5 15.4 %collective-permute-start.5 = (bf16[96,3072]{1,0:T(8,128)(2,1)S(1)}, bf16[96,3072]{1,0:T(8,128)(2,1)}, u32[]{:S(2)}, u32[]{:S(2)}) collective-permute-start(bf16[96,3072]{1,0:T(8,128)(2,1)S(1)} %get-tuple-element.344), channel_id=1, source_target_pairs={{0,2},{1,3},{2,0},{3,1},{4,6},{5,7},{6,4},{7,5},{8,10},{9,11},{10,... | collective-permute-start | bytes 1769480 | tf_op jit(solution)/shard_map/ppermute | solution.py:22
  40.0 13.9 %collective-permute-start.2 = (bf16[96,3072]{1,0:T(8,128)(2,1)}, bf16[96,3072]{1,0:T(8,128)(2,1)}, u32[]{:S(2)}, u32[]{:S(2)}) collective-permute-start(bf16[96,3072]{1,0:T(8,128)(2,1)} %collective-permute-done.1.rest_4_), channel_id=1, source_target_pairs={{0,1},{1,0},{2,3},{3,2},{4,5},{5,4},{6,7},{7,6},{8,9},{9,8},{10,11... | collective-permute-start | bytes 1769480 | tf_op jit(solution)/shard_map/ppermute | solution.py:22
  40.0 30.8 %collective-permute-start.6 = (bf16[2,192,2304]{2,1,0:T(8,128)(2,1)S(1)}, bf16[2,192,2304]{2,1,0:T(8,128)(2,1)S(1)}, u32[]{:S(2)}, u32[]{:S(2)}) collective-permute-start(bf16[2,192,2304]{2,1,0:T(8,128)(2,1)S(1)} %copy-done.2), channel_id=1, source_target_pairs={{0,1},{1,0},{2,3},{3,2},{4,5},{5,4},{6,7},{7,6},{8,9},{9,8},{10,11... | collective-permute-start | bytes 5308424 | tf_op jit(solution)/shard_map/ppermute | solution.py:22
  53.9 39.2 %collective-permute-start.15 = (bf16[2,192,3072]{2,1,0:T(8,128)(2,1)S(1)}, bf16[2,192,3072]{2,1,0:T(8,128)(2,1)}, u32[]{:S(2)}, u32[]{:S(2)}) collective-permute-start(bf16[2,192,3072]{2,1,0:T(8,128)(2,1)S(1)} %copy-done), channel_id=1, source_target_pairs={{0,1},{1,0},{2,3},{3,2},{4,5},{5,4},{6,7},{7,6},{8,9},{9,8},{10,11... | collective-permute-start | bytes 7077896 | tf_op jit(solution)/shard_map/ppermute | solution.py:22
  53.9 39.2 %collective-permute-start.16 = (bf16[2,768,768]{2,1,0:T(8,128)(2,1)}, bf16[2,768,768]{2,1,0:T(8,128)(2,1)}, u32[]{:S(2)}, u32[]{:S(2)}) collective-permute-start(bf16[2,768,768]{2,1,0:T(8,128)(2,1)} %rest_6_.7), channel_id=1, source_target_pairs={{0,1},{1,0},{2,3},{3,2},{4,5},{5,4},{6,7},{7,6},{8,9},{9,8},{10,11... | collective-permute-start | bytes 7077896 | tf_op jit(solution)/shard_map/ppermute | solution.py:22
  54.5 15.3 %collective-permute-start.11 = (bf16[96,3072]{1,0:T(8,128)(2,1)S(1)}, bf16[96,3072]{1,0:T(8,128)(2,1)S(1)}, u32[]{:S(2)}, u32[]{:S(2)}) collective-permute-start(bf16[96,3072]{1,0:T(8,128)(2,1)S(1)} %pad_maximum_fusion.1), channel_id=1, source_target_pairs={{0,2},{1,3},{2,0},{3,1},{4,6},{5,7},{6,4},{7,5},{8,10},{9,11},{10,... | collective-permute-start | bytes 1769480 | tf_op jit(solution)/shard_map/ppermute | solution.py:22
  56.1 31.9 %collective-permute-start.10 = (bf16[96,3072]{1,0:T(8,128)(2,1)}, bf16[96,3072]{1,0:T(8,128)(2,1)}, u32[]{:S(2)}, u32[]{:S(2)}) collective-permute-start(bf16[96,3072]{1,0:T(8,128)(2,1)} %collective-permute-done.5.rest_2_), channel_id=1, source_target_pairs={{0,4},{4,0},{8,12},{12,8},{16,20},{20,16},{24,28},{28,24},{1,5},{5... | collective-permute-start | bytes 1769480 | tf_op jit(solution)/shard_map/ppermute | solution.py:22
  69.8 18.7 %collective-permute-start.9 = (bf16[384,768]{1,0:T(8,128)(2,1)}, bf16[384,768]{1,0:T(8,128)(2,1)}, u32[]{:S(2)}, u32[]{:S(2)}) collective-permute-start(bf16[384,768]{1,0:T(8,128)(2,1)} %collective-permute-done.rest_8_), channel_id=1, source_target_pairs={{0,4},{4,0},{8,12},{12,8},{16,20},{20,16},{24,28},{28,24},{1,5},{5... | collective-permute-start | bytes 1769480 | tf_op jit(solution)/shard_map/ppermute | solution.py:22
  72.1 16.5 %collective-permute-start.13 = (bf16[96,3072]{1,0:T(8,128)(2,1)}, bf16[96,3072]{1,0:T(8,128)(2,1)}, u32[]{:S(2)}, u32[]{:S(2)}) collective-permute-start(bf16[96,3072]{1,0:T(8,128)(2,1)} %collective-permute-done.5.rest_2_), channel_id=1, source_target_pairs={{0,1},{1,0},{2,3},{3,2},{4,5},{5,4},{6,7},{7,6},{8,9},{9,8},{10,11... | collective-permute-start | bytes 1769480 | tf_op jit(solution)/shard_map/ppermute | solution.py:22
  90.4 15.6 %collective-permute-start.19 = (bf16[96,3072]{1,0:T(8,128)(2,1)S(1)}, bf16[96,3072]{1,0:T(8,128)(2,1)S(1)}, u32[]{:S(2)}, u32[]{:S(2)}) collective-permute-start(bf16[96,3072]{1,0:T(8,128)(2,1)S(1)} %copy-done.41), channel_id=1, source_target_pairs={{0,2},{1,3},{2,0},{3,1},{4,6},{5,7},{6,4},{7,5},{8,10},{9,11},{10,... | collective-permute-start | bytes 1769480 | tf_op jit(solution)/shard_map/ppermute | solution.py:22
  91.9 15.4 %collective-permute-start.18 = (bf16[96,3072]{1,0:T(8,128)(2,1)S(1)}, bf16[96,3072]{1,0:T(8,128)(2,1)S(1)}, u32[]{:S(2)}, u32[]{:S(2)}) collective-permute-start(bf16[96,3072]{1,0:T(8,128)(2,1)S(1)} %copy-done.11), channel_id=1, source_target_pairs={{0,4},{4,0},{8,12},{12,8},{16,20},{20,16},{24,28},{28,24},{1,5},{5... | collective-permute-start | bytes 1769480 | tf_op jit(solution)/shard_map/ppermute | solution.py:22
  93.1 16.4 %collective-permute-start.17 = (bf16[96,3072]{1,0:T(8,128)(2,1)S(1)}, bf16[96,3072]{1,0:T(8,128)(2,1)S(1)}, u32[]{:S(2)}, u32[]{:S(2)}) collective-permute-start(bf16[96,3072]{1,0:T(8,128)(2,1)S(1)} %copy-done.11), channel_id=1, source_target_pairs={{0,1},{1,0},{2,3},{3,2},{4,5},{5,4},{6,7},{7,6},{8,9},{9,8},{10,11... | collective-permute-start | bytes 1769480 | tf_op jit(solution)/shard_map/ppermute | solution.py:22
  107.3 16.2 %collective-permute-start.21 = (bf16[384,768]{1,0:T(8,128)(2,1)S(1)}, bf16[384,768]{1,0:T(8,128)(2,1)S(1)}, u32[]{:S(2)}, u32[]{:S(2)}) collective-permute-start(bf16[384,768]{1,0:T(8,128)(2,1)S(1)} %copy-done.40), channel_id=1, source_target_pairs={{0,2},{1,3},{2,0},{3,1},{4,6},{5,7},{6,4},{7,5},{8,10},{9,11},{10,... | collective-permute-start | bytes 1769480 | tf_op jit(solution)/shard_map/ppermute | solution.py:22
  108.4 16.6 %collective-permute-start.24 = (bf16[96,3072]{1,0:T(8,128)(2,1)S(1)}, bf16[96,3072]{1,0:T(8,128)(2,1)S(1)}, u32[]{:S(2)}, u32[]{:S(2)}) collective-permute-start(bf16[96,3072]{1,0:T(8,128)(2,1)S(1)} %collective-permute-done.19.rest_2_), channel_id=1, source_target_pairs={{0,4},{4,0},{8,12},{12,8},{16,20},{20,16},{24,28},{28,24},{1,5},{5... | collective-permute-start | bytes 1769480 | tf_op jit(solution)/shard_map/ppermute | solution.py:22
  123.5 15.2 %collective-permute-start.23 = (bf16[384,768]{1,0:T(8,128)(2,1)S(1)}, bf16[384,768]{1,0:T(8,128)(2,1)S(1)}, u32[]{:S(2)}, u32[]{:S(2)}) collective-permute-start(bf16[384,768]{1,0:T(8,128)(2,1)S(1)} %collective-permute-done.21.rest_8_), channel_id=1, source_target_pairs={{0,4},{4,0},{8,12},{12,8},{16,20},{20,16},{24,28},{28,24},{1,5},{5... | collective-permute-start | bytes 1769480 | tf_op jit(solution)/shard_map/ppermute | solution.py:22
  124.5 14.2 %collective-permute-start.26 = (bf16[96,3072]{1,0:T(8,128)(2,1)S(1)}, bf16[96,3072]{1,0:T(8,128)(2,1)S(1)}, u32[]{:S(2)}, u32[]{:S(2)}) collective-permute-start(bf16[96,3072]{1,0:T(8,128)(2,1)S(1)} %collective-permute-done.19.rest_2_), channel_id=1, source_target_pairs={{0,1},{1,0},{2,3},{3,2},{4,5},{5,4},{6,7},{7,6},{8,9},{9,8},{10,11... | collective-permute-start | bytes 1769480 | tf_op jit(solution)/shard_map/ppermute | solution.py:22
  124.5 14.2 %collective-permute-start.22 = (bf16[384,768]{1,0:T(8,128)(2,1)S(1)}, bf16[384,768]{1,0:T(8,128)(2,1)S(1)}, u32[]{:S(2)}, u32[]{:S(2)}) collective-permute-start(bf16[384,768]{1,0:T(8,128)(2,1)S(1)} %collective-permute-done.21.rest_8_), channel_id=1, source_target_pairs={{0,1},{1,0},{2,3},{3,2},{4,5},{5,4},{6,7},{7,6},{8,9},{9,8},{10,11... | collective-permute-start | bytes 1769480 | tf_op jit(solution)/shard_map/ppermute | solution.py:22
  125.1 13.7 %collective-permute-start.27 = (bf16[96,3072]{1,0:T(8,128)(2,1)S(1)}, bf16[96,3072]{1,0:T(8,128)(2,1)S(1)}, u32[]{:S(2)}, u32[]{:S(2)}) collective-permute-start(bf16[96,3072]{1,0:T(8,128)(2,1)S(1)} %collective-permute-done.24.rest_3_), channel_id=1, source_target_pairs={{0,1},{1,0},{2,3},{3,2},{4,5},{5,4},{6,7},{7,6},{8,9},{9,8},{10,11... | collective-permute-start | bytes 1769480 | tf_op jit(solution)/shard_map/ppermute | solution.py:22
  169.4 24.0 %collective-permute-start.29 = (bf16[2,2,2,2,192,384]{5,4,3,2,1,0:T(8,128)(2,1)}, bf16[2,2,2,2,192,384]{5,4,3,2,1,0:T(8,128)(2,1)}, u32[]{:S(2)}, u32[]{:S(2)}) collective-permute-start(bf16[2,2,2,2,192,384]{5,4,3,2,1,0:T(8,128)(2,1)} %bitcast.404), channel_id=1, source_target_pairs={{0,1},{1,0},{2,3},{3,2},{4,5},{5,4},{6,7},{7,6},{8,9},{9,8},{10,11... | collective-permute-start | bytes 7077896 | tf_op jit(solution)/shard_map/ppermute | solution.py:22
  172.9 24.2 %collective-permute-start.28 = (bf16[2,2,2,2,192,384]{5,4,3,2,0,1:T(8,128)(2,1)}, bf16[2,2,2,2,192,384]{5,4,3,2,0,1:T(8,128)(2,1)}, u32[]{:S(2)}, u32[]{:S(2)}) collective-permute-start(bf16[2,2,2,2,192,384]{5,4,3,2,0,1:T(8,128)(2,1)} %copy.109), channel_id=1, source_target_pairs={{0,1},{1,0},{2,3},{3,2},{4,5},{5,4},{6,7},{7,6},{8,9},{9,8},{10,11... | collective-permute-start | bytes 7077896 | tf_op jit(solution)/shard_map/ppermute | solution.py:22
  189.0 31.5 %collective-permute-start.30 = (bf16[2,2,2,2,192,384]{5,4,3,2,1,0:T(8,128)(2,1)}, bf16[2,2,2,2,192,384]{5,4,3,2,1,0:T(8,128)(2,1)}, u32[]{:S(2)}, u32[]{:S(2)}) collective-permute-start(bf16[2,2,2,2,192,384]{5,4,3,2,1,0:T(8,128)(2,1)} %bitcast.403), channel_id=1, source_target_pairs={{0,1},{1,0},{2,3},{3,2},{4,5},{5,4},{6,7},{7,6},{8,9},{9,8},{10,11... | collective-permute-start | bytes 7077896 | tf_op jit(solution)/shard_map/ppermute | solution.py:22
  218.0 73.2 %collective-permute-start.37 = (bf16[2,2,2,2,192,384]{5,4,3,2,1,0:T(8,128)(2,1)}, bf16[2,2,2,2,192,384]{5,4,3,2,1,0:T(8,128)(2,1)}, u32[]{:S(2)}, u32[]{:S(2)}) collective-permute-start(bf16[2,2,2,2,192,384]{5,4,3,2,1,0:T(8,128)(2,1)} %bitcast.402), channel_id=1, source_target_pairs={{0,1},{1,0},{2,3},{3,2},{4,5},{5,4},{6,7},{7,6},{8,9},{9,8},{10,11... | collective-permute-start | bytes 7077896 | tf_op jit(solution)/shard_map/ppermute | solution.py:22
  218.4 35.7 %collective-permute-start.33 = (bf16[2,2,2,192,384]{4,3,2,1,0:T(8,128)(2,1)}, bf16[2,2,2,192,384]{4,3,2,1,0:T(8,128)(2,1)}, u32[]{:S(2)}, u32[]{:S(2)}) collective-permute-start(bf16[2,2,2,192,384]{4,3,2,1,0:T(8,128)(2,1)} %get-tuple-element.338), channel_id=1, source_target_pairs={{0,2},{1,3},{2,0},{3,1},{4,6},{5,7},{6,4},{7,5},{8,10},{9,11},{10,... | collective-permute-start | bytes 3538952 | tf_op jit(solution)/shard_map/ppermute | solution.py:22
  219.5 38.2 %collective-permute-start.35 = (bf16[2,2,2,192,384]{4,3,2,1,0:T(8,128)(2,1)}, bf16[2,2,2,192,384]{4,3,2,1,0:T(8,128)(2,1)}, u32[]{:S(2)}, u32[]{:S(2)}) collective-permute-start(bf16[2,2,2,192,384]{4,3,2,1,0:T(8,128)(2,1)} %get-tuple-element.312), channel_id=1, source_target_pairs={{0,4},{4,0},{8,12},{12,8},{16,20},{20,16},{24,28},{28,24},{1,5},{5... | collective-permute-start | bytes 3538952 | tf_op jit(solution)/shard_map/ppermute | solution.py:22
  220.5 74.2 %collective-permute-start.39 = (bf16[2,2,2,2,192,384]{5,4,3,2,1,0:T(8,128)(2,1)}, bf16[2,2,2,2,192,384]{5,4,3,2,1,0:T(8,128)(2,1)}, u32[]{:S(2)}, u32[]{:S(2)}) collective-permute-start(bf16[2,2,2,2,192,384]{5,4,3,2,1,0:T(8,128)(2,1)} %bitcast.401), channel_id=1, source_target_pairs={{0,1},{1,0},{2,3},{3,2},{4,5},{5,4},{6,7},{7,6},{8,9},{9,8},{10,11... | collective-permute-start | bytes 7077896 | tf_op jit(solution)/shard_map/ppermute | solution.py:22
  253.6 48.9 %collective-permute-start.31 = (bf16[2,2,2,2,192,384]{5,4,3,2,0,1:T(8,128)(2,1)S(1)}, bf16[2,2,2,2,192,384]{5,4,3,2,0,1:T(8,128)(2,1)S(1)}, u32[]{:S(2)}, u32[]{:S(2)}) collective-permute-start(bf16[2,2,2,2,192,384]{5,4,3,2,0,1:T(8,128)(2,1)S(1)} %copy.111), channel_id=1, source_target_pairs={{0,1},{1,0},{2,3},{3,2},{4,5},{5,4},{6,7},{7,6},{8,9},{9,8},{10,11... | collective-permute-start | bytes 7077896 | tf_op jit(solution)/shard_map/ppermute | solution.py:22
  255.1 51.8 %collective-permute-start.43 = (bf16[2,2,2,192,384]{4,3,2,1,0:T(8,128)(2,1)S(1)}, bf16[2,2,2,192,384]{4,3,2,1,0:T(8,128)(2,1)S(1)}, u32[]{:S(2)}, u32[]{:S(2)}) collective-permute-start(bf16[2,2,2,192,384]{4,3,2,1,0:T(8,128)(2,1)S(1)} %copy-done.38), channel_id=1, source_target_pairs={{0,2},{1,3},{2,0},{3,1},{4,6},{5,7},{6,4},{7,5},{8,10},{9,11},{10,... | collective-permute-start | bytes 3538952 | tf_op jit(solution)/shard_map/ppermute | solution.py:22
  257.7 27.8 %collective-permute-start.34 = (f32[2,12,768]{2,1,0:T(8,128)S(1)}, f32[2,12,768]{2,1,0:T(8,128)S(1)}, u32[]{:S(2)}, u32[]{:S(2)}) collective-permute-start(f32[2,12,768]{2,1,0:T(8,128)S(1)} %add.242), channel_id=1, source_target_pairs={{0,2},{1,3},{2,0},{3,1},{4,6},{5,7},{6,4},{7,5},{8,10},{9,11},{10,... | collective-permute-start | bytes 221192 | tf_op jit(solution)/shard_map/ppermute | solution.py:22
  290.2 29.5 %collective-permute-start.41 = (bf16[2,2,192,384]{3,2,1,0:T(8,128)(2,1)S(1)}, bf16[2,2,192,384]{3,2,1,0:T(8,128)(2,1)S(1)}, u32[]{:S(2)}, u32[]{:S(2)}) collective-permute-start(bf16[2,2,192,384]{3,2,1,0:T(8,128)(2,1)S(1)} %get-tuple-element.336), channel_id=1, source_target_pairs={{0,2},{1,3},{2,0},{3,1},{4,6},{5,7},{6,4},{7,5},{8,10},{9,11},{10,... | collective-permute-start | bytes 1769480 | tf_op jit(solution)/shard_map/ppermute | solution.py:22
  291.2 16.0 %collective-permute-start.42 = (bf16[2,2,192,384]{3,2,1,0:T(8,128)(2,1)S(1)}, bf16[2,2,192,384]{3,2,1,0:T(8,128)(2,1)S(1)}, u32[]{:S(2)}, u32[]{:S(2)}) collective-permute-start(bf16[2,2,192,384]{3,2,1,0:T(8,128)(2,1)S(1)} %get-tuple-element.334), channel_id=1, source_target_pairs={{0,4},{4,0},{8,12},{12,8},{16,20},{20,16},{24,28},{28,24},{1,5},{5... | collective-permute-start | bytes 1769480 | tf_op jit(solution)/shard_map/ppermute | solution.py:22
  307.4 10.3 %collective-permute-start.45 = (bf16[2,192,384]{2,1,0:T(8,128)(2,1)S(1)}, bf16[2,192,384]{2,1,0:T(8,128)(2,1)S(1)}, u32[]{:S(2)}, u32[]{:S(2)}) collective-permute-start(bf16[2,192,384]{2,1,0:T(8,128)(2,1)S(1)} %get-tuple-element.357), channel_id=1, source_target_pairs={{0,8},{4,12},{8,0},{12,4},{16,24},{20,28},{24,16},{28,20},{1,9},{5... | collective-permute-start | bytes 884744 | tf_op jit(solution)/shard_map/ppermute | solution.py:22
  307.8 28.9 %collective-permute-start.40 = (bf16[2,2,2,192,384]{4,3,2,1,0:T(8,128)(2,1)S(1)}, bf16[2,2,2,192,384]{4,3,2,1,0:T(8,128)(2,1)S(1)}, u32[]{:S(2)}, u32[]{:S(2)}) collective-permute-start(bf16[2,2,2,192,384]{4,3,2,1,0:T(8,128)(2,1)S(1)} %get-tuple-element.309), channel_id=1, source_target_pairs={{0,4},{4,0},{8,12},{12,8},{16,20},{20,16},{24,28},{28,24},{1,5},{5... | collective-permute-start | bytes 3538952 | tf_op jit(solution)/shard_map/ppermute | solution.py:22
  308.8 37.5 %collective-permute-start.52 = (bf16[2,2,2,192,384]{4,3,2,1,0:T(8,128)(2,1)S(1)}, bf16[2,2,2,192,384]{4,3,2,1,0:T(8,128)(2,1)S(1)}, u32[]{:S(2)}, u32[]{:S(2)}) collective-permute-start(bf16[2,2,2,192,384]{4,3,2,1,0:T(8,128)(2,1)S(1)} %get-tuple-element.322), channel_id=1, source_target_pairs={{0,2},{1,3},{2,0},{3,1},{4,6},{5,7},{6,4},{7,5},{8,10},{9,11},{10,... | collective-permute-start | bytes 3538952 | tf_op jit(solution)/shard_map/ppermute | solution.py:22
  317.7 10.6 %collective-permute-start.47 = (bf16[192,384]{1,0:T(8,128)(2,1)S(1)}, bf16[192,384]{1,0:T(8,128)(2,1)S(1)}, u32[]{:S(2)}, u32[]{:S(2)}) collective-permute-start(bf16[192,384]{1,0:T(8,128)(2,1)S(1)} %fusion.56), channel_id=1, source_target_pairs={{0,16},{4,20},{8,24},{12,28},{16,0},{20,4},{24,8},{28,12},{1,17},{... | collective-permute-start | bytes 442376 | tf_op jit(solution)/shard_map/ppermute | solution.py:22
  319.8 9.5 %collective-permute-start.46 = (bf16[2,192,384]{2,1,0:T(8,128)(2,1)S(1)}, bf16[2,192,384]{2,1,0:T(8,128)(2,1)S(1)}, u32[]{:S(2)}, u32[]{:S(2)}) collective-permute-start(bf16[2,192,384]{2,1,0:T(8,128)(2,1)S(1)} %get-tuple-element.355), channel_id=1, source_target_pairs={{0,8},{4,12},{8,0},{12,4},{16,24},{20,28},{24,16},{28,20},{1,9},{5... | collective-permute-start | bytes 884744 | tf_op jit(solution)/shard_map/ppermute | solution.py:22
  322.4 56.2 %collective-permute-start.57 = (bf16[2,2,2,192,384]{4,3,2,1,0:T(8,128)(2,1)S(1)}, bf16[2,2,2,192,384]{4,3,2,1,0:T(8,128)(2,1)S(1)}, u32[]{:S(2)}, u32[]{:S(2)}) collective-permute-start(bf16[2,2,2,192,384]{4,3,2,1,0:T(8,128)(2,1)S(1)} %get-tuple-element.318), channel_id=1, source_target_pairs={{0,2},{1,3},{2,0},{3,1},{4,6},{5,7},{6,4},{7,5},{8,10},{9,11},{10,... | collective-permute-start | bytes 3538952 | tf_op jit(solution)/shard_map/ppermute | solution.py:22
  328.3 23.1 %collective-permute-start.49 = (bf16[2,2,192,384]{3,2,1,0:T(8,128)(2,1)S(1)}, bf16[2,2,192,384]{3,2,1,0:T(8,128)(2,1)S(1)}, u32[]{:S(2)}, u32[]{:S(2)}) collective-permute-start(bf16[2,2,192,384]{3,2,1,0:T(8,128)(2,1)S(1)} %get-tuple-element.326), channel_id=1, source_target_pairs={{0,4},{4,0},{8,12},{12,8},{16,20},{20,16},{24,28},{28,24},{1,5},{5... | collective-permute-start | bytes 1769480 | tf_op jit(solution)/shard_map/ppermute | solution.py:22
  329.3 11.3 %collective-permute-start.50 = (bf16[1,192,384]{2,1,0:T(8,128)(2,1)S(1)}, bf16[1,192,384]{2,1,0:T(8,128)(2,1)S(1)}, u32[]{:S(2)}, u32[]{:S(2)}) collective-permute-start(bf16[1,192,384]{2,1,0:T(8,128)(2,1)S(1)} %fusion.59), channel_id=1, source_target_pairs={{0,16},{4,20},{8,24},{12,28},{16,0},{20,4},{24,8},{28,12},{1,17},{... | collective-permute-start | bytes 442376 | tf_op jit(solution)/shard_map/ppermute | solution.py:22
  336.8 9.5 %collective-permute-start.53 = (bf16[192,384]{1,0:T(8,128)(2,1)S(1)}, bf16[192,384]{1,0:T(8,128)(2,1)S(1)}, u32[]{:S(2)}, u32[]{:S(2)}) collective-permute-start(bf16[192,384]{1,0:T(8,128)(2,1)S(1)} %fusion.57), channel_id=1, source_target_pairs={{0,16},{4,20},{8,24},{12,28},{16,0},{20,4},{24,8},{28,12},{1,17},{... | collective-permute-start | bytes 442376 | tf_op jit(solution)/shard_map/ppermute | solution.py:22
  340.7 10.7 %collective-permute-start.51 = (bf16[2,192,384]{2,1,0:T(8,128)(2,1)S(1)}, bf16[2,192,384]{2,1,0:T(8,128)(2,1)S(1)}, u32[]{:S(2)}, u32[]{:S(2)}) collective-permute-start(bf16[2,192,384]{2,1,0:T(8,128)(2,1)S(1)} %pad_maximum_fusion.8), channel_id=1, source_target_pairs={{0,8},{4,12},{8,0},{12,4},{16,24},{20,28},{24,16},{28,20},{1,9},{5... | collective-permute-start | bytes 884744 | tf_op jit(solution)/shard_map/ppermute | solution.py:22
  346.6 20.0 %collective-permute-start.59 = (bf16[2,2,192,384]{3,2,1,0:T(8,128)(2,1)S(1)}, bf16[2,2,192,384]{3,2,1,0:T(8,128)(2,1)S(1)}, u32[]{:S(2)}, u32[]{:S(2)}) collective-permute-start(bf16[2,2,192,384]{3,2,1,0:T(8,128)(2,1)S(1)} %get-tuple-element.316), channel_id=1, source_target_pairs={{0,4},{4,0},{8,12},{12,8},{16,20},{20,16},{24,28},{28,24},{1,5},{5... | collective-permute-start | bytes 1769480 | tf_op jit(solution)/shard_map/ppermute | solution.py:22
  351.6 14.8 %collective-permute-start.54 = (bf16[2,192,384]{2,1,0:T(8,128)(2,1)S(1)}, bf16[2,192,384]{2,1,0:T(8,128)(2,1)S(1)}, u32[]{:S(2)}, u32[]{:S(2)}) collective-permute-start(bf16[2,192,384]{2,1,0:T(8,128)(2,1)S(1)} %get-tuple-element.353), channel_id=1, source_target_pairs={{0,8},{4,12},{8,0},{12,4},{16,24},{20,28},{24,16},{28,20},{1,9},{5... | collective-permute-start | bytes 884744 | tf_op jit(solution)/shard_map/ppermute | solution.py:22
  352.0 10.5 %collective-permute-start.55 = (bf16[1,192,384]{2,1,0:T(8,128)(2,1)S(1)}, bf16[1,192,384]{2,1,0:T(8,128)(2,1)S(1)}, u32[]{:S(2)}, u32[]{:S(2)}) collective-permute-start(bf16[1,192,384]{2,1,0:T(8,128)(2,1)S(1)} %fusion.61), channel_id=1, source_target_pairs={{0,16},{4,20},{8,24},{12,28},{16,0},{20,4},{24,8},{28,12},{1,17},{... | collective-permute-start | bytes 442376 | tf_op jit(solution)/shard_map/ppermute | solution.py:22
  354.6 34.2 %collective-permute-start.48 = (bf16[2,2,192,384]{3,2,1,0:T(8,128)(2,1)S(1)}, bf16[2,2,192,384]{3,2,1,0:T(8,128)(2,1)S(1)}, u32[]{:S(2)}, u32[]{:S(2)}) collective-permute-start(bf16[2,2,192,384]{3,2,1,0:T(8,128)(2,1)S(1)} %get-tuple-element.327), channel_id=1, source_target_pairs={{0,2},{1,3},{2,0},{3,1},{4,6},{5,7},{6,4},{7,5},{8,10},{9,11},{10,... | collective-permute-start | bytes 1769480 | tf_op jit(solution)/shard_map/ppermute | solution.py:22
  362.6 15.9 %collective-permute-start.58 = (bf16[2,192,384]{2,1,0:T(8,128)(2,1)S(1)}, bf16[2,192,384]{2,1,0:T(8,128)(2,1)S(1)}, u32[]{:S(2)}, u32[]{:S(2)}) collective-permute-start(bf16[2,192,384]{2,1,0:T(8,128)(2,1)S(1)} %pad_maximum_fusion.9), channel_id=1, source_target_pairs={{0,8},{4,12},{8,0},{12,4},{16,24},{20,28},{24,16},{28,20},{1,9},{5... | collective-permute-start | bytes 884744 | tf_op jit(solution)/shard_map/ppermute | solution.py:22
  366.5 13.5 %collective-permute-start.56 = (bf16[192,384]{1,0:T(8,128)(2,1)S(1)}, bf16[192,384]{1,0:T(8,128)(2,1)S(1)}, u32[]{:S(2)}, u32[]{:S(2)}) collective-permute-start(bf16[192,384]{1,0:T(8,128)(2,1)S(1)} %fusion.64), channel_id=1, source_target_pairs={{0,16},{4,20},{8,24},{12,28},{16,0},{20,4},{24,8},{28,12},{1,17},{... | collective-permute-start | bytes 442376 | tf_op jit(solution)/shard_map/ppermute | solution.py:22
  366.7 18.4 %collective-permute-start.61 = (bf16[2,192,384]{2,1,0:T(8,128)(2,1)S(1)}, bf16[2,192,384]{2,1,0:T(8,128)(2,1)S(1)}, u32[]{:S(2)}, u32[]{:S(2)}) collective-permute-start(bf16[2,192,384]{2,1,0:T(8,128)(2,1)S(1)} %get-tuple-element.352), channel_id=1, source_target_pairs={{0,8},{4,12},{8,0},{12,4},{16,24},{20,28},{24,16},{28,20},{1,9},{5... | collective-permute-start | bytes 884744 | tf_op jit(solution)/shard_map/ppermute | solution.py:22
  378.9 31.7 %collective-permute-start.67 = (bf16[2,2,192,384]{3,2,1,0:T(8,128)(2,1)S(1)}, bf16[2,2,192,384]{3,2,1,0:T(8,128)(2,1)S(1)}, u32[]{:S(2)}, u32[]{:S(2)}) collective-permute-start(bf16[2,2,192,384]{3,2,1,0:T(8,128)(2,1)S(1)} %get-tuple-element.314), channel_id=1, source_target_pairs={{0,4},{4,0},{8,12},{12,8},{16,20},{20,16},{24,28},{28,24},{1,5},{5... | collective-permute-start | bytes 1769480 | tf_op jit(solution)/shard_map/ppermute | solution.py:22
  385.1 10.8 %collective-permute-start.64 = (bf16[192,384]{1,0:T(8,128)(2,1)S(1)}, bf16[192,384]{1,0:T(8,128)(2,1)S(1)}, u32[]{:S(2)}, u32[]{:S(2)}) collective-permute-start(bf16[192,384]{1,0:T(8,128)(2,1)S(1)} %fusion.65), channel_id=1, source_target_pairs={{0,16},{4,20},{8,24},{12,28},{16,0},{20,4},{24,8},{28,12},{1,17},{... | collective-permute-start | bytes 442376 | tf_op jit(solution)/shard_map/ppermute | solution.py:22
  388.7 17.7 %collective-permute-start.63 = (bf16[2,192,384]{2,1,0:T(8,128)(2,1)S(1)}, bf16[2,192,384]{2,1,0:T(8,128)(2,1)S(1)}, u32[]{:S(2)}, u32[]{:S(2)}) collective-permute-start(bf16[2,192,384]{2,1,0:T(8,128)(2,1)S(1)} %pad_maximum_fusion.10), channel_id=1, source_target_pairs={{0,8},{4,12},{8,0},{12,4},{16,24},{20,28},{24,16},{28,20},{1,9},{5... | collective-permute-start | bytes 884744 | tf_op jit(solution)/shard_map/ppermute | solution.py:22
  389.0 21.5 %collective-permute-start.62 = (bf16[2,192,384]{2,1,0:T(8,128)(2,1)S(1)}, bf16[2,192,384]{2,1,0:T(8,128)(2,1)S(1)}, u32[]{:S(2)}, u32[]{:S(2)}) collective-permute-start(bf16[2,192,384]{2,1,0:T(8,128)(2,1)S(1)} %get-tuple-element.349), channel_id=1, source_target_pairs={{0,8},{4,12},{8,0},{12,4},{16,24},{20,28},{24,16},{28,20},{1,9},{5... | collective-permute-start | bytes 884744 | tf_op jit(solution)/shard_map/ppermute | solution.py:22
  396.0 15.2 %collective-permute-start.66 = (bf16[1,192,384]{2,1,0:T(8,128)(2,1)S(1)}, bf16[1,192,384]{2,1,0:T(8,128)(2,1)S(1)}, u32[]{:S(2)}, u32[]{:S(2)}) collective-permute-start(bf16[1,192,384]{2,1,0:T(8,128)(2,1)S(1)} %fusion.68), channel_id=1, source_target_pairs={{0,16},{4,20},{8,24},{12,28},{16,0},{20,4},{24,8},{28,12},{1,17},{... | collective-permute-start | bytes 442376 | tf_op jit(solution)/shard_map/ppermute | solution.py:22
  410.8 10.2 %collective-permute-start.70 = (bf16[2,192,384]{2,1,0:T(8,128)(2,1)S(1)}, bf16[2,192,384]{2,1,0:T(8,128)(2,1)S(1)}, u32[]{:S(2)}, u32[]{:S(2)}) collective-permute-start(bf16[2,192,384]{2,1,0:T(8,128)(2,1)S(1)} %get-tuple-element.348), channel_id=1, source_target_pairs={{0,8},{4,12},{8,0},{12,4},{16,24},{20,28},{24,16},{28,20},{1,9},{5... | collective-permute-start | bytes 884744 | tf_op jit(solution)/shard_map/ppermute | solution.py:22
  411.3 18.8 %collective-permute-start.69 = (bf16[2,192,384]{2,1,0:T(8,128)(2,1)S(1)}, bf16[2,192,384]{2,1,0:T(8,128)(2,1)S(1)}, u32[]{:S(2)}, u32[]{:S(2)}) collective-permute-start(bf16[2,192,384]{2,1,0:T(8,128)(2,1)S(1)} %pad_maximum_fusion.11), channel_id=1, source_target_pairs={{0,8},{4,12},{8,0},{12,4},{16,24},{20,28},{24,16},{28,20},{1,9},{5... | collective-permute-start | bytes 884744 | tf_op jit(solution)/shard_map/ppermute | solution.py:22
  419.5 10.6 %collective-permute-start.68 = (bf16[1,192,384]{2,1,0:T(8,128)(2,1)S(1)}, bf16[1,192,384]{2,1,0:T(8,128)(2,1)S(1)}, u32[]{:S(2)}, u32[]{:S(2)}) collective-permute-start(bf16[1,192,384]{2,1,0:T(8,128)(2,1)S(1)} %fusion.69), channel_id=1, source_target_pairs={{0,16},{4,20},{8,24},{12,28},{16,0},{20,4},{24,8},{28,12},{1,17},{... | collective-permute-start | bytes 442376 | tf_op jit(solution)/shard_map/ppermute | solution.py:22
  432.3 16.3 %collective-permute-start.80 = (bf16[4,192,384]{2,1,0:T(8,128)(2,1)S(1)}, bf16[4,192,384]{2,1,0:T(8,128)(2,1)S(1)}, u32[]{:S(2)}, u32[]{:S(2)}) collective-permute-start(bf16[4,192,384]{2,1,0:T(8,128)(2,1)S(1)} %pad_maximum_fusion.2.near), channel_id=1, source_target_pairs={{0,4},{4,0},{8,12},{12,8},{16,20},{20,16},{24,28},{28,24},{1,5},{5... | collective-permute-start | bytes 1769480 | tf_op jit(solution)/shard_map/ppermute | solution.py:22
  439.0 22.3 %collective-permute-start.78 = (bf16[4,192,384]{2,1,0:T(8,128)(2,1)S(1)}, bf16[4,192,384]{2,1,0:T(8,128)(2,1)}, u32[]{:S(2)}, u32[]{:S(2)}) collective-permute-start(bf16[4,192,384]{2,1,0:T(8,128)(2,1)S(1)} %pad_maximum_fusion.3.near), channel_id=1, source_target_pairs={{0,4},{4,0},{8,12},{12,8},{16,20},{20,16},{24,28},{28,24},{1,5},{5... | collective-permute-start | bytes 1769480 | tf_op jit(solution)/shard_map/ppermute | solution.py:22
  439.7 32.2 %collective-permute-start.76 = (bf16[4,192,384]{2,1,0:T(8,128)(2,1)S(1)}, bf16[4,192,384]{2,1,0:T(8,128)(2,1)}, u32[]{:S(2)}, u32[]{:S(2)}) collective-permute-start(bf16[4,192,384]{2,1,0:T(8,128)(2,1)S(1)} %pad_maximum_fusion.4.near), channel_id=1, source_target_pairs={{0,4},{4,0},{8,12},{12,8},{16,20},{20,16},{24,28},{28,24},{1,5},{5... | collective-permute-start | bytes 1769480 | tf_op jit(solution)/shard_map/ppermute | solution.py:22
  441.1 37.2 %collective-permute-start.79 = (bf16[4,192,384]{2,1,0:T(8,128)(2,1)S(1)}, bf16[4,192,384]{2,1,0:T(8,128)(2,1)}, u32[]{:S(2)}, u32[]{:S(2)}) collective-permute-start(bf16[4,192,384]{2,1,0:T(8,128)(2,1)S(1)} %pad_maximum_fusion.5.near), channel_id=1, source_target_pairs={{0,4},{4,0},{8,12},{12,8},{16,20},{20,16},{24,28},{28,24},{1,5},{5... | collective-permute-start | bytes 1769480 | tf_op jit(solution)/shard_map/ppermute | solution.py:22
  445.5 39.1 %collective-permute-start.72 = (bf16[4,192,384]{2,1,0:T(8,128)(2,1)S(1)}, bf16[4,192,384]{2,1,0:T(8,128)(2,1)}, u32[]{:S(2)}, u32[]{:S(2)}) collective-permute-start(bf16[4,192,384]{2,1,0:T(8,128)(2,1)S(1)} %pad_maximum_fusion.6.near), channel_id=1, source_target_pairs={{0,4},{4,0},{8,12},{12,8},{16,20},{20,16},{24,28},{28,24},{1,5},{5... | collective-permute-start | bytes 1769480 | tf_op jit(solution)/shard_map/ppermute | solution.py:22
  449.4 41.4 %collective-permute-start.77 = (bf16[4,192,384]{2,1,0:T(8,128)(2,1)S(1)}, bf16[4,192,384]{2,1,0:T(8,128)(2,1)S(1)}, u32[]{:S(2)}, u32[]{:S(2)}) collective-permute-start(bf16[4,192,384]{2,1,0:T(8,128)(2,1)S(1)} %pad_maximum_fusion.7.near), channel_id=1, source_target_pairs={{0,4},{4,0},{8,12},{12,8},{16,20},{20,16},{24,28},{28,24},{1,5},{5... | collective-permute-start | bytes 1769480 | tf_op jit(solution)/shard_map/ppermute | solution.py:22
  (76 other events, 751.6 us)

commit v3 on v2

v3 whole, which is shorter than its diff:
```python
import functools
import math

import jax
import jax.numpy as jnp
from jax import lax
from jax.experimental import pallas as pl
from jax.experimental.pallas import tpu as pltpu
from jax.sharding import PartitionSpec as P

HEADS = 12
norm_eps = 1e-12
masked_score = -1000000000.0
low = jnp.bfloat16
f32 = jnp.float32
VMEM_BYTES = 56 * 1024 * 1024
HALVINGS = 3


def swap(value, axis, bit):
    count = lax.axis_size(axis)
    return lax.ppermute(value, axis, [(i, i ^ bit) for i in range(count)])


def dot(a, b):
    return jnp.dot(a, b, preferred_element_type=f32)


def dot_nt(a, b):
    return lax.dot_general(a, b, (((1,), (1,)), ((), ())), preferred_element_type=f32)


def dot_tn(a, b):
    return lax.dot_general(a, b, (((0,), (0,)), ((), ())), preferred_element_type=f32)


def normalize(residual):
    center = residual - jnp.mean(residual, axis=-1, keepdims=True)
    inverse = lax.rsqrt(jnp.mean(center * center, axis=-1, keepdims=True) + norm_eps)
    return center * inverse, inverse


def normalize_back(grad_unit, unit, inverse):
    centered = grad_unit - jnp.mean(grad_unit, axis=-1, keepdims=True)
    return inverse * (centered - unit * jnp.mean(grad_unit * unit, axis=-1, keepdims=True))


def weight_copies(ids, layer, pieces, target, columns, sems, base):
    own, core, near_x, far_x, diagonal = pieces
    rows = own.shape[1]
    half = rows // 2
    n, y = ids[0], ids[4]
    copies = []

    def add(source, start, count):
        where = target.at[pl.ds(pl.multiple_of(start, half), count), :]
        copies.append(pltpu.make_async_copy(source, where, sems.at[base + len(copies)]))

    at = pl.ds(columns, target.shape[1])
    add(own.at[layer], n * rows, rows)
    add(core.at[layer], ids[1] * rows, rows)
    add(near_x.at[:, at], ids[2] * rows + y * half, half)
    add(far_x.at[:, at], ids[2] * rows + (1 - y) * half, half)
    add(diagonal.at[pl.ds(0, half), at], ids[3] * rows + y * half, half)
    add(diagonal.at[pl.ds(half, half), at], ids[3] * rows + (1 - y) * half, half)
    return copies


def begin(copies):
    for copy in copies:
        copy.start()


def finish(copies):
    for copy in copies:
        copy.wait()


def attn_copies(layer, ids, refs, w_qkv, w_o, sems):
    qkv_own, qkv_core, o_own, o_core = refs[:4]
    halves = refs[4:]
    qkv = weight_copies(ids, layer, (qkv_own, qkv_core) + halves, w_qkv, 0, sems, 0)
    o = weight_copies(ids, layer, (o_own, o_core) + halves, w_o, w_qkv.shape[1], sems, 6)
    return qkv, o


def ffn_copies(layer, ids, refs, w_in, w_out, sems):
    in_copies = weight_copies(ids, layer, refs[:5], w_in, 0, sems, 0)
    out_copies = weight_copies(ids, layer, refs[5:], w_out, 0, sems, 6)
    return in_copies, out_copies


def attn_fwd_kernel(layer, ids, length, x, cell_row, small, *rest):
    weights, rest = rest[:7], rest[7:]
    qkv_rows, probs, context, unit_out, inverse_out, w_qkv, w_o, mask, sems = rest
    tokens, width = x.shape
    qkv_copies, o_copies = attn_copies(layer, ids, weights, w_qkv, w_o, sems)
    begin(qkv_copies)
    begin(o_copies)
    position = lax.broadcasted_iota(jnp.int32, (1, tokens), 1)
    key_cell = cell_row[...]
    square = (tokens, tokens)
    diagonal = lax.broadcasted_iota(jnp.int32, square, 0) == lax.broadcasted_iota(jnp.int32, square, 1)
    query_cell = jnp.sum(jnp.where(diagonal, key_cell, 0), axis=1, keepdims=True)
    allowed = (query_cell == key_cell) | (key_cell == 0) | (query_cell == 0)
    allowed = allowed & (position < length[0])
    mask[...] = jnp.where(allowed, 0.0, masked_score)
    scale = 1.0 / math.sqrt(width // HEADS)
    finish(qkv_copies)
    tile = width // 2

    for t in range(6):
        columns = slice(t * tile, (t + 1) * tile)
        rows = dot(x[...], w_qkv[:, columns])
        if t // 2 != 1:
            part = slice((t % 2) * tile, (t % 2 + 1) * tile)
            rows = rows + small[layer, t // 4 : t // 4 + 1, part]
        if t < 2:
            rows = rows * scale
        qkv_rows[:, columns] = rows.astype(low)

    pair_width = 2 * width // HEADS
    first = lax.broadcasted_iota(jnp.int32, (1, pair_width), 1) < pair_width // 2

    @pl.loop(0, HEADS // 2)
    def _(pair):
        start = pl.multiple_of(pair * pair_width, pair_width)
        query = qkv_rows[:, pl.ds(start, pair_width)]
        key = qkv_rows[:, pl.ds(width + start, pair_width)]
        value = qkv_rows[:, pl.ds(2 * width + start, pair_width)]
        sides = []
        for side in range(2):
            mine = first if side == 0 else jnp.logical_not(first)
            scores = dot_nt(jnp.where(mine, query, jnp.zeros_like(query)), key) + mask[...]
            shifted = jnp.exp(scores - jnp.max(scores, axis=-1, keepdims=True))
            total = jnp.sum(shifted, axis=-1, keepdims=True)
            prob = (shifted / total).astype(low)
            probs[2 * pair + side] = prob
            sides.append(dot(prob, value))
        context[:, pl.ds(start, pair_width)] = jnp.where(first, sides[0], sides[1]).astype(low)

    finish(o_copies)
    residual = x[...].astype(f32) + (dot(context[...], w_o[...]) + small[layer, 2:3, :])
    unit, inverse = normalize(residual)
    unit_out[...] = unit
    inverse_out[...] = inverse


def ffn_fwd_kernel(layer, ids, unit_one, in_bias, small, *rest):
    weights, rest = rest[:10], rest[10:]
    hidden, slope, unit_out, inverse_out, result, w_in, w_out, normed_low, sems = rest
    in_copies, out_copies = ffn_copies(layer, ids, weights, w_in, w_out, sems)
    begin(in_copies)
    begin(out_copies)
    normed = unit_one[...] * small[layer, 3:4, :] + small[layer, 4:5, :]
    normed_low[...] = normed.astype(low)
    finish(in_copies)
    tile = w_in.shape[1] // 8

    @pl.loop(0, 8)
    def _(t):
        columns = pl.ds(pl.multiple_of(t * tile, tile), tile)
        pre = dot(normed_low[...], w_in[:, columns]) + in_bias[layer, :, columns]
        cdf = 0.5 * (1.0 + lax.erf(pre * (1.0 / math.sqrt(2.0))))
        density = jnp.exp(-0.5 * pre * pre) * (1.0 / math.sqrt(2.0 * math.pi))
        hidden[:, columns] = (pre * cdf).astype(low)
        slope[:, columns] = cdf + pre * density

    finish(out_copies)
    residual = unit_one[...] * small[layer, 3:4, :] + small[layer, 4:5, :] + (dot(hidden[...], w_out[...]) + small[layer, 5:6, :])
    unit, inverse = normalize(residual)
    unit_out[...] = unit
    inverse_out[...] = inverse
    result[...] = (unit * small[layer, 6:7, :] + small[layer, 7:8, :]).astype(low)


WIDE_BIT = {"y": 2, "z": 1, "w": 0}


def place_of(ids, owner, piece, way):
    away, off = ids[0] ^ owner, piece ^ ids[5]
    return (away & 1,) + tuple(away >> 1 if name == "x" else (off >> WIDE_BIT[name]) & 1 for name in way)


def store_rows(stage, ids, product, piece, way):
    share = product.shape[0] // 4
    for owner in range(4):
        block = product[owner * share : (owner + 1) * share].astype(low)
        stage[place_of(ids, owner, piece, way) + (pl.ds(0, share),)] = block


def send_out(stage, kept, sent, sems):
    copies = [
        pltpu.make_async_copy(stage.at[1], sent, sems.at[0]),
        pltpu.make_async_copy(stage.at[0], kept, sems.at[1]),
    ]
    begin(copies)
    return copies


def out_bwd_kernel(layer, way, ids, grad, unit_two, inverse_two, hidden, small, *rest):
    d_ffn, d_resid_two, small_grads, kept, sent, stage, out_sems = rest
    g = grad[...].astype(f32)
    unit = unit_two[...]
    small_grads[0:1, :] = jnp.sum(g * unit, axis=0, keepdims=True)
    small_grads[1:2, :] = jnp.sum(g, axis=0, keepdims=True)
    d_two = normalize_back(g * small[layer, 6:7, :], unit, inverse_two[...])
    d_resid_two[...] = d_two
    d_low = d_two.astype(low)
    d_ffn[...] = d_low
    small_grads[2:3, :] = jnp.sum(d_low.astype(f32), axis=0, keepdims=True)
    small_grads[3:8, :] = jnp.zeros((5, unit.shape[1]), f32)
    tile = hidden.shape[1] // 8
    share = d_ffn.shape[1] // 4

    @pl.loop(0, 8)
    def _(t):
        columns = pl.ds(pl.multiple_of(t * tile, tile), tile)
        out_grad = dot_tn(hidden[:, columns], d_ffn[...])
        for row_group in range(2):
            for column_group in range(2):
                piece = ((t % 2) * 2 + row_group) * 2 + column_group
                block = out_grad[
                    row_group * share : (row_group + 1) * share,
                    column_group * tile : (column_group + 1) * tile,
                ]
                stage[place_of(ids, t // 2, piece, way)] = block.astype(low)

    finish(send_out(stage, kept, sent, out_sems))


def in_bwd_kernel(layer, way, ids, d_ffn, d_resid_two, unit_one, inverse_one, slope, small, *rest):
    weights, rest = rest[:10], rest[10:]
    d_resid, small_grads, in_bias_grad, kept, sent = rest[:5]
    w_in, w_out, d_pre, normed_t, stage, sems, out_sems = rest[5:]
    in_copies, out_copies = ffn_copies(layer, ids, weights, w_in, w_out, sems)
    begin(out_copies)
    begin(in_copies)
    normed = unit_one[...] * small[layer, 3:4, :] + small[layer, 4:5, :]
    normed_t[...] = normed.astype(low).T
    finish(out_copies)
    tile = w_in.shape[1] // 8

    @pl.loop(0, 8)
    def _(t):
        columns = pl.ds(pl.multiple_of(t * tile, tile), tile)
        d_hidden = dot_nt(d_ffn[...], w_out[columns, :])
        d_tile = (d_hidden * slope[:, columns]).astype(low)
        d_pre[:, columns] = d_tile
        in_bias_grad[:, columns] = jnp.sum(d_tile.astype(f32), axis=0, keepdims=True)
        store_rows(stage, ids, dot(normed_t[...], d_tile), t, way)

    going = send_out(stage, kept, sent, out_sems)
    finish(in_copies)
    d_normed = d_resid_two[...] + dot_nt(d_pre[...], w_in[...])
    unit = unit_one[...]
    small_grads[0:1, :] = jnp.sum(d_normed * unit, axis=0, keepdims=True)
    small_grads[1:2, :] = jnp.sum(d_normed, axis=0, keepdims=True)
    small_grads[2:8, :] = jnp.zeros((6, unit.shape[1]), f32)
    d_resid[...] = normalize_back(d_normed * small[layer, 3:4, :], unit, inverse_one[...])
    finish(going)


def attn_bwd_kernel(layer, way, ids, d_resid, x, qkv_rows, probs, context, *rest):
    weights, others, rest = rest[:7], rest[7:-13], rest[-13:]
    d_input, small_grads, kept, sent = rest[:4]
    w_qkv, w_o, d_attn, d_context, d_qkv, x_t, stage, sems, out_sems = rest[4:]
    tokens, width = x.shape
    qkv_copies, o_copies = attn_copies(layer, ids, weights, w_qkv, w_o, sems)
    begin(o_copies)
    begin(qkv_copies)
    d_low = d_resid[...].astype(low)
    d_attn[...] = d_low
    small_grads[2:3, :] = jnp.sum(d_low.astype(f32), axis=0, keepdims=True)
    x_t[...] = x[...].T
    tile = width // 2
    for half in range(2):
        product = dot_tn(context[...], d_attn[:, half * tile : (half + 1) * tile])
        store_rows(stage, ids, product, 6 + half, way)
    finish(o_copies)
    d_context[...] = dot_nt(d_attn[...], w_o[...]).astype(low)
    pair_width = 2 * width // HEADS
    first = lax.broadcasted_iota(jnp.int32, (1, pair_width), 1) < pair_width // 2
    scale = 1.0 / math.sqrt(width // HEADS)

    @pl.loop(0, HEADS // 2)
    def _(pair):
        start = pl.multiple_of(pair * pair_width, pair_width)
        at_query = pl.ds(start, pair_width)
        at_key = pl.ds(width + start, pair_width)
        at_value = pl.ds(2 * width + start, pair_width)
        query, key, value = qkv_rows[:, at_query], qkv_rows[:, at_key], qkv_rows[:, at_value]
        d_ctx = d_context[:, at_query]
        sides = []
        for side in range(2):
            mine = first if side == 0 else jnp.logical_not(first)
            prob_low = probs[2 * pair + side]
            prob = prob_low.astype(f32)
            d_prob = dot_nt(jnp.where(mine, d_ctx, jnp.zeros_like(d_ctx)), value)
            inner = jnp.sum(prob * d_prob, axis=-1, keepdims=True)
            d_scores = (prob * (d_prob - inner)).astype(low)
            sides.append((dot(d_scores, key), dot_tn(d_scores, query), dot_tn(prob_low, d_ctx)))
        d_qkv[:, at_query] = (jnp.where(first, sides[0][0], sides[1][0]) * scale).astype(low)
        d_qkv[:, at_key] = jnp.where(first, sides[0][1], sides[1][1]).astype(low)
        d_qkv[:, at_value] = jnp.where(first, sides[0][2], sides[1][2]).astype(low)

    @pl.loop(0, 6)
    def _(t):
        columns = pl.ds(pl.multiple_of(t * tile, tile), tile)
        store_rows(stage, ids, dot(x_t[...], d_qkv[:, columns]), t, way)

    small_grads[0:1, :] = jnp.sum(d_qkv[:, :width].astype(f32), axis=0, keepdims=True)
    small_grads[1:2, :] = jnp.sum(d_qkv[:, 2 * width :].astype(f32), axis=0, keepdims=True)
    small_grads[3:8, :] = jnp.zeros((5, width), f32)
    if others:
        share = width // 4
        sources = small_sources(layer, small_grads, others)
        for owner in range(4):
            for piece in range(8):
                lines = []
                for source, row, start, step in sources[3 * piece : 3 * piece + 3]:
                    line = source[row : row + 1, start + owner * step : start + owner * step + share]
                    lines.append(jnp.concatenate([line, jnp.zeros_like(line)], axis=1))
                lines.append(jnp.zeros((SMALL_ROWS - 3, tile), f32))
                block = jnp.concatenate(lines, axis=0).astype(low)
                stage[place_of(ids, owner, piece, way) + (pl.ds(share, SMALL_ROWS),)] = block
    going = send_out(stage, kept, sent, out_sems)
    finish(qkv_copies)
    d_input[...] = (d_resid[...] + dot_nt(d_qkv[...], w_qkv[...])).astype(low)
    finish(going)


SMALL_ROWS = 16
SMALL_LINES = (("attn", 0), ("attn", 1), ("attn", 2), ("in", 0), ("in", 1), ("out", 2), ("out", 0), ("out", 1))


def small_sources(layer, own, others):
    found = []
    out_0, in_0, bias_0, out_1, in_1, bias_1, attn_1 = others
    refs = ({"attn": own, "in": in_0, "out": out_0}, {"attn": attn_1, "in": in_1, "out": out_1})
    width = own.shape[1]
    for of_layer, bias in zip(refs, (bias_0, bias_1)):
        found += [(of_layer[name], row, 0, width // 4) for name, row in SMALL_LINES]
        found += [(bias, 0, i * (width // 4), width) for i in range(4)]
    return found


def unpack_kernel(layer, slab, back, earlier, ids, near, far, *rest):
    outs = rest[earlier:-4]
    buffer, wide_buffer, in_sems, out_sems = rest[-4:]
    share, tile = wide_buffer.shape[1:]

    def fetch(piece, ref, index):
        return pltpu.make_async_copy(ref.at[index], buffer.at[piece], in_sems.at[piece])

    for piece in range(8):
        off = piece ^ ids[5]
        bits = [(off >> WIDE_BIT[name]) & 1 for name in back]
        index = bits[1] * 2 + bits[0]

        @pl.when(bits[2] == 0)
        def _():
            fetch(piece, near, index).start()

        @pl.when(bits[2] == 1)
        def _():
            fetch(piece, far, index).start()

    copies = []
    for piece in range(8):
        fetch(piece, near, 0).wait()
        wide_buffer[piece] = buffer[piece, :share].astype(f32)
        columns = pl.ds(piece * tile, tile)
        if slab == "in":
            target = outs[0].at[layer, :, columns]
        elif slab == "out":
            rows = pl.ds((piece // 2) * share, share)
            target = outs[0].at[layer, rows, pl.ds((piece % 2) * tile, tile)]
        elif piece < 6:
            target = outs[0].at[layer, :, columns]
        else:
            target = outs[1].at[layer, :, pl.ds((piece - 6) * tile, tile)]
        copies.append(pltpu.make_async_copy(wide_buffer.at[piece], target, out_sems.at[piece]))
        copies[-1].start()
    if slab == "attn" and layer == 0:
        for line in range(24):
            of_layer, which = line // 12, line % 12
            row = share + line % 3
            values = buffer[line // 3, row : row + 1, :share].astype(f32)
            if which < 8:
                outs[2 + which][of_layer : of_layer + 1, :] = values
            else:
                at = (which - 8) * share
                outs[10][of_layer : of_layer + 1, at : at + share] = values
    else:
        outs[-1][...] = jnp.zeros(outs[-1].shape, f32)
    finish(copies)


SMEM = pl.BlockSpec(memory_space=pltpu.SMEM)
VMEM = pl.BlockSpec(memory_space=pltpu.VMEM)
ANY = pl.BlockSpec(memory_space=pl.ANY)


def call(kernel, name, in_specs, out_specs, out_shape, scratch, args, aliases=()):
    return pl.pallas_call(
        kernel,
        name=name,
        in_specs=in_specs,
        out_specs=out_specs,
        out_shape=out_shape,
        scratch_shapes=scratch,
        input_output_aliases=dict(aliases),
        compiler_params=pltpu.CompilerParams(vmem_limit_bytes=VMEM_BYTES),
        cost_estimate=pl.CostEstimate(flops=1, bytes_accessed=1, transcendentals=0),
    )(*args)


def shape(dims, kind):
    return jax.ShapeDtypeStruct(dims, kind)


def reverse_bits(value, bits):
    result = jnp.zeros_like(value)
    for bit in range(bits):
        result = result | (((value >> bit) & 1) << (bits - 1 - bit))
    return result


def added(a, b):
    return (a.astype(f32) + b.astype(f32)).astype(low)


WAYS = ("xyzw", "yxzw", "xyzw", "xyzw", "xyzw", "xyzw")
BACKS = ("wzy",) * 6
PLAN = (
    "out1", "in1", 0, "attn1", "out0", 0, 2, 1, 3, 0, "in0", 0, 2, 0, 0, 1, 2, 0, 3, 2, 4, 1, 0, "attn0", 2,
    3, 1, 5, 4, 3, 2, 3, 2, 4, 1, 3, 5, 4, 1, 3, 4, 5, 1, 5, 4, 5, 4, 5, 3, 5, 4, 1, 2, 5,
)


class Order:
    def __init__(self):
        self.last = None

    def after(self, values):
        if self.last is None:
            return values
        values, self.last = lax.optimization_barrier((values, self.last))
        return values

    def wait(self, values):
        values = self.after(values)
        self.last = values
        return values


STEPS = {"x": ("narrow", 2), "y": ("wide", 1), "z": ("wide", 2), "w": ("wide", 4)}


class Slab:
    def __init__(self, way, back, wide_bits, kept, sent):
        self.way, self.back, self.wide_bits = way, back, wide_bits
        self.kept = kept
        self.flying = swap(sent, "narrow", 1)
        self.stage = 0

    def step(self, order):
        received = order.after(self.flying)
        if self.stage < len(self.way):
            send = added(self.kept[1], received[1])
            self.kept = added(self.kept[0], received[0])
            self.flying = swap(send, *STEPS[self.way[self.stage]])
            order.last = send
        elif self.stage == len(self.way):
            piece = added(self.kept, received)
            for b in range(HALVINGS, self.wide_bits):
                piece = added(piece, swap(piece, "wide", 1 << b))
            self.block = piece[None]
            order.last = self.block
            self.flying = swap(self.block, *STEPS[self.back[0]])
        elif self.stage < len(self.way) + len(self.back):
            self.block = jnp.concatenate([self.block, received], axis=0)
            order.last = self.block
            self.flying = swap(self.block, *STEPS[self.back[self.stage - len(self.way)]])
        else:
            self.far = received
        self.stage += 1

    def ended(self):
        return self.stage == len(self.way) + len(self.back) + 1


def body(
    tables_in,
    cotangent,
    cell_ids,
    lengths,
    qkv_weight,
    q_bias,
    v_bias,
    o_weight,
    o_bias,
    norm1_gain,
    norm1_bias,
    in_weight,
    in_bias,
    out_weight,
    out_bias,
    norm2_gain,
    norm2_bias,
):
    tokens, width = tables_in.shape
    layers, share, ffn = in_weight.shape
    ffn_share = out_weight.shape[1]
    wide_count = lax.axis_size("wide")
    wide_bits = wide_count.bit_length() - 1
    assert wide_count == 1 << wide_bits and wide_bits >= HALVINGS and lax.axis_size("narrow") == 4
    tile = ffn // 8
    me = lax.axis_index("narrow").astype(jnp.int32)
    wide_me = lax.axis_index("wide").astype(jnp.int32)
    y = wide_me & 1
    place = reverse_bits(wide_me & (2**HALVINGS - 1), HALVINGS)
    ids = jnp.stack([me, me ^ 1, me ^ 2, me ^ 3, y, place])

    order = Order()

    def half_of(weight, layer):
        rows = weight.shape[1] // 2
        return lax.dynamic_slice(weight, (layer, y * rows, 0), (1, rows, weight.shape[2]))[0]

    halves = []
    for layer in range(layers):
        joint = jnp.concatenate([half_of(qkv_weight, layer), half_of(o_weight, layer)], axis=1)
        halves += [joint, half_of(in_weight, layer), half_of(out_weight, layer)]
    near_x, far_x, diagonal = [None] * len(halves), [None] * len(halves), [None] * len(halves)
    core = [None] * 4
    own = (qkv_weight, o_weight, in_weight, out_weight)

    def send_x(*which):
        for i in which:
            near_x[i] = swap(order.after(halves[i]), "narrow", 2)

    def send_core(i):
        core[i] = swap(order.after(own[i]), "narrow", 1)

    def arrive(*events):
        for kind, i in events:
            if kind == "x":
                near_x[i] = order.wait(near_x[i])
                far_x[i] = swap(near_x[i], "wide", 1)
            elif kind == "y":
                far_x[i] = order.wait(far_x[i])
                both = jnp.concatenate([near_x[i], far_x[i]], axis=0)
                order.last = both
                diagonal[i] = swap(both, "narrow", 1)
            elif kind == "d":
                diagonal[i] = order.wait(diagonal[i])
            else:
                core[i] = order.wait(core[i])

    def group(i):
        return near_x[i], far_x[i], diagonal[i]

    def attn_weights(layer):
        return (qkv_weight, core[0], o_weight, core[1]) + group(3 * layer)

    def ffn_weights(layer):
        return (in_weight, core[2]) + group(3 * layer + 1) + (out_weight, core[3]) + group(3 * layer + 2)

    send_x(0)
    short = [q_bias, v_bias, o_bias, norm1_gain, norm1_bias, out_bias, norm2_gain, norm2_bias]
    packed = jnp.concatenate([jnp.stack(short, axis=1), in_bias.reshape(layers, 4, share)], axis=1)
    others = [
        lax.ppermute(packed, "narrow", [(i, i ^ away) for i in range(4)]) for away in (1, 2, 3)
    ]
    send_core(0)
    arrive(("c", 0))
    near_x[0], others = order.wait((near_x[0], others))
    far_x[0] = swap(near_x[0], "wide", 1)
    send_x(1, 2)
    send_core(1)

    def in_order(low_one, high_one, bit):
        swapped = (me & bit) != 0
        return jnp.stack([jnp.where(swapped, high_one, low_one), jnp.where(swapped, low_one, high_one)])

    packed = in_order(in_order(packed, others[0], 1), in_order(others[1], others[2], 1), 2)
    packed = packed.reshape(4, layers, 12, share).astype(f32)
    small = packed[:, :, :8].transpose(1, 2, 0, 3).reshape(layers, 8, width)
    full_in_bias = packed[:, :, 8:].transpose(1, 0, 2, 3).reshape(layers, 1, ffn)
    ids, small, full_in_bias = order.wait((ids, small, full_in_bias))
    arrive(("c", 1))
    send_core(2)
    arrive(("c", 2))
    send_core(3)

    w_qkv = pltpu.VMEM((width, 3 * width), low)
    w_o = pltpu.VMEM((width, width), low)
    w_in = pltpu.VMEM((width, ffn), low)
    w_out = pltpu.VMEM((ffn, width), low)
    copy_sems = pltpu.SemaphoreType.DMA((12,))
    pair_sems = pltpu.SemaphoreType.DMA((2,))
    rows_f32 = shape((tokens, width), f32)
    rows_low = shape((tokens, width), low)
    column_f32 = shape((tokens, 1), f32)
    eight_f32 = shape((8, width), f32)

    def pieces(rows):
        return [shape((2, 2, 2, 2, rows, tile), low)] * 2

    def stage(rows):
        return pltpu.VMEM((2, 2, 2, 2, 2, rows, tile), low)

    def attn_forward(layer, x):
        x = order.after(x)
        outs = call(
            functools.partial(attn_fwd_kernel, layer),
            "attn_fwd",
            [SMEM, SMEM] + [VMEM] * 3 + [ANY] * 7,
            [VMEM] * 5,
            [shape((tokens, 3 * width), low), shape((HEADS, tokens, tokens), low), rows_low, rows_f32, column_f32],
            [w_qkv, w_o, pltpu.VMEM((tokens, tokens), f32), copy_sems],
            (ids, lengths, x, cell_ids, small) + attn_weights(layer),
        )
        order.last = outs[-1]
        return outs

    def ffn_forward(layer, unit_one):
        unit_one = order.after(unit_one)
        outs = call(
            functools.partial(ffn_fwd_kernel, layer),
            "ffn_fwd",
            [SMEM] + [VMEM] * 3 + [ANY] * 10,
            [VMEM] * 5,
            [shape((tokens, ffn), low), shape((tokens, ffn), f32), rows_f32, column_f32, rows_low],
            [w_in, w_out, pltpu.VMEM((tokens, width), low), copy_sems],
            (ids, unit_one, full_in_bias, small) + ffn_weights(layer),
        )
        order.last = outs[-2]
        return outs

    def out_backward(layer, way, grad, unit_two, inverse_two, hidden):
        grad = order.after(grad)
        outs = call(
            functools.partial(out_bwd_kernel, layer, way),
            "out_bwd",
            [SMEM] + [VMEM] * 5,
            [VMEM] * 3 + [ANY] * 2,
            [rows_low, rows_f32, eight_f32] + pieces(share),
            [stage(share), pair_sems],
            (ids, grad, unit_two, inverse_two, hidden, small),
        )
        order.last = outs[2]
        return outs

    def in_backward(layer, way, d_ffn, d_resid_two, unit_one, inverse_one, slope):
        d_ffn = order.after(d_ffn)
        outs = call(
            functools.partial(in_bwd_kernel, layer, way),
            "in_bwd",
            [SMEM] + [VMEM] * 6 + [ANY] * 10,
            [VMEM] * 3 + [ANY] * 2,
            [rows_f32, eight_f32, shape((1, ffn), f32)] + pieces(share),
            [
                w_in,
                w_out,
                pltpu.VMEM((tokens, ffn), low),
                pltpu.VMEM((width, tokens), low),
                stage(share),
                copy_sems,
                pair_sems,
            ],
            (ids, d_ffn, d_resid_two, unit_one, inverse_one, slope, small) + ffn_weights(layer),
        )
        order.last = outs[1]
        return outs

    def attn_backward(layer, way, d_resid, x, qkv_rows, probs, context, small_others):
        d_resid = order.after(d_resid)
        rows = share + (SMALL_ROWS if small_others else 0)
        outs = call(
            functools.partial(attn_bwd_kernel, layer, way),
            "attn_bwd",
            [SMEM] + [VMEM] * 5 + [ANY] * 7 + [VMEM] * len(small_others),
            [VMEM] * 2 + [ANY] * 2,
            [rows_low, eight_f32] + pieces(rows),
            [
                w_qkv,
                w_o,
                pltpu.VMEM((tokens, width), low),
                pltpu.VMEM((tokens, width), low),
                pltpu.VMEM((tokens, 3 * width), low),
                pltpu.VMEM((width, tokens), low),
                stage(rows),
                copy_sems,
                pair_sems,
            ],
            (ids, d_resid, x, qkv_rows, probs, context) + attn_weights(layer) + tuple(small_others),
        )
        order.last = outs[1]
        return outs

    def unpack(layer, name, slab, earlier):
        dims = {
            "attn": [(layers, share, 3 * width), (layers, share, width)],
            "in": [(layers, share, ffn)],
            "out": [(layers, ffn_share, width)],
        }[name]
        last = name == "attn" and layer == 0
        extra = [(layers, share)] * 8 + [(layers, ffn_share)] if last else [(8, 128)]
        near, far = order.after((slab.block, slab.far))
        rows = near.shape[1]
        outs = call(
            functools.partial(unpack_kernel, layer, name, slab.back, len(earlier)),
            "unpack",
            [SMEM] + [ANY] * (2 + len(earlier)),
            [ANY] * len(dims) + [VMEM] * len(extra),
            [shape(d, f32) for d in dims + extra],
            [
                pltpu.VMEM((8, rows, tile), low),
                pltpu.VMEM((8, share, tile), f32),
                pltpu.SemaphoreType.DMA((8,)),
                pltpu.SemaphoreType.DMA((8,)),
            ],
            (ids, near, far, *earlier),
            {3 + i: i for i in range(len(earlier))},
        )
        order.last = outs[-1]
        return tuple(outs)

    arrive(("y", 0), ("x", 1))
    send_x(3)
    arrive(("c", 3), ("d", 0), ("x", 2))
    send_x(4)
    first_attn = attn_forward(0, tables_in)
    arrive(("x", 3))
    send_x(5)
    arrive(("y", 1), ("y", 2), ("d", 1), ("d", 2))
    first_ffn = ffn_forward(0, first_attn[3])
    arrive(("x", 4), ("y", 3), ("d", 3), ("x", 5))
    second_attn = attn_forward(1, first_ffn[4])
    arrive(("y", 4), ("y", 5), ("d", 4), ("d", 5))
    second_ffn = ffn_forward(1, second_attn[3])
    mixed_out = second_ffn[4]
    inputs = (tables_in, first_ffn[4])
    attn_kept, ffn_kept = (first_attn, second_attn), (first_ffn, second_ffn)

    slabs = [None] * 6
    grad = cotangent
    small_out, small_in, small_attn, bias_grads = [None] * 2, [None] * 2, [None] * 2, [None] * 2
    unpacked = {"attn": (), "in": (), "out": ()}
    for action in PLAN:
        if isinstance(action, int):
            slab = slabs[action]
            slab.step(order)
            if slab.ended():
                name = ("out", "in", "attn")[action % 3]
                unpacked[name] = unpack(layers - 1 - action // 3, name, slab, unpacked[name][: 2 if name == "attn" else 1])
            continue
        name, layer = action[:-1], int(action[-1])
        which = 3 * (layers - 1 - layer) + ("out", "in", "attn").index(name)
        way = WAYS[which]
        qkv_rows, probs, context, unit_one, inverse_one = attn_kept[layer]
        hidden, slope, unit_two, inverse_two, _ = ffn_kept[layer]
        if name == "out":
            d_ffn, d_resid_two, small_out[layer], kept, sent = out_backward(
                layer, way, grad, unit_two, inverse_two, hidden
            )
        elif name == "in":
            d_resid, small_in[layer], bias_grads[layer], kept, sent = in_backward(
                layer, way, d_ffn, d_resid_two, unit_one, inverse_one, slope
            )
        else:
            small_others = ()
            if layer == 0:
                small_others = (
                    small_out[0],
                    small_in[0],
                    bias_grads[0],
                    small_out[1],
                    small_in[1],
                    bias_grads[1],
                    small_attn[1],
                )
            grad, small_attn[layer], kept, sent = attn_backward(
                layer, way, d_resid, inputs[layer], qkv_rows, probs, context, small_others
            )
        slabs[which] = Slab(way, BACKS[which], wide_bits, kept, sent)
    qkv_grad, o_grad, *vectors = unpacked["attn"]
    in_grad, out_grad = unpacked["in"][0], unpacked["out"][0]
    return (
        mixed_out,
        grad,
        qkv_grad,
        vectors[0],
        vectors[1],
        o_grad,
        vectors[2],
        vectors[3],
        vectors[4],
        in_grad,
        vectors[8],
        out_grad,
        vectors[5],
        vectors[6],
        vectors[7],
    )


def solution(mesh):
    by_table = P(("wide", "narrow"), None)
    matrix = P(None, "narrow", None)
    vector = P(None, "narrow")
    return jax.shard_map(
        body,
        mesh=mesh,
        in_specs=(
            by_table,
            by_table,
            by_table,
            P(("wide", "narrow")),
            matrix,
            vector,
            vector,
            matrix,
            vector,
            vector,
            vector,
            matrix,
            vector,
            matrix,
            vector,
            vector,
            vector,
        ),
        out_specs=(
            by_table,
            by_table,
            matrix,
            vector,
            vector,
            matrix,
            vector,
            vector,
            vector,
            matrix,
            vector,
            matrix,
            vector,
            vector,
            vector,
        ),
        check_vma=False,
    )
```

time: 501 us -> 527 us (1.052)
  waiting for transfers between devices: 192 us -> 263 us
  blocking collectives: 24.6 us -> 0 us
  local copies, waits for them, and re-layouts: 34.9 us -> 23.4 us
  starting transfers between devices: 73.7 us -> 68.2 us
    ppermute x81 -> x70, waiting for transfers between devices: 192 us -> 251 us  [swap(): return lax.ppermute(value, axis, [(i, i ^ bit) for i in range(count)])]
    all_gather x1 -> x0, blocking collectives: 24.6 us -> none  [body(): packed = lax.all_gather(packed, 'narrow', axis=0).astype(f32)]
    ppermute x0 -> x3, waiting for transfers between devices: none -> 12 us  [body(): lax.ppermute(packed, 'narrow', [(i, i ^ away) for i in range(4)])]
    reshape x8 -> x0, local copies, waits for them, and re-layouts: 8.21 us -> none  [the longest x2 5.48 us: __init__(): self.flying = swap(sent.reshape(self.kept.shape), 'narrow', 1)]
    ppermute x81 -> x70, starting transfers between devices: 73.7 us -> 66.3 us  [swap(): return lax.ppermute(value, axis, [(i, i ^ bit) for i in range(count)])]
    convert_element_type x24, other arithmetic: 21.3 us -> 15.9 us  [added(): return (a.astype(f32) + b.astype(f32)).astype(low)]
    unnamed x127 -> x111, local copies, waits for them, and re-layouts: 13.9 us -> 11.2 us
    pallas_call x14 -> x16, Pallas kernels: 141 us -> 144 us  [call(): pl.pallas_call(kernel, name=name, in_specs=in_specs, out_specs=out_specs,...]
  transfers between devices with their start and end apart: 81 -> 73, of which waited for: 35 -> 41; matrix products, arithmetic and copies ran while one was open for 10% -> 6% of each run, Pallas kernels for 22% -> 20%
where the time goes in v3:
time: 527 us; the launch traced here: 522 us
  waiting for transfers between devices  263 us (50%)
  Pallas kernels  144 us (27%)
  starting transfers between devices  68.2 us (13%)
  local copies, waits for them, and re-layouts  23.4 us (4%)
  other arithmetic  21.1 us (4%)
    ppermute x70, waiting for transfers between devices, swap(): return lax.ppermute(value, axis, [(i, i ^ bit) for i in range(count)])  251 us
    pallas_call x16, Pallas kernels, call(): pl.pallas_call(kernel, name=name, in_specs=in_specs, out_specs=out_specs,...  144 us
    ppermute x70, starting transfers between devices, swap(): return lax.ppermute(value, axis, [(i, i ^ bit) for i in range(count)])  66.3 us
    convert_element_type x24, other arithmetic, added(): return (a.astype(f32) + b.astype(f32)).astype(low)  15.9 us
    ppermute x3, waiting for transfers between devices, body(): lax.ppermute(packed, 'narrow', [(i, i ^ away) for i in range(4)])  12 us
    unnamed x111, local copies, waits for them, and re-layouts  11.2 us
  transfers between devices with their start and end apart: 73, of which 41 were waited for; matrix products, arithmetic and copies ran while one was open for 6% of the time, Pallas kernels for 20%

profile of v3, /device:TPU:0, one launch (start us, length us, event | category | flops | bytes accessed | tf_op | source)
XLA Modules:
  0.0 522.4 jit_solution(7910100165443492092)
XLA Ops:
  2.9 2.0 dynamic-slice_bitcast_fusion.4
  5.8 2.5 collective-permute-start
  8.8 1.7 collective-permute-start.2
  11.2 11.6 %collective-permute-done.3 = bf16[2,12,192]{2,1,0:T(8,128)(2,1)} collective-permute-done((bf16[2,12,192]{2,1,0:T(8,128)(2,1)S(1)}, bf16[2,12,192]{2,1,0:T(8,128)(2,1)}, u32[]{:S(2)}, u32[]{:S(2)}) %collective-permute-start.3) | collective-permute-done | bytes 9248 | tf_op jit(solution)/shard_map/ppermute | solution.py:575
  30.1 1.8 collective-permute-start.6
  31.9 2.7 collective-permute-done.8.rest_1_
  36.1 9.9 %collective-permute-done.6.rest_5_ = bf16[96,3072]{1,0:T(8,128)(2,1)S(1)} collective-permute-done((bf16[96,3072]{1,0:T(8,128)(2,1)}, bf16[96,3072]{1,0:T(8,128)(2,1)S(1)}, u32[]{:S(2)}, u32[]{:S(2)}) %collective-permute-start.6) | collective-permute-done | bytes 589856 | tf_op jit(solution)/shard_map/ppermute | solution.py:22
  46.1 2.4 pad_maximum_fusion
  52.7 12.9 %collective-permute-done.12.rest_2_ = bf16[96,3072]{1,0:T(8,128)(2,1)S(1)} collective-permute-done((bf16[96,3072]{1,0:T(8,128)(2,1)}, bf16[96,3072]{1,0:T(8,128)(2,1)S(1)}, u32[]{:S(2)}, u32[]{:S(2)}) %collective-permute-start.12) | collective-permute-done | bytes 589856 | tf_op jit(solution)/shard_map/ppermute | solution.py:22
  65.7 1.8 collective-permute-start.13
  67.4 10.5 %collective-permute-done.10.rest_7_ = bf16[384,768]{1,0:T(8,128)(2,1)S(1)} collective-permute-done((bf16[384,768]{1,0:T(8,128)(2,1)S(1)}, bf16[384,768]{1,0:T(8,128)(2,1)S(1)}, u32[]{:S(2)}, u32[]{:S(2)}) %collective-permute-start.10) | collective-permute-done | bytes 589856 | tf_op jit(solution)/shard_map/ppermute | solution.py:22
  77.9 1.8 collective-permute-start.11
  81.9 10.9 %collective-permute-done.11.rest_8_ = bf16[384,768]{1,0:T(8,128)(2,1)S(1)} collective-permute-done((bf16[384,768]{1,0:T(8,128)(2,1)S(1)}, bf16[384,768]{1,0:T(8,128)(2,1)S(1)}, u32[]{:S(2)}, u32[]{:S(2)}) %collective-permute-start.11) | collective-permute-done | bytes 589856 | tf_op jit(solution)/shard_map/ppermute | solution.py:22
  96.7 12.2 %attn_fwd.2 = (bf16[256,2304]{1,0:T(8,128)(2,1)}, bf16[12,256,256]{2,1,0:T(8,128)(2,1)}, bf16[256,768]{1,0:T(8,128)(2,1)}, f32[256,768]{1,0:T(8,128)}, f32[256,1]{1,0:T(8,128)}) custom-call(s32[6]{0:T(128)} %stack.74.ids, s32[1]{0:T(128)S(6)} %copy.60.length, bf16[256,768]{1,0:T(8,128)(2,1)} %x.2, s32[1,256]{1,0:T(1,128)} %cell_row.3, ...), custom_call_target="tpu_custom_call" | custom-call | flops 1 | bytes 1 | tf_op jit(solution)/shard_map/attn_fwd/pallas_call | solution.py:406
  110.0 1.7 collective-permute-start.18
  113.3 10.0 %ffn_fwd.2 = (bf16[256,3072]{1,0:T(8,128)(2,1)}, f32[256,3072]{1,0:T(8,128)}, f32[256,768]{1,0:T(8,128)}, f32[256,1]{1,0:T(8,128)}, bf16[256,768]{1,0:T(8,128)(2,1)}) custom-call(s32[6]{0:T(128)} %stack.74.ids, f32[256,768]{1,0:T(8,128)} %get-tuple-element.189.unit_one, f32[2,1,3072]{2,1,0:T(1,128)} %reshape.474.in_bias, f32[2,8,768]{2,1,0:T(8,128)} %reshape.473.small, ...), custom_call_target="tpu_custom_call" | custom-call | flops 1 | bytes 1 | tf_op jit(solution)/shard_map/ffn_fwd/pallas_call | solution.py:406
  124.7 1.8 collective-permute-start.17
  128.0 12.4 %collective-permute-done.17.rest_7_ = bf16[384,768]{1,0:T(8,128)(2,1)S(1)} collective-permute-done((bf16[384,768]{1,0:T(8,128)(2,1)S(1)}, bf16[384,768]{1,0:T(8,128)(2,1)S(1)}, u32[]{:S(2)}, u32[]{:S(2)}) %collective-permute-start.17) | collective-permute-done | bytes 589856 | tf_op jit(solution)/shard_map/ppermute | solution.py:22
  140.5 1.7 collective-permute-start.21
  142.3 12.0 %attn_fwd.3 = (bf16[256,2304]{1,0:T(8,128)(2,1)}, bf16[12,256,256]{2,1,0:T(8,128)(2,1)}, bf16[256,768]{1,0:T(8,128)(2,1)}, f32[256,768]{1,0:T(8,128)}, f32[256,1]{1,0:T(8,128)}) custom-call(s32[6]{0:T(128)} %stack.74.ids, s32[1]{0:T(128)S(6)} %copy.60.length, bf16[256,768]{1,0:T(8,128)(2,1)} %get-tuple-element.201.x, s32[1,256]{1,0:T(1,128)} %cell_row.3, ...), custom_call_target="tpu_custom_call" | custom-call | flops 1 | bytes 1 | tf_op jit(solution)/shard_map/attn_fwd/pallas_call | solution.py:406
  155.5 1.8 collective-permute-done.24.rest_4_
  160.0 10.0 %ffn_fwd.3 = (bf16[256,3072]{1,0:T(8,128)(2,1)}, f32[256,3072]{1,0:T(8,128)}, f32[256,768]{1,0:T(8,128)}, f32[256,1]{1,0:T(8,128)}, bf16[256,768]{1,0:T(8,128)(2,1)}) custom-call(s32[6]{0:T(128)} %stack.74.ids, f32[256,768]{1,0:T(8,128)} %get-tuple-element.208.unit_one, f32[2,1,3072]{2,1,0:T(1,128)} %reshape.474.in_bias, f32[2,8,768]{2,1,0:T(8,128)} %reshape.473.small, ...), custom_call_target="tpu_custom_call" | custom-call | flops 1 | bytes 1 | tf_op jit(solution)/shard_map/ffn_fwd/pallas_call | solution.py:406
  170.0 8.6 %out_bwd.2 = (bf16[256,768]{1,0:T(8,128)(2,1)}, f32[256,768]{1,0:T(8,128)}, f32[8,768]{1,0:T(8,128)}, bf16[2,2,2,2,192,384]{5,4,3,2,1,0:T(8,128)(2,1)}, bf16[2,2,2,2,192,384]{5,4,3,2,1,0:T(8,128)(2,1)}) custom-call(s32[6]{0:T(128)} %stack.74.ids, bf16[256,768]{1,0:T(8,128)(2,1)} %grad, f32[256,768]{1,0:T(8,128)} %get-tuple-element.212.unit_two, ...), custom_call_target="tpu_custom_call" | custom-call | flops 1 | bytes 1 | tf_op jit(solution)/shard_map/out_bwd/pallas_call | solution.py:406
  178.8 14.3 %in_bwd.2 = (f32[256,768]{1,0:T(8,128)}, f32[8,768]{1,0:T(8,128)}, f32[1,3072]{1,0:T(1,128)}, bf16[2,2,2,2,192,384]{5,4,3,2,1,0:T(8,128)(2,1)}, bf16[2,2,2,2,192,384]{5,4,3,2,1,0:T(8,128)(2,1)}) custom-call(s32[6]{0:T(128)} %stack.74.ids, bf16[256,768]{1,0:T(8,128)(2,1)} %get-tuple-element.216.d_ffn, f32[256,768]{1,0:T(8,128)} %get-tuple-element.217.d_resid_two, ...), custom_call_target="tpu_custom_call" | custom-call | flops 1 | bytes 1 | tf_op jit(solution)/shard_map/in_bwd/pallas_call | solution.py:406
  194.9 15.5 %attn_bwd.2 = (bf16[256,768]{1,0:T(8,128)(2,1)}, f32[8,768]{1,0:T(8,128)}, bf16[2,2,2,2,192,384]{5,4,3,2,1,0:T(8,128)(2,1)}, bf16[2,2,2,2,192,384]{5,4,3,2,1,0:T(8,128)(2,1)}) custom-call(s32[6]{0:T(128)} %stack.74.ids, f32[256,768]{1,0:T(8,128)} %get-tuple-element.224.d_resid, bf16[256,768]{1,0:T(8,128)(2,1)} %get-tuple-element.201.x, ...), custom_call_target="tpu_custom_call" | custom-call | flops 1 | bytes 1 | tf_op jit(solution)/shard_map/attn_bwd/pallas_call | solution.py:406
  211.0 8.7 %out_bwd.3 = (bf16[256,768]{1,0:T(8,128)(2,1)}, f32[256,768]{1,0:T(8,128)}, f32[8,768]{1,0:T(8,128)}, bf16[2,2,2,2,192,384]{5,4,3,2,1,0:T(8,128)(2,1)}, bf16[2,2,2,2,192,384]{5,4,3,2,1,0:T(8,128)(2,1)}) custom-call(s32[6]{0:T(128)} %stack.74.ids, bf16[256,768]{1,0:T(8,128)(2,1)} %get-tuple-element.230.grad, f32[256,768]{1,0:T(8,128)} %get-tuple-element.231.unit_two, ...), custom_call_target="tpu_custom_call" | custom-call | flops 1 | bytes 1 | tf_op jit(solution)/shard_map/out_bwd/pallas_call | solution.py:406
  221.6 26.5 %collective-permute-done.26 = bf16[2,2,2,192,384]{4,3,2,1,0:T(8,128)(2,1)S(1)} collective-permute-done((bf16[2,2,2,192,384]{4,3,2,1,0:T(8,128)(2,1)S(1)}, bf16[2,2,2,192,384]{4,3,2,1,0:T(8,128)(2,1)S(1)}, u32[]{:S(2)}, u32[]{:S(2)}) %collective-permute-start.26) | collective-permute-done | bytes 1179680 | tf_op jit(solution)/shard_map/ppermute | solution.py:22
  255.4 7.6 %collective-permute-done.27 = bf16[2,2,192,384]{3,2,1,0:T(8,128)(2,1)S(1)} collective-permute-done((bf16[2,2,192,384]{3,2,1,0:T(8,128)(2,1)S(1)}, bf16[2,2,192,384]{3,2,1,0:T(8,128)(2,1)S(1)}, u32[]{:S(2)}, u32[]{:S(2)}) %collective-permute-start.27) | collective-permute-done | bytes 589856 | tf_op jit(solution)/shard_map/ppermute | solution.py:22
  265.9 14.0 %in_bwd.3 = (f32[256,768]{1,0:T(8,128)}, f32[8,768]{1,0:T(8,128)}, f32[1,3072]{1,0:T(1,128)}, bf16[2,2,2,2,192,384]{5,4,3,2,1,0:T(8,128)(2,1)}, bf16[2,2,2,2,192,384]{5,4,3,2,1,0:T(8,128)(2,1)}) custom-call(s32[6]{0:T(128)} %stack.74.ids, bf16[256,768]{1,0:T(8,128)(2,1)} %get-tuple-element.246.d_ffn, f32[256,768]{1,0:T(8,128)} %get-tuple-element.247.d_resid_two, ...), custom_call_target="tpu_custom_call" | custom-call | flops 1 | bytes 1 | tf_op jit(solution)/shard_map/in_bwd/pallas_call | solution.py:406
  281.7 2.6 collective-permute-start.34
  284.3 2.4 fusion.12
  287.6 4.0 collective-permute-done.34
  291.8 16.2 %attn_bwd.3 = (bf16[256,768]{1,0:T(8,128)(2,1)}, f32[8,768]{1,0:T(8,128)}, bf16[2,2,2,2,208,384]{5,4,3,2,1,0:T(8,128)(2,1)}, bf16[2,2,2,2,208,384]{5,4,3,2,1,0:T(8,128)(2,1)}) custom-call(s32[6]{0:T(128)} %stack.74.ids, f32[256,768]{1,0:T(8,128)} %get-tuple-element.249.d_resid, bf16[256,768]{1,0:T(8,128)(2,1)} %x.2, ...), custom_call_target="tpu_custom_call" | custom-call | flops 1 | bytes 1 | tf_op jit(solution)/shard_map/attn_bwd/pallas_call | solution.py:406
  308.1 3.1 collective-permute-start.42
  314.6 4.3 collective-permute-done.42
  318.9 1.7 collective-permute-start.40
  320.7 1.8 fusion.10
  322.5 5.2 collective-permute-done.40
  330.1 6.6 %collective-permute-done.45 = bf16[192,384]{1,0:T(8,128)(2,1)S(1)} collective-permute-done((bf16[192,384]{1,0:T(8,128)(2,1)S(1)}, bf16[192,384]{1,0:T(8,128)(2,1)S(1)}, u32[]{:S(2)}, u32[]{:S(2)}) %collective-permute-start.45) | collective-permute-done | bytes 147488 | tf_op jit(solution)/shard_map/ppermute | solution.py:22
  339.9 3.0 collective-permute-done.44
  343.7 6.7 %collective-permute-done.43 = bf16[2,192,384]{2,1,0:T(8,128)(2,1)S(1)} collective-permute-done((bf16[2,192,384]{2,1,0:T(8,128)(2,1)S(1)}, bf16[2,192,384]{2,1,0:T(8,128)(2,1)S(1)}, u32[]{:S(2)}, u32[]{:S(2)}) %collective-permute-start.43) | collective-permute-done | bytes 294944 | tf_op jit(solution)/shard_map/ppermute | solution.py:22
  352.7 13.7 %collective-permute-done.48 = bf16[2,2,2,192,384]{4,3,2,1,0:T(8,128)(2,1)S(1)} collective-permute-done((bf16[2,2,2,192,384]{4,3,2,1,0:T(8,128)(2,1)S(1)}, bf16[2,2,2,192,384]{4,3,2,1,0:T(8,128)(2,1)S(1)}, u32[]{:S(2)}, u32[]{:S(2)}) %collective-permute-start.48) | collective-permute-done | bytes 1179680 | tf_op jit(solution)/shard_map/ppermute | solution.py:22
  370.9 8.0 %collective-permute-done.49 = bf16[192,384]{1,0:T(8,128)(2,1)S(1)} collective-permute-done((bf16[192,384]{1,0:T(8,128)(2,1)S(1)}, bf16[192,384]{1,0:T(8,128)(2,1)S(1)}, u32[]{:S(2)}, u32[]{:S(2)}) %collective-permute-start.49) | collective-permute-done | bytes 147488 | tf_op jit(solution)/shard_map/ppermute | solution.py:22
  383.9 4.8 collective-permute-done.51
  388.8 3.1 collective-permute-done.46
  394.2 2.6 collective-permute-start.61
  396.8 6.7 %collective-permute-done.58 = bf16[2,192,384]{2,1,0:T(8,128)(2,1)S(1)} collective-permute-done((bf16[2,192,384]{2,1,0:T(8,128)(2,1)S(1)}, bf16[2,192,384]{2,1,0:T(8,128)(2,1)S(1)}, u32[]{:S(2)}, u32[]{:S(2)}) %collective-permute-start.58) | collective-permute-done | bytes 294944 | tf_op jit(solution)/shard_map/ppermute | solution.py:22
  403.7 3.2 collective-permute-done.55
  410.0 7.7 %collective-permute-done.60 = bf16[2,208,384]{2,1,0:T(8,128)(2,1)S(1)} collective-permute-done((bf16[2,208,384]{2,1,0:T(8,128)(2,1)S(1)}, bf16[2,208,384]{2,1,0:T(8,128)(2,1)S(1)}, u32[]{:S(2)}, u32[]{:S(2)}) %collective-permute-start.60) | collective-permute-done | bytes 319520 | tf_op jit(solution)/shard_map/ppermute | solution.py:22
  417.9 2.3 collective-permute-start.65
  420.2 5.7 %collective-permute-done.62 = bf16[208,384]{1,0:T(8,128)(2,1)S(1)} collective-permute-done((bf16[208,384]{1,0:T(8,128)(2,1)S(1)}, bf16[208,384]{1,0:T(8,128)(2,1)S(1)}, u32[]{:S(2)}, u32[]{:S(2)}) %collective-permute-start.62) | collective-permute-done | bytes 159776 | tf_op jit(solution)/shard_map/ppermute | solution.py:22
  427.4 2.1 collective-permute-done.65
  429.6 5.6 %collective-permute-done.64 = bf16[1,208,384]{2,1,0:T(8,128)(2,1)S(1)} collective-permute-done((bf16[1,208,384]{2,1,0:T(8,128)(2,1)S(1)}, bf16[1,208,384]{2,1,0:T(8,128)(2,1)S(1)}, u32[]{:S(2)}, u32[]{:S(2)}) %collective-permute-start.64) | collective-permute-done | bytes 159776 | tf_op jit(solution)/shard_map/ppermute | solution.py:22
  435.4 8.5 %collective-permute-done.66 = bf16[2,208,384]{2,1,0:T(8,128)(2,1)S(1)} collective-permute-done((bf16[2,208,384]{2,1,0:T(8,128)(2,1)S(1)}, bf16[2,208,384]{2,1,0:T(8,128)(2,1)S(1)}, u32[]{:S(2)}, u32[]{:S(2)}) %collective-permute-start.66) | collective-permute-done | bytes 319520 | tf_op jit(solution)/shard_map/ppermute | solution.py:22
  449.5 3.7 unpack.10
  453.2 20.8 %collective-permute-done.68.far = bf16[4,192,384]{2,1,0:T(8,128)(2,1)S(1)} collective-permute-done((bf16[4,192,384]{2,1,0:T(8,128)(2,1)S(1)}, bf16[4,192,384]{2,1,0:T(8,128)(2,1)S(1)}, u32[]{:S(2)}, u32[]{:S(2)}) %collective-permute-start.68) | collective-permute-done | bytes 589856 | tf_op jit(solution)/shard_map/ppermute | solution.py:22
  474.8 3.7 unpack.6
  478.6 8.1 %collective-permute-done.69.far = bf16[4,192,384]{2,1,0:T(8,128)(2,1)S(1)} collective-permute-done((bf16[4,192,384]{2,1,0:T(8,128)(2,1)S(1)}, bf16[4,192,384]{2,1,0:T(8,128)(2,1)S(1)}, u32[]{:S(2)}, u32[]{:S(2)}) %collective-permute-start.69) | collective-permute-done | bytes 589856 | tf_op jit(solution)/shard_map/ppermute | solution.py:22
  486.6 12.6 %collective-permute-done.71.far = bf16[4,192,384]{2,1,0:T(8,128)(2,1)S(1)} collective-permute-done((bf16[4,192,384]{2,1,0:T(8,128)(2,1)S(1)}, bf16[4,192,384]{2,1,0:T(8,128)(2,1)S(1)}, u32[]{:S(2)}, u32[]{:S(2)}) %collective-permute-start.71) | collective-permute-done | bytes 589856 | tf_op jit(solution)/shard_map/ppermute | solution.py:22
  500.1 3.7 unpack.11
  503.8 5.2 collective-permute-done.70.far
  509.8 3.7 unpack.8
  513.6 3.7 unpack.9
  518.1 3.8 unpack.7
  (283 shorter events, 87.3 us)
Async XLA Ops:
  0.6 22.7 %collective-permute-start.4 = (bf16[2,192,2304]{2,1,0:T(8,128)(2,1)}, bf16[2,192,2304]{2,1,0:T(8,128)(2,1)}, u32[]{:S(2)}, u32[]{:S(2)}) collective-permute-start(bf16[2,192,2304]{2,1,0:T(8,128)(2,1)} %rest_0_.15), channel_id=1, source_target_pairs={{0,1},{1,0},{2,3},{3,2},{4,5},{5,4},{6,7},{7,6},{8,9},{9,8},{10,11... | collective-permute-start | bytes 5308424 | tf_op jit(solution)/shard_map/ppermute | solution.py:22
  5.8 17.5 %collective-permute-start = (bf16[96,3072]{1,0:T(8,128)(2,1)}, bf16[96,3072]{1,0:T(8,128)(2,1)}, u32[]{:S(2)}, u32[]{:S(2)}) collective-permute-start(bf16[96,3072]{1,0:T(8,128)(2,1)} %pad_maximum_fusion.3), channel_id=1, source_target_pairs={{0,2},{1,3},{2,0},{3,1},{4,6},{5,7},{6,4},{7,5},{8,10},{9,11},{10,... | collective-permute-start | bytes 1769480 | tf_op jit(solution)/shard_map/ppermute | solution.py:22
  8.6 14.1 %collective-permute-start.3 = (bf16[2,12,192]{2,1,0:T(8,128)(2,1)S(1)}, bf16[2,12,192]{2,1,0:T(8,128)(2,1)}, u32[]{:S(2)}, u32[]{:S(2)}) collective-permute-start(bf16[2,12,192]{2,1,0:T(8,128)(2,1)S(1)} %concatenate.98), channel_id=1, source_target_pairs={{0,3},{1,2},{2,1},{3,0},{4,7},{5,6},{6,5},{7,4},{8,11},{9,10},{10,... | collective-permute-start | bytes 27656 | tf_op jit(solution)/shard_map/ppermute | solution.py:575
  8.8 14.5 %collective-permute-start.2 = (bf16[2,12,192]{2,1,0:T(8,128)(2,1)S(1)}, bf16[2,12,192]{2,1,0:T(8,128)(2,1)}, u32[]{:S(2)}, u32[]{:S(2)}) collective-permute-start(bf16[2,12,192]{2,1,0:T(8,128)(2,1)S(1)} %concatenate.98), channel_id=1, source_target_pairs={{0,2},{1,3},{2,0},{3,1},{4,6},{5,7},{6,4},{7,5},{8,10},{9,11},{10,... | collective-permute-start | bytes 27656 | tf_op jit(solution)/shard_map/ppermute | solution.py:575
  10.5 12.8 %collective-permute-start.1 = (bf16[2,12,192]{2,1,0:T(8,128)(2,1)S(1)}, bf16[2,12,192]{2,1,0:T(8,128)(2,1)}, u32[]{:S(2)}, u32[]{:S(2)}) collective-permute-start(bf16[2,12,192]{2,1,0:T(8,128)(2,1)S(1)} %concatenate.98), channel_id=1, source_target_pairs={{0,1},{1,0},{2,3},{3,2},{4,5},{5,4},{6,7},{7,6},{8,9},{9,8},{10,11... | collective-permute-start | bytes 27656 | tf_op jit(solution)/shard_map/ppermute | solution.py:575
  30.1 16.0 %collective-permute-start.6 = (bf16[96,3072]{1,0:T(8,128)(2,1)}, bf16[96,3072]{1,0:T(8,128)(2,1)S(1)}, u32[]{:S(2)}, u32[]{:S(2)}) collective-permute-start(bf16[96,3072]{1,0:T(8,128)(2,1)} %collective-permute-done.rest_4_), channel_id=1, source_target_pairs={{0,4},{4,0},{8,12},{12,8},{16,20},{20,16},{24,28},{28,24},{1,5},{5... | collective-permute-start | bytes 1769480 | tf_op jit(solution)/shard_map/ppermute | solution.py:22
  36.0 31.4 %collective-permute-start.9 = (bf16[2,768,768]{2,1,0:T(8,128)(2,1)}, bf16[2,768,768]{2,1,0:T(8,128)(2,1)}, u32[]{:S(2)}, u32[]{:S(2)}) collective-permute-start(bf16[2,768,768]{2,1,0:T(8,128)(2,1)} %rest_5_.7), channel_id=1, source_target_pairs={{0,1},{1,0},{2,3},{3,2},{4,5},{5,4},{6,7},{7,6},{8,9},{9,8},{10,11... | collective-permute-start | bytes 7077896 | tf_op jit(solution)/shard_map/ppermute | solution.py:22
  48.4 19.0 %collective-permute-start.7 = (bf16[192,3072]{1,0:T(8,128)(2,1)}, bf16[192,3072]{1,0:T(8,128)(2,1)}, u32[]{:S(2)}, u32[]{:S(2)}) collective-permute-start(bf16[192,3072]{1,0:T(8,128)(2,1)} %pad_maximum_fusion), channel_id=1, source_target_pairs={{0,1},{1,0},{2,3},{3,2},{4,5},{5,4},{6,7},{7,6},{8,9},{9,8},{10,11... | collective-permute-start | bytes 3538952 | tf_op jit(solution)/shard_map/ppermute | solution.py:22
  49.3 16.3 %collective-permute-start.12 = (bf16[96,3072]{1,0:T(8,128)(2,1)}, bf16[96,3072]{1,0:T(8,128)(2,1)S(1)}, u32[]{:S(2)}, u32[]{:S(2)}) collective-permute-start(bf16[96,3072]{1,0:T(8,128)(2,1)} %get-tuple-element.184), channel_id=1, source_target_pairs={{0,2},{1,3},{2,0},{3,1},{4,6},{5,7},{6,4},{7,5},{8,10},{9,11},{10,... | collective-permute-start | bytes 1769480 | tf_op jit(solution)/shard_map/ppermute | solution.py:22
  52.4 25.5 %collective-permute-start.10 = (bf16[384,768]{1,0:T(8,128)(2,1)S(1)}, bf16[384,768]{1,0:T(8,128)(2,1)S(1)}, u32[]{:S(2)}, u32[]{:S(2)}) collective-permute-start(bf16[384,768]{1,0:T(8,128)(2,1)S(1)} %get-tuple-element.354), channel_id=1, source_target_pairs={{0,2},{1,3},{2,0},{3,1},{4,6},{5,7},{6,4},{7,5},{8,10},{9,11},{10,... | collective-permute-start | bytes 1769480 | tf_op jit(solution)/shard_map/ppermute | solution.py:22
  65.7 14.6 %collective-permute-start.13 = (bf16[96,3072]{1,0:T(8,128)(2,1)S(1)}, bf16[96,3072]{1,0:T(8,128)(2,1)S(1)}, u32[]{:S(2)}, u32[]{:S(2)}) collective-permute-start(bf16[96,3072]{1,0:T(8,128)(2,1)S(1)} %collective-permute-done.12.rest_2_), channel_id=1, source_target_pairs={{0,4},{4,0},{8,12},{12,8},{16,20},{20,16},{24,28},{28,24},{1,5},{5... | collective-permute-start | bytes 1769480 | tf_op jit(solution)/shard_map/ppermute | solution.py:22
  77.9 15.0 %collective-permute-start.11 = (bf16[384,768]{1,0:T(8,128)(2,1)S(1)}, bf16[384,768]{1,0:T(8,128)(2,1)S(1)}, u32[]{:S(2)}, u32[]{:S(2)}) collective-permute-start(bf16[384,768]{1,0:T(8,128)(2,1)S(1)} %collective-permute-done.10.rest_7_), channel_id=1, source_target_pairs={{0,4},{4,0},{8,12},{12,8},{16,20},{20,16},{24,28},{28,24},{1,5},{5... | collective-permute-start | bytes 1769480 | tf_op jit(solution)/shard_map/ppermute | solution.py:22
  81.1 30.8 %collective-permute-start.15 = (bf16[192,3072]{1,0:T(8,128)(2,1)S(1)}, bf16[192,3072]{1,0:T(8,128)(2,1)S(1)}, u32[]{:S(2)}, u32[]{:S(2)}) collective-permute-start(bf16[192,3072]{1,0:T(8,128)(2,1)S(1)} %pad_maximum_fusion.1), channel_id=1, source_target_pairs={{0,1},{1,0},{2,3},{3,2},{4,5},{5,4},{6,7},{7,6},{8,9},{9,8},{10,11... | collective-permute-start | bytes 3538952 | tf_op jit(solution)/shard_map/ppermute | solution.py:22
  93.8 18.1 %collective-permute-start.14 = (bf16[768,768]{1,0:T(8,128)(2,1)}, bf16[768,768]{1,0:T(8,128)(2,1)S(1)}, u32[]{:S(2)}, u32[]{:S(2)}) collective-permute-start(bf16[768,768]{1,0:T(8,128)(2,1)} %constant_dynamic-update-slice_fusion), channel_id=1, source_target_pairs={{0,1},{1,0},{2,3},{3,2},{4,5},{5,4},{6,7},{7,6},{8,9},{9,8},{10,11... | collective-permute-start | bytes 3538952 | tf_op jit(solution)/shard_map/ppermute | solution.py:22
  93.9 16.1 %collective-permute-start.16 = (bf16[96,3072]{1,0:T(8,128)(2,1)S(1)}, bf16[96,3072]{1,0:T(8,128)(2,1)S(1)}, u32[]{:S(2)}, u32[]{:S(2)}) collective-permute-start(bf16[96,3072]{1,0:T(8,128)(2,1)S(1)} %pad_maximum_fusion.4), channel_id=1, source_target_pairs={{0,2},{1,3},{2,0},{3,1},{4,6},{5,7},{6,4},{7,5},{8,10},{9,11},{10,... | collective-permute-start | bytes 1769480 | tf_op jit(solution)/shard_map/ppermute | solution.py:22
  96.3 27.0 %collective-permute-start.19 = (bf16[96,3072]{1,0:T(8,128)(2,1)S(1)}, bf16[96,3072]{1,0:T(8,128)(2,1)S(1)}, u32[]{:S(2)}, u32[]{:S(2)}) collective-permute-start(bf16[96,3072]{1,0:T(8,128)(2,1)S(1)} %get-tuple-element.195), channel_id=1, source_target_pairs={{0,2},{1,3},{2,0},{3,1},{4,6},{5,7},{6,4},{7,5},{8,10},{9,11},{10,... | collective-permute-start | bytes 1769480 | tf_op jit(solution)/shard_map/ppermute | solution.py:22
  110.0 14.6 %collective-permute-start.18 = (bf16[96,3072]{1,0:T(8,128)(2,1)S(1)}, bf16[96,3072]{1,0:T(8,128)(2,1)S(1)}, u32[]{:S(2)}, u32[]{:S(2)}) collective-permute-start(bf16[96,3072]{1,0:T(8,128)(2,1)S(1)} %collective-permute-done.16.rest_4_), channel_id=1, source_target_pairs={{0,4},{4,0},{8,12},{12,8},{16,20},{20,16},{24,28},{28,24},{1,5},{5... | collective-permute-start | bytes 1769480 | tf_op jit(solution)/shard_map/ppermute | solution.py:22
  124.7 15.7 %collective-permute-start.17 = (bf16[384,768]{1,0:T(8,128)(2,1)S(1)}, bf16[384,768]{1,0:T(8,128)(2,1)S(1)}, u32[]{:S(2)}, u32[]{:S(2)}) collective-permute-start(bf16[384,768]{1,0:T(8,128)(2,1)S(1)} %get-tuple-element.194), channel_id=1, source_target_pairs={{0,2},{1,3},{2,0},{3,1},{4,6},{5,7},{6,4},{7,5},{8,10},{9,11},{10,... | collective-permute-start | bytes 1769480 | tf_op jit(solution)/shard_map/ppermute | solution.py:22
  126.5 27.8 %collective-permute-start.22 = (bf16[96,3072]{1,0:T(8,128)(2,1)S(1)}, bf16[96,3072]{1,0:T(8,128)(2,1)S(1)}, u32[]{:S(2)}, u32[]{:S(2)}) collective-permute-start(bf16[96,3072]{1,0:T(8,128)(2,1)S(1)} %collective-permute-done.19.rest_2_), channel_id=1, source_target_pairs={{0,4},{4,0},{8,12},{12,8},{16,20},{20,16},{24,28},{28,24},{1,5},{5... | collective-permute-start | bytes 1769480 | tf_op jit(solution)/shard_map/ppermute | solution.py:22
  140.5 14.9 %collective-permute-start.21 = (bf16[384,768]{1,0:T(8,128)(2,1)S(1)}, bf16[384,768]{1,0:T(8,128)(2,1)S(1)}, u32[]{:S(2)}, u32[]{:S(2)}) collective-permute-start(bf16[384,768]{1,0:T(8,128)(2,1)S(1)} %collective-permute-done.17.rest_7_), channel_id=1, source_target_pairs={{0,4},{4,0},{8,12},{12,8},{16,20},{20,16},{24,28},{28,24},{1,5},{5... | collective-permute-start | bytes 1769480 | tf_op jit(solution)/shard_map/ppermute | solution.py:22
  178.6 14.6 %collective-permute-start.25 = (bf16[2,2,2,2,192,384]{5,4,3,2,1,0:T(8,128)(2,1)}, bf16[2,2,2,2,192,384]{5,4,3,2,1,0:T(8,128)(2,1)S(1)}, u32[]{:S(2)}, u32[]{:S(2)}) collective-permute-start(bf16[2,2,2,2,192,384]{5,4,3,2,1,0:T(8,128)(2,1)} %get-tuple-element.221), channel_id=1, source_target_pairs={{0,1},{1,0},{2,3},{3,2},{4,5},{5,4},{6,7},{7,6},{8,9},{9,8},{10,11... | collective-permute-start | bytes 7077896 | tf_op jit(solution)/shard_map/ppermute | solution.py:22
  210.4 39.2 %collective-permute-start.30 = (bf16[2,2,2,2,192,384]{5,4,3,2,1,0:T(8,128)(2,1)}, bf16[2,2,2,2,192,384]{5,4,3,2,1,0:T(8,128)(2,1)S(1)}, u32[]{:S(2)}, u32[]{:S(2)}) collective-permute-start(bf16[2,2,2,2,192,384]{5,4,3,2,1,0:T(8,128)(2,1)} %get-tuple-element.241), channel_id=1, source_target_pairs={{0,1},{1,0},{2,3},{3,2},{4,5},{5,4},{6,7},{7,6},{8,9},{9,8},{10,11... | collective-permute-start | bytes 7077896 | tf_op jit(solution)/shard_map/ppermute | solution.py:22
  210.8 42.1 %collective-permute-start.29 = (bf16[2,2,2,2,192,384]{5,4,3,2,1,0:T(8,128)(2,1)}, bf16[2,2,2,2,192,384]{5,4,3,2,1,0:T(8,128)(2,1)S(1)}, u32[]{:S(2)}, u32[]{:S(2)}) collective-permute-start(bf16[2,2,2,2,192,384]{5,4,3,2,1,0:T(8,128)(2,1)} %get-tuple-element.239), channel_id=1, source_target_pairs={{0,1},{1,0},{2,3},{3,2},{4,5},{5,4},{6,7},{7,6},{8,9},{9,8},{10,11... | collective-permute-start | bytes 7077896 | tf_op jit(solution)/shard_map/ppermute | solution.py:22
  219.7 35.0 %collective-permute-start.28 = (bf16[2,2,2,2,192,384]{5,4,3,2,1,0:T(8,128)(2,1)}, bf16[2,2,2,2,192,384]{5,4,3,2,1,0:T(8,128)(2,1)S(1)}, u32[]{:S(2)}, u32[]{:S(2)}) collective-permute-start(bf16[2,2,2,2,192,384]{5,4,3,2,1,0:T(8,128)(2,1)} %get-tuple-element.237), channel_id=1, source_target_pairs={{0,1},{1,0},{2,3},{3,2},{4,5},{5,4},{6,7},{7,6},{8,9},{9,8},{10,11... | collective-permute-start | bytes 7077896 | tf_op jit(solution)/shard_map/ppermute | solution.py:22
  220.1 28.0 %collective-permute-start.26 = (bf16[2,2,2,192,384]{4,3,2,1,0:T(8,128)(2,1)S(1)}, bf16[2,2,2,192,384]{4,3,2,1,0:T(8,128)(2,1)S(1)}, u32[]{:S(2)}, u32[]{:S(2)}) collective-permute-start(bf16[2,2,2,192,384]{4,3,2,1,0:T(8,128)(2,1)S(1)} %copy-done.33), channel_id=1, source_target_pairs={{0,2},{1,3},{2,0},{3,1},{4,6},{5,7},{6,4},{7,5},{8,10},{9,11},{10,... | collective-permute-start | bytes 3538952 | tf_op jit(solution)/shard_map/ppermute | solution.py:22
  248.4 14.6 %collective-permute-start.27 = (bf16[2,2,192,384]{3,2,1,0:T(8,128)(2,1)S(1)}, bf16[2,2,192,384]{3,2,1,0:T(8,128)(2,1)S(1)}, u32[]{:S(2)}, u32[]{:S(2)}) collective-permute-start(bf16[2,2,192,384]{3,2,1,0:T(8,128)(2,1)S(1)} %get-tuple-element.349), channel_id=1, source_target_pairs={{0,4},{4,0},{8,12},{12,8},{16,20},{20,16},{24,28},{28,24},{1,5},{5... | collective-permute-start | bytes 1769480 | tf_op jit(solution)/shard_map/ppermute | solution.py:22
  251.5 32.8 %collective-permute-start.35 = (bf16[2,2,2,192,384]{4,3,2,1,0:T(8,128)(2,1)}, bf16[2,2,2,192,384]{4,3,2,1,0:T(8,128)(2,1)}, u32[]{:S(2)}, u32[]{:S(2)}) collective-permute-start(bf16[2,2,2,192,384]{4,3,2,1,0:T(8,128)(2,1)} %get-tuple-element.334), channel_id=1, source_target_pairs={{0,2},{1,3},{2,0},{3,1},{4,6},{5,7},{6,4},{7,5},{8,10},{9,11},{10,... | collective-permute-start | bytes 3538952 | tf_op jit(solution)/shard_map/ppermute | solution.py:22
  263.2 18.4 %collective-permute-start.33 = (bf16[2,192,384]{2,1,0:T(8,128)(2,1)S(1)}, bf16[2,192,384]{2,1,0:T(8,128)(2,1)S(1)}, u32[]{:S(2)}, u32[]{:S(2)}) collective-permute-start(bf16[2,192,384]{2,1,0:T(8,128)(2,1)S(1)} %get-tuple-element.368), channel_id=1, source_target_pairs={{0,8},{4,12},{8,0},{12,4},{16,24},{20,28},{24,16},{28,20},{1,9},{5... | collective-permute-start | bytes 884744 | tf_op jit(solution)/shard_map/ppermute | solution.py:22
  264.8 43.3 %collective-permute-start.32 = (bf16[2,2,2,192,384]{4,3,2,1,0:T(8,128)(2,1)}, bf16[2,2,2,192,384]{4,3,2,1,0:T(8,128)(2,1)}, u32[]{:S(2)}, u32[]{:S(2)}) collective-permute-start(bf16[2,2,2,192,384]{4,3,2,1,0:T(8,128)(2,1)} %get-tuple-element.336), channel_id=1, source_target_pairs={{0,4},{4,0},{8,12},{12,8},{16,20},{20,16},{24,28},{28,24},{1,5},{5... | collective-permute-start | bytes 3538952 | tf_op jit(solution)/shard_map/ppermute | solution.py:22
  280.0 56.7 %collective-permute-start.38 = (bf16[2,2,2,2,192,384]{5,4,3,2,1,0:T(8,128)(2,1)}, bf16[2,2,2,2,192,384]{5,4,3,2,1,0:T(8,128)(2,1)S(1)}, u32[]{:S(2)}, u32[]{:S(2)}) collective-permute-start(bf16[2,2,2,2,192,384]{5,4,3,2,1,0:T(8,128)(2,1)} %get-tuple-element.265), channel_id=1, source_target_pairs={{0,1},{1,0},{2,3},{3,2},{4,5},{5,4},{6,7},{7,6},{8,9},{9,8},{10,11... | collective-permute-start | bytes 7077896 | tf_op jit(solution)/shard_map/ppermute | solution.py:22
  280.1 40.7 %collective-permute-start.41 = (bf16[2,2,2,192,384]{4,3,2,1,0:T(8,128)(2,1)S(1)}, bf16[2,2,2,192,384]{4,3,2,1,0:T(8,128)(2,1)}, u32[]{:S(2)}, u32[]{:S(2)}) collective-permute-start(bf16[2,2,2,192,384]{4,3,2,1,0:T(8,128)(2,1)S(1)} %get-tuple-element.332), channel_id=1, source_target_pairs={{0,2},{1,3},{2,0},{3,1},{4,6},{5,7},{6,4},{7,5},{8,10},{9,11},{10,... | collective-permute-start | bytes 3538952 | tf_op jit(solution)/shard_map/ppermute | solution.py:22
  281.7 9.9 %collective-permute-start.34 = (bf16[192,384]{1,0:T(8,128)(2,1)S(1)}, bf16[192,384]{1,0:T(8,128)(2,1)S(1)}, u32[]{:S(2)}, u32[]{:S(2)}) collective-permute-start(bf16[192,384]{1,0:T(8,128)(2,1)S(1)} %fusion.65), channel_id=1, source_target_pairs={{0,16},{4,20},{8,24},{12,28},{16,0},{20,4},{24,8},{28,12},{1,17},{... | collective-permute-start | bytes 442376 | tf_op jit(solution)/shard_map/ppermute | solution.py:22
  286.7 26.1 %collective-permute-start.39 = (bf16[2,2,192,384]{3,2,1,0:T(8,128)(2,1)}, bf16[2,2,192,384]{3,2,1,0:T(8,128)(2,1)}, u32[]{:S(2)}, u32[]{:S(2)}) collective-permute-start(bf16[2,2,192,384]{3,2,1,0:T(8,128)(2,1)} %get-tuple-element.346), channel_id=1, source_target_pairs={{0,4},{4,0},{8,12},{12,8},{16,20},{20,16},{24,28},{28,24},{1,5},{5... | collective-permute-start | bytes 1769480 | tf_op jit(solution)/shard_map/ppermute | solution.py:22
  291.7 16.3 %collective-permute-start.36 = (bf16[1,192,384]{2,1,0:T(8,128)(2,1)S(1)}, bf16[1,192,384]{2,1,0:T(8,128)(2,1)S(1)}, u32[]{:S(2)}, u32[]{:S(2)}) collective-permute-start(bf16[1,192,384]{2,1,0:T(8,128)(2,1)S(1)} %fusion.64), channel_id=1, source_target_pairs={{0,16},{4,20},{8,24},{12,28},{16,0},{20,4},{24,8},{28,12},{1,17},{... | collective-permute-start | bytes 442376 | tf_op jit(solution)/shard_map/ppermute | solution.py:22
  307.9 42.5 %collective-permute-start.31 = (bf16[2,2,2,2,208,384]{5,4,3,2,1,0:T(8,128)(2,1)}, bf16[2,2,2,2,208,384]{5,4,3,2,1,0:T(8,128)(2,1)S(1)}, u32[]{:S(2)}, u32[]{:S(2)}) collective-permute-start(bf16[2,2,2,2,208,384]{5,4,3,2,1,0:T(8,128)(2,1)} %get-tuple-element.258), channel_id=1, source_target_pairs={{0,1},{1,0},{2,3},{3,2},{4,5},{5,4},{6,7},{7,6},{8,9},{9,8},{10,11... | collective-permute-start | bytes 7667720 | tf_op jit(solution)/shard_map/ppermute | solution.py:22
  308.1 10.8 %collective-permute-start.42 = (bf16[2,192,384]{2,1,0:T(8,128)(2,1)S(1)}, bf16[2,192,384]{2,1,0:T(8,128)(2,1)S(1)}, u32[]{:S(2)}, u32[]{:S(2)}) collective-permute-start(bf16[2,192,384]{2,1,0:T(8,128)(2,1)S(1)} %pad_maximum_fusion.11), channel_id=1, source_target_pairs={{0,8},{4,12},{8,0},{12,4},{16,24},{20,28},{24,16},{28,20},{1,9},{5... | collective-permute-start | bytes 884744 | tf_op jit(solution)/shard_map/ppermute | solution.py:22
  312.8 25.2 %collective-permute-start.37 = (bf16[2,2,192,384]{3,2,1,0:T(8,128)(2,1)S(1)}, bf16[2,2,192,384]{3,2,1,0:T(8,128)(2,1)S(1)}, u32[]{:S(2)}, u32[]{:S(2)}) collective-permute-start(bf16[2,2,192,384]{3,2,1,0:T(8,128)(2,1)S(1)} %get-tuple-element.347), channel_id=1, source_target_pairs={{0,2},{1,3},{2,0},{3,1},{4,6},{5,7},{6,4},{7,5},{8,10},{9,11},{10,... | collective-permute-start | bytes 1769480 | tf_op jit(solution)/shard_map/ppermute | solution.py:22
  329.2 13.8 %collective-permute-start.44 = (bf16[2,2,192,384]{3,2,1,0:T(8,128)(2,1)S(1)}, bf16[2,2,192,384]{3,2,1,0:T(8,128)(2,1)S(1)}, u32[]{:S(2)}, u32[]{:S(2)}) collective-permute-start(bf16[2,2,192,384]{3,2,1,0:T(8,128)(2,1)S(1)} %get-tuple-element.344), channel_id=1, source_target_pairs={{0,4},{4,0},{8,12},{12,8},{16,20},{20,16},{24,28},{28,24},{1,5},{5... | collective-permute-start | bytes 1769480 | tf_op jit(solution)/shard_map/ppermute | solution.py:22
  337.4 29.0 %collective-permute-start.48 = (bf16[2,2,2,192,384]{4,3,2,1,0:T(8,128)(2,1)S(1)}, bf16[2,2,2,192,384]{4,3,2,1,0:T(8,128)(2,1)S(1)}, u32[]{:S(2)}, u32[]{:S(2)}) collective-permute-start(bf16[2,2,2,192,384]{4,3,2,1,0:T(8,128)(2,1)S(1)} %get-tuple-element.330), channel_id=1, source_target_pairs={{0,2},{1,3},{2,0},{3,1},{4,6},{5,7},{6,4},{7,5},{8,10},{9,11},{10,... | collective-permute-start | bytes 3538952 | tf_op jit(solution)/shard_map/ppermute | solution.py:22
  338.1 12.3 %collective-permute-start.43 = (bf16[2,192,384]{2,1,0:T(8,128)(2,1)S(1)}, bf16[2,192,384]{2,1,0:T(8,128)(2,1)S(1)}, u32[]{:S(2)}, u32[]{:S(2)}) collective-permute-start(bf16[2,192,384]{2,1,0:T(8,128)(2,1)S(1)} %get-tuple-element.363), channel_id=1, source_target_pairs={{0,8},{4,12},{8,0},{12,4},{16,24},{20,28},{24,16},{28,20},{1,9},{5... | collective-permute-start | bytes 884744 | tf_op jit(solution)/shard_map/ppermute | solution.py:22
  338.3 29.5 %collective-permute-start.50 = (bf16[1,192,384]{2,1,0:T(8,128)(2,1)S(1)}, bf16[1,192,384]{2,1,0:T(8,128)(2,1)S(1)}, u32[]{:S(2)}, u32[]{:S(2)}) collective-permute-start(bf16[1,192,384]{2,1,0:T(8,128)(2,1)S(1)} %fusion.69), channel_id=1, source_target_pairs={{0,16},{4,20},{8,24},{12,28},{16,0},{20,4},{24,8},{28,12},{1,17},{... | collective-permute-start | bytes 442376 | tf_op jit(solution)/shard_map/ppermute | solution.py:22
  343.1 24.5 %collective-permute-start.47 = (bf16[2,192,384]{2,1,0:T(8,128)(2,1)S(1)}, bf16[2,192,384]{2,1,0:T(8,128)(2,1)S(1)}, u32[]{:S(2)}, u32[]{:S(2)}) collective-permute-start(bf16[2,192,384]{2,1,0:T(8,128)(2,1)S(1)} %get-tuple-element.362), channel_id=1, source_target_pairs={{0,8},{4,12},{8,0},{12,4},{16,24},{20,28},{24,16},{28,20},{1,9},{5... | collective-permute-start | bytes 884744 | tf_op jit(solution)/shard_map/ppermute | solution.py:22
  351.1 40.8 %collective-permute-start.46 = (bf16[2,2,2,208,384]{4,3,2,1,0:T(8,128)(2,1)S(1)}, bf16[2,2,2,208,384]{4,3,2,1,0:T(8,128)(2,1)S(1)}, u32[]{:S(2)}, u32[]{:S(2)}) collective-permute-start(bf16[2,2,2,208,384]{4,3,2,1,0:T(8,128)(2,1)S(1)} %get-tuple-element.327), channel_id=1, source_target_pairs={{0,2},{1,3},{2,0},{3,1},{4,6},{5,7},{6,4},{7,5},{8,10},{9,11},{10,... | collective-permute-start | bytes 3833864 | tf_op jit(solution)/shard_map/ppermute | solution.py:22
  366.6 13.9 %collective-permute-start.53 = (bf16[2,2,192,384]{3,2,1,0:T(8,128)(2,1)S(1)}, bf16[2,2,192,384]{3,2,1,0:T(8,128)(2,1)S(1)}, u32[]{:S(2)}, u32[]{:S(2)}) collective-permute-start(bf16[2,2,192,384]{3,2,1,0:T(8,128)(2,1)S(1)} %get-tuple-element.342), channel_id=1, source_target_pairs={{0,4},{4,0},{8,12},{12,8},{16,20},{20,16},{24,28},{28,24},{1,5},{5... | collective-permute-start | bytes 1769480 | tf_op jit(solution)/shard_map/ppermute | solution.py:22
  367.7 11.2 %collective-permute-start.49 = (bf16[192,384]{1,0:T(8,128)(2,1)S(1)}, bf16[192,384]{1,0:T(8,128)(2,1)S(1)}, u32[]{:S(2)}, u32[]{:S(2)}) collective-permute-start(bf16[192,384]{1,0:T(8,128)(2,1)S(1)} %fusion.72), channel_id=1, source_target_pairs={{0,16},{4,20},{8,24},{12,28},{16,0},{20,4},{24,8},{28,12},{1,17},{... | collective-permute-start | bytes 442376 | tf_op jit(solution)/shard_map/ppermute | solution.py:22
  367.8 12.6 %collective-permute-start.54 = (bf16[2,192,384]{2,1,0:T(8,128)(2,1)S(1)}, bf16[2,192,384]{2,1,0:T(8,128)(2,1)S(1)}, u32[]{:S(2)}, u32[]{:S(2)}) collective-permute-start(bf16[2,192,384]{2,1,0:T(8,128)(2,1)S(1)} %pad_maximum_fusion.12), channel_id=1, source_target_pairs={{0,8},{4,12},{8,0},{12,4},{16,24},{20,28},{24,16},{28,20},{1,9},{5... | collective-permute-start | bytes 884744 | tf_op jit(solution)/shard_map/ppermute | solution.py:22
  369.4 13.5 %collective-permute-start.52 = (bf16[192,384]{1,0:T(8,128)(2,1)S(1)}, bf16[192,384]{1,0:T(8,128)(2,1)S(1)}, u32[]{:S(2)}, u32[]{:S(2)}) collective-permute-start(bf16[192,384]{1,0:T(8,128)(2,1)S(1)} %fusion.67), channel_id=1, source_target_pairs={{0,16},{4,20},{8,24},{12,28},{16,0},{20,4},{24,8},{28,12},{1,17},{... | collective-permute-start | bytes 442376 | tf_op jit(solution)/shard_map/ppermute | solution.py:22
  378.9 9.7 %collective-permute-start.51 = (bf16[1,192,384]{2,1,0:T(8,128)(2,1)S(1)}, bf16[1,192,384]{2,1,0:T(8,128)(2,1)S(1)}, u32[]{:S(2)}, u32[]{:S(2)}) collective-permute-start(bf16[1,192,384]{2,1,0:T(8,128)(2,1)S(1)} %fusion.71), channel_id=1, source_target_pairs={{0,16},{4,20},{8,24},{12,28},{16,0},{20,4},{24,8},{28,12},{1,17},{... | collective-permute-start | bytes 442376 | tf_op jit(solution)/shard_map/ppermute | solution.py:22
  380.7 13.4 %collective-permute-start.56 = (bf16[2,192,384]{2,1,0:T(8,128)(2,1)S(1)}, bf16[2,192,384]{2,1,0:T(8,128)(2,1)S(1)}, u32[]{:S(2)}, u32[]{:S(2)}) collective-permute-start(bf16[2,192,384]{2,1,0:T(8,128)(2,1)S(1)} %get-tuple-element.360), channel_id=1, source_target_pairs={{0,8},{4,12},{8,0},{12,4},{16,24},{20,28},{24,16},{28,20},{1,9},{5... | collective-permute-start | bytes 884744 | tf_op jit(solution)/shard_map/ppermute | solution.py:22
  383.0 11.2 %collective-permute-start.59 = (bf16[1,192,384]{2,1,0:T(8,128)(2,1)S(1)}, bf16[1,192,384]{2,1,0:T(8,128)(2,1)S(1)}, u32[]{:S(2)}, u32[]{:S(2)}) collective-permute-start(bf16[1,192,384]{2,1,0:T(8,128)(2,1)S(1)} %fusion.74), channel_id=1, source_target_pairs={{0,16},{4,20},{8,24},{12,28},{16,0},{20,4},{24,8},{28,12},{1,17},{... | collective-permute-start | bytes 442376 | tf_op jit(solution)/shard_map/ppermute | solution.py:22
  388.7 14.8 %collective-permute-start.58 = (bf16[2,192,384]{2,1,0:T(8,128)(2,1)S(1)}, bf16[2,192,384]{2,1,0:T(8,128)(2,1)S(1)}, u32[]{:S(2)}, u32[]{:S(2)}) collective-permute-start(bf16[2,192,384]{2,1,0:T(8,128)(2,1)S(1)} %pad_maximum_fusion.13), channel_id=1, source_target_pairs={{0,8},{4,12},{8,0},{12,4},{16,24},{20,28},{24,16},{28,20},{1,9},{5... | collective-permute-start | bytes 884744 | tf_op jit(solution)/shard_map/ppermute | solution.py:22
  392.2 14.6 %collective-permute-start.55 = (bf16[2,2,208,384]{3,2,1,0:T(8,128)(2,1)S(1)}, bf16[2,2,208,384]{3,2,1,0:T(8,128)(2,1)S(1)}, u32[]{:S(2)}, u32[]{:S(2)}) collective-permute-start(bf16[2,2,208,384]{3,2,1,0:T(8,128)(2,1)S(1)} %get-tuple-element.339), channel_id=1, source_target_pairs={{0,4},{4,0},{8,12},{12,8},{16,20},{20,16},{24,28},{28,24},{1,5},{5... | collective-permute-start | bytes 1916936 | tf_op jit(solution)/shard_map/ppermute | solution.py:22
  394.1 9.5 %collective-permute-start.57 = (bf16[192,384]{1,0:T(8,128)(2,1)S(1)}, bf16[192,384]{1,0:T(8,128)(2,1)S(1)}, u32[]{:S(2)}, u32[]{:S(2)}) collective-permute-start(bf16[192,384]{1,0:T(8,128)(2,1)S(1)} %fusion.77), channel_id=1, source_target_pairs={{0,16},{4,20},{8,24},{12,28},{16,0},{20,4},{24,8},{28,12},{1,17},{... | collective-permute-start | bytes 442376 | tf_op jit(solution)/shard_map/ppermute | solution.py:22
  394.2 15.7 %collective-permute-start.61 = (bf16[2,192,384]{2,1,0:T(8,128)(2,1)S(1)}, bf16[2,192,384]{2,1,0:T(8,128)(2,1)S(1)}, u32[]{:S(2)}, u32[]{:S(2)}) collective-permute-start(bf16[2,192,384]{2,1,0:T(8,128)(2,1)S(1)} %pad_maximum_fusion.14), channel_id=1, source_target_pairs={{0,8},{4,12},{8,0},{12,4},{16,24},{20,28},{24,16},{28,20},{1,9},{5... | collective-permute-start | bytes 884744 | tf_op jit(solution)/shard_map/ppermute | solution.py:22
  407.0 10.7 %collective-permute-start.60 = (bf16[2,208,384]{2,1,0:T(8,128)(2,1)S(1)}, bf16[2,208,384]{2,1,0:T(8,128)(2,1)S(1)}, u32[]{:S(2)}, u32[]{:S(2)}) collective-permute-start(bf16[2,208,384]{2,1,0:T(8,128)(2,1)S(1)} %get-tuple-element.357), channel_id=1, source_target_pairs={{0,8},{4,12},{8,0},{12,4},{16,24},{20,28},{24,16},{28,20},{1,9},{5... | collective-permute-start | bytes 958472 | tf_op jit(solution)/shard_map/ppermute | solution.py:22
  407.1 10.8 %collective-permute-start.63 = (bf16[1,192,384]{2,1,0:T(8,128)(2,1)S(1)}, bf16[1,192,384]{2,1,0:T(8,128)(2,1)S(1)}, u32[]{:S(2)}, u32[]{:S(2)}) collective-permute-start(bf16[1,192,384]{2,1,0:T(8,128)(2,1)S(1)} %fusion.76), channel_id=1, source_target_pairs={{0,16},{4,20},{8,24},{12,28},{16,0},{20,4},{24,8},{28,12},{1,17},{... | collective-permute-start | bytes 442376 | tf_op jit(solution)/shard_map/ppermute | solution.py:22
  417.9 11.6 %collective-permute-start.65 = (bf16[2,192,384]{2,1,0:T(8,128)(2,1)S(1)}, bf16[2,192,384]{2,1,0:T(8,128)(2,1)S(1)}, u32[]{:S(2)}, u32[]{:S(2)}) collective-permute-start(bf16[2,192,384]{2,1,0:T(8,128)(2,1)S(1)} %pad_maximum_fusion.15), channel_id=1, source_target_pairs={{0,8},{4,12},{8,0},{12,4},{16,24},{20,28},{24,16},{28,20},{1,9},{5... | collective-permute-start | bytes 884744 | tf_op jit(solution)/shard_map/ppermute | solution.py:22
  426.0 9.3 %collective-permute-start.64 = (bf16[1,208,384]{2,1,0:T(8,128)(2,1)S(1)}, bf16[1,208,384]{2,1,0:T(8,128)(2,1)S(1)}, u32[]{:S(2)}, u32[]{:S(2)}) collective-permute-start(bf16[1,208,384]{2,1,0:T(8,128)(2,1)S(1)} %fusion.61), channel_id=1, source_target_pairs={{0,16},{4,20},{8,24},{12,28},{16,0},{20,4},{24,8},{28,12},{1,17},{... | collective-permute-start | bytes 479240 | tf_op jit(solution)/shard_map/ppermute | solution.py:22
  426.1 22.0 %collective-permute-start.72 = (bf16[4,192,384]{2,1,0:T(8,128)(2,1)S(1)}, bf16[4,192,384]{2,1,0:T(8,128)(2,1)S(1)}, u32[]{:S(2)}, u32[]{:S(2)}) collective-permute-start(bf16[4,192,384]{2,1,0:T(8,128)(2,1)S(1)} %pad_maximum_fusion.5.near), channel_id=1, source_target_pairs={{0,4},{4,0},{8,12},{12,8},{16,20},{20,16},{24,28},{28,24},{1,5},{5... | collective-permute-start | bytes 1769480 | tf_op jit(solution)/shard_map/ppermute | solution.py:22
  444.0 73.3 %collective-permute-start.67 = (bf16[4,208,384]{2,1,0:T(8,128)(2,1)S(1)}, bf16[4,208,384]{2,1,0:T(8,128)(2,1)S(1)}, u32[]{:S(2)}, u32[]{:S(2)}) collective-permute-start(bf16[4,208,384]{2,1,0:T(8,128)(2,1)S(1)} %pad_maximum_fusion.2.near), channel_id=1, source_target_pairs={{0,4},{4,0},{8,12},{12,8},{16,20},{20,16},{24,28},{28,24},{1,5},{5... | collective-permute-start | bytes 1916936 | tf_op jit(solution)/shard_map/ppermute | solution.py:22
  445.4 28.6 %collective-permute-start.68 = (bf16[4,192,384]{2,1,0:T(8,128)(2,1)S(1)}, bf16[4,192,384]{2,1,0:T(8,128)(2,1)S(1)}, u32[]{:S(2)}, u32[]{:S(2)}) collective-permute-start(bf16[4,192,384]{2,1,0:T(8,128)(2,1)S(1)} %pad_maximum_fusion.6.near), channel_id=1, source_target_pairs={{0,4},{4,0},{8,12},{12,8},{16,20},{20,16},{24,28},{28,24},{1,5},{5... | collective-permute-start | bytes 1769480 | tf_op jit(solution)/shard_map/ppermute | solution.py:22
  446.1 40.6 %collective-permute-start.69 = (bf16[4,192,384]{2,1,0:T(8,128)(2,1)S(1)}, bf16[4,192,384]{2,1,0:T(8,128)(2,1)S(1)}, u32[]{:S(2)}, u32[]{:S(2)}) collective-permute-start(bf16[4,192,384]{2,1,0:T(8,128)(2,1)S(1)} %pad_maximum_fusion.8.near), channel_id=1, source_target_pairs={{0,4},{4,0},{8,12},{12,8},{16,20},{20,16},{24,28},{28,24},{1,5},{5... | collective-permute-start | bytes 1769480 | tf_op jit(solution)/shard_map/ppermute | solution.py:22
  447.5 51.8 %collective-permute-start.71 = (bf16[4,192,384]{2,1,0:T(8,128)(2,1)S(1)}, bf16[4,192,384]{2,1,0:T(8,128)(2,1)S(1)}, u32[]{:S(2)}, u32[]{:S(2)}) collective-permute-start(bf16[4,192,384]{2,1,0:T(8,128)(2,1)S(1)} %pad_maximum_fusion.7.near), channel_id=1, source_target_pairs={{0,4},{4,0},{8,12},{12,8},{16,20},{20,16},{24,28},{28,24},{1,5},{5... | collective-permute-start | bytes 1769480 | tf_op jit(solution)/shard_map/ppermute | solution.py:22
  448.1 60.9 %collective-permute-start.70 = (bf16[4,192,384]{2,1,0:T(8,128)(2,1)S(1)}, bf16[4,192,384]{2,1,0:T(8,128)(2,1)S(1)}, u32[]{:S(2)}, u32[]{:S(2)}) collective-permute-start(bf16[4,192,384]{2,1,0:T(8,128)(2,1)S(1)} %pad_maximum_fusion.9.near), channel_id=1, source_target_pairs={{0,4},{4,0},{8,12},{12,8},{16,20},{20,16},{24,28},{28,24},{1,5},{5... | collective-permute-start | bytes 1769480 | tf_op jit(solution)/shard_map/ppermute | solution.py:22
  (62 other events, 709.2 us)

commit v4 on v3

--- a/solution.py
+++ b/solution.py
@@ -402,7 +402,7 @@
 ANY = pl.BlockSpec(memory_space=pl.ANY)
 
 
-def call(kernel, name, in_specs, out_specs, out_shape, scratch, args, aliases=()):
+def call(kernel, name, time, in_specs, out_specs, out_shape, scratch, args, aliases=()):
     return pl.pallas_call(
         kernel,
         name=name,
@@ -412,7 +412,9 @@
         scratch_shapes=scratch,
         input_output_aliases=dict(aliases),
         compiler_params=pltpu.CompilerParams(vmem_limit_bytes=VMEM_BYTES),
-        cost_estimate=pl.CostEstimate(flops=1, bytes_accessed=1, transcendentals=0),
+        cost_estimate=pl.CostEstimate(
+            flops=int(time * 1.1e9), bytes_accessed=int(time * 3.6e6), transcendentals=0
+        ),
     )(*args)
 
 
@@ -431,11 +433,11 @@
     return (a.astype(f32) + b.astype(f32)).astype(low)
 
 
-WAYS = ("xyzw", "yxzw", "xyzw", "xyzw", "xyzw", "xyzw")
+WAYS = ("xyzw", "xyzw", "yxzw", "xyzw", "xyzw", "xyzw")
 BACKS = ("wzy",) * 6
 PLAN = (
-    "out1", "in1", 0, "attn1", "out0", 0, 2, 1, 3, 0, "in0", 0, 2, 0, 0, 1, 2, 0, 3, 2, 4, 1, 0, "attn0", 2,
-    3, 1, 5, 4, 3, 2, 3, 2, 4, 1, 3, 5, 4, 1, 3, 4, 5, 1, 5, 4, 5, 4, 5, 3, 5, 4, 1, 2, 5,
+    "out1", 0, "in1", "attn1", 0, 1, "out0", 0, 2, 0, 3, 1, 0, "in0", 0, 2, 4, 0, 1, 3, 2, 1, 0, "attn0", 1,
+    3, 4, 5, 2, 1, 3, 2, 1, 4, 3, 2, 5, 1, 4, 3, 2, 4, 5, 3, 5, 4, 2, 5, 4, 3, 5, 5, 4, 5,
 )
 
 
@@ -575,11 +577,12 @@
         lax.ppermute(packed, "narrow", [(i, i ^ away) for i in range(4)]) for away in (1, 2, 3)
     ]
     send_core(0)
+    halves[1:] = order.wait(halves[1:])
     arrive(("c", 0))
+    send_core(1)
     near_x[0], others = order.wait((near_x[0], others))
     far_x[0] = swap(near_x[0], "wide", 1)
-    send_x(1, 2)
-    send_core(1)
+    send_x(1)
 
     def in_order(low_one, high_one, bit):
         swapped = (me & bit) != 0
@@ -617,6 +620,7 @@
         outs = call(
             functools.partial(attn_fwd_kernel, layer),
             "attn_fwd",
+            13,
             [SMEM, SMEM] + [VMEM] * 3 + [ANY] * 7,
             [VMEM] * 5,
             [shape((tokens, 3 * width), low), shape((HEADS, tokens, tokens), low), rows_low, rows_f32, column_f32],
@@ -631,6 +635,7 @@
         outs = call(
             functools.partial(ffn_fwd_kernel, layer),
             "ffn_fwd",
+            10,
             [SMEM] + [VMEM] * 3 + [ANY] * 10,
             [VMEM] * 5,
             [shape((tokens, ffn), low), shape((tokens, ffn), f32), rows_f32, column_f32, rows_low],
@@ -645,6 +650,7 @@
         outs = call(
             functools.partial(out_bwd_kernel, layer, way),
             "out_bwd",
+            8,
             [SMEM] + [VMEM] * 5,
             [VMEM] * 3 + [ANY] * 2,
             [rows_low, rows_f32, eight_f32] + pieces(share),
@@ -659,6 +665,7 @@
         outs = call(
             functools.partial(in_bwd_kernel, layer, way),
             "in_bwd",
+            14,
             [SMEM] + [VMEM] * 6 + [ANY] * 10,
             [VMEM] * 3 + [ANY] * 2,
             [rows_f32, eight_f32, shape((1, ffn), f32)] + pieces(share),
@@ -682,6 +689,7 @@
         outs = call(
             functools.partial(attn_bwd_kernel, layer, way),
             "attn_bwd",
+            16,
             [SMEM] + [VMEM] * 5 + [ANY] * 7 + [VMEM] * len(small_others),
             [VMEM] * 2 + [ANY] * 2,
             [rows_low, eight_f32] + pieces(rows),
@@ -714,6 +722,7 @@
         outs = call(
             functools.partial(unpack_kernel, layer, name, slab.back, len(earlier)),
             "unpack",
+            4,
             [SMEM] + [ANY] * (2 + len(earlier)),
             [ANY] * len(dims) + [VMEM] * len(extra),
             [shape(d, f32) for d in dims + extra],
@@ -729,18 +738,21 @@
         order.last = outs[-1]
         return tuple(outs)
 
-    arrive(("y", 0), ("x", 1))
+    arrive(("x", 1))
+    send_x(2)
+    arrive(("y", 0), ("c", 3), ("d", 0), ("x", 2))
     send_x(3)
-    arrive(("c", 3), ("d", 0), ("x", 2))
-    send_x(4)
+    arrive(("y", 1))
     first_attn = attn_forward(0, tables_in)
     arrive(("x", 3))
+    send_x(4)
+    arrive(("y", 2), ("d", 1), ("d", 2))
+    first_ffn = ffn_forward(0, first_attn[3])
+    arrive(("x", 4))
     send_x(5)
-    arrive(("y", 1), ("y", 2), ("d", 1), ("d", 2))
-    first_ffn = ffn_forward(0, first_attn[3])
-    arrive(("x", 4), ("y", 3), ("d", 3), ("x", 5))
+    arrive(("y", 3), ("d", 3))
     second_attn = attn_forward(1, first_ffn[4])
-    arrive(("y", 4), ("y", 5), ("d", 4), ("d", 5))
+    arrive(("x", 5), ("y", 4), ("y", 5), ("d", 4), ("d", 5))
     second_ffn = ffn_forward(1, second_attn[3])
     mixed_out = second_ffn[4]
     inputs = (tables_in, first_ffn[4])

time: 527 us -> 488 us (0.926)
  waiting for transfers between devices: 263 us -> 221 us
  starting transfers between devices: 68.2 us -> 74.9 us
    ppermute x70, waiting for transfers between devices: 251 us -> 221 us  [swap(): return lax.ppermute(value, axis, [(i, i ^ bit) for i in range(count)])]
    ppermute x3, waiting for transfers between devices: 12 us -> 0.01 us  [body(): lax.ppermute(packed, 'narrow', [(i, i ^ away) for i in range(4)])]
    ppermute x70, starting transfers between devices: 66.3 us -> 71.8 us  [swap(): return lax.ppermute(value, axis, [(i, i ^ bit) for i in range(count)])]
    another operation x8, local copies, waits for them, and re-layouts: 0.04 us -> 5.46 us  [body(): jnp.stack(short, axis=1)]
    unnamed x111 -> x75, local copies, waits for them, and re-layouts: 11.2 us -> 9.41 us
  transfers between devices with their start and end apart: 73 -> 73, of which waited for: 41 -> 36; matrix products, arithmetic and copies ran while one was open for 6% -> 5% of each run, Pallas kernels for 20% -> 19%
where the time goes in v4:
time: 488 us; the launch traced here: 484 us
  waiting for transfers between devices  221 us (45%)
  Pallas kernels  144 us (30%)
  starting transfers between devices  74.9 us (15%)
  local copies, waits for them, and re-layouts  21.6 us (4%)
  other arithmetic  18.7 us (4%)
    ppermute x70, waiting for transfers between devices, swap(): return lax.ppermute(value, axis, [(i, i ^ bit) for i in range(count)])  221 us
    pallas_call x16, Pallas kernels, call(): pl.pallas_call(kernel, name=name, in_specs=in_specs, out_specs=out_specs,...  144 us
    ppermute x70, starting transfers between devices, swap(): return lax.ppermute(value, axis, [(i, i ^ bit) for i in range(count)])  71.8 us
    convert_element_type x24, other arithmetic, added(): return (a.astype(f32) + b.astype(f32)).astype(low)  15.1 us
  transfers between devices with their start and end apart: 73, of which 36 were waited for; matrix products, arithmetic and copies ran while one was open for 5% of the time, Pallas kernels for 19%

profile of v4, /device:TPU:0, one launch (start us, length us, event | category | flops | bytes accessed | tf_op | source)
XLA Modules:
  0.0 483.6 jit_solution(6851390418348859961)
XLA Ops:
  6.9 2.4 collective-permute-start.3
  17.1 11.1 %collective-permute-done.rest_4_ = bf16[96,3072]{1,0:T(8,128)(2,1)} collective-permute-done((bf16[96,3072]{1,0:T(8,128)(2,1)S(1)}, bf16[96,3072]{1,0:T(8,128)(2,1)}, u32[]{:S(2)}, u32[]{:S(2)}) %collective-permute-start) | collective-permute-done | bytes 589856 | tf_op jit(solution)/shard_map/ppermute | solution.py:22
  31.5 4.6 collective-permute-done.10.rest_1_
  36.3 1.8 collective-permute-start.8
  39.6 12.5 %collective-permute-done.8.rest_5_ = bf16[96,3072]{1,0:T(8,128)(2,1)S(1)} collective-permute-done((bf16[96,3072]{1,0:T(8,128)(2,1)}, bf16[96,3072]{1,0:T(8,128)(2,1)S(1)}, u32[]{:S(2)}, u32[]{:S(2)}) %collective-permute-start.8) | collective-permute-done | bytes 589856 | tf_op jit(solution)/shard_map/ppermute | solution.py:22
  53.6 1.8 collective-permute-start.12
  57.0 12.4 %collective-permute-done.12.rest_7_ = bf16[384,768]{1,0:T(8,128)(2,1)S(1)} collective-permute-done((bf16[384,768]{1,0:T(8,128)(2,1)S(1)}, bf16[384,768]{1,0:T(8,128)(2,1)S(1)}, u32[]{:S(2)}, u32[]{:S(2)}) %collective-permute-start.12) | collective-permute-done | bytes 589856 | tf_op jit(solution)/shard_map/ppermute | solution.py:22
  69.3 1.7 collective-permute-start.13
  73.5 10.7 %collective-permute-done.13.rest_8_ = bf16[384,768]{1,0:T(8,128)(2,1)S(1)} collective-permute-done((bf16[384,768]{1,0:T(8,128)(2,1)S(1)}, bf16[384,768]{1,0:T(8,128)(2,1)S(1)}, u32[]{:S(2)}, u32[]{:S(2)}) %collective-permute-start.13) | collective-permute-done | bytes 589856 | tf_op jit(solution)/shard_map/ppermute | solution.py:22
  85.1 12.2 %attn_fwd.2 = (bf16[256,2304]{1,0:T(8,128)(2,1)}, bf16[12,256,256]{2,1,0:T(8,128)(2,1)}, bf16[256,768]{1,0:T(8,128)(2,1)}, f32[256,768]{1,0:T(8,128)}, f32[256,1]{1,0:T(8,128)}) custom-call(s32[6]{0:T(128)} %stack.74.ids, s32[1]{0:T(128)S(6)} %copy.58.length, bf16[256,768]{1,0:T(8,128)(2,1)} %x.2, s32[1,256]{1,0:T(1,128)} %cell_row.3, ...), custom_call_target="tpu_custom_call" | custom-call | flops 14300000256 | bytes 46800000 | tf_op jit(solution)/shard_map/attn_fwd/pallas_call | solution.py:406
  97.3 1.8 collective-permute-start.17
  99.1 14.0 %collective-permute-done.17.rest_5_ = bf16[96,3072]{1,0:T(8,128)(2,1)S(1)} collective-permute-done((bf16[96,3072]{1,0:T(8,128)(2,1)S(1)}, bf16[96,3072]{1,0:T(8,128)(2,1)S(1)}, u32[]{:S(2)}, u32[]{:S(2)}) %collective-permute-start.17) | collective-permute-done | bytes 589856 | tf_op jit(solution)/shard_map/ppermute | solution.py:22
  113.9 1.7 collective-permute-start.19
  115.7 10.0 %ffn_fwd.2 = (bf16[256,3072]{1,0:T(8,128)(2,1)}, f32[256,3072]{1,0:T(8,128)}, f32[256,768]{1,0:T(8,128)}, f32[256,1]{1,0:T(8,128)}, bf16[256,768]{1,0:T(8,128)(2,1)}) custom-call(s32[6]{0:T(128)} %stack.74.ids, f32[256,768]{1,0:T(8,128)} %get-tuple-element.194.unit_one, f32[2,1,3072]{2,1,0:T(1,128)} %reshape.474.in_bias, f32[2,8,768]{2,1,0:T(8,128)} %reshape.473.small, ...), custom_call_target="tpu_custom_call" | custom-call | flops 11000000512 | bytes 36000000 | tf_op jit(solution)/shard_map/ffn_fwd/pallas_call | solution.py:406
  125.7 4.0 collective-permute-done.19.rest_2_
  134.0 12.1 %attn_fwd.3 = (bf16[256,2304]{1,0:T(8,128)(2,1)}, bf16[12,256,256]{2,1,0:T(8,128)(2,1)}, bf16[256,768]{1,0:T(8,128)(2,1)}, f32[256,768]{1,0:T(8,128)}, f32[256,1]{1,0:T(8,128)}) custom-call(s32[6]{0:T(128)} %stack.74.ids, s32[1]{0:T(128)S(6)} %copy.58.length, bf16[256,768]{1,0:T(8,128)(2,1)} %get-tuple-element.200.x, s32[1,256]{1,0:T(1,128)} %cell_row.3, ...), custom_call_target="tpu_custom_call" | custom-call | flops 14300000256 | bytes 46800000 | tf_op jit(solution)/shard_map/attn_fwd/pallas_call | solution.py:406
  146.9 13.6 %collective-permute-done.21.rest_8_ = bf16[384,768]{1,0:T(8,128)(2,1)S(1)} collective-permute-done((bf16[384,768]{1,0:T(8,128)(2,1)S(1)}, bf16[384,768]{1,0:T(8,128)(2,1)S(1)}, u32[]{:S(2)}, u32[]{:S(2)}) %collective-permute-start.21) | collective-permute-done | bytes 589856 | tf_op jit(solution)/shard_map/ppermute | solution.py:22
  160.7 2.8 collective-permute-done.23.rest_9_
  164.6 10.0 %ffn_fwd.3 = (bf16[256,3072]{1,0:T(8,128)(2,1)}, f32[256,3072]{1,0:T(8,128)}, f32[256,768]{1,0:T(8,128)}, f32[256,1]{1,0:T(8,128)}, bf16[256,768]{1,0:T(8,128)(2,1)}) custom-call(s32[6]{0:T(128)} %stack.74.ids, f32[256,768]{1,0:T(8,128)} %get-tuple-element.212.unit_one, f32[2,1,3072]{2,1,0:T(1,128)} %reshape.474.in_bias, f32[2,8,768]{2,1,0:T(8,128)} %reshape.473.small, ...), custom_call_target="tpu_custom_call" | custom-call | flops 11000000512 | bytes 36000000 | tf_op jit(solution)/shard_map/ffn_fwd/pallas_call | solution.py:406
  174.6 8.6 %out_bwd.2 = (bf16[256,768]{1,0:T(8,128)(2,1)}, f32[256,768]{1,0:T(8,128)}, f32[8,768]{1,0:T(8,128)}, bf16[2,2,2,2,192,384]{5,4,3,2,1,0:T(8,128)(2,1)}, bf16[2,2,2,2,192,384]{5,4,3,2,1,0:T(8,128)(2,1)}) custom-call(s32[6]{0:T(128)} %stack.74.ids, bf16[256,768]{1,0:T(8,128)(2,1)} %grad, f32[256,768]{1,0:T(8,128)} %get-tuple-element.216.unit_two, ...), custom_call_target="tpu_custom_call" | custom-call | flops 8800000000 | bytes 28800000 | tf_op jit(solution)/shard_map/out_bwd/pallas_call | solution.py:406
  183.5 4.6 collective-permute-done.25
  188.1 2.3 add_convert_fusion.10
  190.4 14.3 %in_bwd.2 = (f32[256,768]{1,0:T(8,128)}, f32[8,768]{1,0:T(8,128)}, f32[1,3072]{1,0:T(1,128)}, bf16[2,2,2,2,192,384]{5,4,3,2,1,0:T(8,128)(2,1)}, bf16[2,2,2,2,192,384]{5,4,3,2,1,0:T(8,128)(2,1)}) custom-call(s32[6]{0:T(128)} %stack.74.ids, bf16[256,768]{1,0:T(8,128)(2,1)} %get-tuple-element.223.d_ffn, f32[256,768]{1,0:T(8,128)} %get-tuple-element.224.d_resid_two, ...), custom_call_target="tpu_custom_call" | custom-call | flops 15399999488 | bytes 50400000 | tf_op jit(solution)/shard_map/in_bwd/pallas_call | solution.py:406
  205.7 15.5 %attn_bwd.2 = (bf16[256,768]{1,0:T(8,128)(2,1)}, f32[8,768]{1,0:T(8,128)}, bf16[2,2,2,2,192,384]{5,4,3,2,1,0:T(8,128)(2,1)}, bf16[2,2,2,2,192,384]{5,4,3,2,1,0:T(8,128)(2,1)}) custom-call(s32[6]{0:T(128)} %stack.74.ids, f32[256,768]{1,0:T(8,128)} %get-tuple-element.228.d_resid, bf16[256,768]{1,0:T(8,128)(2,1)} %get-tuple-element.200.x, ...), custom_call_target="tpu_custom_call" | custom-call | flops 17600000000 | bytes 57600000 | tf_op jit(solution)/shard_map/attn_bwd/pallas_call | solution.py:406
  221.3 11.8 %collective-permute-done.27 = bf16[2,2,2,192,384]{4,3,2,1,0:T(8,128)(2,1)S(1)} collective-permute-done((bf16[2,2,2,192,384]{4,3,2,1,0:T(8,128)(2,1)S(1)}, bf16[2,2,2,192,384]{4,3,2,1,0:T(8,128)(2,1)S(1)}, u32[]{:S(2)}, u32[]{:S(2)}) %collective-permute-start.27) | collective-permute-done | bytes 1179680 | tf_op jit(solution)/shard_map/ppermute | solution.py:22
  236.5 8.8 %out_bwd.3 = (bf16[256,768]{1,0:T(8,128)(2,1)}, f32[256,768]{1,0:T(8,128)}, f32[8,768]{1,0:T(8,128)}, bf16[2,2,2,2,192,384]{5,4,3,2,1,0:T(8,128)(2,1)}, bf16[2,2,2,2,192,384]{5,4,3,2,1,0:T(8,128)(2,1)}) custom-call(s32[6]{0:T(128)} %stack.74.ids, bf16[256,768]{1,0:T(8,128)(2,1)} %get-tuple-element.238.grad, f32[256,768]{1,0:T(8,128)} %get-tuple-element.239.unit_two, ...), custom_call_target="tpu_custom_call" | custom-call | flops 8800000000 | bytes 28800000 | tf_op jit(solution)/shard_map/out_bwd/pallas_call | solution.py:406
  246.7 14.4 %collective-permute-done.28 = bf16[2,2,192,384]{3,2,1,0:T(8,128)(2,1)S(1)} collective-permute-done((bf16[2,2,192,384]{3,2,1,0:T(8,128)(2,1)S(1)}, bf16[2,2,192,384]{3,2,1,0:T(8,128)(2,1)S(1)}, u32[]{:S(2)}, u32[]{:S(2)}) %collective-permute-start.28) | collective-permute-done | bytes 589856 | tf_op jit(solution)/shard_map/ppermute | solution.py:22
  264.6 5.3 %collective-permute-done.29 = bf16[2,192,384]{2,1,0:T(8,128)(2,1)S(1)} collective-permute-done((bf16[2,192,384]{2,1,0:T(8,128)(2,1)S(1)}, bf16[2,192,384]{2,1,0:T(8,128)(2,1)S(1)}, u32[]{:S(2)}, u32[]{:S(2)}) %collective-permute-start.29) | collective-permute-done | bytes 294944 | tf_op jit(solution)/shard_map/ppermute | solution.py:22
  269.9 2.7 collective-permute-start.31
  275.3 3.3 collective-permute-done.31
  278.6 14.1 %in_bwd.3 = (f32[256,768]{1,0:T(8,128)}, f32[8,768]{1,0:T(8,128)}, f32[1,3072]{1,0:T(1,128)}, bf16[2,2,2,2,192,384]{5,4,3,2,1,0:T(8,128)(2,1)}, bf16[2,2,2,2,192,384]{5,4,3,2,1,0:T(8,128)(2,1)}) custom-call(s32[6]{0:T(128)} %stack.74.ids, bf16[256,768]{1,0:T(8,128)(2,1)} %get-tuple-element.253.d_ffn, f32[256,768]{1,0:T(8,128)} %get-tuple-element.254.d_resid_two, ...), custom_call_target="tpu_custom_call" | custom-call | flops 15399999488 | bytes 50400000 | tf_op jit(solution)/shard_map/in_bwd/pallas_call | solution.py:406
  295.9 16.1 %attn_bwd.3 = (bf16[256,768]{1,0:T(8,128)(2,1)}, f32[8,768]{1,0:T(8,128)}, bf16[2,2,2,2,208,384]{5,4,3,2,1,0:T(8,128)(2,1)}, bf16[2,2,2,2,208,384]{5,4,3,2,1,0:T(8,128)(2,1)}) custom-call(s32[6]{0:T(128)} %stack.74.ids, f32[256,768]{1,0:T(8,128)} %get-tuple-element.256.d_resid, bf16[256,768]{1,0:T(8,128)(2,1)} %x.2, ...), custom_call_target="tpu_custom_call" | custom-call | flops 17600000000 | bytes 57600000 | tf_op jit(solution)/shard_map/attn_bwd/pallas_call | solution.py:406
  312.2 9.6 %collective-permute-done.36 = bf16[2,2,2,192,384]{4,3,2,1,0:T(8,128)(2,1)} collective-permute-done((bf16[2,2,2,192,384]{4,3,2,1,0:T(8,128)(2,1)S(1)}, bf16[2,2,2,192,384]{4,3,2,1,0:T(8,128)(2,1)}, u32[]{:S(2)}, u32[]{:S(2)}) %collective-permute-start.36) | collective-permute-done | bytes 1179680 | tf_op jit(solution)/shard_map/ppermute | solution.py:22
  325.8 4.1 collective-permute-done.41
  330.8 3.2 collective-permute-done.40
  338.1 2.5 collective-permute-done.44
  340.7 3.1 collective-permute-done.43
  343.9 2.4 collective-permute-start.45
  348.0 4.5 collective-permute-done.45
  353.1 4.1 collective-permute-start.50
  357.3 6.3 %collective-permute-done.38 = bf16[2,2,2,192,384]{4,3,2,1,0:T(8,128)(2,1)S(1)} collective-permute-done((bf16[2,2,2,192,384]{4,3,2,1,0:T(8,128)(2,1)S(1)}, bf16[2,2,2,192,384]{4,3,2,1,0:T(8,128)(2,1)S(1)}, u32[]{:S(2)}, u32[]{:S(2)}) %collective-permute-start.38) | collective-permute-done | bytes 1179680 | tf_op jit(solution)/shard_map/ppermute | solution.py:22
  368.3 2.4 collective-permute-start.48
  370.7 2.6 collective-permute-done.49
  375.0 3.4 collective-permute-start.52
  378.4 4.8 collective-permute-done.54
  383.2 2.6 collective-permute-start.51
  387.0 6.0 %collective-permute-done.51 = bf16[1,192,384]{2,1,0:T(8,128)(2,1)S(1)} collective-permute-done((bf16[1,192,384]{2,1,0:T(8,128)(2,1)S(1)}, bf16[1,192,384]{2,1,0:T(8,128)(2,1)S(1)}, u32[]{:S(2)}, u32[]{:S(2)}) %collective-permute-start.51) | collective-permute-done | bytes 147488 | tf_op jit(solution)/shard_map/ppermute | solution.py:22
  394.1 6.6 %collective-permute-done.56 = bf16[2,192,384]{2,1,0:T(8,128)(2,1)S(1)} collective-permute-done((bf16[2,192,384]{2,1,0:T(8,128)(2,1)S(1)}, bf16[2,192,384]{2,1,0:T(8,128)(2,1)S(1)}, u32[]{:S(2)}, u32[]{:S(2)}) %collective-permute-start.56) | collective-permute-done | bytes 294944 | tf_op jit(solution)/shard_map/ppermute | solution.py:22
  404.0 4.3 collective-permute-done.58
  409.1 5.0 %collective-permute-done.55 = bf16[2,2,208,384]{3,2,1,0:T(8,128)(2,1)S(1)} collective-permute-done((bf16[2,2,208,384]{3,2,1,0:T(8,128)(2,1)S(1)}, bf16[2,2,208,384]{3,2,1,0:T(8,128)(2,1)S(1)}, u32[]{:S(2)}, u32[]{:S(2)}) %collective-permute-start.55) | collective-permute-done | bytes 639008 | tf_op jit(solution)/shard_map/ppermute | solution.py:22
  416.0 3.2 collective-permute-start.67
  419.3 2.7 collective-permute-done.60
  422.0 3.8 collective-permute-start.62
  425.9 3.7 unpack.10
  430.8 3.3 collective-permute-start.63
  434.0 3.7 unpack.8
  437.9 7.5 %collective-permute-done.66.far = bf16[4,192,384]{2,1,0:T(8,128)(2,1)S(1)} collective-permute-done((bf16[4,192,384]{2,1,0:T(8,128)(2,1)S(1)}, bf16[4,192,384]{2,1,0:T(8,128)(2,1)S(1)}, u32[]{:S(2)}, u32[]{:S(2)}) %collective-permute-start.66) | collective-permute-done | bytes 589856 | tf_op jit(solution)/shard_map/ppermute | solution.py:22
  446.1 3.7 unpack.6
  449.9 8.1 %collective-permute-done.71.far = bf16[4,192,384]{2,1,0:T(8,128)(2,1)S(1)} collective-permute-done((bf16[4,192,384]{2,1,0:T(8,128)(2,1)S(1)}, bf16[4,192,384]{2,1,0:T(8,128)(2,1)S(1)}, u32[]{:S(2)}, u32[]{:S(2)}) %collective-permute-start.71) | collective-permute-done | bytes 589856 | tf_op jit(solution)/shard_map/ppermute | solution.py:22
  458.8 3.7 unpack.11
  462.5 8.1 %collective-permute-done.69.far = bf16[4,192,384]{2,1,0:T(8,128)(2,1)S(1)} collective-permute-done((bf16[4,192,384]{2,1,0:T(8,128)(2,1)S(1)}, bf16[4,192,384]{2,1,0:T(8,128)(2,1)S(1)}, u32[]{:S(2)}, u32[]{:S(2)}) %collective-permute-start.69) | collective-permute-done | bytes 589856 | tf_op jit(solution)/shard_map/ppermute | solution.py:22
  471.4 3.7 unpack.9
  475.2 3.4 collective-permute-done.65.far
  479.3 3.8 unpack.7
  (247 shorter events, 77.9 us)
Async XLA Ops:
  6.9 10.2 %collective-permute-start.3 = (bf16[2,12,192]{2,1,0:T(8,128)(2,1)S(1)}, bf16[2,12,192]{2,1,0:T(8,128)(2,1)}, u32[]{:S(2)}, u32[]{:S(2)}) collective-permute-start(bf16[2,12,192]{2,1,0:T(8,128)(2,1)S(1)} %concatenate.98), channel_id=1, source_target_pairs={{0,3},{1,2},{2,1},{3,0},{4,7},{5,6},{6,5},{7,4},{8,11},{9,10},{10,... | collective-permute-start | bytes 27656 | tf_op jit(solution)/shard_map/ppermute | solution.py:577
  9.4 7.7 %collective-permute-start.2 = (bf16[2,12,192]{2,1,0:T(8,128)(2,1)S(1)}, bf16[2,12,192]{2,1,0:T(8,128)(2,1)}, u32[]{:S(2)}, u32[]{:S(2)}) collective-permute-start(bf16[2,12,192]{2,1,0:T(8,128)(2,1)S(1)} %concatenate.98), channel_id=1, source_target_pairs={{0,2},{1,3},{2,0},{3,1},{4,6},{5,7},{6,4},{7,5},{8,10},{9,11},{10,... | collective-permute-start | bytes 27656 | tf_op jit(solution)/shard_map/ppermute | solution.py:577
  10.0 19.0 %collective-permute-start.6 = (bf16[2,192,2304]{2,1,0:T(8,128)(2,1)}, bf16[2,192,2304]{2,1,0:T(8,128)(2,1)}, u32[]{:S(2)}, u32[]{:S(2)}) collective-permute-start(bf16[2,192,2304]{2,1,0:T(8,128)(2,1)} %rest_0_.15), channel_id=1, source_target_pairs={{0,1},{1,0},{2,3},{3,2},{4,5},{5,4},{6,7},{7,6},{8,9},{9,8},{10,11... | collective-permute-start | bytes 5308424 | tf_op jit(solution)/shard_map/ppermute | solution.py:22
  12.8 15.4 %collective-permute-start = (bf16[96,3072]{1,0:T(8,128)(2,1)S(1)}, bf16[96,3072]{1,0:T(8,128)(2,1)}, u32[]{:S(2)}, u32[]{:S(2)}) collective-permute-start(bf16[96,3072]{1,0:T(8,128)(2,1)S(1)} %pad_maximum_fusion.5), channel_id=1, source_target_pairs={{0,2},{1,3},{2,0},{3,1},{4,6},{5,7},{6,4},{7,5},{8,10},{9,11},{10,... | collective-permute-start | bytes 1769480 | tf_op jit(solution)/shard_map/ppermute | solution.py:22
  36.2 20.8 %collective-permute-start.11 = (bf16[2,768,768]{2,1,0:T(8,128)(2,1)}, bf16[2,768,768]{2,1,0:T(8,128)(2,1)S(1)}, u32[]{:S(2)}, u32[]{:S(2)}) collective-permute-start(bf16[2,768,768]{2,1,0:T(8,128)(2,1)} %rest_5_.7), channel_id=1, source_target_pairs={{0,1},{1,0},{2,3},{3,2},{4,5},{5,4},{6,7},{7,6},{8,9},{9,8},{10,11... | collective-permute-start | bytes 7077896 | tf_op jit(solution)/shard_map/ppermute | solution.py:22
  36.3 15.8 %collective-permute-start.8 = (bf16[96,3072]{1,0:T(8,128)(2,1)}, bf16[96,3072]{1,0:T(8,128)(2,1)S(1)}, u32[]{:S(2)}, u32[]{:S(2)}) collective-permute-start(bf16[96,3072]{1,0:T(8,128)(2,1)} %collective-permute-done.rest_4_), channel_id=1, source_target_pairs={{0,4},{4,0},{8,12},{12,8},{16,20},{20,16},{24,28},{28,24},{1,5},{5... | collective-permute-start | bytes 1769480 | tf_op jit(solution)/shard_map/ppermute | solution.py:22
  38.1 15.5 %collective-permute-start.4 = (bf16[96,3072]{1,0:T(8,128)(2,1)S(1)}, bf16[96,3072]{1,0:T(8,128)(2,1)S(1)}, u32[]{:S(2)}, u32[]{:S(2)}) collective-permute-start(bf16[96,3072]{1,0:T(8,128)(2,1)S(1)} %get-tuple-element.178), channel_id=1, source_target_pairs={{0,2},{1,3},{2,0},{3,1},{4,6},{5,7},{6,4},{7,5},{8,10},{9,11},{10,... | collective-permute-start | bytes 1769480 | tf_op jit(solution)/shard_map/ppermute | solution.py:22
  53.6 15.7 %collective-permute-start.12 = (bf16[384,768]{1,0:T(8,128)(2,1)S(1)}, bf16[384,768]{1,0:T(8,128)(2,1)S(1)}, u32[]{:S(2)}, u32[]{:S(2)}) collective-permute-start(bf16[384,768]{1,0:T(8,128)(2,1)S(1)} %get-tuple-element.190), channel_id=1, source_target_pairs={{0,2},{1,3},{2,0},{3,1},{4,6},{5,7},{6,4},{7,5},{8,10},{9,11},{10,... | collective-permute-start | bytes 1769480 | tf_op jit(solution)/shard_map/ppermute | solution.py:22
  55.4 16.3 %collective-permute-start.5 = (bf16[96,3072]{1,0:T(8,128)(2,1)S(1)}, bf16[96,3072]{1,0:T(8,128)(2,1)S(1)}, u32[]{:S(2)}, u32[]{:S(2)}) collective-permute-start(bf16[96,3072]{1,0:T(8,128)(2,1)S(1)} %collective-permute-done.4.rest_2_), channel_id=1, source_target_pairs={{0,4},{4,0},{8,12},{12,8},{16,20},{20,16},{24,28},{28,24},{1,5},{5... | collective-permute-start | bytes 1769480 | tf_op jit(solution)/shard_map/ppermute | solution.py:22
  69.3 14.9 %collective-permute-start.13 = (bf16[384,768]{1,0:T(8,128)(2,1)S(1)}, bf16[384,768]{1,0:T(8,128)(2,1)S(1)}, u32[]{:S(2)}, u32[]{:S(2)}) collective-permute-start(bf16[384,768]{1,0:T(8,128)(2,1)S(1)} %collective-permute-done.12.rest_7_), channel_id=1, source_target_pairs={{0,4},{4,0},{8,12},{12,8},{16,20},{20,16},{24,28},{28,24},{1,5},{5... | collective-permute-start | bytes 1769480 | tf_op jit(solution)/shard_map/ppermute | solution.py:22
  71.9 42.1 %collective-permute-start.15 = (bf16[192,3072]{1,0:T(8,128)(2,1)S(1)}, bf16[192,3072]{1,0:T(8,128)(2,1)}, u32[]{:S(2)}, u32[]{:S(2)}) collective-permute-start(bf16[192,3072]{1,0:T(8,128)(2,1)S(1)} %pad_maximum_fusion), channel_id=1, source_target_pairs={{0,1},{1,0},{2,3},{3,2},{4,5},{5,4},{6,7},{7,6},{8,9},{9,8},{10,11... | collective-permute-start | bytes 3538952 | tf_op jit(solution)/shard_map/ppermute | solution.py:22
  71.9 25.3 %collective-permute-start.16 = (bf16[96,3072]{1,0:T(8,128)(2,1)S(1)}, bf16[96,3072]{1,0:T(8,128)(2,1)S(1)}, u32[]{:S(2)}, u32[]{:S(2)}) collective-permute-start(bf16[96,3072]{1,0:T(8,128)(2,1)S(1)} %pad_maximum_fusion.6), channel_id=1, source_target_pairs={{0,2},{1,3},{2,0},{3,1},{4,6},{5,7},{6,4},{7,5},{8,10},{9,11},{10,... | collective-permute-start | bytes 1769480 | tf_op jit(solution)/shard_map/ppermute | solution.py:22
  85.0 30.6 %collective-permute-start.14 = (bf16[768,768]{1,0:T(8,128)(2,1)S(1)}, bf16[768,768]{1,0:T(8,128)(2,1)}, u32[]{:S(2)}, u32[]{:S(2)}) collective-permute-start(bf16[768,768]{1,0:T(8,128)(2,1)S(1)} %pad_maximum_fusion.2), channel_id=1, source_target_pairs={{0,1},{1,0},{2,3},{3,2},{4,5},{5,4},{6,7},{7,6},{8,9},{9,8},{10,11... | collective-permute-start | bytes 3538952 | tf_op jit(solution)/shard_map/ppermute | solution.py:22
  97.3 15.8 %collective-permute-start.17 = (bf16[96,3072]{1,0:T(8,128)(2,1)S(1)}, bf16[96,3072]{1,0:T(8,128)(2,1)S(1)}, u32[]{:S(2)}, u32[]{:S(2)}) collective-permute-start(bf16[96,3072]{1,0:T(8,128)(2,1)S(1)} %collective-permute-done.16.rest_4_), channel_id=1, source_target_pairs={{0,4},{4,0},{8,12},{12,8},{16,20},{20,16},{24,28},{28,24},{1,5},{5... | collective-permute-start | bytes 1769480 | tf_op jit(solution)/shard_map/ppermute | solution.py:22
  113.9 19.0 %collective-permute-start.18 = (bf16[192,3072]{1,0:T(8,128)(2,1)S(1)}, bf16[192,3072]{1,0:T(8,128)(2,1)S(1)}, u32[]{:S(2)}, u32[]{:S(2)}) collective-permute-start(bf16[192,3072]{1,0:T(8,128)(2,1)S(1)} %pad_maximum_fusion.3), channel_id=1, source_target_pairs={{0,1},{1,0},{2,3},{3,2},{4,5},{5,4},{6,7},{7,6},{8,9},{9,8},{10,11... | collective-permute-start | bytes 3538952 | tf_op jit(solution)/shard_map/ppermute | solution.py:22
  113.9 15.7 %collective-permute-start.19 = (bf16[96,3072]{1,0:T(8,128)(2,1)S(1)}, bf16[96,3072]{1,0:T(8,128)(2,1)S(1)}, u32[]{:S(2)}, u32[]{:S(2)}) collective-permute-start(bf16[96,3072]{1,0:T(8,128)(2,1)S(1)} %get-tuple-element.202), channel_id=1, source_target_pairs={{0,2},{1,3},{2,0},{3,1},{4,6},{5,7},{6,4},{7,5},{8,10},{9,11},{10,... | collective-permute-start | bytes 1769480 | tf_op jit(solution)/shard_map/ppermute | solution.py:22
  129.7 17.0 %collective-permute-start.22 = (bf16[96,3072]{1,0:T(8,128)(2,1)S(1)}, bf16[96,3072]{1,0:T(8,128)(2,1)S(1)}, u32[]{:S(2)}, u32[]{:S(2)}) collective-permute-start(bf16[96,3072]{1,0:T(8,128)(2,1)S(1)} %collective-permute-done.19.rest_2_), channel_id=1, source_target_pairs={{0,4},{4,0},{8,12},{12,8},{16,20},{20,16},{24,28},{28,24},{1,5},{5... | collective-permute-start | bytes 1769480 | tf_op jit(solution)/shard_map/ppermute | solution.py:22
  131.4 14.7 %collective-permute-start.20 = (bf16[384,768]{1,0:T(8,128)(2,1)S(1)}, bf16[384,768]{1,0:T(8,128)(2,1)S(1)}, u32[]{:S(2)}, u32[]{:S(2)}) collective-permute-start(bf16[384,768]{1,0:T(8,128)(2,1)S(1)} %get-tuple-element.205), channel_id=1, source_target_pairs={{0,2},{1,3},{2,0},{3,1},{4,6},{5,7},{6,4},{7,5},{8,10},{9,11},{10,... | collective-permute-start | bytes 1769480 | tf_op jit(solution)/shard_map/ppermute | solution.py:22
  146.1 14.5 %collective-permute-start.21 = (bf16[384,768]{1,0:T(8,128)(2,1)S(1)}, bf16[384,768]{1,0:T(8,128)(2,1)S(1)}, u32[]{:S(2)}, u32[]{:S(2)}) collective-permute-start(bf16[384,768]{1,0:T(8,128)(2,1)S(1)} %collective-permute-done.20.rest_7_), channel_id=1, source_target_pairs={{0,4},{4,0},{8,12},{12,8},{16,20},{20,16},{24,28},{28,24},{1,5},{5... | collective-permute-start | bytes 1769480 | tf_op jit(solution)/shard_map/ppermute | solution.py:22
  146.8 13.9 %collective-permute-start.24 = (bf16[192,3072]{1,0:T(8,128)(2,1)S(1)}, bf16[192,3072]{1,0:T(8,128)(2,1)S(1)}, u32[]{:S(2)}, u32[]{:S(2)}) collective-permute-start(bf16[192,3072]{1,0:T(8,128)(2,1)S(1)} %constant_dynamic-update-slice_fusion), channel_id=1, source_target_pairs={{0,1},{1,0},{2,3},{3,2},{4,5},{5,4},{6,7},{7,6},{8,9},{9,8},{10,11... | collective-permute-start | bytes 3538952 | tf_op jit(solution)/shard_map/ppermute | solution.py:22
  204.7 28.7 %collective-permute-start.26 = (bf16[2,2,2,2,192,384]{5,4,3,2,1,0:T(8,128)(2,1)}, bf16[2,2,2,2,192,384]{5,4,3,2,1,0:T(8,128)(2,1)S(1)}, u32[]{:S(2)}, u32[]{:S(2)}) collective-permute-start(bf16[2,2,2,2,192,384]{5,4,3,2,1,0:T(8,128)(2,1)} %get-tuple-element.234), channel_id=1, source_target_pairs={{0,1},{1,0},{2,3},{3,2},{4,5},{5,4},{6,7},{7,6},{8,9},{9,8},{10,11... | collective-permute-start | bytes 7077896 | tf_op jit(solution)/shard_map/ppermute | solution.py:22
  204.9 28.2 %collective-permute-start.27 = (bf16[2,2,2,192,384]{4,3,2,1,0:T(8,128)(2,1)S(1)}, bf16[2,2,2,192,384]{4,3,2,1,0:T(8,128)(2,1)S(1)}, u32[]{:S(2)}, u32[]{:S(2)}) collective-permute-start(bf16[2,2,2,192,384]{4,3,2,1,0:T(8,128)(2,1)S(1)} %get-tuple-element.342), channel_id=1, source_target_pairs={{0,2},{1,3},{2,0},{3,1},{4,6},{5,7},{6,4},{7,5},{8,10},{9,11},{10,... | collective-permute-start | bytes 3538952 | tf_op jit(solution)/shard_map/ppermute | solution.py:22
  221.2 41.7 %collective-permute-start.30 = (bf16[2,2,2,2,192,384]{5,4,3,2,1,0:T(8,128)(2,1)}, bf16[2,2,2,2,192,384]{5,4,3,2,1,0:T(8,128)(2,1)S(1)}, u32[]{:S(2)}, u32[]{:S(2)}) collective-permute-start(bf16[2,2,2,2,192,384]{5,4,3,2,1,0:T(8,128)(2,1)} %get-tuple-element.245), channel_id=1, source_target_pairs={{0,1},{1,0},{2,3},{3,2},{4,5},{5,4},{6,7},{7,6},{8,9},{9,8},{10,11... | collective-permute-start | bytes 7077896 | tf_op jit(solution)/shard_map/ppermute | solution.py:22
  245.3 27.3 %collective-permute-start.33 = (bf16[2,2,2,2,192,384]{5,4,3,2,1,0:T(8,128)(2,1)}, bf16[2,2,2,2,192,384]{5,4,3,2,1,0:T(8,128)(2,1)S(1)}, u32[]{:S(2)}, u32[]{:S(2)}) collective-permute-start(bf16[2,2,2,2,192,384]{5,4,3,2,1,0:T(8,128)(2,1)} %get-tuple-element.249), channel_id=1, source_target_pairs={{0,1},{1,0},{2,3},{3,2},{4,5},{5,4},{6,7},{7,6},{8,9},{9,8},{10,11... | collective-permute-start | bytes 7077896 | tf_op jit(solution)/shard_map/ppermute | solution.py:22
  245.3 15.7 %collective-permute-start.28 = (bf16[2,2,192,384]{3,2,1,0:T(8,128)(2,1)S(1)}, bf16[2,2,192,384]{3,2,1,0:T(8,128)(2,1)S(1)}, u32[]{:S(2)}, u32[]{:S(2)}) collective-permute-start(bf16[2,2,192,384]{3,2,1,0:T(8,128)(2,1)S(1)} %get-tuple-element.354), channel_id=1, source_target_pairs={{0,4},{4,0},{8,12},{12,8},{16,20},{20,16},{24,28},{28,24},{1,5},{5... | collective-permute-start | bytes 1769480 | tf_op jit(solution)/shard_map/ppermute | solution.py:22
  245.9 28.2 %collective-permute-start.32 = (bf16[2,2,2,192,384]{4,3,2,1,0:T(8,128)(2,1)}, bf16[2,2,2,192,384]{4,3,2,1,0:T(8,128)(2,1)S(1)}, u32[]{:S(2)}, u32[]{:S(2)}) collective-permute-start(bf16[2,2,2,192,384]{4,3,2,1,0:T(8,128)(2,1)} %get-tuple-element.340), channel_id=1, source_target_pairs={{0,2},{1,3},{2,0},{3,1},{4,6},{5,7},{6,4},{7,5},{8,10},{9,11},{10,... | collective-permute-start | bytes 3538952 | tf_op jit(solution)/shard_map/ppermute | solution.py:22
  261.2 8.6 %collective-permute-start.29 = (bf16[2,192,384]{2,1,0:T(8,128)(2,1)S(1)}, bf16[2,192,384]{2,1,0:T(8,128)(2,1)S(1)}, u32[]{:S(2)}, u32[]{:S(2)}) collective-permute-start(bf16[2,192,384]{2,1,0:T(8,128)(2,1)S(1)} %get-tuple-element.371), channel_id=1, source_target_pairs={{0,8},{4,12},{8,0},{12,4},{16,24},{20,28},{24,16},{28,20},{1,9},{5... | collective-permute-start | bytes 884744 | tf_op jit(solution)/shard_map/ppermute | solution.py:22
  269.9 8.6 %collective-permute-start.31 = (bf16[192,384]{1,0:T(8,128)(2,1)S(1)}, bf16[192,384]{1,0:T(8,128)(2,1)S(1)}, u32[]{:S(2)}, u32[]{:S(2)}) collective-permute-start(bf16[192,384]{1,0:T(8,128)(2,1)S(1)} %fusion.65), channel_id=1, source_target_pairs={{0,16},{4,20},{8,24},{12,28},{16,0},{20,4},{24,8},{28,12},{1,17},{... | collective-permute-start | bytes 442376 | tf_op jit(solution)/shard_map/ppermute | solution.py:22
  292.8 31.4 %collective-permute-start.35 = (bf16[2,2,2,2,192,384]{5,4,3,2,1,0:T(8,128)(2,1)}, bf16[2,2,2,2,192,384]{5,4,3,2,1,0:T(8,128)(2,1)S(1)}, u32[]{:S(2)}, u32[]{:S(2)}) collective-permute-start(bf16[2,2,2,2,192,384]{5,4,3,2,1,0:T(8,128)(2,1)} %get-tuple-element.267), channel_id=1, source_target_pairs={{0,1},{1,0},{2,3},{3,2},{4,5},{5,4},{6,7},{7,6},{8,9},{9,8},{10,11... | collective-permute-start | bytes 7077896 | tf_op jit(solution)/shard_map/ppermute | solution.py:22
  292.9 28.9 %collective-permute-start.36 = (bf16[2,2,2,192,384]{4,3,2,1,0:T(8,128)(2,1)S(1)}, bf16[2,2,2,192,384]{4,3,2,1,0:T(8,128)(2,1)}, u32[]{:S(2)}, u32[]{:S(2)}) collective-permute-start(bf16[2,2,2,192,384]{4,3,2,1,0:T(8,128)(2,1)S(1)} %copy-done.5), channel_id=1, source_target_pairs={{0,4},{4,0},{8,12},{12,8},{16,20},{20,16},{24,28},{28,24},{1,5},{5... | collective-permute-start | bytes 3538952 | tf_op jit(solution)/shard_map/ppermute | solution.py:22
  293.4 18.6 %collective-permute-start.37 = (bf16[1,192,384]{2,1,0:T(8,128)(2,1)S(1)}, bf16[1,192,384]{2,1,0:T(8,128)(2,1)S(1)}, u32[]{:S(2)}, u32[]{:S(2)}) collective-permute-start(bf16[1,192,384]{2,1,0:T(8,128)(2,1)S(1)} %fusion.64), channel_id=1, source_target_pairs={{0,16},{4,20},{8,24},{12,28},{16,0},{20,4},{24,8},{28,12},{1,17},{... | collective-permute-start | bytes 442376 | tf_op jit(solution)/shard_map/ppermute | solution.py:22
  293.8 40.2 %collective-permute-start.40 = (bf16[2,2,192,384]{3,2,1,0:T(8,128)(2,1)}, bf16[2,2,192,384]{3,2,1,0:T(8,128)(2,1)}, u32[]{:S(2)}, u32[]{:S(2)}) collective-permute-start(bf16[2,2,192,384]{3,2,1,0:T(8,128)(2,1)} %get-tuple-element.352), channel_id=1, source_target_pairs={{0,4},{4,0},{8,12},{12,8},{16,20},{20,16},{24,28},{28,24},{1,5},{5... | collective-permute-start | bytes 1769480 | tf_op jit(solution)/shard_map/ppermute | solution.py:22
  295.1 40.8 %collective-permute-start.39 = (bf16[2,2,2,192,384]{4,3,2,1,0:T(8,128)(2,1)S(1)}, bf16[2,2,2,192,384]{4,3,2,1,0:T(8,128)(2,1)}, u32[]{:S(2)}, u32[]{:S(2)}) collective-permute-start(bf16[2,2,2,192,384]{4,3,2,1,0:T(8,128)(2,1)S(1)} %get-tuple-element.334), channel_id=1, source_target_pairs={{0,2},{1,3},{2,0},{3,1},{4,6},{5,7},{6,4},{7,5},{8,10},{9,11},{10,... | collective-permute-start | bytes 3538952 | tf_op jit(solution)/shard_map/ppermute | solution.py:22
  312.1 53.2 %collective-permute-start.34 = (bf16[2,2,2,2,208,384]{5,4,3,2,1,0:T(8,128)(2,1)}, bf16[2,2,2,2,208,384]{5,4,3,2,1,0:T(8,128)(2,1)S(1)}, u32[]{:S(2)}, u32[]{:S(2)}) collective-permute-start(bf16[2,2,2,2,208,384]{5,4,3,2,1,0:T(8,128)(2,1)} %get-tuple-element.265), channel_id=1, source_target_pairs={{0,1},{1,0},{2,3},{3,2},{4,5},{5,4},{6,7},{7,6},{8,9},{9,8},{10,11... | collective-permute-start | bytes 7667720 | tf_op jit(solution)/shard_map/ppermute | solution.py:22
  321.8 8.1 %collective-permute-start.41 = (bf16[2,192,384]{2,1,0:T(8,128)(2,1)S(1)}, bf16[2,192,384]{2,1,0:T(8,128)(2,1)S(1)}, u32[]{:S(2)}, u32[]{:S(2)}) collective-permute-start(bf16[2,192,384]{2,1,0:T(8,128)(2,1)S(1)} %pad_maximum_fusion.13), channel_id=1, source_target_pairs={{0,8},{4,12},{8,0},{12,4},{16,24},{20,28},{24,16},{28,20},{1,9},{5... | collective-permute-start | bytes 884744 | tf_op jit(solution)/shard_map/ppermute | solution.py:22
  324.2 16.3 %collective-permute-start.44 = (bf16[2,2,192,384]{3,2,1,0:T(8,128)(2,1)S(1)}, bf16[2,2,192,384]{3,2,1,0:T(8,128)(2,1)S(1)}, u32[]{:S(2)}, u32[]{:S(2)}) collective-permute-start(bf16[2,2,192,384]{3,2,1,0:T(8,128)(2,1)S(1)} %get-tuple-element.348), channel_id=1, source_target_pairs={{0,2},{1,3},{2,0},{3,1},{4,6},{5,7},{6,4},{7,5},{8,10},{9,11},{10,... | collective-permute-start | bytes 1769480 | tf_op jit(solution)/shard_map/ppermute | solution.py:22
  329.9 33.8 %collective-permute-start.38 = (bf16[2,2,2,192,384]{4,3,2,1,0:T(8,128)(2,1)S(1)}, bf16[2,2,2,192,384]{4,3,2,1,0:T(8,128)(2,1)S(1)}, u32[]{:S(2)}, u32[]{:S(2)}) collective-permute-start(bf16[2,2,2,192,384]{4,3,2,1,0:T(8,128)(2,1)S(1)} %get-tuple-element.335), channel_id=1, source_target_pairs={{0,2},{1,3},{2,0},{3,1},{4,6},{5,7},{6,4},{7,5},{8,10},{9,11},{10,... | collective-permute-start | bytes 3538952 | tf_op jit(solution)/shard_map/ppermute | solution.py:22
  335.2 8.6 %collective-permute-start.43 = (bf16[2,192,384]{2,1,0:T(8,128)(2,1)S(1)}, bf16[2,192,384]{2,1,0:T(8,128)(2,1)S(1)}, u32[]{:S(2)}, u32[]{:S(2)}) collective-permute-start(bf16[2,192,384]{2,1,0:T(8,128)(2,1)S(1)} %get-tuple-element.370), channel_id=1, source_target_pairs={{0,8},{4,12},{8,0},{12,4},{16,24},{20,28},{24,16},{28,20},{1,9},{5... | collective-permute-start | bytes 884744 | tf_op jit(solution)/shard_map/ppermute | solution.py:22
  337.5 15.6 %collective-permute-start.42 = (bf16[2,2,192,384]{3,2,1,0:T(8,128)(2,1)S(1)}, bf16[2,2,192,384]{3,2,1,0:T(8,128)(2,1)S(1)}, u32[]{:S(2)}, u32[]{:S(2)}) collective-permute-start(bf16[2,2,192,384]{3,2,1,0:T(8,128)(2,1)S(1)} %get-tuple-element.349), channel_id=1, source_target_pairs={{0,4},{4,0},{8,12},{12,8},{16,20},{20,16},{24,28},{28,24},{1,5},{5... | collective-permute-start | bytes 1769480 | tf_op jit(solution)/shard_map/ppermute | solution.py:22
  343.9 8.7 %collective-permute-start.45 = (bf16[192,384]{1,0:T(8,128)(2,1)S(1)}, bf16[192,384]{1,0:T(8,128)(2,1)S(1)}, u32[]{:S(2)}, u32[]{:S(2)}) collective-permute-start(bf16[192,384]{1,0:T(8,128)(2,1)S(1)} %fusion.68), channel_id=1, source_target_pairs={{0,16},{4,20},{8,24},{12,28},{16,0},{20,4},{24,8},{28,12},{1,17},{... | collective-permute-start | bytes 442376 | tf_op jit(solution)/shard_map/ppermute | solution.py:22
  346.2 21.1 %collective-permute-start.47 = (bf16[2,192,384]{2,1,0:T(8,128)(2,1)S(1)}, bf16[2,192,384]{2,1,0:T(8,128)(2,1)S(1)}, u32[]{:S(2)}, u32[]{:S(2)}) collective-permute-start(bf16[2,192,384]{2,1,0:T(8,128)(2,1)S(1)} %get-tuple-element.368), channel_id=1, source_target_pairs={{0,8},{4,12},{8,0},{12,4},{16,24},{20,28},{24,16},{28,20},{1,9},{5... | collective-permute-start | bytes 884744 | tf_op jit(solution)/shard_map/ppermute | solution.py:22
  352.5 61.8 %collective-permute-start.72 = (bf16[4,192,384]{2,1,0:T(8,128)(2,1)S(1)}, bf16[4,192,384]{2,1,0:T(8,128)(2,1)S(1)}, u32[]{:S(2)}, u32[]{:S(2)}) collective-permute-start(bf16[4,192,384]{2,1,0:T(8,128)(2,1)S(1)} %pad_maximum_fusion.7.near), channel_id=1, source_target_pairs={{0,4},{4,0},{8,12},{12,8},{16,20},{20,16},{24,28},{28,24},{1,5},{5... | collective-permute-start | bytes 1769480 | tf_op jit(solution)/shard_map/ppermute | solution.py:22
  353.1 15.2 %collective-permute-start.50 = (bf16[1,192,384]{2,1,0:T(8,128)(2,1)S(1)}, bf16[1,192,384]{2,1,0:T(8,128)(2,1)S(1)}, u32[]{:S(2)}, u32[]{:S(2)}) collective-permute-start(bf16[1,192,384]{2,1,0:T(8,128)(2,1)S(1)} %fusion.67), channel_id=1, source_target_pairs={{0,16},{4,20},{8,24},{12,28},{16,0},{20,4},{24,8},{28,12},{1,17},{... | collective-permute-start | bytes 442376 | tf_op jit(solution)/shard_map/ppermute | solution.py:22
  363.7 9.6 %collective-permute-start.49 = (bf16[2,192,384]{2,1,0:T(8,128)(2,1)S(1)}, bf16[2,192,384]{2,1,0:T(8,128)(2,1)S(1)}, u32[]{:S(2)}, u32[]{:S(2)}) collective-permute-start(bf16[2,192,384]{2,1,0:T(8,128)(2,1)S(1)} %get-tuple-element.366), channel_id=1, source_target_pairs={{0,8},{4,12},{8,0},{12,4},{16,24},{20,28},{24,16},{28,20},{1,9},{5... | collective-permute-start | bytes 884744 | tf_op jit(solution)/shard_map/ppermute | solution.py:22
  365.3 20.6 %collective-permute-start.53 = (bf16[2,2,192,384]{3,2,1,0:T(8,128)(2,1)S(1)}, bf16[2,2,192,384]{3,2,1,0:T(8,128)(2,1)S(1)}, u32[]{:S(2)}, u32[]{:S(2)}) collective-permute-start(bf16[2,2,192,384]{3,2,1,0:T(8,128)(2,1)S(1)} %get-tuple-element.346), channel_id=1, source_target_pairs={{0,4},{4,0},{8,12},{12,8},{16,20},{20,16},{24,28},{28,24},{1,5},{5... | collective-permute-start | bytes 1769480 | tf_op jit(solution)/shard_map/ppermute | solution.py:22
  367.4 33.4 %collective-permute-start.46 = (bf16[2,2,2,208,384]{4,3,2,1,0:T(8,128)(2,1)S(1)}, bf16[2,2,2,208,384]{4,3,2,1,0:T(8,128)(2,1)S(1)}, u32[]{:S(2)}, u32[]{:S(2)}) collective-permute-start(bf16[2,2,2,208,384]{4,3,2,1,0:T(8,128)(2,1)S(1)} %get-tuple-element.331), channel_id=1, source_target_pairs={{0,2},{1,3},{2,0},{3,1},{4,6},{5,7},{6,4},{7,5},{8,10},{9,11},{10,... | collective-permute-start | bytes 3833864 | tf_op jit(solution)/shard_map/ppermute | solution.py:22
  373.3 9.9 %collective-permute-start.54 = (bf16[2,192,384]{2,1,0:T(8,128)(2,1)S(1)}, bf16[2,192,384]{2,1,0:T(8,128)(2,1)S(1)}, u32[]{:S(2)}, u32[]{:S(2)}) collective-permute-start(bf16[2,192,384]{2,1,0:T(8,128)(2,1)S(1)} %pad_maximum_fusion.14), channel_id=1, source_target_pairs={{0,8},{4,12},{8,0},{12,4},{16,24},{20,28},{24,16},{28,20},{1,9},{5... | collective-permute-start | bytes 884744 | tf_op jit(solution)/shard_map/ppermute | solution.py:22
  375.0 11.8 %collective-permute-start.52 = (bf16[192,384]{1,0:T(8,128)(2,1)S(1)}, bf16[192,384]{1,0:T(8,128)(2,1)S(1)}, u32[]{:S(2)}, u32[]{:S(2)}) collective-permute-start(bf16[192,384]{1,0:T(8,128)(2,1)S(1)} %fusion.72), channel_id=1, source_target_pairs={{0,16},{4,20},{8,24},{12,28},{16,0},{20,4},{24,8},{28,12},{1,17},{... | collective-permute-start | bytes 442376 | tf_op jit(solution)/shard_map/ppermute | solution.py:22
  383.2 9.7 %collective-permute-start.51 = (bf16[1,192,384]{2,1,0:T(8,128)(2,1)S(1)}, bf16[1,192,384]{2,1,0:T(8,128)(2,1)S(1)}, u32[]{:S(2)}, u32[]{:S(2)}) collective-permute-start(bf16[1,192,384]{2,1,0:T(8,128)(2,1)S(1)} %fusion.70), channel_id=1, source_target_pairs={{0,16},{4,20},{8,24},{12,28},{16,0},{20,4},{24,8},{28,12},{1,17},{... | collective-permute-start | bytes 442376 | tf_op jit(solution)/shard_map/ppermute | solution.py:22
  386.1 14.7 %collective-permute-start.56 = (bf16[2,192,384]{2,1,0:T(8,128)(2,1)S(1)}, bf16[2,192,384]{2,1,0:T(8,128)(2,1)S(1)}, u32[]{:S(2)}, u32[]{:S(2)}) collective-permute-start(bf16[2,192,384]{2,1,0:T(8,128)(2,1)S(1)} %get-tuple-element.364), channel_id=1, source_target_pairs={{0,8},{4,12},{8,0},{12,4},{16,24},{20,28},{24,16},{28,20},{1,9},{5... | collective-permute-start | bytes 884744 | tf_op jit(solution)/shard_map/ppermute | solution.py:22
  386.9 15.3 %collective-permute-start.59 = (bf16[1,192,384]{2,1,0:T(8,128)(2,1)S(1)}, bf16[1,192,384]{2,1,0:T(8,128)(2,1)S(1)}, u32[]{:S(2)}, u32[]{:S(2)}) collective-permute-start(bf16[1,192,384]{2,1,0:T(8,128)(2,1)S(1)} %fusion.74), channel_id=1, source_target_pairs={{0,16},{4,20},{8,24},{12,28},{16,0},{20,4},{24,8},{28,12},{1,17},{... | collective-permute-start | bytes 442376 | tf_op jit(solution)/shard_map/ppermute | solution.py:22
  393.0 15.3 %collective-permute-start.58 = (bf16[2,192,384]{2,1,0:T(8,128)(2,1)S(1)}, bf16[2,192,384]{2,1,0:T(8,128)(2,1)S(1)}, u32[]{:S(2)}, u32[]{:S(2)}) collective-permute-start(bf16[2,192,384]{2,1,0:T(8,128)(2,1)S(1)} %pad_maximum_fusion.15), channel_id=1, source_target_pairs={{0,8},{4,12},{8,0},{12,4},{16,24},{20,28},{24,16},{28,20},{1,9},{5... | collective-permute-start | bytes 884744 | tf_op jit(solution)/shard_map/ppermute | solution.py:22
  401.1 13.0 %collective-permute-start.55 = (bf16[2,2,208,384]{3,2,1,0:T(8,128)(2,1)S(1)}, bf16[2,2,208,384]{3,2,1,0:T(8,128)(2,1)S(1)}, u32[]{:S(2)}, u32[]{:S(2)}) collective-permute-start(bf16[2,2,208,384]{3,2,1,0:T(8,128)(2,1)S(1)} %get-tuple-element.343), channel_id=1, source_target_pairs={{0,4},{4,0},{8,12},{12,8},{16,20},{20,16},{24,28},{28,24},{1,5},{5... | collective-permute-start | bytes 1916936 | tf_op jit(solution)/shard_map/ppermute | solution.py:22
  402.2 17.0 %collective-permute-start.61 = (bf16[2,192,384]{2,1,0:T(8,128)(2,1)S(1)}, bf16[2,192,384]{2,1,0:T(8,128)(2,1)S(1)}, u32[]{:S(2)}, u32[]{:S(2)}) collective-permute-start(bf16[2,192,384]{2,1,0:T(8,128)(2,1)S(1)} %pad_maximum_fusion.16), channel_id=1, source_target_pairs={{0,8},{4,12},{8,0},{12,4},{16,24},{20,28},{24,16},{28,20},{1,9},{5... | collective-permute-start | bytes 884744 | tf_op jit(solution)/shard_map/ppermute | solution.py:22
  414.4 15.3 %collective-permute-start.70 = (bf16[4,192,384]{2,1,0:T(8,128)(2,1)S(1)}, bf16[4,192,384]{2,1,0:T(8,128)(2,1)S(1)}, u32[]{:S(2)}, u32[]{:S(2)}) collective-permute-start(bf16[4,192,384]{2,1,0:T(8,128)(2,1)S(1)} %pad_maximum_fusion.8.near), channel_id=1, source_target_pairs={{0,4},{4,0},{8,12},{12,8},{16,20},{20,16},{24,28},{28,24},{1,5},{5... | collective-permute-start | bytes 1769480 | tf_op jit(solution)/shard_map/ppermute | solution.py:22
  416.0 13.7 %collective-permute-start.67 = (bf16[1,192,384]{2,1,0:T(8,128)(2,1)S(1)}, bf16[1,192,384]{2,1,0:T(8,128)(2,1)S(1)}, u32[]{:S(2)}, u32[]{:S(2)}) collective-permute-start(bf16[1,192,384]{2,1,0:T(8,128)(2,1)S(1)} %fusion.76), channel_id=1, source_target_pairs={{0,16},{4,20},{8,24},{12,28},{16,0},{20,4},{24,8},{28,12},{1,17},{... | collective-permute-start | bytes 442376 | tf_op jit(solution)/shard_map/ppermute | solution.py:22
  422.0 8.7 %collective-permute-start.62 = (bf16[208,384]{1,0:T(8,128)(2,1)S(1)}, bf16[208,384]{1,0:T(8,128)(2,1)S(1)}, u32[]{:S(2)}, u32[]{:S(2)}) collective-permute-start(bf16[208,384]{1,0:T(8,128)(2,1)S(1)} %fusion.62), channel_id=1, source_target_pairs={{0,16},{4,20},{8,24},{12,28},{16,0},{20,4},{24,8},{28,12},{1,17},{... | collective-permute-start | bytes 479240 | tf_op jit(solution)/shard_map/ppermute | solution.py:22
  429.6 15.7 %collective-permute-start.66 = (bf16[4,192,384]{2,1,0:T(8,128)(2,1)S(1)}, bf16[4,192,384]{2,1,0:T(8,128)(2,1)S(1)}, u32[]{:S(2)}, u32[]{:S(2)}) collective-permute-start(bf16[4,192,384]{2,1,0:T(8,128)(2,1)S(1)} %pad_maximum_fusion.9.near), channel_id=1, source_target_pairs={{0,4},{4,0},{8,12},{12,8},{16,20},{20,16},{24,28},{28,24},{1,5},{5... | collective-permute-start | bytes 1769480 | tf_op jit(solution)/shard_map/ppermute | solution.py:22
  429.8 15.6 %collective-permute-start.68 = (bf16[2,192,384]{2,1,0:T(8,128)(2,1)S(1)}, bf16[2,192,384]{2,1,0:T(8,128)(2,1)S(1)}, u32[]{:S(2)}, u32[]{:S(2)}) collective-permute-start(bf16[2,192,384]{2,1,0:T(8,128)(2,1)S(1)} %pad_maximum_fusion.17), channel_id=1, source_target_pairs={{0,8},{4,12},{8,0},{12,4},{16,24},{20,28},{24,16},{28,20},{1,9},{5... | collective-permute-start | bytes 884744 | tf_op jit(solution)/shard_map/ppermute | solution.py:22
  430.8 14.8 %collective-permute-start.63 = (bf16[1,208,384]{2,1,0:T(8,128)(2,1)S(1)}, bf16[1,208,384]{2,1,0:T(8,128)(2,1)S(1)}, u32[]{:S(2)}, u32[]{:S(2)}) collective-permute-start(bf16[1,208,384]{2,1,0:T(8,128)(2,1)S(1)} %fusion.61), channel_id=1, source_target_pairs={{0,16},{4,20},{8,24},{12,28},{16,0},{20,4},{24,8},{28,12},{1,17},{... | collective-permute-start | bytes 479240 | tf_op jit(solution)/shard_map/ppermute | solution.py:22
  437.8 20.2 %collective-permute-start.71 = (bf16[4,192,384]{2,1,0:T(8,128)(2,1)S(1)}, bf16[4,192,384]{2,1,0:T(8,128)(2,1)S(1)}, u32[]{:S(2)}, u32[]{:S(2)}) collective-permute-start(bf16[4,192,384]{2,1,0:T(8,128)(2,1)S(1)} %pad_maximum_fusion.10.near), channel_id=1, source_target_pairs={{0,4},{4,0},{8,12},{12,8},{16,20},{20,16},{24,28},{28,24},{1,5},{5... | collective-permute-start | bytes 1769480 | tf_op jit(solution)/shard_map/ppermute | solution.py:22
  445.4 25.2 %collective-permute-start.69 = (bf16[4,192,384]{2,1,0:T(8,128)(2,1)S(1)}, bf16[4,192,384]{2,1,0:T(8,128)(2,1)S(1)}, u32[]{:S(2)}, u32[]{:S(2)}) collective-permute-start(bf16[4,192,384]{2,1,0:T(8,128)(2,1)S(1)} %pad_maximum_fusion.11.near), channel_id=1, source_target_pairs={{0,4},{4,0},{8,12},{12,8},{16,20},{20,16},{24,28},{28,24},{1,5},{5... | collective-permute-start | bytes 1769480 | tf_op jit(solution)/shard_map/ppermute | solution.py:22
  445.6 12.4 %collective-permute-start.64 = (bf16[2,208,384]{2,1,0:T(8,128)(2,1)S(1)}, bf16[2,208,384]{2,1,0:T(8,128)(2,1)S(1)}, u32[]{:S(2)}, u32[]{:S(2)}) collective-permute-start(bf16[2,208,384]{2,1,0:T(8,128)(2,1)S(1)} %pad_maximum_fusion.12), channel_id=1, source_target_pairs={{0,8},{4,12},{8,0},{12,4},{16,24},{20,28},{24,16},{28,20},{1,9},{5... | collective-permute-start | bytes 958472 | tf_op jit(solution)/shard_map/ppermute | solution.py:22
  458.1 20.4 %collective-permute-start.65 = (bf16[4,208,384]{2,1,0:T(8,128)(2,1)S(1)}, bf16[4,208,384]{2,1,0:T(8,128)(2,1)S(1)}, u32[]{:S(2)}, u32[]{:S(2)}) collective-permute-start(bf16[4,208,384]{2,1,0:T(8,128)(2,1)S(1)} %pad_maximum_fusion.4.near), channel_id=1, source_target_pairs={{0,4},{4,0},{8,12},{12,8},{16,20},{20,16},{24,28},{28,24},{1,5},{5... | collective-permute-start | bytes 1916936 | tf_op jit(solution)/shard_map/ppermute | solution.py:22
  (45 other events, 391.1 us)

commit v5 on v4

--- a/solution.py
+++ b/solution.py
@@ -46,6 +46,9 @@
 
 
 def weight_copies(ids, layer, pieces, target, columns, sems, base):
+    at = pl.ds(columns, target.shape[1])
+    if len(pieces) == 1:
+        return [pltpu.make_async_copy(pieces[0].at[:, at], target, sems.at[base])]
     own, core, near_x, far_x, diagonal = pieces
     rows = own.shape[1]
     half = rows // 2
@@ -56,7 +59,6 @@
         where = target.at[pl.ds(pl.multiple_of(start, half), count), :]
         copies.append(pltpu.make_async_copy(source, where, sems.at[base + len(copies)]))
 
-    at = pl.ds(columns, target.shape[1])
     add(own.at[layer], n * rows, rows)
     add(core.at[layer], ids[1] * rows, rows)
     add(near_x.at[:, at], ids[2] * rows + y * half, half)
@@ -77,21 +79,30 @@
 
 
 def attn_copies(layer, ids, refs, w_qkv, w_o, sems):
-    qkv_own, qkv_core, o_own, o_core = refs[:4]
-    halves = refs[4:]
-    qkv = weight_copies(ids, layer, (qkv_own, qkv_core) + halves, w_qkv, 0, sems, 0)
-    o = weight_copies(ids, layer, (o_own, o_core) + halves, w_o, w_qkv.shape[1], sems, 6)
+    first, second = (refs, refs) if len(refs) == 1 else (refs[:2] + refs[4:], refs[2:])
+    qkv = weight_copies(ids, layer, first, w_qkv, 0, sems, 0)
+    o = weight_copies(ids, layer, second, w_o, w_qkv.shape[1], sems, 6)
     return qkv, o
 
 
 def ffn_copies(layer, ids, refs, w_in, w_out, sems):
-    in_copies = weight_copies(ids, layer, refs[:5], w_in, 0, sems, 0)
-    out_copies = weight_copies(ids, layer, refs[5:], w_out, 0, sems, 6)
+    in_copies = weight_copies(ids, layer, refs[:-5], w_in, 0, sems, 0)
+    out_copies = weight_copies(ids, layer, refs[-5:], w_out, 0, sems, 6)
     return in_copies, out_copies
 
 
+def pack_kernel(*refs):
+    shorts, in_bias, packed = refs[:8], refs[8], refs[9]
+    layers, share = shorts[0].shape
+    for layer in range(layers):
+        for i, short in enumerate(shorts):
+            packed[layer, i : i + 1, :] = short[layer : layer + 1, :].astype(f32)
+        for i in range(4):
+            packed[layer, 8 + i : 9 + i, :] = in_bias[layer : layer + 1, i * share : (i + 1) * share].astype(f32)
+
+
 def attn_fwd_kernel(layer, ids, length, x, cell_row, small, *rest):
-    weights, rest = rest[:7], rest[7:]
+    weights, rest = rest[:-9], rest[-9:]
     qkv_rows, probs, context, unit_out, inverse_out, w_qkv, w_o, mask, sems = rest
     tokens, width = x.shape
     qkv_copies, o_copies = attn_copies(layer, ids, weights, w_qkv, w_o, sems)
@@ -147,7 +158,7 @@
 
 
 def ffn_fwd_kernel(layer, ids, unit_one, in_bias, small, *rest):
-    weights, rest = rest[:10], rest[10:]
+    weights, rest = rest[:-9], rest[-9:]
     hidden, slope, unit_out, inverse_out, result, w_in, w_out, normed_low, sems = rest
     in_copies, out_copies = ffn_copies(layer, ids, weights, w_in, w_out, sems)
     begin(in_copies)
@@ -174,7 +185,7 @@
     result[...] = (unit * small[layer, 6:7, :] + small[layer, 7:8, :]).astype(low)
 
 
-WIDE_BIT = {"y": 2, "z": 1, "w": 0}
+WIDE_BIT = {"y": 0, "z": 1, "w": 2}
 
 
 def place_of(ids, owner, piece, way):
@@ -230,7 +241,7 @@
 
 
 def in_bwd_kernel(layer, way, ids, d_ffn, d_resid_two, unit_one, inverse_one, slope, small, *rest):
-    weights, rest = rest[:10], rest[10:]
+    weights, rest = rest[:-12], rest[-12:]
     d_resid, small_grads, in_bias_grad, kept, sent = rest[:5]
     w_in, w_out, d_pre, normed_t, stage, sems, out_sems = rest[5:]
     in_copies, out_copies = ffn_copies(layer, ids, weights, w_in, w_out, sems)
@@ -262,7 +273,8 @@
 
 
 def attn_bwd_kernel(layer, way, ids, d_resid, x, qkv_rows, probs, context, *rest):
-    weights, others, rest = rest[:7], rest[7:-13], rest[-13:]
+    weights = rest[:-13][: 7 if layer == 0 else 1]
+    others, rest = rest[len(weights) : -13], rest[-13:]
     d_input, small_grads, kept, sent = rest[:4]
     w_qkv, w_o, d_attn, d_context, d_qkv, x_t, stage, sems, out_sems = rest[4:]
     tokens, width = x.shape
@@ -345,30 +357,17 @@
     return found
 
 
-def unpack_kernel(layer, slab, back, earlier, ids, near, far, *rest):
+def unpack_kernel(layer, slab, earlier, gathered, *rest):
     outs = rest[earlier:-4]
     buffer, wide_buffer, in_sems, out_sems = rest[-4:]
     share, tile = wide_buffer.shape[1:]
-
-    def fetch(piece, ref, index):
-        return pltpu.make_async_copy(ref.at[index], buffer.at[piece], in_sems.at[piece])
-
-    for piece in range(8):
-        off = piece ^ ids[5]
-        bits = [(off >> WIDE_BIT[name]) & 1 for name in back]
-        index = bits[1] * 2 + bits[0]
-
-        @pl.when(bits[2] == 0)
-        def _():
-            fetch(piece, near, index).start()
-
-        @pl.when(bits[2] == 1)
-        def _():
-            fetch(piece, far, index).start()
-
+    arriving = [
+        pltpu.make_async_copy(gathered.at[piece], buffer.at[piece], in_sems.at[piece]) for piece in range(8)
+    ]
+    begin(arriving)
     copies = []
     for piece in range(8):
-        fetch(piece, near, 0).wait()
+        arriving[piece].wait()
         wide_buffer[piece] = buffer[piece, :share].astype(f32)
         columns = pl.ds(piece * tile, tile)
         if slab == "in":
@@ -422,22 +421,14 @@
     return jax.ShapeDtypeStruct(dims, kind)
 
 
-def reverse_bits(value, bits):
-    result = jnp.zeros_like(value)
-    for bit in range(bits):
-        result = result | (((value >> bit) & 1) << (bits - 1 - bit))
-    return result
-
-
 def added(a, b):
     return (a.astype(f32) + b.astype(f32)).astype(low)
 
 
-WAYS = ("xyzw", "xyzw", "yxzw", "xyzw", "xyzw", "xyzw")
-BACKS = ("wzy",) * 6
+WAYS = ("yxzw", "xyzw", "xyzw", "yxzw", "xyzw", "xyzw")
 PLAN = (
-    "out1", 0, "in1", "attn1", 0, 1, "out0", 0, 2, 0, 3, 1, 0, "in0", 0, 2, 4, 0, 1, 3, 2, 1, 0, "attn0", 1,
-    3, 4, 5, 2, 1, 3, 2, 1, 4, 3, 2, 5, 1, 4, 3, 2, 4, 5, 3, 5, 4, 2, 5, 4, 3, 5, 5, 4, 5,
+    "out1", "in1", 0, 1, "attn1", "out0", 0, 2, 1, "in0", 0, 3, 4, 0, 1, 0, 2, 1, "attn0", 1, 3, 2, 5, 4, 2,
+    0, 3, 2, 4, 3, 1, 4, 3, 5, 4, 2, 5, 5, 3, 5, 4, 5,
 )
 
 
@@ -461,8 +452,8 @@
 
 
 class Slab:
-    def __init__(self, way, back, wide_bits, kept, sent):
-        self.way, self.back, self.wide_bits = way, back, wide_bits
+    def __init__(self, way, wide_count, kept, sent):
+        self.way, self.wide_count = way, wide_count
         self.kept = kept
         self.flying = swap(sent, "narrow", 1)
         self.stage = 0
@@ -476,21 +467,22 @@
             order.last = send
         elif self.stage == len(self.way):
             piece = added(self.kept, received)
-            for b in range(HALVINGS, self.wide_bits):
-                piece = added(piece, swap(piece, "wide", 1 << b))
-            self.block = piece[None]
-            order.last = self.block
-            self.flying = swap(self.block, *STEPS[self.back[0]])
-        elif self.stage < len(self.way) + len(self.back):
-            self.block = jnp.concatenate([self.block, received], axis=0)
-            order.last = self.block
-            self.flying = swap(self.block, *STEPS[self.back[self.stage - len(self.way)]])
+            pieces = 1 << HALVINGS
+            groups = None
+            if self.wide_count > pieces:
+                bit = pieces
+                while bit < self.wide_count:
+                    piece = added(piece, swap(piece, "wide", bit))
+                    bit *= 2
+                groups = [list(range(i, i + pieces)) for i in range(0, self.wide_count, pieces)]
+            order.last = piece
+            self.flying = lax.all_gather(piece, "wide", axis=0, axis_index_groups=groups)
         else:
-            self.far = received
+            self.gathered = received
         self.stage += 1
 
     def ended(self):
-        return self.stage == len(self.way) + len(self.back) + 1
+        return self.stage == len(self.way) + 2
 
 
 def body(
@@ -516,14 +508,12 @@
     layers, share, ffn = in_weight.shape
     ffn_share = out_weight.shape[1]
     wide_count = lax.axis_size("wide")
-    wide_bits = wide_count.bit_length() - 1
-    assert wide_count == 1 << wide_bits and wide_bits >= HALVINGS and lax.axis_size("narrow") == 4
+    assert wide_count & (wide_count - 1) == 0 and wide_count >= 1 << HALVINGS and lax.axis_size("narrow") == 4
     tile = ffn // 8
     me = lax.axis_index("narrow").astype(jnp.int32)
     wide_me = lax.axis_index("wide").astype(jnp.int32)
     y = wide_me & 1
-    place = reverse_bits(wide_me & (2**HALVINGS - 1), HALVINGS)
-    ids = jnp.stack([me, me ^ 1, me ^ 2, me ^ 3, y, place])
+    ids = jnp.stack([me, me ^ 1, me ^ 2, me ^ 3, y, wide_me & (2**HALVINGS - 1)])
 
     order = Order()
 
@@ -531,17 +521,14 @@
         rows = weight.shape[1] // 2
         return lax.dynamic_slice(weight, (layer, y * rows, 0), (1, rows, weight.shape[2]))[0]
 
-    halves = []
-    for layer in range(layers):
-        joint = jnp.concatenate([half_of(qkv_weight, layer), half_of(o_weight, layer)], axis=1)
-        halves += [joint, half_of(in_weight, layer), half_of(out_weight, layer)]
-    near_x, far_x, diagonal = [None] * len(halves), [None] * len(halves), [None] * len(halves)
+    own = (qkv_weight, o_weight, in_weight, out_weight)
+    joint = jnp.concatenate([half_of(qkv_weight, 0), half_of(o_weight, 0)], axis=1)
+    halves = [joint, half_of(in_weight, 0), half_of(out_weight, 0), half_of(out_weight, 1)]
+    near_x, far_x, diagonal = [None] * 4, [None] * 4, [None] * 4
     core = [None] * 4
-    own = (qkv_weight, o_weight, in_weight, out_weight)
-
-    def send_x(*which):
-        for i in which:
-            near_x[i] = swap(order.after(halves[i]), "narrow", 2)
+
+    def send_x(i):
+        near_x[i] = swap(order.after(halves[i]), "narrow", 2)
 
     def send_core(i):
         core[i] = swap(order.after(own[i]), "narrow", 1)
@@ -564,19 +551,25 @@
     def group(i):
         return near_x[i], far_x[i], diagonal[i]
 
-    def attn_weights(layer):
-        return (qkv_weight, core[0], o_weight, core[1]) + group(3 * layer)
-
-    def ffn_weights(layer):
-        return (in_weight, core[2]) + group(3 * layer + 1) + (out_weight, core[3]) + group(3 * layer + 2)
-
     send_x(0)
-    short = [q_bias, v_bias, o_bias, norm1_gain, norm1_bias, out_bias, norm2_gain, norm2_bias]
-    packed = jnp.concatenate([jnp.stack(short, axis=1), in_bias.reshape(layers, 4, share)], axis=1)
-    others = [
-        lax.ppermute(packed, "narrow", [(i, i ^ away) for i in range(4)]) for away in (1, 2, 3)
-    ]
+    order.last = halves[0]
     send_core(0)
+    second_attn_weights = lax.all_gather(
+        jnp.concatenate([qkv_weight[1], o_weight[1]], axis=1), "narrow", axis=0, tiled=True
+    )
+    second_in_weight = lax.all_gather(in_weight[1], "narrow", axis=0, tiled=True)
+    short = (q_bias, v_bias, o_bias, norm1_gain, norm1_bias, out_bias, norm2_gain, norm2_bias)
+    packed = call(
+        pack_kernel,
+        "pack",
+        1,
+        [VMEM] * 9,
+        VMEM,
+        shape((layers, 12, share), f32),
+        [],
+        order.after(short) + (in_bias,),
+    )
+    others = [lax.ppermute(packed, "narrow", [(i, i ^ away) for i in range(4)]) for away in (1, 2, 3)]
     halves[1:] = order.wait(halves[1:])
     arrive(("c", 0))
     send_core(1)
@@ -589,7 +582,7 @@
         return jnp.stack([jnp.where(swapped, high_one, low_one), jnp.where(swapped, low_one, high_one)])
 
     packed = in_order(in_order(packed, others[0], 1), in_order(others[1], others[2], 1), 2)
-    packed = packed.reshape(4, layers, 12, share).astype(f32)
+    packed = packed.reshape(4, layers, 12, share)
     small = packed[:, :, :8].transpose(1, 2, 0, 3).reshape(layers, 8, width)
     full_in_bias = packed[:, :, 8:].transpose(1, 0, 2, 3).reshape(layers, 1, ffn)
     ids, small, full_in_bias = order.wait((ids, small, full_in_bias))
@@ -597,6 +590,15 @@
     send_core(2)
     arrive(("c", 2))
     send_core(3)
+
+    def attn_weights(layer):
+        if layer == 1:
+            return (second_attn_weights,)
+        return (qkv_weight, core[0], o_weight, core[1]) + group(0)
+
+    def ffn_weights(layer):
+        in_refs = (second_in_weight,) if layer == 1 else (in_weight, core[2]) + group(1)
+        return in_refs + (out_weight, core[3]) + group(2 + layer)
 
     w_qkv = pltpu.VMEM((width, 3 * width), low)
     w_o = pltpu.VMEM((width, width), low)
@@ -621,7 +623,7 @@
             functools.partial(attn_fwd_kernel, layer),
             "attn_fwd",
             13,
-            [SMEM, SMEM] + [VMEM] * 3 + [ANY] * 7,
+            [SMEM, SMEM] + [VMEM] * 3 + [ANY] * len(attn_weights(layer)),
             [VMEM] * 5,
             [shape((tokens, 3 * width), low), shape((HEADS, tokens, tokens), low), rows_low, rows_f32, column_f32],
             [w_qkv, w_o, pltpu.VMEM((tokens, tokens), f32), copy_sems],
@@ -636,7 +638,7 @@
             functools.partial(ffn_fwd_kernel, layer),
             "ffn_fwd",
             10,
-            [SMEM] + [VMEM] * 3 + [ANY] * 10,
+            [SMEM] + [VMEM] * 3 + [ANY] * len(ffn_weights(layer)),
             [VMEM] * 5,
             [shape((tokens, ffn), low), shape((tokens, ffn), f32), rows_f32, column_f32, rows_low],
             [w_in, w_out, pltpu.VMEM((tokens, width), low), copy_sems],
@@ -666,7 +668,7 @@
             functools.partial(in_bwd_kernel, layer, way),
             "in_bwd",
             14,
-            [SMEM] + [VMEM] * 6 + [ANY] * 10,
+            [SMEM] + [VMEM] * 6 + [ANY] * len(ffn_weights(layer)),
             [VMEM] * 3 + [ANY] * 2,
             [rows_f32, eight_f32, shape((1, ffn), f32)] + pieces(share),
             [
@@ -690,7 +692,7 @@
             functools.partial(attn_bwd_kernel, layer, way),
             "attn_bwd",
             16,
-            [SMEM] + [VMEM] * 5 + [ANY] * 7 + [VMEM] * len(small_others),
+            [SMEM] + [VMEM] * 5 + [ANY] * len(attn_weights(layer)) + [VMEM] * len(small_others),
             [VMEM] * 2 + [ANY] * 2,
             [rows_low, eight_f32] + pieces(rows),
             [
@@ -717,13 +719,13 @@
         }[name]
         last = name == "attn" and layer == 0
         extra = [(layers, share)] * 8 + [(layers, ffn_share)] if last else [(8, 128)]
-        near, far = order.after((slab.block, slab.far))
-        rows = near.shape[1]
+        gathered = order.after(slab.gathered)
+        rows = gathered.shape[1]
         outs = call(
-            functools.partial(unpack_kernel, layer, name, slab.back, len(earlier)),
+            functools.partial(unpack_kernel, layer, name, len(earlier)),
             "unpack",
             4,
-            [SMEM] + [ANY] * (2 + len(earlier)),
+            [ANY] * (1 + len(earlier)),
             [ANY] * len(dims) + [VMEM] * len(extra),
             [shape(d, f32) for d in dims + extra],
             [
@@ -732,27 +734,25 @@
                 pltpu.SemaphoreType.DMA((8,)),
                 pltpu.SemaphoreType.DMA((8,)),
             ],
-            (ids, near, far, *earlier),
-            {3 + i: i for i in range(len(earlier))},
+            (gathered, *earlier),
+            {1 + i: i for i in range(len(earlier))},
         )
         order.last = outs[-1]
         return tuple(outs)
 
     arrive(("x", 1))
     send_x(2)
-    arrive(("y", 0), ("c", 3), ("d", 0), ("x", 2))
+    arrive(("y", 0), ("c", 3), ("d", 0))
+    first_attn = attn_forward(0, tables_in)
+    arrive(("x", 2))
     send_x(3)
-    arrive(("y", 1))
-    first_attn = attn_forward(0, tables_in)
+    arrive(("y", 1), ("y", 2), ("d", 1), ("d", 2))
+    first_ffn = ffn_forward(0, first_attn[3])
     arrive(("x", 3))
-    send_x(4)
-    arrive(("y", 2), ("d", 1), ("d", 2))
-    first_ffn = ffn_forward(0, first_attn[3])
-    arrive(("x", 4))
-    send_x(5)
+    second_attn_weights = order.wait(second_attn_weights)
+    second_attn = attn_forward(1, first_ffn[4])
+    second_in_weight = order.wait(second_in_weight)
     arrive(("y", 3), ("d", 3))
-    second_attn = attn_forward(1, first_ffn[4])
-    arrive(("x", 5), ("y", 4), ("y", 5), ("d", 4), ("d", 5))
     second_ffn = ffn_forward(1, second_attn[3])
     mixed_out = second_ffn[4]
     inputs = (tables_in, first_ffn[4])
@@ -798,7 +798,7 @@
             grad, small_attn[layer], kept, sent = attn_backward(
                 layer, way, d_resid, inputs[layer], qkv_rows, probs, context, small_others
             )
-        slabs[which] = Slab(way, BACKS[which], wide_bits, kept, sent)
+        slabs[which] = Slab(way, wide_count, kept, sent)
     qkv_grad, o_grad, *vectors = unpacked["attn"]
     in_grad, out_grad = unpacked["in"][0], unpacked["out"][0]
     return (

time: 488 us -> 608 us (1.25)
  waiting for transfers between devices: 221 us -> 338 us
  starting transfers between devices: 74.9 us -> 49.8 us
  other arithmetic: 18.7 us -> 38.3 us
  between operations: 2.77 us -> 15.8 us
    all_gather x0 -> x8, waiting for transfers between devices: none -> 62.2 us  [the longest x6 62.1 us: step(): lax.all_gather(piece, 'wide', axis=0, axis_index_groups=groups)]
    ppermute x70 -> x46, waiting for transfers between devices: 221 us -> 257 us  [swap(): return lax.ppermute(value, axis, [(i, i ^ bit) for i in range(count)])]
    ppermute x70 -> x46, starting transfers between devices: 71.8 us -> 47.6 us  [swap(): return lax.ppermute(value, axis, [(i, i ^ bit) for i in range(count)])]
    convert_element_type x24 -> x30, other arithmetic: 15.1 us -> 34 us  [added(): return (a.astype(f32) + b.astype(f32)).astype(low)]
    ppermute x3, waiting for transfers between devices: 0.01 us -> 18.5 us  [body(): lax.ppermute(packed, 'narrow', [(i, i ^ away) for i in range(4)])]
    pallas_call x16 -> x17, Pallas kernels: 144 us -> 141 us  [call(): pl.pallas_call(kernel, name=name, in_specs=in_specs, out_specs=out_specs,...]
  transfers between devices with their start and end apart: 73 -> 57, of which waited for: 36 -> 31; matrix products, arithmetic and copies ran while one was open for 5% -> 8% of each run, Pallas kernels for 19% -> 17%
where the time goes in v5:
time: 608 us; the launch traced here: 603 us
  waiting for transfers between devices  338 us (56%)
  Pallas kernels  141 us (23%)
  starting transfers between devices  49.8 us (8%)
  other arithmetic  38.3 us (6%)
  local copies, waits for them, and re-layouts  20 us (3%)
  between operations  15.8 us (3%)
    ppermute x46, waiting for transfers between devices, swap(): return lax.ppermute(value, axis, [(i, i ^ bit) for i in range(count)])  257 us
    pallas_call x17, Pallas kernels, call(): pl.pallas_call(kernel, name=name, in_specs=in_specs, out_specs=out_specs,...  141 us
    all_gather x6, waiting for transfers between devices, step(): lax.all_gather(piece, 'wide', axis=0, axis_index_groups=groups)  62.1 us
    ppermute x46, starting transfers between devices, swap(): return lax.ppermute(value, axis, [(i, i ^ bit) for i in range(count)])  47.6 us
    convert_element_type x30, other arithmetic, added(): return (a.astype(f32) + b.astype(f32)).astype(low)  34 us
    ppermute x3, waiting for transfers between devices, body(): lax.ppermute(packed, 'narrow', [(i, i ^ away) for i in range(4)])  18.5 us
  transfers between devices with their start and end apart: 57, of which 31 were waited for; matrix products, arithmetic and copies ran while one was open for 8% of the time, Pallas kernels for 17%

profile of v5, /device:TPU:0, one launch (start us, length us, event | category | flops | bytes accessed | tf_op | source)
XLA Modules:
  0.0 603.3 jit_solution(16836050122132725931)
XLA Ops:
  14.0 2.5 collective-permute-start
  18.1 1.7 collective-permute-start.2
  22.7 17.4 %collective-permute-done.3 = f32[2,12,192]{2,1,0:T(8,128)} collective-permute-done((f32[2,12,192]{2,1,0:T(8,128)}, f32[2,12,192]{2,1,0:T(8,128)}, u32[]{:S(2)}, u32[]{:S(2)}) %collective-permute-start.3) | collective-permute-done | bytes 18464 | tf_op jit(solution)/shard_map/ppermute | solution.py:572
  48.4 4.2 collective-permute-done.8.rest_1_
  57.2 12.9 %collective-permute-done.4.rest_5_ = bf16[96,3072]{1,0:T(8,128)(2,1)} collective-permute-done((bf16[96,3072]{1,0:T(8,128)(2,1)}, bf16[96,3072]{1,0:T(8,128)(2,1)}, u32[]{:S(2)}, u32[]{:S(2)}) %collective-permute-start.4) | collective-permute-done | bytes 589856 | tf_op jit(solution)/shard_map/ppermute | solution.py:22
  71.6 2.5 collective-permute-start.10
  74.8 26.0 %collective-permute-done.10.rest_2_ = bf16[96,3072]{1,0:T(8,128)(2,1)S(1)} collective-permute-done((bf16[96,3072]{1,0:T(8,128)(2,1)S(1)}, bf16[96,3072]{1,0:T(8,128)(2,1)S(1)}, u32[]{:S(2)}, u32[]{:S(2)}) %collective-permute-start.10) | collective-permute-done | bytes 589856 | tf_op jit(solution)/shard_map/ppermute | solution.py:22
  102.2 2.0 collective-permute-start.11
  105.1 12.2 %attn_fwd.2 = (bf16[256,2304]{1,0:T(8,128)(2,1)}, bf16[12,256,256]{2,1,0:T(8,128)(2,1)}, bf16[256,768]{1,0:T(8,128)(2,1)}, f32[256,768]{1,0:T(8,128)}, f32[256,1]{1,0:T(8,128)}) custom-call(s32[6]{0:T(128)} %stack.50.ids, s32[1]{0:T(128)S(6)} %copy.49.length, bf16[256,768]{1,0:T(8,128)(2,1)} %x.2, s32[1,256]{1,0:T(1,128)} %cell_row.3, ...), custom_call_target="tpu_custom_call" | custom-call | flops 14300000256 | bytes 46800000 | tf_op jit(solution)/shard_map/attn_fwd/pallas_call | solution.py:405
  117.3 6.7 %collective-permute-done.11.rest_7_ = bf16[384,768]{1,0:T(8,128)(2,1)S(1)} collective-permute-done((bf16[384,768]{1,0:T(8,128)(2,1)S(1)}, bf16[384,768]{1,0:T(8,128)(2,1)S(1)}, u32[]{:S(2)}, u32[]{:S(2)}) %collective-permute-start.11) | collective-permute-done | bytes 589856 | tf_op jit(solution)/shard_map/ppermute | solution.py:22
  126.4 12.5 %collective-permute-done.12.rest_8_ = bf16[384,768]{1,0:T(8,128)(2,1)S(1)} collective-permute-done((bf16[384,768]{1,0:T(8,128)(2,1)S(1)}, bf16[384,768]{1,0:T(8,128)(2,1)S(1)}, u32[]{:S(2)}, u32[]{:S(2)}) %collective-permute-start.12) | collective-permute-done | bytes 589856 | tf_op jit(solution)/shard_map/ppermute | solution.py:22
  139.3 2.5 collective-permute-done.14.rest_9_
  142.9 10.0 %ffn_fwd.2 = (bf16[256,3072]{1,0:T(8,128)(2,1)}, f32[256,3072]{1,0:T(8,128)}, f32[256,768]{1,0:T(8,128)}, f32[256,1]{1,0:T(8,128)}, bf16[256,768]{1,0:T(8,128)(2,1)}) custom-call(s32[6]{0:T(128)} %stack.50.ids, f32[256,768]{1,0:T(8,128)} %get-tuple-element.198.unit_one, f32[2,1,3072]{2,1,0:T(1,128)} %reshape.471.in_bias, f32[2,8,768]{2,1,0:T(8,128)} %reshape.470.small, ...), custom_call_target="tpu_custom_call" | custom-call | flops 11000000512 | bytes 36000000 | tf_op jit(solution)/shard_map/ffn_fwd/pallas_call | solution.py:405
  153.0 1.8 collective-permute-done.16.rest_3_
  156.3 12.1 %attn_fwd.3 = (bf16[256,2304]{1,0:T(8,128)(2,1)}, bf16[12,256,256]{2,1,0:T(8,128)(2,1)}, bf16[256,768]{1,0:T(8,128)(2,1)}, f32[256,768]{1,0:T(8,128)}, f32[256,1]{1,0:T(8,128)}) custom-call(s32[6]{0:T(128)} %stack.50.ids, s32[1]{0:T(128)S(6)} %copy.49.length, bf16[256,768]{1,0:T(8,128)(2,1)} %get-tuple-element.204.x, s32[1,256]{1,0:T(1,128)} %cell_row.3, ...), custom_call_target="tpu_custom_call" | custom-call | flops 14300000256 | bytes 46800000 | tf_op jit(solution)/shard_map/attn_fwd/pallas_call | solution.py:405
  169.8 2.8 collective-permute-done.18.rest_5_
  173.7 10.0 %ffn_fwd.3 = (bf16[256,3072]{1,0:T(8,128)(2,1)}, f32[256,3072]{1,0:T(8,128)}, f32[256,768]{1,0:T(8,128)}, f32[256,1]{1,0:T(8,128)}, bf16[256,768]{1,0:T(8,128)(2,1)}) custom-call(s32[6]{0:T(128)} %stack.50.ids, f32[256,768]{1,0:T(8,128)} %get-tuple-element.210.unit_one, f32[2,1,3072]{2,1,0:T(1,128)} %reshape.471.in_bias, f32[2,8,768]{2,1,0:T(8,128)} %reshape.470.small, ...), custom_call_target="tpu_custom_call" | custom-call | flops 11000000512 | bytes 36000000 | tf_op jit(solution)/shard_map/ffn_fwd/pallas_call | solution.py:405
  183.7 8.5 %out_bwd.2 = (bf16[256,768]{1,0:T(8,128)(2,1)}, f32[256,768]{1,0:T(8,128)}, f32[8,768]{1,0:T(8,128)}, bf16[2,2,2,2,192,384]{5,4,3,2,1,0:T(8,128)(2,1)}, bf16[2,2,2,2,192,384]{5,4,3,2,1,0:T(8,128)(2,1)}) custom-call(s32[6]{0:T(128)} %stack.50.ids, bf16[256,768]{1,0:T(8,128)(2,1)} %grad, f32[256,768]{1,0:T(8,128)} %get-tuple-element.214.unit_two, ...), custom_call_target="tpu_custom_call" | custom-call | flops 8800000000 | bytes 28800000 | tf_op jit(solution)/shard_map/out_bwd/pallas_call | solution.py:405
  192.4 14.3 %in_bwd.2 = (f32[256,768]{1,0:T(8,128)}, f32[8,768]{1,0:T(8,128)}, f32[1,3072]{1,0:T(1,128)}, bf16[2,2,2,2,192,384]{5,4,3,2,1,0:T(8,128)(2,1)}, bf16[2,2,2,2,192,384]{5,4,3,2,1,0:T(8,128)(2,1)}) custom-call(s32[6]{0:T(128)} %stack.50.ids, bf16[256,768]{1,0:T(8,128)(2,1)} %get-tuple-element.218.d_ffn, f32[256,768]{1,0:T(8,128)} %get-tuple-element.219.d_resid_two, ...), custom_call_target="tpu_custom_call" | custom-call | flops 15399999488 | bytes 50400000 | tf_op jit(solution)/shard_map/in_bwd/pallas_call | solution.py:405
  207.8 3.7 collective-permute-done.19
  211.5 1.7 add_convert_fusion.9
  213.2 15.5 %attn_bwd.2 = (bf16[256,768]{1,0:T(8,128)(2,1)}, f32[8,768]{1,0:T(8,128)}, bf16[2,2,2,2,192,384]{5,4,3,2,1,0:T(8,128)(2,1)}, bf16[2,2,2,2,192,384]{5,4,3,2,1,0:T(8,128)(2,1)}) custom-call(s32[6]{0:T(128)} %stack.50.ids, f32[256,768]{1,0:T(8,128)} %get-tuple-element.229.d_resid, bf16[256,768]{1,0:T(8,128)(2,1)} %get-tuple-element.204.x, ...), custom_call_target="tpu_custom_call" | custom-call | flops 17600000000 | bytes 57600000 | tf_op jit(solution)/shard_map/attn_bwd/pallas_call | solution.py:405
  231.2 8.5 %out_bwd.3 = (bf16[256,768]{1,0:T(8,128)(2,1)}, f32[256,768]{1,0:T(8,128)}, f32[8,768]{1,0:T(8,128)}, bf16[2,2,2,2,192,384]{5,4,3,2,1,0:T(8,128)(2,1)}, bf16[2,2,2,2,192,384]{5,4,3,2,1,0:T(8,128)(2,1)}) custom-call(s32[6]{0:T(128)} %stack.50.ids, bf16[256,768]{1,0:T(8,128)(2,1)} %get-tuple-element.235.grad, f32[256,768]{1,0:T(8,128)} %get-tuple-element.236.unit_two, ...), custom_call_target="tpu_custom_call" | custom-call | flops 8800000000 | bytes 28800000 | tf_op jit(solution)/shard_map/out_bwd/pallas_call | solution.py:405
  239.7 17.6 %collective-permute-done.23 = bf16[2,2,2,192,384]{4,3,2,1,0:T(8,128)(2,1)} collective-permute-done((bf16[2,2,2,192,384]{4,3,2,1,0:T(8,128)(2,1)S(1)}, bf16[2,2,2,192,384]{4,3,2,1,0:T(8,128)(2,1)}, u32[]{:S(2)}, u32[]{:S(2)}) %collective-permute-start.23) | collective-permute-done | bytes 1179680 | tf_op jit(solution)/shard_map/ppermute | solution.py:22
  257.3 2.7 fusion.14
  260.0 3.3 add_convert_fusion.4
  263.3 2.6 fusion.15
  266.0 14.4 %in_bwd.3 = (f32[256,768]{1,0:T(8,128)}, f32[8,768]{1,0:T(8,128)}, f32[1,3072]{1,0:T(1,128)}, bf16[2,2,2,2,192,384]{5,4,3,2,1,0:T(8,128)(2,1)}, bf16[2,2,2,2,192,384]{5,4,3,2,1,0:T(8,128)(2,1)}) custom-call(s32[6]{0:T(128)} %stack.50.ids, bf16[256,768]{1,0:T(8,128)(2,1)} %get-tuple-element.245.d_ffn, f32[256,768]{1,0:T(8,128)} %get-tuple-element.246.d_resid_two, ...), custom_call_target="tpu_custom_call" | custom-call | flops 15399999488 | bytes 50400000 | tf_op jit(solution)/shard_map/in_bwd/pallas_call | solution.py:405
  284.1 12.6 %collective-permute-done.25 = bf16[2,2,192,384]{3,2,1,0:T(8,128)(2,1)S(1)} collective-permute-done((bf16[2,2,192,384]{3,2,1,0:T(8,128)(2,1)S(1)}, bf16[2,2,192,384]{3,2,1,0:T(8,128)(2,1)S(1)}, u32[]{:S(2)}, u32[]{:S(2)}) %collective-permute-start.25) | collective-permute-done | bytes 589856 | tf_op jit(solution)/shard_map/ppermute | solution.py:22
  298.4 1.8 add_convert_fusion.3
  300.2 1.7 add_convert_fusion.2
  301.9 3.1 collective-permute-done.26
  305.0 2.5 collective-permute-start.31
  310.0 2.9 collective-permute-done.31
  313.7 7.9 %collective-permute-done.30 = bf16[2,2,2,192,384]{4,3,2,1,0:T(8,128)(2,1)} collective-permute-done((bf16[2,2,2,192,384]{4,3,2,1,0:T(8,128)(2,1)}, bf16[2,2,2,192,384]{4,3,2,1,0:T(8,128)(2,1)}, u32[]{:S(2)}, u32[]{:S(2)}) %collective-permute-start.30) | collective-permute-done | bytes 1179680 | tf_op jit(solution)/shard_map/ppermute | solution.py:22
  321.6 2.6 fusion.12
  325.2 16.0 %attn_bwd.3 = (bf16[256,768]{1,0:T(8,128)(2,1)}, f32[8,768]{1,0:T(8,128)}, bf16[2,2,2,2,208,384]{5,4,3,2,1,0:T(8,128)(2,1)}, bf16[2,2,2,2,208,384]{5,4,3,2,1,0:T(8,128)(2,1)}) custom-call(s32[6]{0:T(128)} %stack.50.ids, f32[256,768]{1,0:T(8,128)} %get-tuple-element.262.d_resid, bf16[256,768]{1,0:T(8,128)(2,1)} %x.2, ...), custom_call_target="tpu_custom_call" | custom-call | flops 17600000000 | bytes 57600000 | tf_op jit(solution)/shard_map/attn_bwd/pallas_call | solution.py:405
  342.8 2.4 collective-permute-start.35
  346.3 12.0 %collective-permute-done.35 = bf16[192,384]{1,0:T(8,128)(2,1)S(1)} collective-permute-done((bf16[192,384]{1,0:T(8,128)(2,1)S(1)}, bf16[192,384]{1,0:T(8,128)(2,1)S(1)}, u32[]{:S(2)}, u32[]{:S(2)}) %collective-permute-start.35) | collective-permute-done | bytes 147488 | tf_op jit(solution)/shard_map/ppermute | solution.py:22
  360.0 14.8 %collective-permute-done.34 = bf16[2,2,2,192,384]{4,3,2,1,0:T(8,128)(2,1)} collective-permute-done((bf16[2,2,2,192,384]{4,3,2,1,0:T(8,128)(2,1)S(1)}, bf16[2,2,2,192,384]{4,3,2,1,0:T(8,128)(2,1)}, u32[]{:S(2)}, u32[]{:S(2)}) %collective-permute-start.34) | collective-permute-done | bytes 1179680 | tf_op jit(solution)/shard_map/ppermute | solution.py:22
  374.9 1.7 fusion.10
  378.1 9.2 %collective-permute-done.33 = bf16[2,2,192,384]{3,2,1,0:T(8,128)(2,1)} collective-permute-done((bf16[2,2,192,384]{3,2,1,0:T(8,128)(2,1)}, bf16[2,2,192,384]{3,2,1,0:T(8,128)(2,1)}, u32[]{:S(2)}, u32[]{:S(2)}) %collective-permute-start.33) | collective-permute-done | bytes 589856 | tf_op jit(solution)/shard_map/ppermute | solution.py:22
  391.6 3.4 fusion
  395.0 2.3 fusion.25
  397.3 7.2 %collective-permute-done.41 = bf16[2,192,384]{2,1,0:T(8,128)(2,1)S(1)} collective-permute-done((bf16[2,192,384]{2,1,0:T(8,128)(2,1)S(1)}, bf16[2,192,384]{2,1,0:T(8,128)(2,1)S(1)}, u32[]{:S(2)}, u32[]{:S(2)}) %collective-permute-start.41) | collective-permute-done | bytes 294944 | tf_op jit(solution)/shard_map/ppermute | solution.py:22
  404.5 2.3 collective-permute-start.42
  407.0 6.8 %collective-permute-done.42 = bf16[192,384]{1,0:T(8,128)(2,1)S(1)} collective-permute-done((bf16[192,384]{1,0:T(8,128)(2,1)S(1)}, bf16[192,384]{1,0:T(8,128)(2,1)S(1)}, u32[]{:S(2)}, u32[]{:S(2)}) %collective-permute-start.42) | collective-permute-done | bytes 147488 | tf_op jit(solution)/shard_map/ppermute | solution.py:22
  414.6 1.7 collective-permute-start.40
  416.4 15.2 %collective-permute-done.40 = bf16[2,2,192,384]{3,2,1,0:T(8,128)(2,1)S(1)} collective-permute-done((bf16[2,2,192,384]{3,2,1,0:T(8,128)(2,1)S(1)}, bf16[2,2,192,384]{3,2,1,0:T(8,128)(2,1)S(1)}, u32[]{:S(2)}, u32[]{:S(2)}) %collective-permute-start.40) | collective-permute-done | bytes 589856 | tf_op jit(solution)/shard_map/ppermute | solution.py:22
  431.8 2.8 collective-permute-start.43
  434.7 9.5 %collective-permute-done.44 = bf16[2,192,384]{2,1,0:T(8,128)(2,1)S(1)} collective-permute-done((bf16[2,192,384]{2,1,0:T(8,128)(2,1)S(1)}, bf16[2,192,384]{2,1,0:T(8,128)(2,1)S(1)}, u32[]{:S(2)}, u32[]{:S(2)}) %collective-permute-start.44) | collective-permute-done | bytes 294944 | tf_op jit(solution)/shard_map/ppermute | solution.py:22
  447.6 27.3 %collective-permute-done.36 = bf16[2,2,2,208,384]{4,3,2,1,0:T(8,128)(2,1)S(1)} collective-permute-done((bf16[2,2,2,208,384]{4,3,2,1,0:T(8,128)(2,1)}, bf16[2,2,2,208,384]{4,3,2,1,0:T(8,128)(2,1)S(1)}, u32[]{:S(2)}, u32[]{:S(2)}) %collective-permute-start.36) | collective-permute-done | bytes 1277984 | tf_op jit(solution)/shard_map/ppermute | solution.py:22
  477.5 16.5 %collective-permute-done.45 = bf16[2,2,208,384]{3,2,1,0:T(8,128)(2,1)S(1)} collective-permute-done((bf16[2,2,208,384]{3,2,1,0:T(8,128)(2,1)S(1)}, bf16[2,2,208,384]{3,2,1,0:T(8,128)(2,1)S(1)}, u32[]{:S(2)}, u32[]{:S(2)}) %collective-permute-start.45) | collective-permute-done | bytes 639008 | tf_op jit(solution)/shard_map/ppermute | solution.py:22
  494.2 12.5 %collective-permute-done.46 = bf16[2,208,384]{2,1,0:T(8,128)(2,1)S(1)} collective-permute-done((bf16[2,208,384]{2,1,0:T(8,128)(2,1)S(1)}, bf16[2,208,384]{2,1,0:T(8,128)(2,1)S(1)}, u32[]{:S(2)}, u32[]{:S(2)}) %collective-permute-start.46) | collective-permute-done | bytes 319520 | tf_op jit(solution)/shard_map/ppermute | solution.py:22
  506.8 1.9 collective-permute-start.47
  508.8 5.9 collective-permute-done.47
  515.4 3.1 unpack.10
  518.5 3.1 unpack.8
  521.6 3.1 unpack.6
  524.7 3.1 unpack.11
  527.8 22.4 %all-gather.24.cloned.1.call-done = bf16[1536,384]{1,0:T(8,128)(2,1)} async-done(((bf16[192,384]{1,0:T(8,128)(2,1)}), bf16[1536,384]{1,0:T(8,128)(2,1)}) %all-gather.24.cloned.1.call-update) | async-done | bytes 1179664 | tf_op jit(solution)/shard_map/all_gather | solution.py:479
  550.1 3.1 unpack.9
  553.2 39.7 %all-gather.20.cloned.1.call-done = bf16[1664,384]{1,0:T(8,128)(2,1)} async-done(((bf16[208,384]{1,0:T(8,128)(2,1)}), bf16[1664,384]{1,0:T(8,128)(2,1)}) %all-gather.20.cloned.1.call-update) | async-done | bytes 1277968 | tf_op jit(solution)/shard_map/all_gather | solution.py:479
  592.9 3.1 unpack.7
  (185 shorter events, 67.6 us)
Async XLA Ops:
  7.2 149.1 %all-gather.16.cloned.1.call-start = ((), (), s32[]{:S(2)}) async-start(), calls=%async_computation | async-start | bytes 5898240 | tf_op jit(solution)/shard_map/all_gather | solution.py:557
  10.6 157.8 %all-gather.18.cloned.1.call-start = ((), (), s32[]{:S(2)}) async-start(), calls=%async_computation.1 | async-start | bytes 5898240 | tf_op jit(solution)/shard_map/all_gather | solution.py:560
  13.5 27.7 %collective-permute-start.6 = (bf16[2,192,2304]{2,1,0:T(8,128)(2,1)}, bf16[2,192,2304]{2,1,0:T(8,128)(2,1)}, u32[]{:S(2)}, u32[]{:S(2)}) collective-permute-start(bf16[2,192,2304]{2,1,0:T(8,128)(2,1)} %rest_0_.7), channel_id=1, source_target_pairs={{0,1},{1,0},{2,3},{3,2},{4,5},{5,4},{6,7},{7,6},{8,9},{9,8},{10,11... | collective-permute-start | bytes 5308424 | tf_op jit(solution)/shard_map/ppermute | solution.py:22
  14.0 27.2 %collective-permute-start = (bf16[96,3072]{1,0:T(8,128)(2,1)}, bf16[96,3072]{1,0:T(8,128)(2,1)}, u32[]{:S(2)}, u32[]{:S(2)}) collective-permute-start(bf16[96,3072]{1,0:T(8,128)(2,1)} %pad_maximum_fusion.3), channel_id=1, source_target_pairs={{0,2},{1,3},{2,0},{3,1},{4,6},{5,7},{6,4},{7,5},{8,10},{9,11},{10,... | collective-permute-start | bytes 1769480 | tf_op jit(solution)/shard_map/ppermute | solution.py:22
  18.0 22.2 %collective-permute-start.3 = (f32[2,12,192]{2,1,0:T(8,128)}, f32[2,12,192]{2,1,0:T(8,128)}, u32[]{:S(2)}, u32[]{:S(2)}) collective-permute-start(f32[2,12,192]{2,1,0:T(8,128)} %pack.1), channel_id=1, source_target_pairs={{0,3},{1,2},{2,1},{3,0},{4,7},{5,6},{6,5},{7,4},{8,11},{9,10},{10,... | collective-permute-start | bytes 55304 | tf_op jit(solution)/shard_map/ppermute | solution.py:572
  18.1 23.1 %collective-permute-start.2 = (f32[2,12,192]{2,1,0:T(8,128)}, f32[2,12,192]{2,1,0:T(8,128)}, u32[]{:S(2)}, u32[]{:S(2)}) collective-permute-start(f32[2,12,192]{2,1,0:T(8,128)} %pack.1), channel_id=1, source_target_pairs={{0,2},{1,3},{2,0},{3,1},{4,6},{5,7},{6,4},{7,5},{8,10},{9,11},{10,... | collective-permute-start | bytes 55304 | tf_op jit(solution)/shard_map/ppermute | solution.py:572
  19.8 21.4 %collective-permute-start.1 = (f32[2,12,192]{2,1,0:T(8,128)}, f32[2,12,192]{2,1,0:T(8,128)}, u32[]{:S(2)}, u32[]{:S(2)}) collective-permute-start(f32[2,12,192]{2,1,0:T(8,128)} %pack.1), channel_id=1, source_target_pairs={{0,1},{1,0},{2,3},{3,2},{4,5},{5,4},{6,7},{7,6},{8,9},{9,8},{10,11... | collective-permute-start | bytes 55304 | tf_op jit(solution)/shard_map/ppermute | solution.py:572
  41.2 6.7 %collective-permute-start.7 = (bf16[2,192,768]{2,1,0:T(8,128)(2,1)}, bf16[2,192,768]{2,1,0:T(8,128)(2,1)}, u32[]{:S(2)}, u32[]{:S(2)}) collective-permute-start(bf16[2,192,768]{2,1,0:T(8,128)(2,1)} %rest_2_.3), channel_id=1, source_target_pairs={{0,1},{1,0},{2,3},{3,2},{4,5},{5,4},{6,7},{7,6},{8,9},{9,8},{10,11... | collective-permute-start | bytes 1769480 | tf_op jit(solution)/shard_map/ppermute | solution.py:22
  47.9 4.7 collective-permute-start.8
  54.0 50.1 %collective-permute-start.9 = (bf16[2,768,768]{2,1,0:T(8,128)(2,1)}, bf16[2,768,768]{2,1,0:T(8,128)(2,1)}, u32[]{:S(2)}, u32[]{:S(2)}) collective-permute-start(bf16[2,768,768]{2,1,0:T(8,128)(2,1)} %rest_5_.3), channel_id=1, source_target_pairs={{0,1},{1,0},{2,3},{3,2},{4,5},{5,4},{6,7},{7,6},{8,9},{9,8},{10,11... | collective-permute-start | bytes 7077896 | tf_op jit(solution)/shard_map/ppermute | solution.py:22
  54.4 15.7 %collective-permute-start.4 = (bf16[96,3072]{1,0:T(8,128)(2,1)}, bf16[96,3072]{1,0:T(8,128)(2,1)}, u32[]{:S(2)}, u32[]{:S(2)}) collective-permute-start(bf16[96,3072]{1,0:T(8,128)(2,1)} %collective-permute-done.rest_4_), channel_id=1, source_target_pairs={{0,4},{4,0},{8,12},{12,8},{16,20},{20,16},{24,28},{28,24},{1,5},{5... | collective-permute-start | bytes 1769480 | tf_op jit(solution)/shard_map/ppermute | solution.py:22
  57.1 458.3 %all-gather.30.cloned.1.call-start = ((), (), s32[]{:S(2)}) async-start(), calls=%async_computation.7 | async-start | bytes 1327104 | tf_op jit(solution)/shard_map/all_gather | solution.py:479
  71.5 32.6 %collective-permute-start.5 = (bf16[192,3072]{1,0:T(8,128)(2,1)S(1)}, bf16[192,3072]{1,0:T(8,128)(2,1)S(1)}, u32[]{:S(2)}, u32[]{:S(2)}) collective-permute-start(bf16[192,3072]{1,0:T(8,128)(2,1)S(1)} %pad_maximum_fusion), channel_id=1, source_target_pairs={{0,1},{1,0},{2,3},{3,2},{4,5},{5,4},{6,7},{7,6},{8,9},{9,8},{10,11... | collective-permute-start | bytes 3538952 | tf_op jit(solution)/shard_map/ppermute | solution.py:22
  71.6 29.2 %collective-permute-start.10 = (bf16[96,3072]{1,0:T(8,128)(2,1)S(1)}, bf16[96,3072]{1,0:T(8,128)(2,1)S(1)}, u32[]{:S(2)}, u32[]{:S(2)}) collective-permute-start(bf16[96,3072]{1,0:T(8,128)(2,1)S(1)} %copy-done.16), channel_id=1, source_target_pairs={{0,2},{1,3},{2,0},{3,1},{4,6},{5,7},{6,4},{7,5},{8,10},{9,11},{10,... | collective-permute-start | bytes 1769480 | tf_op jit(solution)/shard_map/ppermute | solution.py:22
  100.8 24.7 %copy-start.19 = (bf16[96,3072]{1,0:T(8,128)(2,1)}, bf16[96,3072]{1,0:T(8,128)(2,1)S(1)}, u32[]{:S(2)}) copy-start(bf16[96,3072]{1,0:T(8,128)(2,1)S(1)} %collective-permute-done.10.rest_2_) | copy-start | bytes 1769476
  100.8 24.7 %collective-permute-start.13 = (bf16[96,3072]{1,0:T(8,128)(2,1)S(1)}, bf16[96,3072]{1,0:T(8,128)(2,1)S(1)}, u32[]{:S(2)}, u32[]{:S(2)}) collective-permute-start(bf16[96,3072]{1,0:T(8,128)(2,1)S(1)} %collective-permute-done.10.rest_2_), channel_id=1, source_target_pairs={{0,4},{4,0},{8,12},{12,8},{16,20},{20,16},{24,28},{28,24},{1,5},{5... | collective-permute-start | bytes 1769480 | tf_op jit(solution)/shard_map/ppermute | solution.py:22
  102.2 21.8 %collective-permute-start.11 = (bf16[384,768]{1,0:T(8,128)(2,1)S(1)}, bf16[384,768]{1,0:T(8,128)(2,1)S(1)}, u32[]{:S(2)}, u32[]{:S(2)}) collective-permute-start(bf16[384,768]{1,0:T(8,128)(2,1)S(1)} %get-tuple-element.192), channel_id=1, source_target_pairs={{0,2},{1,3},{2,0},{3,1},{4,6},{5,7},{6,4},{7,5},{8,10},{9,11},{10,... | collective-permute-start | bytes 1769480 | tf_op jit(solution)/shard_map/ppermute | solution.py:22
  124.0 14.9 %collective-permute-start.12 = (bf16[384,768]{1,0:T(8,128)(2,1)S(1)}, bf16[384,768]{1,0:T(8,128)(2,1)S(1)}, u32[]{:S(2)}, u32[]{:S(2)}) collective-permute-start(bf16[384,768]{1,0:T(8,128)(2,1)S(1)} %collective-permute-done.11.rest_7_), channel_id=1, source_target_pairs={{0,4},{4,0},{8,12},{12,8},{16,20},{20,16},{24,28},{28,24},{1,5},{5... | collective-permute-start | bytes 1769480 | tf_op jit(solution)/shard_map/ppermute | solution.py:22
  126.3 13.0 %collective-permute-start.15 = (bf16[192,3072]{1,0:T(8,128)(2,1)S(1)}, bf16[192,3072]{1,0:T(8,128)(2,1)S(1)}, u32[]{:S(2)}, u32[]{:S(2)}) collective-permute-start(bf16[192,3072]{1,0:T(8,128)(2,1)S(1)} %pad_maximum_fusion.1), channel_id=1, source_target_pairs={{0,1},{1,0},{2,3},{3,2},{4,5},{5,4},{6,7},{7,6},{8,9},{9,8},{10,11... | collective-permute-start | bytes 3538952 | tf_op jit(solution)/shard_map/ppermute | solution.py:22
  139.0 2.9 collective-permute-start.14
  139.0 15.7 %collective-permute-start.16 = (bf16[384,768]{1,0:T(8,128)(2,1)S(1)}, bf16[384,768]{1,0:T(8,128)(2,1)S(1)}, u32[]{:S(2)}, u32[]{:S(2)}) collective-permute-start(bf16[384,768]{1,0:T(8,128)(2,1)S(1)} %get-tuple-element.200), channel_id=1, source_target_pairs={{0,2},{1,3},{2,0},{3,1},{4,6},{5,7},{6,4},{7,5},{8,10},{9,11},{10,... | collective-permute-start | bytes 1769480 | tf_op jit(solution)/shard_map/ppermute | solution.py:22
  154.8 14.9 %collective-permute-start.17 = (bf16[384,768]{1,0:T(8,128)(2,1)S(1)}, bf16[384,768]{1,0:T(8,128)(2,1)S(1)}, u32[]{:S(2)}, u32[]{:S(2)}) collective-permute-start(bf16[384,768]{1,0:T(8,128)(2,1)S(1)} %collective-permute-done.16.rest_3_), channel_id=1, source_target_pairs={{0,4},{4,0},{8,12},{12,8},{16,20},{20,16},{24,28},{28,24},{1,5},{5... | collective-permute-start | bytes 1769480 | tf_op jit(solution)/shard_map/ppermute | solution.py:22
  169.7 2.9 collective-permute-start.18
  192.2 15.0 %collective-permute-start.20 = (bf16[2,2,2,2,192,384]{5,4,3,2,1,0:T(8,128)(2,1)}, bf16[2,2,2,2,192,384]{5,4,3,2,1,0:T(8,128)(2,1)S(1)}, u32[]{:S(2)}, u32[]{:S(2)}) collective-permute-start(bf16[2,2,2,2,192,384]{5,4,3,2,1,0:T(8,128)(2,1)} %get-tuple-element.225), channel_id=1, source_target_pairs={{0,1},{1,0},{2,3},{3,2},{4,5},{5,4},{6,7},{7,6},{8,9},{9,8},{10,11... | collective-permute-start | bytes 7077896 | tf_op jit(solution)/shard_map/ppermute | solution.py:22
  192.4 14.7 %copy-start.4 = (bf16[2,2,2,2,192,384]{5,4,3,2,1,0:T(8,128)(2,1)S(1)}, bf16[2,2,2,2,192,384]{5,4,3,2,1,0:T(8,128)(2,1)}, u32[]{:S(2)}) copy-start(bf16[2,2,2,2,192,384]{5,4,3,2,1,0:T(8,128)(2,1)} %get-tuple-element.224) | copy-start | bytes 7077892
  206.7 4.8 collective-permute-start.19
  228.7 31.3 %collective-permute-start.22 = (bf16[2,2,2,2,192,384]{5,4,3,2,1,0:T(8,128)(2,1)}, bf16[2,2,2,2,192,384]{5,4,3,2,1,0:T(8,128)(2,1)}, u32[]{:S(2)}, u32[]{:S(2)}) collective-permute-start(bf16[2,2,2,2,192,384]{5,4,3,2,1,0:T(8,128)(2,1)} %get-tuple-element.240), channel_id=1, source_target_pairs={{0,1},{1,0},{2,3},{3,2},{4,5},{5,4},{6,7},{7,6},{8,9},{9,8},{10,11... | collective-permute-start | bytes 7077896 | tf_op jit(solution)/shard_map/ppermute | solution.py:22
  229.2 28.1 %collective-permute-start.23 = (bf16[2,2,2,192,384]{4,3,2,1,0:T(8,128)(2,1)S(1)}, bf16[2,2,2,192,384]{4,3,2,1,0:T(8,128)(2,1)}, u32[]{:S(2)}, u32[]{:S(2)}) collective-permute-start(bf16[2,2,2,192,384]{4,3,2,1,0:T(8,128)(2,1)S(1)} %get-tuple-element.314), channel_id=1, source_target_pairs={{0,4},{4,0},{8,12},{12,8},{16,20},{20,16},{24,28},{28,24},{1,5},{5... | collective-permute-start | bytes 3538952 | tf_op jit(solution)/shard_map/ppermute | solution.py:22
  230.7 32.7 %collective-permute-start.21 = (bf16[2,2,2,192,384]{4,3,2,1,0:T(8,128)(2,1)}, bf16[2,2,2,192,384]{4,3,2,1,0:T(8,128)(2,1)}, u32[]{:S(2)}, u32[]{:S(2)}) collective-permute-start(bf16[2,2,2,192,384]{4,3,2,1,0:T(8,128)(2,1)} %get-tuple-element.316), channel_id=1, source_target_pairs={{0,2},{1,3},{2,0},{3,1},{4,6},{5,7},{6,4},{7,5},{8,10},{9,11},{10,... | collective-permute-start | bytes 3538952 | tf_op jit(solution)/shard_map/ppermute | solution.py:22
  239.6 58.8 %collective-permute-start.28 = (bf16[2,2,2,2,192,384]{5,4,3,2,1,0:T(8,128)(2,1)}, bf16[2,2,2,2,192,384]{5,4,3,2,1,0:T(8,128)(2,1)S(1)}, u32[]{:S(2)}, u32[]{:S(2)}) collective-permute-start(bf16[2,2,2,2,192,384]{5,4,3,2,1,0:T(8,128)(2,1)} %get-tuple-element.254), channel_id=1, source_target_pairs={{0,1},{1,0},{2,3},{3,2},{4,5},{5,4},{6,7},{7,6},{8,9},{9,8},{10,11... | collective-permute-start | bytes 7077896 | tf_op jit(solution)/shard_map/ppermute | solution.py:22
  265.9 30.7 %copy-start.8 = (bf16[1,2,2,192,384]{4,3,2,1,0:T(8,128)(2,1)S(1)}, bf16[1,2,2,192,384]{4,3,2,1,0:T(8,128)(2,1)}, u32[]{:S(2)}) copy-start(bf16[1,2,2,192,384]{4,3,2,1,0:T(8,128)(2,1)} %get-tuple-element.325) | copy-start | bytes 1769476
  265.9 32.5 %copy-start.1 = (bf16[2,2,2,2,192,384]{5,4,3,2,1,0:T(8,128)(2,1)S(1)}, bf16[2,2,2,2,192,384]{5,4,3,2,1,0:T(8,128)(2,1)}, u32[]{:S(2)}) copy-start(bf16[2,2,2,2,192,384]{5,4,3,2,1,0:T(8,128)(2,1)} %get-tuple-element.253) | copy-start | bytes 7077892
  280.4 19.8 %collective-permute-start.27 = (bf16[2,2,2,2,192,384]{5,4,3,2,1,0:T(8,128)(2,1)}, bf16[2,2,2,2,192,384]{5,4,3,2,1,0:T(8,128)(2,1)S(1)}, u32[]{:S(2)}, u32[]{:S(2)}) collective-permute-start(bf16[2,2,2,2,192,384]{5,4,3,2,1,0:T(8,128)(2,1)} %get-tuple-element.252), channel_id=1, source_target_pairs={{0,1},{1,0},{2,3},{3,2},{4,5},{5,4},{6,7},{7,6},{8,9},{9,8},{10,11... | collective-permute-start | bytes 7077896 | tf_op jit(solution)/shard_map/ppermute | solution.py:22
  280.5 16.2 %collective-permute-start.25 = (bf16[2,2,192,384]{3,2,1,0:T(8,128)(2,1)S(1)}, bf16[2,2,192,384]{3,2,1,0:T(8,128)(2,1)S(1)}, u32[]{:S(2)}, u32[]{:S(2)}) collective-permute-start(bf16[2,2,192,384]{3,2,1,0:T(8,128)(2,1)S(1)} %copy-done.12), channel_id=1, source_target_pairs={{0,2},{1,3},{2,0},{3,1},{4,6},{5,7},{6,4},{7,5},{8,10},{9,11},{10,... | collective-permute-start | bytes 1769480 | tf_op jit(solution)/shard_map/ppermute | solution.py:22
  280.8 26.7 %collective-permute-start.24 = (bf16[2,2,192,384]{3,2,1,0:T(8,128)(2,1)}, bf16[2,2,192,384]{3,2,1,0:T(8,128)(2,1)S(1)}, u32[]{:S(2)}, u32[]{:S(2)}) collective-permute-start(bf16[2,2,192,384]{3,2,1,0:T(8,128)(2,1)} %get-tuple-element.328), channel_id=1, source_target_pairs={{0,4},{4,0},{8,12},{12,8},{16,20},{20,16},{24,28},{28,24},{1,5},{5... | collective-permute-start | bytes 1769480 | tf_op jit(solution)/shard_map/ppermute | solution.py:22
  282.5 39.1 %collective-permute-start.30 = (bf16[2,2,2,192,384]{4,3,2,1,0:T(8,128)(2,1)}, bf16[2,2,2,192,384]{4,3,2,1,0:T(8,128)(2,1)}, u32[]{:S(2)}, u32[]{:S(2)}) collective-permute-start(bf16[2,2,2,192,384]{4,3,2,1,0:T(8,128)(2,1)} %get-tuple-element.312), channel_id=1, source_target_pairs={{0,2},{1,3},{2,0},{3,1},{4,6},{5,7},{6,4},{7,5},{8,10},{9,11},{10,... | collective-permute-start | bytes 3538952 | tf_op jit(solution)/shard_map/ppermute | solution.py:22
  296.8 8.2 %collective-permute-start.26 = (bf16[2,192,384]{2,1,0:T(8,128)(2,1)S(1)}, bf16[2,192,384]{2,1,0:T(8,128)(2,1)S(1)}, u32[]{:S(2)}, u32[]{:S(2)}) collective-permute-start(bf16[2,192,384]{2,1,0:T(8,128)(2,1)S(1)} %get-tuple-element.341), channel_id=1, source_target_pairs={{0,8},{4,12},{8,0},{12,4},{16,24},{20,28},{24,16},{28,20},{1,9},{5... | collective-permute-start | bytes 884744 | tf_op jit(solution)/shard_map/ppermute | solution.py:22
  305.0 7.9 %collective-permute-start.31 = (bf16[192,384]{1,0:T(8,128)(2,1)S(1)}, bf16[192,384]{1,0:T(8,128)(2,1)S(1)}, u32[]{:S(2)}, u32[]{:S(2)}) collective-permute-start(bf16[192,384]{1,0:T(8,128)(2,1)S(1)} %fusion.62), channel_id=1, source_target_pairs={{0,16},{4,20},{8,24},{12,28},{16,0},{20,4},{24,8},{28,12},{1,17},{... | collective-permute-start | bytes 442376 | tf_op jit(solution)/shard_map/ppermute | solution.py:22
  308.5 15.7 %collective-permute-start.29 = (bf16[2,192,384]{2,1,0:T(8,128)(2,1)}, bf16[2,192,384]{2,1,0:T(8,128)(2,1)}, u32[]{:S(2)}, u32[]{:S(2)}) collective-permute-start(bf16[2,192,384]{2,1,0:T(8,128)(2,1)} %get-tuple-element.339), channel_id=1, source_target_pairs={{0,8},{4,12},{8,0},{12,4},{16,24},{20,28},{24,16},{28,20},{1,9},{5... | collective-permute-start | bytes 884744 | tf_op jit(solution)/shard_map/ppermute | solution.py:22
  313.7 204.9 %all-gather.26.cloned.1.call-start = ((), (), s32[]{:S(2)}) async-start(), calls=%async_computation.5 | async-start | bytes 1327104 | tf_op jit(solution)/shard_map/all_gather | solution.py:479
  325.2 16.1 %copy-start.10 = (bf16[2,2,2,192,384]{4,3,2,1,0:T(8,128)(2,1)S(1)}, bf16[2,2,2,192,384]{4,3,2,1,0:T(8,128)(2,1)}, u32[]{:S(2)}) copy-start(bf16[2,2,2,192,384]{4,3,2,1,0:T(8,128)(2,1)} %get-tuple-element.310) | copy-start | bytes 3538948
  341.2 50.4 %collective-permute-start.32 = (bf16[2,2,2,2,208,384]{5,4,3,2,1,0:T(8,128)(2,1)}, bf16[2,2,2,2,208,384]{5,4,3,2,1,0:T(8,128)(2,1)}, u32[]{:S(2)}, u32[]{:S(2)}) collective-permute-start(bf16[2,2,2,2,208,384]{5,4,3,2,1,0:T(8,128)(2,1)} %get-tuple-element.270), channel_id=1, source_target_pairs={{0,1},{1,0},{2,3},{3,2},{4,5},{5,4},{6,7},{7,6},{8,9},{9,8},{10,11... | collective-permute-start | bytes 7667720 | tf_op jit(solution)/shard_map/ppermute | solution.py:22
  341.3 33.6 %collective-permute-start.34 = (bf16[2,2,2,192,384]{4,3,2,1,0:T(8,128)(2,1)S(1)}, bf16[2,2,2,192,384]{4,3,2,1,0:T(8,128)(2,1)}, u32[]{:S(2)}, u32[]{:S(2)}) collective-permute-start(bf16[2,2,2,192,384]{4,3,2,1,0:T(8,128)(2,1)S(1)} %copy-done.10), channel_id=1, source_target_pairs={{0,4},{4,0},{8,12},{12,8},{16,20},{20,16},{24,28},{28,24},{1,5},{5... | collective-permute-start | bytes 3538952 | tf_op jit(solution)/shard_map/ppermute | solution.py:22
  342.8 15.5 %collective-permute-start.35 = (bf16[192,384]{1,0:T(8,128)(2,1)S(1)}, bf16[192,384]{1,0:T(8,128)(2,1)S(1)}, u32[]{:S(2)}, u32[]{:S(2)}) collective-permute-start(bf16[192,384]{1,0:T(8,128)(2,1)S(1)} %fusion.63), channel_id=1, source_target_pairs={{0,16},{4,20},{8,24},{12,28},{16,0},{20,4},{24,8},{28,12},{1,17},{... | collective-permute-start | bytes 442376 | tf_op jit(solution)/shard_map/ppermute | solution.py:22
  345.3 49.7 %collective-permute-start.39 = (bf16[2,2,2,192,384]{4,3,2,1,0:T(8,128)(2,1)}, bf16[2,2,2,192,384]{4,3,2,1,0:T(8,128)(2,1)}, u32[]{:S(2)}, u32[]{:S(2)}) collective-permute-start(bf16[2,2,2,192,384]{4,3,2,1,0:T(8,128)(2,1)} %get-tuple-element.308), channel_id=1, source_target_pairs={{0,2},{1,3},{2,0},{3,1},{4,6},{5,7},{6,4},{7,5},{8,10},{9,11},{10,... | collective-permute-start | bytes 3538952 | tf_op jit(solution)/shard_map/ppermute | solution.py:22
  345.7 41.6 %collective-permute-start.33 = (bf16[2,2,192,384]{3,2,1,0:T(8,128)(2,1)}, bf16[2,2,192,384]{3,2,1,0:T(8,128)(2,1)}, u32[]{:S(2)}, u32[]{:S(2)}) collective-permute-start(bf16[2,2,192,384]{3,2,1,0:T(8,128)(2,1)} %get-tuple-element.324), channel_id=1, source_target_pairs={{0,4},{4,0},{8,12},{12,8},{16,20},{20,16},{24,28},{28,24},{1,5},{5... | collective-permute-start | bytes 1769480 | tf_op jit(solution)/shard_map/ppermute | solution.py:22
  360.0 161.6 %all-gather.22.cloned.1.call-start = ((), (), s32[]{:S(2)}) async-start(), calls=%async_computation.3 | async-start | bytes 1327104 | tf_op jit(solution)/shard_map/all_gather | solution.py:479
  374.9 16.8 %copy-start = (bf16[2,2,2,2,208,384]{5,4,3,2,1,0:T(8,128)(2,1)S(1)}, bf16[2,2,2,2,208,384]{5,4,3,2,1,0:T(8,128)(2,1)}, u32[]{:S(2)}) copy-start(bf16[2,2,2,2,208,384]{5,4,3,2,1,0:T(8,128)(2,1)} %get-tuple-element.269) | copy-start | bytes 7667716
  376.5 15.1 %collective-permute-start.37 = (bf16[2,2,192,384]{3,2,1,0:T(8,128)(2,1)S(1)}, bf16[2,2,192,384]{3,2,1,0:T(8,128)(2,1)S(1)}, u32[]{:S(2)}, u32[]{:S(2)}) collective-permute-start(bf16[2,2,192,384]{3,2,1,0:T(8,128)(2,1)S(1)} %get-tuple-element.322), channel_id=1, source_target_pairs={{0,2},{1,3},{2,0},{3,1},{4,6},{5,7},{6,4},{7,5},{8,10},{9,11},{10,... | collective-permute-start | bytes 1769480 | tf_op jit(solution)/shard_map/ppermute | solution.py:22
  388.5 15.9 %collective-permute-start.41 = (bf16[2,192,384]{2,1,0:T(8,128)(2,1)S(1)}, bf16[2,192,384]{2,1,0:T(8,128)(2,1)S(1)}, u32[]{:S(2)}, u32[]{:S(2)}) collective-permute-start(bf16[2,192,384]{2,1,0:T(8,128)(2,1)S(1)} %get-tuple-element.336), channel_id=1, source_target_pairs={{0,8},{4,12},{8,0},{12,4},{16,24},{20,28},{24,16},{28,20},{1,9},{5... | collective-permute-start | bytes 884744 | tf_op jit(solution)/shard_map/ppermute | solution.py:22
  404.5 9.3 %collective-permute-start.42 = (bf16[192,384]{1,0:T(8,128)(2,1)S(1)}, bf16[192,384]{1,0:T(8,128)(2,1)S(1)}, u32[]{:S(2)}, u32[]{:S(2)}) collective-permute-start(bf16[192,384]{1,0:T(8,128)(2,1)S(1)} %fusion.68), channel_id=1, source_target_pairs={{0,16},{4,20},{8,24},{12,28},{16,0},{20,4},{24,8},{28,12},{1,17},{... | collective-permute-start | bytes 442376 | tf_op jit(solution)/shard_map/ppermute | solution.py:22
  414.6 110.1 %all-gather.28.cloned.1.call-start = ((), (), s32[]{:S(2)}) async-start(), calls=%async_computation.6 | async-start | bytes 1327104 | tf_op jit(solution)/shard_map/all_gather | solution.py:479
  414.6 16.9 %collective-permute-start.40 = (bf16[2,2,192,384]{3,2,1,0:T(8,128)(2,1)S(1)}, bf16[2,2,192,384]{3,2,1,0:T(8,128)(2,1)S(1)}, u32[]{:S(2)}, u32[]{:S(2)}) collective-permute-start(bf16[2,2,192,384]{3,2,1,0:T(8,128)(2,1)S(1)} %copy-done.13), channel_id=1, source_target_pairs={{0,4},{4,0},{8,12},{12,8},{16,20},{20,16},{24,28},{28,24},{1,5},{5... | collective-permute-start | bytes 1769480 | tf_op jit(solution)/shard_map/ppermute | solution.py:22
  416.4 15.4 %collective-permute-start.38 = (bf16[2,192,384]{2,1,0:T(8,128)(2,1)S(1)}, bf16[2,192,384]{2,1,0:T(8,128)(2,1)S(1)}, u32[]{:S(2)}, u32[]{:S(2)}) collective-permute-start(bf16[2,192,384]{2,1,0:T(8,128)(2,1)S(1)} %get-tuple-element.337), channel_id=1, source_target_pairs={{0,8},{4,12},{8,0},{12,4},{16,24},{20,28},{24,16},{28,20},{1,9},{5... | collective-permute-start | bytes 884744 | tf_op jit(solution)/shard_map/ppermute | solution.py:22
  431.7 12.5 %collective-permute-start.44 = (bf16[2,192,384]{2,1,0:T(8,128)(2,1)S(1)}, bf16[2,192,384]{2,1,0:T(8,128)(2,1)S(1)}, u32[]{:S(2)}, u32[]{:S(2)}) collective-permute-start(bf16[2,192,384]{2,1,0:T(8,128)(2,1)S(1)} %get-tuple-element.334), channel_id=1, source_target_pairs={{0,8},{4,12},{8,0},{12,4},{16,24},{20,28},{24,16},{28,20},{1,9},{5... | collective-permute-start | bytes 884744 | tf_op jit(solution)/shard_map/ppermute | solution.py:22
  431.8 12.4 %collective-permute-start.43 = (bf16[192,384]{1,0:T(8,128)(2,1)S(1)}, bf16[192,384]{1,0:T(8,128)(2,1)S(1)}, u32[]{:S(2)}, u32[]{:S(2)}) collective-permute-start(bf16[192,384]{1,0:T(8,128)(2,1)S(1)} %fusion.69), channel_id=1, source_target_pairs={{0,16},{4,20},{8,24},{12,28},{16,0},{20,4},{24,8},{28,12},{1,17},{... | collective-permute-start | bytes 442376 | tf_op jit(solution)/shard_map/ppermute | solution.py:22
  444.2 30.7 %copy-start.21 = (bf16[2,192,384]{2,1,0:T(8,128)(2,1)}, bf16[2,192,384]{2,1,0:T(8,128)(2,1)S(1)}, u32[]{:S(2)}) copy-start(bf16[2,192,384]{2,1,0:T(8,128)(2,1)S(1)} %collective-permute-done.44) | copy-start | bytes 884740
  445.0 105.1 %all-gather.24.cloned.1.call-start = ((), (), s32[]{:S(2)}) async-start(), calls=%async_computation.4 | async-start | bytes 1327104 | tf_op jit(solution)/shard_map/all_gather | solution.py:479
  445.1 29.8 %collective-permute-start.36 = (bf16[2,2,2,208,384]{4,3,2,1,0:T(8,128)(2,1)}, bf16[2,2,2,208,384]{4,3,2,1,0:T(8,128)(2,1)S(1)}, u32[]{:S(2)}, u32[]{:S(2)}) collective-permute-start(bf16[2,2,2,208,384]{4,3,2,1,0:T(8,128)(2,1)} %get-tuple-element.305), channel_id=1, source_target_pairs={{0,2},{1,3},{2,0},{3,1},{4,6},{5,7},{6,4},{7,5},{8,10},{9,11},{10,... | collective-permute-start | bytes 3833864 | tf_op jit(solution)/shard_map/ppermute | solution.py:22
  446.6 28.6 %collective-permute-start.48 = (bf16[192,384]{1,0:T(8,128)(2,1)S(1)}, bf16[192,384]{1,0:T(8,128)(2,1)S(1)}, u32[]{:S(2)}, u32[]{:S(2)}) collective-permute-start(bf16[192,384]{1,0:T(8,128)(2,1)S(1)} %fusion.70), channel_id=1, source_target_pairs={{0,16},{4,20},{8,24},{12,28},{16,0},{20,4},{24,8},{28,12},{1,17},{... | collective-permute-start | bytes 442376 | tf_op jit(solution)/shard_map/ppermute | solution.py:22
  476.6 116.3 %all-gather.20.cloned.1.call-start = ((), (), s32[]{:S(2)}) async-start(), calls=%async_computation.2 | async-start | bytes 1437696 | tf_op jit(solution)/shard_map/all_gather | solution.py:479
  476.6 17.3 %collective-permute-start.45 = (bf16[2,2,208,384]{3,2,1,0:T(8,128)(2,1)S(1)}, bf16[2,2,208,384]{3,2,1,0:T(8,128)(2,1)S(1)}, u32[]{:S(2)}, u32[]{:S(2)}) collective-permute-start(bf16[2,2,208,384]{3,2,1,0:T(8,128)(2,1)S(1)} %get-tuple-element.318), channel_id=1, source_target_pairs={{0,4},{4,0},{8,12},{12,8},{16,20},{20,16},{24,28},{28,24},{1,5},{5... | collective-permute-start | bytes 1916936 | tf_op jit(solution)/shard_map/ppermute | solution.py:22
  494.2 12.6 %collective-permute-start.46 = (bf16[2,208,384]{2,1,0:T(8,128)(2,1)S(1)}, bf16[2,208,384]{2,1,0:T(8,128)(2,1)S(1)}, u32[]{:S(2)}, u32[]{:S(2)}) collective-permute-start(bf16[2,208,384]{2,1,0:T(8,128)(2,1)S(1)} %get-tuple-element.331), channel_id=1, source_target_pairs={{0,8},{4,12},{8,0},{12,4},{16,24},{20,28},{24,16},{28,20},{1,9},{5... | collective-permute-start | bytes 958472 | tf_op jit(solution)/shard_map/ppermute | solution.py:22
  506.8 7.8 %collective-permute-start.47 = (bf16[208,384]{1,0:T(8,128)(2,1)S(1)}, bf16[208,384]{1,0:T(8,128)(2,1)S(1)}, u32[]{:S(2)}, u32[]{:S(2)}) collective-permute-start(bf16[208,384]{1,0:T(8,128)(2,1)S(1)} %fusion.61), channel_id=1, source_target_pairs={{0,16},{4,20},{8,24},{12,28},{16,0},{20,4},{24,8},{28,12},{1,17},{... | collective-permute-start | bytes 479240 | tf_op jit(solution)/shard_map/ppermute | solution.py:22
  (21 other events, 105.1 us)
Sparse Core Ops, SparseCore 0:
  10.7 48.4 all-gather.15
  60.8 58.9 all-gather.17
  313.8 45.4 all-gather.29
  361.3 42.7 all-gather.25
  414.7 47.7 all-gather.21
  464.6 42.4 all-gather.27
  509.2 40.8 all-gather.23
  552.3 40.5 all-gather.19
